TPU v7x, 32 devices: a whole 2x2x4 slice. The times are simulated.
32 devices in a mesh: row: 2 (over y), col: 8 (over z, x), leaf: 2 (over core).
Axes of the slice: x: 2, y: 2, z: 4, core: 2. Of those that a mesh axis runs over, the one named last changes fastest.
Arguments:
- front: float32 [4096, 8192], P('row', ('col', 'leaf')), may hold values from -6 to 6
- child: float32 [4096, 8192], P(('row', 'col', 'leaf')), may hold values from -6 to 6
- row_map: int32 [2, 8], P('row'), may hold values from 0 to 7, each once within a row
- col_map: int32 [32], replicated, may hold values from 0 to 31, each once
- x_fac: float32 [16, 16384], P('row', ('col', 'leaf')), may hold values from -0.75 to 0.75
- w_fac: float32 [16, 16384], P('row', ('col', 'leaf')), may hold values from -0.375 to 0.375
- v_fac: float32 [32, 16384], P(('col', 'leaf'), 'row'), may hold values from -6 to 6
- z_fac: float32 [32, 16384], P(('col', 'leaf'), 'row'), may hold values from -0.75 to 0.75
- dinv: float32 [256, 256], replicated, may hold values from -0.375 to 0.375
- pivots: int32 [256], replicated, may hold values from 0 to 255, each once
- rank_rows: int32 [16], P('row'), may hold values from 16 to 64
- rank_cols: int32 [32], P(('col', 'leaf')), may hold values from 16 to 64
- admissible: int32 [16, 32], P('row', ('col', 'leaf')), may hold values 0 or 1
Outputs:
- updated: float32 [4096, 8192], P('row', ('col', 'leaf'))
Inputs may be any that keep to these rules, and one draw needn't show every extreme that they name: Each row of row_map orders the 8 tile rows of one group; col_map orders all 32 tile columns. `pivots`: A permutation of the panel's columns.
All inputs are finite; a program needn't handle non-finite values. No bound on the sum of `admissible` on one device may be relied on, other than what follows from the above.
Results may differ from a plain program's by a relative error of at most 0.0003.
Values sent between devices are 32-bit elements; how exact they have to be, the bound alone decides.
No kernel may reach another device: no remote copies, remote signals or barrier semaphores. Data moves between devices by JAX's collectives and lax.ppermute only.
A program may use at most 128 MiB of HBM per device.

v0:
```python
import functools

import jax
import jax.numpy as jnp
import numpy as np
from jax import lax
from jax.experimental import pallas as pl
from jax.experimental.pallas import tpu as pltpu
from jax.sharding import PartitionSpec as P

RMAX = 64
LANES = 128
NEAR = 4
WINDOW = 5
GROUP = ("col", "leaf")
HIGHEST = lax.Precision.HIGHEST
MIB = 1 << 20


def group_index():
    return lax.axis_index("col") * lax.axis_size("leaf") + lax.axis_index("leaf")


def in_hbm(array):
    return pltpu.with_memory_space_constraint(array, pltpu.HBM)


def place_kernel(tiles, tile, col_tiles, col_map, child, *rest):
    pieces = rest[: tiles // col_tiles]
    inverse, sem = rest[tiles // col_tiles :]
    me = group_index()
    for b in range(tiles):
        inverse[col_map[b]] = b

    def copy(m, j):
        b = inverse[(me ^ m) * col_tiles + j]
        span = pl.ds(pl.multiple_of(b * tile, tile), tile)
        return pltpu.make_async_copy(child.at[:, span], pieces[m].at[j], sem.at[m, j])

    order = [(m, j) for m in reversed(range(len(pieces))) for j in range(col_tiles)]
    for m, j in order:
        copy(m, j).start()
    for m, j in order:
        copy(m, j).wait()


def in_vmem(array):
    return pltpu.with_memory_space_constraint(array, pltpu.VMEM)


def place(child, col_map, tile, devices):
    rows = child.shape[0]
    tiles = col_map.shape[0]
    col_tiles = tiles // devices
    return pl.pallas_call(
        functools.partial(place_kernel, tiles, tile, col_tiles),
        out_shape=[pltpu.VMEM((col_tiles, rows, tile), child.dtype)] * devices,
        in_specs=[pl.BlockSpec(memory_space=pltpu.SMEM), pl.BlockSpec(memory_space=pltpu.HBM)],
        out_specs=[pl.BlockSpec(memory_space=pltpu.VMEM)] * devices,
        scratch_shapes=[pltpu.SMEM((tiles,), jnp.int32), pltpu.SemaphoreType.DMA((devices, col_tiles))],
        compiler_params=pltpu.CompilerParams(vmem_limit_bytes=2 * MIB),
        cost_estimate=pl.CostEstimate(flops=0, bytes_accessed=2 * child.size * 4, transcendentals=0),
        name="place_child",
    )(in_hbm(col_map), in_hbm(child))


def dot(a, b, contract=((1,), (0,))):
    return lax.dot_general(a, b, (contract, ((), ())), precision=HIGHEST, preferred_element_type=jnp.float32)


def update_kernel(
    parts, halves, per, row_tiles, col_tiles, tile,
    front, dinv, pivots, keep, *rest,
):
    xw = rest[:parts]
    vz = rest[parts : parts + halves]
    out, xs, ts, vs, zs = rest[parts + halves :]
    step = pl.program_id(0)
    chunk = vz[0].shape[1] // tile
    slots = xw[0].shape[0]
    rows = slots * row_tiles

    @pl.when(step == 0)
    def _():
        hot = (lax.broadcasted_iota(jnp.int32, (tile, tile), 0) == pivots[...]).astype(jnp.float32)
        turned = dot(hot, dinv[...])
        zs[...] = jnp.zeros_like(zs)
        for h in range(halves):
            for j in range(col_tiles):
                for p in range(chunk):
                    r = j * RMAX + h * chunk + p
                    span = pl.ds(p * tile, tile)
                    vs[pl.ds(r, 1), :] = vz[h][pl.ds(j, 1), span]
                    zs[pl.ds(r, 1), pl.ds(j * tile, tile)] = vz[h][pl.ds(col_tiles + j, 1), span]
        dv = dot(turned, vs[...], ((1,), (1,)))
        for q in range(per):
            span = pl.ds(q * tile, tile)
            for n in range(parts):
                at = pl.ds((q * parts + n) * rows, rows)
                left = xw[n][:, :row_tiles, span].reshape(rows, tile)
                for g in range(tile // LANES):
                    xs[g, at, :] = left[:, g * LANES : (g + 1) * LANES]
                core = dot(xw[n][:, row_tiles:, span].reshape(rows, tile), dv)
                kept = jnp.where(keep[at, :] > 0, core, 0.0)
                right = dot(kept, zs[...])
                for g in range(right.shape[1] // LANES):
                    ts[g, at, :] = right[:, g * LANES : (g + 1) * LANES]

    mine = pl.ds(step, RMAX, stride=row_tiles)
    left = jnp.concatenate([xs[g, mine, :] for g in range(xs.shape[0])], axis=1)
    right = jnp.concatenate([ts[g, mine, :] for g in range(ts.shape[0])], axis=1)
    out[...] = front[...] - dot(left, right, ((0,), (0,)))


def subtract_update(front, dinv, pivots, keep, xw, vz):
    tile = dinv.shape[0]
    row_tiles = front.shape[0] // tile
    width = front.shape[1]
    col_tiles = width // tile
    per = xw[0].shape[2] // tile
    total = RMAX * row_tiles

    def whole(array):
        return pl.BlockSpec(array.shape, lambda i: (0,) * array.ndim)

    block = pl.BlockSpec((tile, width), lambda i: (i, 0))
    pivots = pivots.reshape(1, tile)
    return pl.pallas_call(
        functools.partial(update_kernel, len(xw), len(vz), per, row_tiles, col_tiles, tile),
        grid=(row_tiles,),
        out_shape=pltpu.VMEM(front.shape, front.dtype),
        in_specs=[block, whole(dinv), whole(pivots), whole(keep)] + [whole(a) for a in xw] + [whole(a) for a in vz],
        out_specs=block,
        scratch_shapes=[
            pltpu.VMEM((tile // LANES, total, LANES), jnp.float32),
            pltpu.VMEM((width // LANES, total, LANES), jnp.float32),
            pltpu.VMEM((col_tiles * RMAX, tile), jnp.float32),
            pltpu.VMEM((col_tiles * RMAX, width), jnp.float32),
        ],
        compiler_params=pltpu.CompilerParams(vmem_limit_bytes=24 * MIB),
        cost_estimate=pl.CostEstimate(flops=2 * front.size * 256, bytes_accessed=2 * front.size * 4, transcendentals=0),
        name="front_less_update",
    )(in_hbm(front), dinv, pivots, keep, *xw, *vz)


def add_kernel(members, tile, row_map, base, *rest):
    arrived = rest[: len(members)]
    out, held, sem = rest[-3:]
    me = group_index()
    col_tiles, rows, _ = arrived[0].shape
    per_tile = tile // rows

    def at(n):
        source = me ^ members[n]
        low = row_map[0, source // per_tile] * tile + source % per_tile * rows
        return pl.ds(pl.multiple_of(low, rows), rows)

    def store(n):
        return pltpu.make_async_copy(held.at[n], out.at[at(n), :], sem.at[n])

    for n in range(len(members)):
        for j in range(col_tiles):
            span = pl.ds(j * tile, tile)
            held[n, :, span] = base[at(n), span] + arrived[n][j]
        store(n).start()
    for n in range(len(members)):
        store(n).wait()


def add_child(out, base, arrived, members, row_map, tile):
    rows = arrived[0].shape[1]
    inner = pl.BlockSpec(memory_space=pltpu.VMEM)
    outer = pl.BlockSpec(memory_space=pltpu.HBM)
    size = len(members) * rows * base.shape[1]
    before = [] if out is None else [out]
    return pl.pallas_call(
        functools.partial(add_kernel, members, tile),
        out_shape=pltpu.HBM(base.shape, base.dtype),
        in_specs=[pl.BlockSpec(memory_space=pltpu.SMEM)] + [inner] * (1 + len(members)) + [outer] * len(before),
        out_specs=outer,
        scratch_shapes=[
            pltpu.VMEM((len(members), rows, base.shape[1]), base.dtype),
            pltpu.SemaphoreType.DMA((len(members),)),
        ],
        input_output_aliases={2 + len(members): 0} if before else {},
        compiler_params=pltpu.CompilerParams(vmem_limit_bytes=16 * MIB),
        cost_estimate=pl.CostEstimate(flops=size, bytes_accessed=size * 4, transcendentals=0),
        name="add_child",
    )(in_hbm(row_map), in_vmem(base), *[in_vmem(piece) for piece in arrived], *before)


class Sender:
    def __init__(self):
        self.arrived = []

    def send(self, array, axes, m):
        spot = len(self.arrived) - WINDOW
        if spot >= 0:
            array, self.arrived[spot] = lax.optimization_barrier((array, self.arrived[spot]))
        size = int(np.prod([lax.axis_size(axis) for axis in axes]))
        self.arrived.append(lax.ppermute(array, axes, [(d, d ^ m) for d in range(size)]))
        return len(self.arrived) - 1


def on_device(
    front,
    child,
    row_map,
    col_map,
    x_fac,
    w_fac,
    v_fac,
    z_fac,
    dinv,
    pivots,
    rank_rows,
    rank_cols,
    admissible,
):
    tile = dinv.shape[0]
    row_tiles = front.shape[0] // tile
    col_tiles = front.shape[1] // tile
    devices = lax.axis_size("col") * lax.axis_size("leaf")
    per = x_fac.shape[1] // tile
    chunk = v_fac.shape[1] // tile

    sender = Sender()
    mine = jnp.pad(x_fac, ((0, row_tiles), (0, 0))) + jnp.pad(w_fac, ((row_tiles, 0), (0, 0)))
    mine, child = lax.optimization_barrier((mine, child))
    line = [sender.send(mine, GROUP, m) for m in range(NEAR, devices, NEAR)]
    pieces = place(child, col_map, tile, devices)
    pieces, v_fac, z_fac, rank_rows, rank_cols, admissible = lax.optimization_barrier(
        (pieces, v_fac, z_fac, rank_rows, rank_cols, admissible)
    )

    half = devices // 2
    spots = {}
    crossing = list(reversed(range(half, devices)))
    local = [m for pair in zip(reversed(range(NEAR, half)), [3, 2, 1] + [None] * half) for m in pair if m]
    between = [("xw", m) for m in range(1, NEAR)] + [("vz", m) for m in range(1, lax.axis_size("row"))]
    between += [("child", m) for m in local]
    gaps = len(crossing) - 2
    xw, vz = [None], [None]
    for n, m in enumerate(crossing):
        for i, (kind, other) in enumerate(between):
            if n >= 2 and i * gaps // len(between) == n - 2:
                if kind == "xw":
                    if xw == [None]:
                        xw[0] = jnp.stack([mine] + [sender.arrived[i] for i in line])
                    xw.append(sender.send(xw[0], GROUP, other))
                elif kind == "vz":
                    if vz == [None]:
                        vz[0] = jnp.concatenate([v_fac, z_fac], axis=0)
                    vz.append(sender.send(vz[0], ("row",), other))
                else:
                    spots[other] = sender.send(pieces[other], GROUP, other)
        spots[m] = sender.send(pieces[m], GROUP, m)
    xw = xw[:1] + [sender.arrived[i] for i in xw[1:]]
    vz = vz[:1] + [sender.arrived[i] for i in vz[1:]]
    order = [0] + sorted(spots, key=lambda m: spots[m])
    got = {m: sender.arrived[spots[m]] for m in spots}
    got[0] = pieces[0]

    far = np.arange(0, devices, NEAR, dtype=np.int32)
    source = group_index() ^ (far + np.arange(NEAR, dtype=np.int32)[:, None])
    r = source * per + np.arange(per, dtype=np.int32)[:, None, None]
    source = lax.axis_index("row") ^ np.arange(lax.axis_size("row"), dtype=np.int32)
    s = source[:, None] * chunk + np.arange(chunk, dtype=np.int32)
    keep_rows = r.reshape(RMAX, 1) < rank_rows[None, :]
    keep_cols = s.reshape(1, RMAX) < rank_cols[:, None]
    dense = (admissible == 0)[None, :, :, None]
    keep = (keep_rows[:, :, None, None] & keep_cols[None, None]) | dense
    keep = keep.astype(jnp.float32).reshape(RMAX * row_tiles, col_tiles * RMAX)

    base = subtract_update(front, dinv, pivots, keep, xw, vz)
    out = None
    for members in (order[: half - 1], order[half - 1 : -2], order[-2:]):
        out = add_child(out, base, [got[m] for m in members], members, row_map, tile)
    return out


def solution(mesh):
    return jax.shard_map(
        on_device,
        mesh=mesh,
        in_specs=(
            P("row", GROUP),
            P(("row", "col", "leaf"), None),
            P("row", None),
            P(),
            P("row", GROUP),
            P("row", GROUP),
            P(GROUP, "row"),
            P(GROUP, "row"),
            P(),
            P(),
            P("row"),
            P(GROUP),
            P("row", GROUP),
        ),
        out_specs=P("row", GROUP),
        check_vma=False,
    )
```

profile of v0, /device:TPU:0, one launch (start us, length us, event | category | flops | bytes accessed | tf_op | source)
XLA Modules:
  0.0 114.8 jit_solution(12726395938501666734)
XLA Ops:
  0.0 0.8 pad_add_fusion
  0.8 5.1 %collective-permute-start.2 = (f32[16,1024]{1,0:T(8,128)S(1)}, f32[16,1024]{1,0:T(8,128)S(1)}, u32[]{:S(2)}, u32[]{:S(2)}) collective-permute-start(f32[16,1024]{1,0:T(8,128)S(1)} %pad_add_fusion), channel_id=1, source_target_pairs={{0,12},{1,13},{2,14},{3,15},{4,8},{5,9},{6,10},{7,11},{8,4},{9,5},... | collective-permute-start | bytes 196616 | tf_op jit(solution)/shard_map/ppermute | solution.py:201
  5.9 0.6 collective-permute-start
  6.5 4.2 %place_child.1 = (f32[2,128,256]{2,1,0:T(8,128)S(1)}, f32[2,128,256]{2,1,0:T(8,128)S(1)}, f32[2,128,256]{2,1,0:T(8,128)S(1)}, f32[2,128,256]{2,1,0:T(8,128)}, f3...) custom-call(s32[32]{0:T(128)} %col_map.1, ...), custom_call_target="tpu_custom_call" | custom-call | bytes 8388608 | tf_op jit(solution)/shard_map/place_child/pallas_call | solution.py:55
  10.8 0.7 copy-done.10
  11.5 0.7 copy-done.11
  12.2 0.7 copy-done.12
  12.9 0.7 copy-done.13
  13.6 0.7 copy-done.14
  14.3 0.7 copy-done.15
  15.0 3.3 %collective-permute-start.5 = (f32[2,128,256]{2,1,0:T(8,128)S(1)}, f32[2,128,256]{2,1,0:T(8,128)S(1)}, u32[]{:S(2)}, u32[]{:S(2)}) collective-permute-start(f32[2,128,256]{2,1,0:T(8,128)S(1)} %get-tuple-element.103), channel_id=1, source_target_pairs={{0,15},{1,14},{2,13},{3,12},{4,11},{5,10},{6,9},{7,8},{8,7},{9,6},... | collective-permute-start | bytes 786440 | tf_op jit(solution)/shard_map/ppermute | solution.py:201
  18.2 1.4 %collective-permute-start.7 = (f32[2,128,256]{2,1,0:T(8,128)S(1)}, f32[2,128,256]{2,1,0:T(8,128)S(1)}, u32[]{:S(2)}, u32[]{:S(2)}) collective-permute-start(f32[2,128,256]{2,1,0:T(8,128)S(1)} %get-tuple-element.109), channel_id=1, source_target_pairs={{0,14},{1,15},{2,12},{3,13},{4,10},{5,11},{6,8},{7,9},{8,6},{9,7},... | collective-permute-start | bytes 786440 | tf_op jit(solution)/shard_map/ppermute | solution.py:201
  19.7 0.0 collective-permute-done.2
  19.7 0.0 collective-permute-done.1
  19.7 0.2 collective-permute-start.3
  19.9 1.4 %collective-permute-start.4 = (f32[4,16,1024]{2,1,0:T(8,128)S(1)}, f32[4,16,1024]{2,1,0:T(8,128)S(1)}, u32[]{:S(2)}, u32[]{:S(2)}) collective-permute-start(f32[4,16,1024]{2,1,0:T(8,128)S(1)} %pad_maximum_fusion.rest_0_), channel_id=1, source_target_pairs={{0,2},{1,3},{2,0},{3,1},{4,6},{5,7},{6,4},{7,5},{8,10},{9,11},{10,... | collective-permute-start | bytes 786440 | tf_op jit(solution)/shard_map/ppermute | solution.py:201
  21.3 0.1 pad_maximum_fusion.1.rest_4_
  21.4 3.1 %collective-permute-start.17 = (f32[2,128,256]{2,1,0:T(8,128)S(1)}, f32[2,128,256]{2,1,0:T(8,128)S(1)}, u32[]{:S(2)}, u32[]{:S(2)}) collective-permute-start(f32[2,128,256]{2,1,0:T(8,128)S(1)} %get-tuple-element.133), channel_id=1, source_target_pairs={{0,13},{1,12},{2,15},{3,14},{4,9},{5,8},{6,11},{7,10},{8,5},{9,4},... | collective-permute-start | bytes 786440 | tf_op jit(solution)/shard_map/ppermute | solution.py:201
  24.4 1.6 %collective-permute-done.5.rest_1_ = f32[2,128,256]{2,1,0:T(8,128)S(1)} collective-permute-done((f32[2,128,256]{2,1,0:T(8,128)S(1)}, f32[2,128,256]{2,1,0:T(8,128)S(1)}, u32[]{:S(2)}, u32[]{:S(2)}) %collective-permute-start.5) | collective-permute-done | bytes 262176 | tf_op jit(solution)/shard_map/ppermute | solution.py:201
  26.0 0.6 collective-permute-start.6
  26.6 5.9 %collective-permute-done.7.rest_2_ = f32[2,128,256]{2,1,0:T(8,128)S(1)} collective-permute-done((f32[2,128,256]{2,1,0:T(8,128)S(1)}, f32[2,128,256]{2,1,0:T(8,128)S(1)}, u32[]{:S(2)}, u32[]{:S(2)}) %collective-permute-start.7) | collective-permute-done | bytes 262176 | tf_op jit(solution)/shard_map/ppermute | solution.py:201
  32.5 1.5 %collective-permute-start.8 = (f32[4,8192]{1,0:T(4,128)S(1)}, f32[4,8192]{1,0:T(4,128)S(1)}, u32[]{:S(2)}, u32[]{:S(2)}) collective-permute-start(f32[4,8192]{1,0:T(4,128)S(1)} %pad_maximum_fusion.1.rest_4_), channel_id=1, source_target_pairs={{0,16},{16,0},{1,17},{17,1},{2,18},{18,2},{3,19},{19,3},{4,20},{20... | collective-permute-start | bytes 393224 | tf_op jit(solution)/shard_map/ppermute | solution.py:201
  34.0 0.7 copy-done.1
  34.7 2.9 %collective-permute-done.4.rest_2_ = f32[4,16,1024]{2,1,0:T(8,128)S(1)} collective-permute-done((f32[4,16,1024]{2,1,0:T(8,128)S(1)}, f32[4,16,1024]{2,1,0:T(8,128)S(1)}, u32[]{:S(2)}, u32[]{:S(2)}) %collective-permute-start.4) | collective-permute-done | bytes 262176 | tf_op jit(solution)/shard_map/ppermute | solution.py:201
  37.7 0.7 copy-done.3
  38.4 13.0 %collective-permute-start.12 = (f32[2,128,256]{2,1,0:T(8,128)S(1)}, f32[2,128,256]{2,1,0:T(8,128)S(1)}, u32[]{:S(2)}, u32[]{:S(2)}) collective-permute-start(f32[2,128,256]{2,1,0:T(8,128)S(1)} %get-tuple-element.119), channel_id=1, source_target_pairs={{0,7},{1,6},{2,5},{3,4},{4,3},{5,2},{6,1},{7,0},{8,15},{9,14},{10,... | collective-permute-start | bytes 786440 | tf_op jit(solution)/shard_map/ppermute | solution.py:201
  51.3 2.4 %collective-permute-start.9 = (f32[2,128,256]{2,1,0:T(8,128)S(1)}, f32[2,128,256]{2,1,0:T(8,128)S(1)}, u32[]{:S(2)}, u32[]{:S(2)}) collective-permute-start(f32[2,128,256]{2,1,0:T(8,128)S(1)} %get-tuple-element.114), channel_id=1, source_target_pairs={{0,12},{1,13},{2,14},{3,15},{4,8},{5,9},{6,10},{7,11},{8,4},{9,5},... | collective-permute-start | bytes 786440 | tf_op jit(solution)/shard_map/ppermute | solution.py:201
  53.7 0.1 collective-permute-start.18
  53.8 0.6 copy-done.7
  54.4 0.7 collective-permute-start.16
  55.1 0.7 copy-done.5
  55.8 2.5 %collective-permute-start.15 = (f32[2,128,256]{2,1,0:T(8,128)}, f32[2,128,256]{2,1,0:T(8,128)S(1)}, u32[]{:S(2)}, u32[]{:S(2)}) collective-permute-start(f32[2,128,256]{2,1,0:T(8,128)} %get-tuple-element.123), channel_id=1, source_target_pairs={{0,11},{1,10},{2,9},{3,8},{4,15},{5,14},{6,13},{7,12},{8,3},{9,2},... | collective-permute-start | bytes 786440 | tf_op jit(solution)/shard_map/ppermute | solution.py:201
  58.3 2.9 %collective-permute-start.13 = (f32[2,128,256]{2,1,0:T(8,128)}, f32[2,128,256]{2,1,0:T(8,128)S(1)}, u32[]{:S(2)}, u32[]{:S(2)}) collective-permute-start(f32[2,128,256]{2,1,0:T(8,128)} %get-tuple-element.120), channel_id=1, source_target_pairs={{0,10},{1,11},{2,8},{3,9},{4,14},{5,15},{6,12},{7,13},{8,2},{9,3},... | collective-permute-start | bytes 786440 | tf_op jit(solution)/shard_map/ppermute | solution.py:201
  61.2 5.4 %collective-permute-done.9.rest_4_ = f32[2,128,256]{2,1,0:T(8,128)S(1)} collective-permute-done((f32[2,128,256]{2,1,0:T(8,128)S(1)}, f32[2,128,256]{2,1,0:T(8,128)S(1)}, u32[]{:S(2)}, u32[]{:S(2)}) %collective-permute-start.9) | collective-permute-done | bytes 262176 | tf_op jit(solution)/shard_map/ppermute | solution.py:201
  66.6 0.5 collective-permute-start.10
  67.1 0.1 iota_add_fusion.1
  67.2 0.6 add.62
  67.8 0.7 lt.47
  68.5 0.6 lt.48
  69.1 0.1 add.57
  69.2 0.7 lt.42
  69.9 0.8 lt.43
  70.7 0.7 broadcast_compare_fusion
  71.4 0.1 copy.21
  71.5 0.7 lt.49
  72.2 0.6 lt.50
  72.8 1.3 %lt.44 = s32[64,1,8]{2,0,1:T(8,128)} broadcast(s32[8]{0:T(128)} %param.27), dimensions={2} | broadcast | bytes 2080 | tf_op jit(solution)/shard_map/lt | solution.py:269
  74.1 0.8 lt.45
  74.9 0.9 or.11
  75.8 2.0 %or.12 = pred[512,128]{1,0:T(8,128)(4,1)} reshape(pred[64,8,2,64]{3,2,1,0:T(4,128)(4,1)} %or.11) | data formatting | bytes 131072 | tf_op jit(solution)/shard_map/or | solution.py:272
  77.8 0.6 lt.51
  78.5 0.1 collective-permute-start.19
  78.6 2.1 %collective-permute-start.21 = (f32[2,128,256]{2,1,0:T(8,128)}, f32[2,128,256]{2,1,0:T(8,128)S(1)}, u32[]{:S(2)}, u32[]{:S(2)}) collective-permute-start(f32[2,128,256]{2,1,0:T(8,128)} %copy-done.13), channel_id=1, source_target_pairs={{0,9},{1,8},{2,11},{3,10},{4,13},{5,12},{6,15},{7,14},{8,1},{9,0},... | collective-permute-start | bytes 786440 | tf_op jit(solution)/shard_map/ppermute | solution.py:201
  80.7 8.5 %collective-permute-done.13.rest_3_ = f32[2,128,256]{2,1,0:T(8,128)S(1)} collective-permute-done((f32[2,128,256]{2,1,0:T(8,128)}, f32[2,128,256]{2,1,0:T(8,128)S(1)}, u32[]{:S(2)}, u32[]{:S(2)}) %collective-permute-start.13) | collective-permute-done | bytes 262176 | tf_op jit(solution)/shard_map/ppermute | solution.py:201
  89.1 2.4 %collective-permute-start.11 = (f32[2,128,256]{2,1,0:T(8,128)}, f32[2,128,256]{2,1,0:T(8,128)S(1)}, u32[]{:S(2)}, u32[]{:S(2)}) collective-permute-start(f32[2,128,256]{2,1,0:T(8,128)} %copy-done.10), channel_id=1, source_target_pairs={{0,4},{1,5},{2,6},{3,7},{4,0},{5,1},{6,2},{7,3},{8,12},{9,13},{10,... | collective-permute-start | bytes 786440 | tf_op jit(solution)/shard_map/ppermute | solution.py:201
  91.6 1.0 or_convert_fusion.keep
  92.6 0.9 copy-done.2
  93.5 0.9 copy-done.4
  94.5 0.9 copy-done.6
  95.4 0.9 copy-done.8
  96.3 12.9 %front_less_update.1.base = f32[2048,512]{1,0:T(8,128)S(1)} custom-call(f32[2048,512]{1,0:T(8,128)} %front.1, f32[256,256]{1,0:T(8,128)S(1)} %copy-done, s32[1,256]{1,0:T(1,128)S(1)} %bitcast.9, f32[512,128]{1,0:T(8,128)S(1)} %or_convert_fusion.keep, f32[4,16,1024]{2,1,0:T(8,128)S(1)} %pad_maximum_fusion.rest_0_, f32[4,16,1024]{2,1,0:T(8,128)S(1)} %copy-done.2, ...), custom_call_target="tpu_custom_call" | custom-call | flops 536870912 | bytes 8388608 | tf_op jit(solution)/shard_map/front_less_update/pallas_call | solution.py:128
  109.3 2.0 %add_child.3.rest_7_ = f32[2048,512]{1,0:T(8,128)} custom-call(s32[1,8]{1,0:T(1,128)} %row_map.5, f32[2048,512]{1,0:T(8,128)S(1)} %front_less_update.1.base, f32[2,128,256]{2,1,0:T(8,128)S(1)} %get-tuple-element.138.rest_0_, f32[2,128,256]{2,1,0:T(8,128)S(1)} %collective-permute-done.5.rest_1_, f32[2,128,256]{2,1,0:T(8,128)S(1)} %collective-permute-done.7.rest_2_, ...), custom_call_target="tpu_custom_call" | custom-call | flops 458752 | bytes 1835008 | tf_op jit(solution)/shard_map/add_child/pallas_call | solution.py:176
  111.3 2.0 %add_child.4.rest_2_ = f32[2048,512]{1,0:T(8,128)} custom-call(s32[1,8]{1,0:T(1,128)} %row_map.5, f32[2048,512]{1,0:T(8,128)S(1)} %front_less_update.1.base, f32[2,128,256]{2,1,0:T(8,128)S(1)} %collective-permute-done.15.rest_0_, f32[2,128,256]{2,1,0:T(8,128)S(1)} %collective-permute-done.16.rest_1_, ...), custom_call_target="tpu_custom_call", output_to_operand_aliasing={{}: (9, {})} | custom-call | flops 458752 | bytes 1835008 | tf_op jit(solution)/shard_map/add_child/pallas_call | solution.py:176
  113.3 1.5 %add_child.5 = f32[2048,512]{1,0:T(8,128)} custom-call(s32[1,8]{1,0:T(1,128)} %row_map.5, f32[2048,512]{1,0:T(8,128)S(1)} %front_less_update.1.base, f32[2,128,256]{2,1,0:T(8,128)S(1)} %collective-permute-done.11.rest_0_, f32[2,128,256]{2,1,0:T(8,128)S(1)} %collective-permute-done.14.rest_1_, ...), custom_call_target="tpu_custom_call", output_to_operand_aliasing={{}: (4, {})} | custom-call | flops 131072 | bytes 524288 | tf_op jit(solution)/shard_map/add_child/pallas_call | solution.py:176
  (47 shorter events, 0.1 us)
Async XLA Ops:
  0.0 21.4 %copy-start.18 = (s32[4,4]{1,0:T(4,128)S(1)}, s32[4,4]{1,0:T(4,128)}, u32[]{:S(2)}) copy-start(s32[4,4]{1,0:T(4,128)} %constant.31.clone) | copy-start | bytes 196
  0.0 21.3 %copy-start.16 = (f32[2,8192]{1,0:T(2,128)S(1)}, f32[2,8192]{1,0:T(2,128)}, u32[]{:S(2)}) copy-start(f32[2,8192]{1,0:T(2,128)} %param.24) | copy-start | bytes 196612
  0.0 21.3 %copy-start.17 = (f32[2,8192]{1,0:T(2,128)S(1)}, f32[2,8192]{1,0:T(2,128)}, u32[]{:S(2)}) copy-start(f32[2,8192]{1,0:T(2,128)} %param.23) | copy-start | bytes 196612
  0.0 92.5 %copy-start.9 = (s32[256]{0:T(256)S(1)}, s32[256]{0:T(256)}, u32[]{:S(2)}) copy-start(s32[256]{0:T(256)} %param.26) | copy-start | bytes 3076
  0.0 92.6 %copy-start = (f32[256,256]{1,0:T(8,128)S(1)}, f32[256,256]{1,0:T(8,128)}, u32[]{:S(2)}) copy-start(f32[256,256]{1,0:T(8,128)} %dinv.1) | copy-start | bytes 786436
  0.8 18.8 %collective-permute-start.2 = (f32[16,1024]{1,0:T(8,128)S(1)}, f32[16,1024]{1,0:T(8,128)S(1)}, u32[]{:S(2)}, u32[]{:S(2)}) collective-permute-start(f32[16,1024]{1,0:T(8,128)S(1)} %pad_add_fusion), channel_id=1, source_target_pairs={{0,12},{1,13},{2,14},{3,15},{4,8},{5,9},{6,10},{7,11},{8,4},{9,5},... | collective-permute-start | bytes 196616 | tf_op jit(solution)/shard_map/ppermute | solution.py:201
  5.9 13.8 %collective-permute-start.1 = (f32[16,1024]{1,0:T(8,128)S(1)}, f32[16,1024]{1,0:T(8,128)S(1)}, u32[]{:S(2)}, u32[]{:S(2)}) collective-permute-start(f32[16,1024]{1,0:T(8,128)S(1)} %pad_add_fusion), channel_id=1, source_target_pairs={{0,8},{1,9},{2,10},{3,11},{4,12},{5,13},{6,14},{7,15},{8,0},{9,1},... | collective-permute-start | bytes 196616 | tf_op jit(solution)/shard_map/ppermute | solution.py:201
  5.9 13.8 %collective-permute-start = (f32[16,1024]{1,0:T(8,128)S(1)}, f32[16,1024]{1,0:T(8,128)S(1)}, u32[]{:S(2)}, u32[]{:S(2)}) collective-permute-start(f32[16,1024]{1,0:T(8,128)S(1)} %pad_add_fusion), channel_id=1, source_target_pairs={{0,4},{1,5},{2,6},{3,7},{4,0},{5,1},{6,2},{7,3},{8,12},{9,13},{10,... | collective-permute-start | bytes 196616 | tf_op jit(solution)/shard_map/ppermute | solution.py:201
  10.8 0.7 copy-start.10
  11.5 0.7 copy-start.11
  12.2 0.7 copy-start.12
  12.9 0.7 copy-start.13
  13.6 0.7 copy-start.14
  14.3 0.7 copy-start.15
  15.0 11.0 %collective-permute-start.5 = (f32[2,128,256]{2,1,0:T(8,128)S(1)}, f32[2,128,256]{2,1,0:T(8,128)S(1)}, u32[]{:S(2)}, u32[]{:S(2)}) collective-permute-start(f32[2,128,256]{2,1,0:T(8,128)S(1)} %get-tuple-element.103), channel_id=1, source_target_pairs={{0,15},{1,14},{2,13},{3,12},{4,11},{5,10},{6,9},{7,8},{8,7},{9,6},... | collective-permute-start | bytes 786440 | tf_op jit(solution)/shard_map/ppermute | solution.py:201
  18.2 14.3 %collective-permute-start.7 = (f32[2,128,256]{2,1,0:T(8,128)S(1)}, f32[2,128,256]{2,1,0:T(8,128)S(1)}, u32[]{:S(2)}, u32[]{:S(2)}) collective-permute-start(f32[2,128,256]{2,1,0:T(8,128)S(1)} %get-tuple-element.109), channel_id=1, source_target_pairs={{0,14},{1,15},{2,12},{3,13},{4,10},{5,11},{6,8},{7,9},{8,6},{9,7},... | collective-permute-start | bytes 786440 | tf_op jit(solution)/shard_map/ppermute | solution.py:201
  19.7 14.3 %collective-permute-start.3 = (f32[4,16,1024]{2,1,0:T(8,128)S(1)}, f32[4,16,1024]{2,1,0:T(8,128)S(1)}, u32[]{:S(2)}, u32[]{:S(2)}) collective-permute-start(f32[4,16,1024]{2,1,0:T(8,128)S(1)} %pad_maximum_fusion.rest_0_), channel_id=1, source_target_pairs={{0,1},{1,0},{2,3},{3,2},{4,5},{5,4},{6,7},{7,6},{8,9},{9,8},{10,11... | collective-permute-start | bytes 786440 | tf_op jit(solution)/shard_map/ppermute | solution.py:201
  19.9 17.8 %collective-permute-start.4 = (f32[4,16,1024]{2,1,0:T(8,128)S(1)}, f32[4,16,1024]{2,1,0:T(8,128)S(1)}, u32[]{:S(2)}, u32[]{:S(2)}) collective-permute-start(f32[4,16,1024]{2,1,0:T(8,128)S(1)} %pad_maximum_fusion.rest_0_), channel_id=1, source_target_pairs={{0,2},{1,3},{2,0},{3,1},{4,6},{5,7},{6,4},{7,5},{8,10},{9,11},{10,... | collective-permute-start | bytes 786440 | tf_op jit(solution)/shard_map/ppermute | solution.py:201
  21.4 32.3 %collective-permute-start.17 = (f32[2,128,256]{2,1,0:T(8,128)S(1)}, f32[2,128,256]{2,1,0:T(8,128)S(1)}, u32[]{:S(2)}, u32[]{:S(2)}) collective-permute-start(f32[2,128,256]{2,1,0:T(8,128)S(1)} %get-tuple-element.133), channel_id=1, source_target_pairs={{0,13},{1,12},{2,15},{3,14},{4,9},{5,8},{6,11},{7,10},{8,5},{9,4},... | collective-permute-start | bytes 786440 | tf_op jit(solution)/shard_map/ppermute | solution.py:201
  26.0 29.1 %collective-permute-start.6 = (f32[4,16,1024]{2,1,0:T(8,128)S(1)}, f32[4,16,1024]{2,1,0:T(8,128)S(1)}, u32[]{:S(2)}, u32[]{:S(2)}) collective-permute-start(f32[4,16,1024]{2,1,0:T(8,128)S(1)} %pad_maximum_fusion.rest_0_), channel_id=1, source_target_pairs={{0,3},{1,2},{2,1},{3,0},{4,7},{5,6},{6,5},{7,4},{8,11},{9,10},{10,... | collective-permute-start | bytes 786440 | tf_op jit(solution)/shard_map/ppermute | solution.py:201
  32.5 21.3 %collective-permute-start.8 = (f32[4,8192]{1,0:T(4,128)S(1)}, f32[4,8192]{1,0:T(4,128)S(1)}, u32[]{:S(2)}, u32[]{:S(2)}) collective-permute-start(f32[4,8192]{1,0:T(4,128)S(1)} %pad_maximum_fusion.1.rest_4_), channel_id=1, source_target_pairs={{0,16},{16,0},{1,17},{17,1},{2,18},{18,2},{3,19},{19,3},{4,20},{20... | collective-permute-start | bytes 393224 | tf_op jit(solution)/shard_map/ppermute | solution.py:201
  34.0 0.7 copy-start.1
  37.7 0.7 copy-start.3
  38.4 20.0 %collective-permute-start.12 = (f32[2,128,256]{2,1,0:T(8,128)S(1)}, f32[2,128,256]{2,1,0:T(8,128)S(1)}, u32[]{:S(2)}, u32[]{:S(2)}) collective-permute-start(f32[2,128,256]{2,1,0:T(8,128)S(1)} %get-tuple-element.119), channel_id=1, source_target_pairs={{0,7},{1,6},{2,5},{3,4},{4,3},{5,2},{6,1},{7,0},{8,15},{9,14},{10,... | collective-permute-start | bytes 786440 | tf_op jit(solution)/shard_map/ppermute | solution.py:201
  51.3 15.3 %collective-permute-start.9 = (f32[2,128,256]{2,1,0:T(8,128)S(1)}, f32[2,128,256]{2,1,0:T(8,128)S(1)}, u32[]{:S(2)}, u32[]{:S(2)}) collective-permute-start(f32[2,128,256]{2,1,0:T(8,128)S(1)} %get-tuple-element.114), channel_id=1, source_target_pairs={{0,12},{1,13},{2,14},{3,15},{4,8},{5,9},{6,10},{7,11},{8,4},{9,5},... | collective-permute-start | bytes 786440 | tf_op jit(solution)/shard_map/ppermute | solution.py:201
  53.7 24.8 %collective-permute-start.18 = (f32[2,128,256]{2,1,0:T(8,128)}, f32[2,128,256]{2,1,0:T(8,128)S(1)}, u32[]{:S(2)}, u32[]{:S(2)}) collective-permute-start(f32[2,128,256]{2,1,0:T(8,128)} %get-tuple-element.134), channel_id=1, source_target_pairs={{0,3},{1,2},{2,1},{3,0},{4,7},{5,6},{6,5},{7,4},{8,11},{9,10},{10,... | collective-permute-start | bytes 786440 | tf_op jit(solution)/shard_map/ppermute | solution.py:201
  53.8 0.6 copy-start.7
  54.4 24.1 %collective-permute-start.16 = (f32[2,128,256]{2,1,0:T(8,128)}, f32[2,128,256]{2,1,0:T(8,128)S(1)}, u32[]{:S(2)}, u32[]{:S(2)}) collective-permute-start(f32[2,128,256]{2,1,0:T(8,128)} %get-tuple-element.126), channel_id=1, source_target_pairs={{0,6},{1,7},{2,4},{3,5},{4,2},{5,3},{6,0},{7,1},{8,14},{9,15},{10,... | collective-permute-start | bytes 786440 | tf_op jit(solution)/shard_map/ppermute | solution.py:201
  55.1 0.7 copy-start.5
  55.8 24.9 %collective-permute-start.15 = (f32[2,128,256]{2,1,0:T(8,128)}, f32[2,128,256]{2,1,0:T(8,128)S(1)}, u32[]{:S(2)}, u32[]{:S(2)}) collective-permute-start(f32[2,128,256]{2,1,0:T(8,128)} %get-tuple-element.123), channel_id=1, source_target_pairs={{0,11},{1,10},{2,9},{3,8},{4,15},{5,14},{6,13},{7,12},{8,3},{9,2},... | collective-permute-start | bytes 786440 | tf_op jit(solution)/shard_map/ppermute | solution.py:201
  58.3 30.8 %collective-permute-start.13 = (f32[2,128,256]{2,1,0:T(8,128)}, f32[2,128,256]{2,1,0:T(8,128)S(1)}, u32[]{:S(2)}, u32[]{:S(2)}) collective-permute-start(f32[2,128,256]{2,1,0:T(8,128)} %get-tuple-element.120), channel_id=1, source_target_pairs={{0,10},{1,11},{2,8},{3,9},{4,14},{5,15},{6,12},{7,13},{8,2},{9,3},... | collective-permute-start | bytes 786440 | tf_op jit(solution)/shard_map/ppermute | solution.py:201
  66.6 22.5 %collective-permute-start.10 = (f32[2,128,256]{2,1,0:T(8,128)}, f32[2,128,256]{2,1,0:T(8,128)S(1)}, u32[]{:S(2)}, u32[]{:S(2)}) collective-permute-start(f32[2,128,256]{2,1,0:T(8,128)} %copy-done.15), channel_id=1, source_target_pairs={{0,2},{1,3},{2,0},{3,1},{4,6},{5,7},{6,4},{7,5},{8,10},{9,11},{10,... | collective-permute-start | bytes 786440 | tf_op jit(solution)/shard_map/ppermute | solution.py:201
  78.5 32.8 %collective-permute-start.19 = (f32[2,128,256]{2,1,0:T(8,128)}, f32[2,128,256]{2,1,0:T(8,128)S(1)}, u32[]{:S(2)}, u32[]{:S(2)}) collective-permute-start(f32[2,128,256]{2,1,0:T(8,128)} %copy-done.14), channel_id=1, source_target_pairs={{0,5},{1,4},{2,7},{3,6},{4,1},{5,0},{6,3},{7,2},{8,13},{9,12},{10,... | collective-permute-start | bytes 786440 | tf_op jit(solution)/shard_map/ppermute | solution.py:201
  78.6 32.7 %collective-permute-start.21 = (f32[2,128,256]{2,1,0:T(8,128)}, f32[2,128,256]{2,1,0:T(8,128)S(1)}, u32[]{:S(2)}, u32[]{:S(2)}) collective-permute-start(f32[2,128,256]{2,1,0:T(8,128)} %copy-done.13), channel_id=1, source_target_pairs={{0,9},{1,8},{2,11},{3,10},{4,13},{5,12},{6,15},{7,14},{8,1},{9,0},... | collective-permute-start | bytes 786440 | tf_op jit(solution)/shard_map/ppermute | solution.py:201
  80.7 30.6 %collective-permute-start.20 = (f32[2,128,256]{2,1,0:T(8,128)}, f32[2,128,256]{2,1,0:T(8,128)S(1)}, u32[]{:S(2)}, u32[]{:S(2)}) collective-permute-start(f32[2,128,256]{2,1,0:T(8,128)} %copy-done.12), channel_id=1, source_target_pairs={{0,1},{1,0},{2,3},{3,2},{4,5},{5,4},{6,7},{7,6},{8,9},{9,8},{10,11... | collective-permute-start | bytes 786440 | tf_op jit(solution)/shard_map/ppermute | solution.py:201
  89.1 24.2 %collective-permute-start.14 = (f32[2,128,256]{2,1,0:T(8,128)}, f32[2,128,256]{2,1,0:T(8,128)S(1)}, u32[]{:S(2)}, u32[]{:S(2)}) collective-permute-start(f32[2,128,256]{2,1,0:T(8,128)} %copy-done.11), channel_id=1, source_target_pairs={{0,8},{1,9},{2,10},{3,11},{4,12},{5,13},{6,14},{7,15},{8,0},{9,1},... | collective-permute-start | bytes 786440 | tf_op jit(solution)/shard_map/ppermute | solution.py:201
  89.1 24.2 %collective-permute-start.11 = (f32[2,128,256]{2,1,0:T(8,128)}, f32[2,128,256]{2,1,0:T(8,128)S(1)}, u32[]{:S(2)}, u32[]{:S(2)}) collective-permute-start(f32[2,128,256]{2,1,0:T(8,128)} %copy-done.10), channel_id=1, source_target_pairs={{0,4},{1,5},{2,6},{3,7},{4,0},{5,1},{6,2},{7,3},{8,12},{9,13},{10,... | collective-permute-start | bytes 786440 | tf_op jit(solution)/shard_map/ppermute | solution.py:201
  92.6 1.0 copy-start.2
  93.5 0.9 copy-start.4
  94.5 0.9 copy-start.6
  95.4 0.9 copy-start.8
where the time goes:
time: 115 us
  starting transfers between devices  43.7 us (38%)
  waiting for transfers between devices  24.3 us (21%)
  Pallas kernels  22.6 us (20%)
  local copies, waits for them, and re-layouts  20.6 us (18%)
  other arithmetic  3.3 us (3%)
    ppermute x22, starting transfers between devices, send(): lax.ppermute(array, axes, [(d, d ^ m) for d in range(size)])  43.7 us
    ppermute x22, waiting for transfers between devices, send(): lax.ppermute(array, axes, [(d, d ^ m) for d in range(size)])  24.3 us
    pallas_call x1, Pallas kernels, subtract_update(): pl.pallas_call(functools.partial(update_kernel, len(xw), len(vz), per, ro...  12.9 us
    unnamed x38, local copies, waits for them, and re-layouts  10.7 us
    pallas_call x3, Pallas kernels, add_child(): pl.pallas_call(functools.partial(add_kernel, members, tile), out_shape=pl...  5.5 us
    pallas_call x1, Pallas kernels, place(): pl.pallas_call(functools.partial(place_kernel, tiles, tile, col_tiles), o...  4.22 us
    lt x4, local copies, waits for them, and re-layouts, on_device(): keep_rows = r.reshape(RMAX, 1) < rank_rows[None, :]  3.66 us
    or x2, local copies, waits for them, and re-layouts, on_device(): keep = keep_rows[:, :, None, None] & keep_cols[None, None] | dense  2.91 us
  transfers between devices with their start and end apart: 22, of which 5 were waited for; matrix products, arithmetic and copies ran while one was open for 11% of the time, Pallas kernels for 18%

commit v1 on v0

--- a/solution.py
+++ b/solution.py
@@ -68,9 +68,13 @@
     return lax.dot_general(a, b, (contract, ((), ())), precision=HIGHEST, preferred_element_type=jnp.float32)
 
 
+def log2(size):
+    return size.bit_length() - 1
+
+
 def update_kernel(
     parts, halves, per, row_tiles, col_tiles, tile,
-    front, dinv, pivots, keep, *rest,
+    front, dinv, pivots, rank_rows, rank_cols, admissible, *rest,
 ):
     xw = rest[:parts]
     vz = rest[parts : parts + halves]
@@ -93,6 +97,22 @@
                     vs[pl.ds(r, 1), :] = vz[h][pl.ds(j, 1), span]
                     zs[pl.ds(r, 1), pl.ds(j * tile, tile)] = vz[h][pl.ds(col_tiles + j, 1), span]
         dv = dot(turned, vs[...], ((1,), (1,)))
+
+        row = lax.broadcasted_iota(jnp.int32, (row_tiles, col_tiles * RMAX), 0)
+        lane = lax.broadcasted_iota(jnp.int32, (row_tiles, col_tiles * RMAX), 1)
+        top_r, top_s = jnp.zeros_like(row), jnp.zeros_like(row)
+        for i in range(row_tiles):
+            for j in range(col_tiles):
+                here = (row == i) & (lane >> log2(RMAX) == j)
+                dense = admissible[i, j] == 0
+                top_r = jnp.where(here, jnp.where(dense, RMAX, rank_rows[i]), top_r)
+                top_s = jnp.where(here, jnp.where(dense, RMAX, rank_cols[j]), top_s)
+        half = (lane & (RMAX - 1)) >> log2(chunk)
+        s = ((lax.axis_index("row") ^ half) << log2(chunk)) + (lane & (chunk - 1))
+        top_r = jnp.where(s < top_s, top_r, 0)
+        top_r = jnp.broadcast_to(top_r[None], (slots,) + top_r.shape).reshape(rows, -1)
+        slot = lax.broadcasted_iota(jnp.int32, top_r.shape, 0) >> log2(row_tiles)
+        me = group_index()
         for q in range(per):
             span = pl.ds(q * tile, tile)
             for n in range(parts):
@@ -101,7 +121,8 @@
                 for g in range(tile // LANES):
                     xs[g, at, :] = left[:, g * LANES : (g + 1) * LANES]
                 core = dot(xw[n][:, row_tiles:, span].reshape(rows, tile), dv)
-                kept = jnp.where(keep[at, :] > 0, core, 0.0)
+                r = (me ^ (slot * parts + n)) * per + q
+                kept = jnp.where(r < top_r, core, 0.0)
                 right = dot(kept, zs[...])
                 for g in range(right.shape[1] // LANES):
                     ts[g, at, :] = right[:, g * LANES : (g + 1) * LANES]
@@ -112,7 +133,7 @@
     out[...] = front[...] - dot(left, right, ((0,), (0,)))
 
 
-def subtract_update(front, dinv, pivots, keep, xw, vz):
+def subtract_update(front, dinv, pivots, rank_rows, rank_cols, admissible, xw, vz):
     tile = dinv.shape[0]
     row_tiles = front.shape[0] // tile
     width = front.shape[1]
@@ -120,16 +141,15 @@
     per = xw[0].shape[2] // tile
     total = RMAX * row_tiles
 
-    def whole(array):
-        return pl.BlockSpec(array.shape, lambda i: (0,) * array.ndim)
-
+    whole = pl.BlockSpec(memory_space=pltpu.VMEM)
+    scalars = pl.BlockSpec(memory_space=pltpu.SMEM)
     block = pl.BlockSpec((tile, width), lambda i: (i, 0))
     pivots = pivots.reshape(1, tile)
     return pl.pallas_call(
         functools.partial(update_kernel, len(xw), len(vz), per, row_tiles, col_tiles, tile),
         grid=(row_tiles,),
         out_shape=pltpu.VMEM(front.shape, front.dtype),
-        in_specs=[block, whole(dinv), whole(pivots), whole(keep)] + [whole(a) for a in xw] + [whole(a) for a in vz],
+        in_specs=[block] + [whole] * 2 + [scalars] * 3 + [whole] * (len(xw) + len(vz)),
         out_specs=block,
         scratch_shapes=[
             pltpu.VMEM((tile // LANES, total, LANES), jnp.float32),
@@ -137,10 +157,10 @@
             pltpu.VMEM((col_tiles * RMAX, tile), jnp.float32),
             pltpu.VMEM((col_tiles * RMAX, width), jnp.float32),
         ],
-        compiler_params=pltpu.CompilerParams(vmem_limit_bytes=24 * MIB),
+        compiler_params=pltpu.CompilerParams(vmem_limit_bytes=8 * MIB),
         cost_estimate=pl.CostEstimate(flops=2 * front.size * 256, bytes_accessed=2 * front.size * 4, transcendentals=0),
         name="front_less_update",
-    )(in_hbm(front), dinv, pivots, keep, *xw, *vz)
+    )(in_hbm(front), dinv, pivots, rank_rows, rank_cols, admissible, *xw, *vz)
 
 
 def add_kernel(members, tile, row_map, base, *rest):
@@ -183,7 +203,7 @@
             pltpu.SemaphoreType.DMA((len(members),)),
         ],
         input_output_aliases={2 + len(members): 0} if before else {},
-        compiler_params=pltpu.CompilerParams(vmem_limit_bytes=16 * MIB),
+        compiler_params=pltpu.CompilerParams(vmem_limit_bytes=4 * MIB),
         cost_estimate=pl.CostEstimate(flops=size, bytes_accessed=size * 4, transcendentals=0),
         name="add_child",
     )(in_hbm(row_map), in_vmem(base), *[in_vmem(piece) for piece in arrived], *before)
@@ -221,8 +241,6 @@
     row_tiles = front.shape[0] // tile
     col_tiles = front.shape[1] // tile
     devices = lax.axis_size("col") * lax.axis_size("leaf")
-    per = x_fac.shape[1] // tile
-    chunk = v_fac.shape[1] // tile
 
     sender = Sender()
     mine = jnp.pad(x_fac, ((0, row_tiles), (0, 0))) + jnp.pad(w_fac, ((row_tiles, 0), (0, 0)))
@@ -233,50 +251,48 @@
         (pieces, v_fac, z_fac, rank_rows, rank_cols, admissible)
     )
 
+    pieces = list(pieces)
     half = devices // 2
-    spots = {}
     crossing = list(reversed(range(half, devices)))
     local = [m for pair in zip(reversed(range(NEAR, half)), [3, 2, 1] + [None] * half) for m in pair if m]
     between = [("xw", m) for m in range(1, NEAR)] + [("vz", m) for m in range(1, lax.axis_size("row"))]
+    ready = len(between)
     between += [("child", m) for m in local]
     gaps = len(crossing) - 2
-    xw, vz = [None], [None]
+    turn = [2 + i * gaps // len(between) for i in range(len(between))]
+    update_at = turn[ready - 1] + 2
+    order, spots, xw, vz = [0], {0: None}, [], []
+
+    def got(m):
+        return pieces[0] if m == 0 else sender.arrived[spots[m]]
+
+    def add(out, members):
+        return add_child(out, base, [got(m) for m in members], members, row_map, tile)
+
     for n, m in enumerate(crossing):
         for i, (kind, other) in enumerate(between):
-            if n >= 2 and i * gaps // len(between) == n - 2:
-                if kind == "xw":
-                    if xw == [None]:
-                        xw[0] = jnp.stack([mine] + [sender.arrived[i] for i in line])
-                    xw.append(sender.send(xw[0], GROUP, other))
-                elif kind == "vz":
-                    if vz == [None]:
-                        vz[0] = jnp.concatenate([v_fac, z_fac], axis=0)
-                    vz.append(sender.send(vz[0], ("row",), other))
-                else:
-                    spots[other] = sender.send(pieces[other], GROUP, other)
+            if turn[i] == n and kind == "xw":
+                if not xw:
+                    line = jnp.stack([mine] + [sender.arrived[i] for i in line])
+                xw.append(sender.send(line, GROUP, other))
+            elif turn[i] == n and kind == "vz":
+                if not vz:
+                    both = jnp.concatenate([v_fac, z_fac], axis=0)
+                vz.append(sender.send(both, ("row",), other))
+            elif turn[i] == n:
+                spots[other] = sender.send(pieces[other], GROUP, other)
+                order.append(other)
+        if n == update_at:
+            xw = [line] + [sender.arrived[i] for i in xw]
+            vz = [both] + [sender.arrived[i] for i in vz]
+            base = subtract_update(front, dinv, pivots, rank_rows, rank_cols, admissible, xw, vz)
+            base, pieces[m] = lax.optimization_barrier((base, pieces[m]))
+        if n == len(crossing) - 1:
+            out = add(None, order[: half - 1])
+            out, pieces[m] = lax.optimization_barrier((out, pieces[m]))
         spots[m] = sender.send(pieces[m], GROUP, m)
-    xw = xw[:1] + [sender.arrived[i] for i in xw[1:]]
-    vz = vz[:1] + [sender.arrived[i] for i in vz[1:]]
-    order = [0] + sorted(spots, key=lambda m: spots[m])
-    got = {m: sender.arrived[spots[m]] for m in spots}
-    got[0] = pieces[0]
-
-    far = np.arange(0, devices, NEAR, dtype=np.int32)
-    source = group_index() ^ (far + np.arange(NEAR, dtype=np.int32)[:, None])
-    r = source * per + np.arange(per, dtype=np.int32)[:, None, None]
-    source = lax.axis_index("row") ^ np.arange(lax.axis_size("row"), dtype=np.int32)
-    s = source[:, None] * chunk + np.arange(chunk, dtype=np.int32)
-    keep_rows = r.reshape(RMAX, 1) < rank_rows[None, :]
-    keep_cols = s.reshape(1, RMAX) < rank_cols[:, None]
-    dense = (admissible == 0)[None, :, :, None]
-    keep = (keep_rows[:, :, None, None] & keep_cols[None, None]) | dense
-    keep = keep.astype(jnp.float32).reshape(RMAX * row_tiles, col_tiles * RMAX)
-
-    base = subtract_update(front, dinv, pivots, keep, xw, vz)
-    out = None
-    for members in (order[: half - 1], order[half - 1 : -2], order[-2:]):
-        out = add_child(out, base, [got[m] for m in members], members, row_map, tile)
-    return out
+        order.append(m)
+    return add(add(out, order[half - 1 : -2]), order[-2:])
 
 
 def solution(mesh):

time: 115 us -> 134 us (1.17)
  waiting for transfers between devices: 24.3 us -> 51.7 us
  local copies, waits for them, and re-layouts: 20.6 us -> 6.48 us
  starting transfers between devices: 43.7 us -> 52 us
  other arithmetic: 3.3 us -> 0.95 us
    ppermute x22, waiting for transfers between devices: 24.3 us -> 51.7 us  [send(): lax.ppermute(array, axes, [(d, d ^ m) for d in range(size)])]
    ppermute x22, starting transfers between devices: 43.7 us -> 52 us  [send(): lax.ppermute(array, axes, [(d, d ^ m) for d in range(size)])]
    lt x8 -> x0, local copies, waits for them, and re-layouts: 6.26 us -> none  [the longest x4 3.66 us: on_device(): keep_rows = r.reshape(RMAX, 1) < rank_rows[None, :]]
    unnamed x38 -> x46, local copies, waits for them, and re-layouts: 10.7 us -> 6.4 us
    or x2 -> x0, local copies, waits for them, and re-layouts: 2.91 us -> none  [on_device(): keep = keep_rows[:, :, None, None] & keep_cols[None, None] | dense]
  transfers between devices with their start and end apart: 22 -> 22, of which waited for: 5 -> 7; matrix products, arithmetic and copies ran while one was open for 11% -> 0% of each run, Pallas kernels for 18% -> 16%
where the time goes in v1:
time: 134 us
  starting transfers between devices  52 us (39%)
  waiting for transfers between devices  51.7 us (39%)
  Pallas kernels  22.8 us (17%)
  local copies, waits for them, and re-layouts  6.48 us (5%)
    ppermute x22, starting transfers between devices, send(): lax.ppermute(array, axes, [(d, d ^ m) for d in range(size)])  52 us
    ppermute x22, waiting for transfers between devices, send(): lax.ppermute(array, axes, [(d, d ^ m) for d in range(size)])  51.7 us
    pallas_call x1, Pallas kernels, subtract_update(): pl.pallas_call(functools.partial(update_kernel, len(xw), len(vz), per, ro...  13.1 us
    unnamed x46, local copies, waits for them, and re-layouts  6.4 us
    pallas_call x3, Pallas kernels, add_child(): pl.pallas_call(functools.partial(add_kernel, members, tile), out_shape=pl...  5.49 us
    pallas_call x1, Pallas kernels, place(): pl.pallas_call(functools.partial(place_kernel, tiles, tile, col_tiles), o...  4.15 us
  transfers between devices with their start and end apart: 22, of which 7 were waited for; matrix products, arithmetic and copies ran while one was open for 0% of the time, Pallas kernels for 16%

profile of v1, /device:TPU:0, one launch (start us, length us, event | category | flops | bytes accessed | tf_op | source)
XLA Modules:
  0.0 134.1 jit_solution(6226898749834876422)
XLA Ops:
  0.0 0.0 copy-start
  0.0 0.0 copy-start.1
  0.0 0.9 pad_add_fusion
  0.9 5.1 %collective-permute-start.2 = (f32[16,1024]{1,0:T(8,128)S(1)}, f32[16,1024]{1,0:T(8,128)S(1)}, u32[]{:S(2)}, u32[]{:S(2)}) collective-permute-start(f32[16,1024]{1,0:T(8,128)S(1)} %pad_add_fusion), channel_id=1, source_target_pairs={{0,12},{1,13},{2,14},{3,15},{4,8},{5,9},{6,10},{7,11},{8,4},{9,5},... | collective-permute-start | bytes 196616 | tf_op jit(solution)/shard_map/ppermute | solution.py:221
  6.0 0.0 collective-permute-start.1
  6.0 0.6 collective-permute-start
  6.6 4.1 %place_child.1 = (f32[2,128,256]{2,1,0:T(8,128)S(1)}, f32[2,128,256]{2,1,0:T(8,128)S(1)}, f32[2,128,256]{2,1,0:T(8,128)S(1)}, f32[2,128,256]{2,1,0:T(8,128)S(1)}...) custom-call(s32[32]{0:T(128)} %col_map.1, ...), custom_call_target="tpu_custom_call" | custom-call | bytes 8388608 | tf_op jit(solution)/shard_map/place_child/pallas_call | solution.py:55
  10.8 0.7 copy-done.4
  11.5 0.7 copy-done.6
  12.2 0.7 copy-done.8
  12.9 0.7 copy-done.10
  13.6 0.7 copy-done.12
  14.3 0.7 copy-done.14
  15.0 0.7 copy-done.16
  15.7 0.7 copy-done.18
  16.4 0.7 copy-done.19
  17.1 3.3 %collective-permute-start.5 = (f32[2,128,256]{2,1,0:T(8,128)S(1)}, f32[2,128,256]{2,1,0:T(8,128)S(1)}, u32[]{:S(2)}, u32[]{:S(2)}) collective-permute-start(f32[2,128,256]{2,1,0:T(8,128)S(1)} %get-tuple-element.107), channel_id=1, source_target_pairs={{0,15},{1,14},{2,13},{3,12},{4,11},{5,10},{6,9},{7,8},{8,7},{9,6},... | collective-permute-start | bytes 786440 | tf_op jit(solution)/shard_map/ppermute | solution.py:221
  20.4 0.0 collective-permute-done.2
  20.4 0.0 collective-permute-done.1
  20.4 0.0 collective-permute-done
  20.4 1.6 %collective-permute-start.3 = (f32[4,16,1024]{2,1,0:T(8,128)S(1)}, f32[4,16,1024]{2,1,0:T(8,128)S(1)}, u32[]{:S(2)}, u32[]{:S(2)}) collective-permute-start(f32[4,16,1024]{2,1,0:T(8,128)S(1)} %pad_maximum_fusion.rest_0_), channel_id=1, source_target_pairs={{0,1},{1,0},{2,3},{3,2},{4,5},{5,4},{6,7},{7,6},{8,9},{9,8},{10,11... | collective-permute-start | bytes 786440 | tf_op jit(solution)/shard_map/ppermute | solution.py:221
  22.0 0.5 collective-permute-start.4
  22.6 1.1 collective-permute-start.7
  23.7 2.7 %collective-permute-start.12 = (f32[2,128,256]{2,1,0:T(8,128)}, f32[2,128,256]{2,1,0:T(8,128)S(1)}, u32[]{:S(2)}, u32[]{:S(2)}) collective-permute-start(f32[2,128,256]{2,1,0:T(8,128)} %get-tuple-element.128), channel_id=1, source_target_pairs={{0,13},{1,12},{2,15},{3,14},{4,9},{5,8},{6,11},{7,10},{8,5},{9,4},... | collective-permute-start | bytes 786440 | tf_op jit(solution)/shard_map/ppermute | solution.py:221
  26.4 1.7 %collective-permute-done.5.rest_1_ = f32[2,128,256]{2,1,0:T(8,128)S(1)} collective-permute-done((f32[2,128,256]{2,1,0:T(8,128)S(1)}, f32[2,128,256]{2,1,0:T(8,128)S(1)}, u32[]{:S(2)}, u32[]{:S(2)}) %collective-permute-start.5) | collective-permute-done | bytes 262176 | tf_op jit(solution)/shard_map/ppermute | solution.py:221
  28.2 0.6 collective-permute-start.6
  28.7 0.0 collective-permute-done.3.rest_1_
  28.8 11.1 %collective-permute-done.4.rest_2_ = f32[4,16,1024]{2,1,0:T(8,128)S(1)} collective-permute-done((f32[4,16,1024]{2,1,0:T(8,128)S(1)}, f32[4,16,1024]{2,1,0:T(8,128)S(1)}, u32[]{:S(2)}, u32[]{:S(2)}) %collective-permute-start.4) | collective-permute-done | bytes 262176 | tf_op jit(solution)/shard_map/ppermute | solution.py:221
  39.8 2.8 %collective-permute-start.9 = (f32[2,128,256]{2,1,0:T(8,128)}, f32[2,128,256]{2,1,0:T(8,128)S(1)}, u32[]{:S(2)}, u32[]{:S(2)}) collective-permute-start(f32[2,128,256]{2,1,0:T(8,128)} %get-tuple-element.120), channel_id=1, source_target_pairs={{0,12},{1,13},{2,14},{3,15},{4,8},{5,9},{6,10},{7,11},{8,4},{9,5},... | collective-permute-start | bytes 786440 | tf_op jit(solution)/shard_map/ppermute | solution.py:221
  42.6 10.2 %collective-permute-start.13 = (f32[2,128,256]{2,1,0:T(8,128)}, f32[2,128,256]{2,1,0:T(8,128)S(1)}, u32[]{:S(2)}, u32[]{:S(2)}) collective-permute-start(f32[2,128,256]{2,1,0:T(8,128)} %get-tuple-element.132), channel_id=1, source_target_pairs={{0,7},{1,6},{2,5},{3,4},{4,3},{5,2},{6,1},{7,0},{8,15},{9,14},{10,... | collective-permute-start | bytes 786440 | tf_op jit(solution)/shard_map/ppermute | solution.py:221
  52.8 0.1 pad_maximum_fusion.1.rest_4_
  52.9 0.0 collective-permute-done.7.rest_2_
  52.9 1.6 %collective-permute-start.8 = (f32[4,8192]{1,0:T(4,128)S(1)}, f32[4,8192]{1,0:T(4,128)S(1)}, u32[]{:S(2)}, u32[]{:S(2)}) collective-permute-start(f32[4,8192]{1,0:T(4,128)S(1)} %pad_maximum_fusion.1.rest_4_), channel_id=1, source_target_pairs={{0,16},{16,0},{1,17},{17,1},{2,18},{18,2},{3,19},{19,3},{4,20},{20... | collective-permute-start | bytes 393224 | tf_op jit(solution)/shard_map/ppermute | solution.py:221
  54.5 0.1 copy.16.admissible
  54.5 0.0 collective-permute-done.12.rest_3_
  54.6 0.1 collective-permute-start.14
  54.6 4.0 %collective-permute-done.8.rest_5_ = f32[4,8192]{1,0:T(4,128)S(1)} collective-permute-done((f32[4,8192]{1,0:T(4,128)S(1)}, f32[4,8192]{1,0:T(4,128)S(1)}, u32[]{:S(2)}, u32[]{:S(2)}) %collective-permute-start.8) | collective-permute-done | bytes 131104 | tf_op jit(solution)/shard_map/ppermute | solution.py:221
  58.6 3.6 %collective-permute-start.18 = (f32[2,128,256]{2,1,0:T(8,128)}, f32[2,128,256]{2,1,0:T(8,128)S(1)}, u32[]{:S(2)}, u32[]{:S(2)}) collective-permute-start(f32[2,128,256]{2,1,0:T(8,128)} %copy-done.18), channel_id=1, source_target_pairs={{0,6},{1,7},{2,4},{3,5},{4,2},{5,3},{6,0},{7,1},{8,14},{9,15},{10,... | collective-permute-start | bytes 786440 | tf_op jit(solution)/shard_map/ppermute | solution.py:221
  62.2 0.0 collective-permute-done.6.rest_3_
  62.2 0.0 copy-done.2
  62.3 13.1 %front_less_update.1.base = f32[2048,512]{1,0:T(8,128)S(1)} custom-call(f32[2048,512]{1,0:T(8,128)} %front.1, f32[256,256]{1,0:T(8,128)S(1)} %copy-done, s32[1,256]{1,0:T(1,128)S(1)} %bitcast.5, s32[8]{0:T(128)S(1)} %copy-done.2, s32[2]{0:T(128)S(1)} %copy-done.3, s32[8,2]{1,0:T(8,128)S(1)} %copy.16.admissible, f32[4,16,1024]{2,1,0:T(8,128)S(1)} %pad_maximum_fusion.rest_0_, ...), custom_call_target="tpu_custom_call" | custom-call | flops 536870912 | bytes 8388608 | tf_op jit(solution)/shard_map/front_less_update/pallas_call | solution.py:148
  75.5 11.7 %collective-permute-start.17 = (f32[2,128,256]{2,1,0:T(8,128)S(1)}, f32[2,128,256]{2,1,0:T(8,128)S(1)}, u32[]{:S(2)}, u32[]{:S(2)}) collective-permute-start(f32[2,128,256]{2,1,0:T(8,128)S(1)} %copy-done.17), channel_id=1, source_target_pairs={{0,11},{1,10},{2,9},{3,8},{4,15},{5,14},{6,13},{7,12},{8,3},{9,2},... | collective-permute-start | bytes 786440 | tf_op jit(solution)/shard_map/ppermute | solution.py:221
  87.2 0.0 collective-permute-done.9.rest_4_
  87.2 0.6 collective-permute-start.10
  87.8 0.0 collective-permute-done.13.rest_5_
  87.8 0.4 collective-permute-start.15
  88.2 0.0 collective-permute-done.14.rest_6_
  88.2 2.0 %add_child.3.rest_7_ = f32[2048,512]{1,0:T(8,128)} custom-call(s32[1,8]{1,0:T(1,128)} %row_map.5, f32[2048,512]{1,0:T(8,128)S(1)} %front_less_update.1.base, f32[2,128,256]{2,1,0:T(8,128)S(1)} %get-tuple-element.123.rest_0_, f32[2,128,256]{2,1,0:T(8,128)S(1)} %collective-permute-done.5.rest_1_, f32[2,128,256]{2,1,0:T(8,128)S(1)} %collective-permute-done.7.rest_2_, ...), custom_call_target="tpu_custom_call" | custom-call | flops 458752 | bytes 1835008 | tf_op jit(solution)/shard_map/add_child/pallas_call | solution.py:196
  90.2 2.0 %collective-permute-start.19 = (f32[2,128,256]{2,1,0:T(8,128)S(1)}, f32[2,128,256]{2,1,0:T(8,128)S(1)}, u32[]{:S(2)}, u32[]{:S(2)}) collective-permute-start(f32[2,128,256]{2,1,0:T(8,128)S(1)} %copy-done.11), channel_id=1, source_target_pairs={{0,5},{1,4},{2,7},{3,6},{4,1},{5,0},{6,3},{7,2},{8,13},{9,12},{10,... | collective-permute-start | bytes 786440 | tf_op jit(solution)/shard_map/ppermute | solution.py:221
  92.2 0.0 collective-permute-done.18.rest_1_
  92.2 1.2 collective-permute-start.21
  93.4 11.2 %collective-permute-done.17.rest_0_ = f32[2,128,256]{2,1,0:T(8,128)S(1)} collective-permute-done((f32[2,128,256]{2,1,0:T(8,128)S(1)}, f32[2,128,256]{2,1,0:T(8,128)S(1)}, u32[]{:S(2)}, u32[]{:S(2)}) %collective-permute-start.17) | collective-permute-done | bytes 262176 | tf_op jit(solution)/shard_map/ppermute | solution.py:221
  104.6 2.3 %collective-permute-start.20 = (f32[2,128,256]{2,1,0:T(8,128)S(1)}, f32[2,128,256]{2,1,0:T(8,128)S(1)}, u32[]{:S(2)}, u32[]{:S(2)}) collective-permute-start(f32[2,128,256]{2,1,0:T(8,128)S(1)} %copy-done.7), channel_id=1, source_target_pairs={{0,1},{1,0},{2,3},{3,2},{4,5},{5,4},{6,7},{7,6},{8,9},{9,8},{10,11... | collective-permute-start | bytes 786440 | tf_op jit(solution)/shard_map/ppermute | solution.py:221
  106.9 0.0 collective-permute-done.10.rest_2_
  106.9 0.0 collective-permute-start.11
  106.9 10.5 %collective-permute-done.15.rest_3_ = f32[2,128,256]{2,1,0:T(8,128)S(1)} collective-permute-done((f32[2,128,256]{2,1,0:T(8,128)S(1)}, f32[2,128,256]{2,1,0:T(8,128)S(1)}, u32[]{:S(2)}, u32[]{:S(2)}) %collective-permute-start.15) | collective-permute-done | bytes 262176 | tf_op jit(solution)/shard_map/ppermute | solution.py:221
  117.4 0.0 collective-permute-start.16
  117.4 0.0 collective-permute-done.19.rest_4_
  117.4 9.1 %collective-permute-done.21.rest_6_ = f32[2,128,256]{2,1,0:T(8,128)S(1)} collective-permute-done((f32[2,128,256]{2,1,0:T(8,128)S(1)}, f32[2,128,256]{2,1,0:T(8,128)S(1)}, u32[]{:S(2)}, u32[]{:S(2)}) %collective-permute-start.21) | collective-permute-done | bytes 262176 | tf_op jit(solution)/shard_map/ppermute | solution.py:221
  126.4 0.0 collective-permute-done.20.rest_5_
  126.4 2.0 %add_child.4.rest_2_ = f32[2048,512]{1,0:T(8,128)} custom-call(s32[1,8]{1,0:T(1,128)} %row_map.5, f32[2048,512]{1,0:T(8,128)S(1)} %front_less_update.1.base, f32[2,128,256]{2,1,0:T(8,128)S(1)} %collective-permute-done.17.rest_0_, f32[2,128,256]{2,1,0:T(8,128)S(1)} %collective-permute-done.18.rest_1_, ...), custom_call_target="tpu_custom_call", output_to_operand_aliasing={{}: (9, {})} | custom-call | flops 458752 | bytes 1835008 | tf_op jit(solution)/shard_map/add_child/pallas_call | solution.py:196
  128.4 0.0 collective-permute-done.11.rest_0_
  128.4 4.1 %collective-permute-done.16.rest_1_ = f32[2,128,256]{2,1,0:T(8,128)S(1)} collective-permute-done((f32[2,128,256]{2,1,0:T(8,128)S(1)}, f32[2,128,256]{2,1,0:T(8,128)S(1)}, u32[]{:S(2)}, u32[]{:S(2)}) %collective-permute-start.16) | collective-permute-done | bytes 262176 | tf_op jit(solution)/shard_map/ppermute | solution.py:221
  132.6 1.5 %add_child.5 = f32[2048,512]{1,0:T(8,128)} custom-call(s32[1,8]{1,0:T(1,128)} %row_map.5, f32[2048,512]{1,0:T(8,128)S(1)} %front_less_update.1.base, f32[2,128,256]{2,1,0:T(8,128)S(1)} %collective-permute-done.11.rest_0_, f32[2,128,256]{2,1,0:T(8,128)S(1)} %collective-permute-done.16.rest_1_, ...), custom_call_target="tpu_custom_call", output_to_operand_aliasing={{}: (4, {})} | custom-call | flops 131072 | bytes 524288 | tf_op jit(solution)/shard_map/add_child/pallas_call | solution.py:196
  (35 shorter events, 0.1 us)
Async XLA Ops:
  0.0 52.8 %copy-start.21 = (f32[2,8192]{1,0:T(2,128)S(1)}, f32[2,8192]{1,0:T(2,128)}, u32[]{:S(2)}) copy-start(f32[2,8192]{1,0:T(2,128)} %param.19) | copy-start | bytes 196612
  0.0 52.8 %copy-start.20 = (f32[2,8192]{1,0:T(2,128)S(1)}, f32[2,8192]{1,0:T(2,128)}, u32[]{:S(2)}) copy-start(f32[2,8192]{1,0:T(2,128)} %param.20) | copy-start | bytes 196612
  0.0 62.2 %copy-start.2 = (s32[8]{0:T(128)S(1)}, s32[8]{0:T(128)}, u32[]{:S(2)}) copy-start(s32[8]{0:T(128)} %rank_rows) | copy-start | bytes 100
  0.0 62.2 %copy-start.3 = (s32[2]{0:T(128)S(1)}, s32[2]{0:T(128)}, u32[]{:S(2)}) copy-start(s32[2]{0:T(128)} %rank_cols) | copy-start | bytes 28
  0.0 54.5 %copy-start.22 = (s32[8,2]{0,1:T(2,128)S(1)}, s32[8,2]{0,1:T(2,128)}, u32[]{:S(2)}) copy-start(s32[8,2]{0,1:T(2,128)} %param.25) | copy-start | bytes 196
  0.0 62.2 %copy-start = (f32[256,256]{1,0:T(8,128)S(1)}, f32[256,256]{1,0:T(8,128)}, u32[]{:S(2)}) copy-start(f32[256,256]{1,0:T(8,128)} %dinv.1) | copy-start | bytes 786436
  0.0 62.2 %copy-start.1 = (s32[256]{0:T(256)S(1)}, s32[256]{0:T(256)}, u32[]{:S(2)}) copy-start(s32[256]{0:T(256)} %param.22) | copy-start | bytes 3076
  0.9 19.5 %collective-permute-start.2 = (f32[16,1024]{1,0:T(8,128)S(1)}, f32[16,1024]{1,0:T(8,128)S(1)}, u32[]{:S(2)}, u32[]{:S(2)}) collective-permute-start(f32[16,1024]{1,0:T(8,128)S(1)} %pad_add_fusion), channel_id=1, source_target_pairs={{0,12},{1,13},{2,14},{3,15},{4,8},{5,9},{6,10},{7,11},{8,4},{9,5},... | collective-permute-start | bytes 196616 | tf_op jit(solution)/shard_map/ppermute | solution.py:221
  6.0 14.4 %collective-permute-start.1 = (f32[16,1024]{1,0:T(8,128)S(1)}, f32[16,1024]{1,0:T(8,128)S(1)}, u32[]{:S(2)}, u32[]{:S(2)}) collective-permute-start(f32[16,1024]{1,0:T(8,128)S(1)} %pad_add_fusion), channel_id=1, source_target_pairs={{0,8},{1,9},{2,10},{3,11},{4,12},{5,13},{6,14},{7,15},{8,0},{9,1},... | collective-permute-start | bytes 196616 | tf_op jit(solution)/shard_map/ppermute | solution.py:221
  6.0 14.4 %collective-permute-start = (f32[16,1024]{1,0:T(8,128)S(1)}, f32[16,1024]{1,0:T(8,128)S(1)}, u32[]{:S(2)}, u32[]{:S(2)}) collective-permute-start(f32[16,1024]{1,0:T(8,128)S(1)} %pad_add_fusion), channel_id=1, source_target_pairs={{0,4},{1,5},{2,6},{3,7},{4,0},{5,1},{6,2},{7,3},{8,12},{9,13},{10,... | collective-permute-start | bytes 196616 | tf_op jit(solution)/shard_map/ppermute | solution.py:221
  10.8 0.7 copy-start.4
  11.5 0.7 copy-start.6
  12.2 0.7 copy-start.8
  12.9 0.7 copy-start.10
  13.6 0.7 copy-start.12
  14.3 0.7 copy-start.14
  15.0 0.7 copy-start.16
  15.7 0.7 copy-start.18
  16.4 0.7 copy-start.19
  17.1 11.0 %collective-permute-start.5 = (f32[2,128,256]{2,1,0:T(8,128)S(1)}, f32[2,128,256]{2,1,0:T(8,128)S(1)}, u32[]{:S(2)}, u32[]{:S(2)}) collective-permute-start(f32[2,128,256]{2,1,0:T(8,128)S(1)} %get-tuple-element.107), channel_id=1, source_target_pairs={{0,15},{1,14},{2,13},{3,12},{4,11},{5,10},{6,9},{7,8},{8,7},{9,6},... | collective-permute-start | bytes 786440 | tf_op jit(solution)/shard_map/ppermute | solution.py:221
  20.4 8.3 %collective-permute-start.3 = (f32[4,16,1024]{2,1,0:T(8,128)S(1)}, f32[4,16,1024]{2,1,0:T(8,128)S(1)}, u32[]{:S(2)}, u32[]{:S(2)}) collective-permute-start(f32[4,16,1024]{2,1,0:T(8,128)S(1)} %pad_maximum_fusion.rest_0_), channel_id=1, source_target_pairs={{0,1},{1,0},{2,3},{3,2},{4,5},{5,4},{6,7},{7,6},{8,9},{9,8},{10,11... | collective-permute-start | bytes 786440 | tf_op jit(solution)/shard_map/ppermute | solution.py:221
  22.0 17.8 %collective-permute-start.4 = (f32[4,16,1024]{2,1,0:T(8,128)S(1)}, f32[4,16,1024]{2,1,0:T(8,128)S(1)}, u32[]{:S(2)}, u32[]{:S(2)}) collective-permute-start(f32[4,16,1024]{2,1,0:T(8,128)S(1)} %pad_maximum_fusion.rest_0_), channel_id=1, source_target_pairs={{0,2},{1,3},{2,0},{3,1},{4,6},{5,7},{6,4},{7,5},{8,10},{9,11},{10,... | collective-permute-start | bytes 786440 | tf_op jit(solution)/shard_map/ppermute | solution.py:221
  22.6 30.3 %collective-permute-start.7 = (f32[2,128,256]{2,1,0:T(8,128)S(1)}, f32[2,128,256]{2,1,0:T(8,128)S(1)}, u32[]{:S(2)}, u32[]{:S(2)}) collective-permute-start(f32[2,128,256]{2,1,0:T(8,128)S(1)} %get-tuple-element.113), channel_id=1, source_target_pairs={{0,14},{1,15},{2,12},{3,13},{4,10},{5,11},{6,8},{7,9},{8,6},{9,7},... | collective-permute-start | bytes 786440 | tf_op jit(solution)/shard_map/ppermute | solution.py:221
  23.7 30.8 %collective-permute-start.12 = (f32[2,128,256]{2,1,0:T(8,128)}, f32[2,128,256]{2,1,0:T(8,128)S(1)}, u32[]{:S(2)}, u32[]{:S(2)}) collective-permute-start(f32[2,128,256]{2,1,0:T(8,128)} %get-tuple-element.128), channel_id=1, source_target_pairs={{0,13},{1,12},{2,15},{3,14},{4,9},{5,8},{6,11},{7,10},{8,5},{9,4},... | collective-permute-start | bytes 786440 | tf_op jit(solution)/shard_map/ppermute | solution.py:221
  28.2 34.1 %collective-permute-start.6 = (f32[4,16,1024]{2,1,0:T(8,128)S(1)}, f32[4,16,1024]{2,1,0:T(8,128)S(1)}, u32[]{:S(2)}, u32[]{:S(2)}) collective-permute-start(f32[4,16,1024]{2,1,0:T(8,128)S(1)} %pad_maximum_fusion.rest_0_), channel_id=1, source_target_pairs={{0,3},{1,2},{2,1},{3,0},{4,7},{5,6},{6,5},{7,4},{8,11},{9,10},{10,... | collective-permute-start | bytes 786440 | tf_op jit(solution)/shard_map/ppermute | solution.py:221
  39.8 47.4 %collective-permute-start.9 = (f32[2,128,256]{2,1,0:T(8,128)}, f32[2,128,256]{2,1,0:T(8,128)S(1)}, u32[]{:S(2)}, u32[]{:S(2)}) collective-permute-start(f32[2,128,256]{2,1,0:T(8,128)} %get-tuple-element.120), channel_id=1, source_target_pairs={{0,12},{1,13},{2,14},{3,15},{4,8},{5,9},{6,10},{7,11},{8,4},{9,5},... | collective-permute-start | bytes 786440 | tf_op jit(solution)/shard_map/ppermute | solution.py:221
  42.6 45.2 %collective-permute-start.13 = (f32[2,128,256]{2,1,0:T(8,128)}, f32[2,128,256]{2,1,0:T(8,128)S(1)}, u32[]{:S(2)}, u32[]{:S(2)}) collective-permute-start(f32[2,128,256]{2,1,0:T(8,128)} %get-tuple-element.132), channel_id=1, source_target_pairs={{0,7},{1,6},{2,5},{3,4},{4,3},{5,2},{6,1},{7,0},{8,15},{9,14},{10,... | collective-permute-start | bytes 786440 | tf_op jit(solution)/shard_map/ppermute | solution.py:221
  52.9 5.7 %collective-permute-start.8 = (f32[4,8192]{1,0:T(4,128)S(1)}, f32[4,8192]{1,0:T(4,128)S(1)}, u32[]{:S(2)}, u32[]{:S(2)}) collective-permute-start(f32[4,8192]{1,0:T(4,128)S(1)} %pad_maximum_fusion.1.rest_4_), channel_id=1, source_target_pairs={{0,16},{16,0},{1,17},{17,1},{2,18},{18,2},{3,19},{19,3},{4,20},{20... | collective-permute-start | bytes 393224 | tf_op jit(solution)/shard_map/ppermute | solution.py:221
  54.6 33.6 %collective-permute-start.14 = (f32[2,128,256]{2,1,0:T(8,128)}, f32[2,128,256]{2,1,0:T(8,128)S(1)}, u32[]{:S(2)}, u32[]{:S(2)}) collective-permute-start(f32[2,128,256]{2,1,0:T(8,128)} %copy-done.19), channel_id=1, source_target_pairs={{0,3},{1,2},{2,1},{3,0},{4,7},{5,6},{6,5},{7,4},{8,11},{9,10},{10,... | collective-permute-start | bytes 786440 | tf_op jit(solution)/shard_map/ppermute | solution.py:221
  58.6 33.6 %collective-permute-start.18 = (f32[2,128,256]{2,1,0:T(8,128)}, f32[2,128,256]{2,1,0:T(8,128)S(1)}, u32[]{:S(2)}, u32[]{:S(2)}) collective-permute-start(f32[2,128,256]{2,1,0:T(8,128)} %copy-done.18), channel_id=1, source_target_pairs={{0,6},{1,7},{2,4},{3,5},{4,2},{5,3},{6,0},{7,1},{8,14},{9,15},{10,... | collective-permute-start | bytes 786440 | tf_op jit(solution)/shard_map/ppermute | solution.py:221
  62.3 13.2 %copy-start.17 = (f32[2,128,256]{2,1,0:T(8,128)S(1)}, f32[2,128,256]{2,1,0:T(8,128)}, u32[]{:S(2)}) copy-start(f32[2,128,256]{2,1,0:T(8,128)} %copy-done.16) | copy-start | bytes 786436
  62.3 24.9 %copy-start.15 = (f32[2,128,256]{2,1,0:T(8,128)S(1)}, f32[2,128,256]{2,1,0:T(8,128)}, u32[]{:S(2)}) copy-start(f32[2,128,256]{2,1,0:T(8,128)} %copy-done.14) | copy-start | bytes 786436
  62.3 25.5 %copy-start.13 = (f32[2,128,256]{2,1,0:T(8,128)S(1)}, f32[2,128,256]{2,1,0:T(8,128)}, u32[]{:S(2)}) copy-start(f32[2,128,256]{2,1,0:T(8,128)} %copy-done.12) | copy-start | bytes 786436
  75.5 14.7 %copy-start.11 = (f32[2,128,256]{2,1,0:T(8,128)S(1)}, f32[2,128,256]{2,1,0:T(8,128)}, u32[]{:S(2)}) copy-start(f32[2,128,256]{2,1,0:T(8,128)} %copy-done.10) | copy-start | bytes 786436
  75.5 16.8 %copy-start.9 = (f32[2,128,256]{2,1,0:T(8,128)S(1)}, f32[2,128,256]{2,1,0:T(8,128)}, u32[]{:S(2)}) copy-start(f32[2,128,256]{2,1,0:T(8,128)} %copy-done.8) | copy-start | bytes 786436
  75.5 29.1 %copy-start.7 = (f32[2,128,256]{2,1,0:T(8,128)S(1)}, f32[2,128,256]{2,1,0:T(8,128)}, u32[]{:S(2)}) copy-start(f32[2,128,256]{2,1,0:T(8,128)} %copy-done.6) | copy-start | bytes 786436
  75.5 31.4 %copy-start.5 = (f32[2,128,256]{2,1,0:T(8,128)S(1)}, f32[2,128,256]{2,1,0:T(8,128)}, u32[]{:S(2)}) copy-start(f32[2,128,256]{2,1,0:T(8,128)} %copy-done.4) | copy-start | bytes 786436
  75.5 29.1 %collective-permute-start.17 = (f32[2,128,256]{2,1,0:T(8,128)S(1)}, f32[2,128,256]{2,1,0:T(8,128)S(1)}, u32[]{:S(2)}, u32[]{:S(2)}) collective-permute-start(f32[2,128,256]{2,1,0:T(8,128)S(1)} %copy-done.17), channel_id=1, source_target_pairs={{0,11},{1,10},{2,9},{3,8},{4,15},{5,14},{6,13},{7,12},{8,3},{9,2},... | collective-permute-start | bytes 786440 | tf_op jit(solution)/shard_map/ppermute | solution.py:221
  87.2 19.7 %collective-permute-start.10 = (f32[2,128,256]{2,1,0:T(8,128)S(1)}, f32[2,128,256]{2,1,0:T(8,128)S(1)}, u32[]{:S(2)}, u32[]{:S(2)}) collective-permute-start(f32[2,128,256]{2,1,0:T(8,128)S(1)} %copy-done.15), channel_id=1, source_target_pairs={{0,2},{1,3},{2,0},{3,1},{4,6},{5,7},{6,4},{7,5},{8,10},{9,11},{10,... | collective-permute-start | bytes 786440 | tf_op jit(solution)/shard_map/ppermute | solution.py:221
  87.8 29.6 %collective-permute-start.15 = (f32[2,128,256]{2,1,0:T(8,128)S(1)}, f32[2,128,256]{2,1,0:T(8,128)S(1)}, u32[]{:S(2)}, u32[]{:S(2)}) collective-permute-start(f32[2,128,256]{2,1,0:T(8,128)S(1)} %copy-done.13), channel_id=1, source_target_pairs={{0,10},{1,11},{2,8},{3,9},{4,14},{5,15},{6,12},{7,13},{8,2},{9,3},... | collective-permute-start | bytes 786440 | tf_op jit(solution)/shard_map/ppermute | solution.py:221
  90.2 27.2 %collective-permute-start.19 = (f32[2,128,256]{2,1,0:T(8,128)S(1)}, f32[2,128,256]{2,1,0:T(8,128)S(1)}, u32[]{:S(2)}, u32[]{:S(2)}) collective-permute-start(f32[2,128,256]{2,1,0:T(8,128)S(1)} %copy-done.11), channel_id=1, source_target_pairs={{0,5},{1,4},{2,7},{3,6},{4,1},{5,0},{6,3},{7,2},{8,13},{9,12},{10,... | collective-permute-start | bytes 786440 | tf_op jit(solution)/shard_map/ppermute | solution.py:221
  92.2 34.2 %collective-permute-start.21 = (f32[2,128,256]{2,1,0:T(8,128)S(1)}, f32[2,128,256]{2,1,0:T(8,128)S(1)}, u32[]{:S(2)}, u32[]{:S(2)}) collective-permute-start(f32[2,128,256]{2,1,0:T(8,128)S(1)} %copy-done.9), channel_id=1, source_target_pairs={{0,9},{1,8},{2,11},{3,10},{4,13},{5,12},{6,15},{7,14},{8,1},{9,0},... | collective-permute-start | bytes 786440 | tf_op jit(solution)/shard_map/ppermute | solution.py:221
  104.6 21.8 %collective-permute-start.20 = (f32[2,128,256]{2,1,0:T(8,128)S(1)}, f32[2,128,256]{2,1,0:T(8,128)S(1)}, u32[]{:S(2)}, u32[]{:S(2)}) collective-permute-start(f32[2,128,256]{2,1,0:T(8,128)S(1)} %copy-done.7), channel_id=1, source_target_pairs={{0,1},{1,0},{2,3},{3,2},{4,5},{5,4},{6,7},{7,6},{8,9},{9,8},{10,11... | collective-permute-start | bytes 786440 | tf_op jit(solution)/shard_map/ppermute | solution.py:221
  106.9 21.6 %collective-permute-start.11 = (f32[2,128,256]{2,1,0:T(8,128)S(1)}, f32[2,128,256]{2,1,0:T(8,128)S(1)}, u32[]{:S(2)}, u32[]{:S(2)}) collective-permute-start(f32[2,128,256]{2,1,0:T(8,128)S(1)} %copy-done.5), channel_id=1, source_target_pairs={{0,4},{1,5},{2,6},{3,7},{4,0},{5,1},{6,2},{7,3},{8,12},{9,13},{10,... | collective-permute-start | bytes 786440 | tf_op jit(solution)/shard_map/ppermute | solution.py:221
  117.4 15.2 %collective-permute-start.16 = (f32[2,128,256]{2,1,0:T(8,128)S(1)}, f32[2,128,256]{2,1,0:T(8,128)S(1)}, u32[]{:S(2)}, u32[]{:S(2)}) collective-permute-start(f32[2,128,256]{2,1,0:T(8,128)S(1)} %get-tuple-element.140), channel_id=1, source_target_pairs={{0,8},{1,9},{2,10},{3,11},{4,12},{5,13},{6,14},{7,15},{8,0},{9,1},... | collective-permute-start | bytes 786440 | tf_op jit(solution)/shard_map/ppermute | solution.py:221

commit v2 on v1

--- a/solution.py
+++ b/solution.py
@@ -25,23 +25,32 @@
     return pltpu.with_memory_space_constraint(array, pltpu.HBM)
 
 
-def place_kernel(tiles, tile, col_tiles, col_map, child, *rest):
+def place_kernel(tiles, groups, tile, col_tiles, col_map, child, *rest):
     pieces = rest[: tiles // col_tiles]
-    inverse, sem = rest[tiles // col_tiles :]
+    inverse, held, in_sem, out_sem = rest[tiles // col_tiles :]
+    width = tiles // groups * tile
     me = group_index()
+
+    def fetch(g):
+        span = pl.ds(g * width, width)
+        return pltpu.make_async_copy(child.at[:, span], held.at[:, span], in_sem.at[g])
+
+    def store(m, j):
+        b = inverse[(me ^ m) * col_tiles + j]
+        span = pl.ds(pl.multiple_of(b * tile, tile), tile)
+        return pltpu.make_async_copy(held.at[:, span], pieces[m].at[j], out_sem.at[m, j])
+
+    for g in range(groups):
+        fetch(g).start()
     for b in range(tiles):
         inverse[col_map[b]] = b
-
-    def copy(m, j):
-        b = inverse[(me ^ m) * col_tiles + j]
-        span = pl.ds(pl.multiple_of(b * tile, tile), tile)
-        return pltpu.make_async_copy(child.at[:, span], pieces[m].at[j], sem.at[m, j])
-
+    for g in range(groups):
+        fetch(g).wait()
     order = [(m, j) for m in reversed(range(len(pieces))) for j in range(col_tiles)]
     for m, j in order:
-        copy(m, j).start()
+        store(m, j).start()
     for m, j in order:
-        copy(m, j).wait()
+        store(m, j).wait()
 
 
 def in_vmem(array):
@@ -52,13 +61,19 @@
     rows = child.shape[0]
     tiles = col_map.shape[0]
     col_tiles = tiles // devices
+    groups = 8
     return pl.pallas_call(
-        functools.partial(place_kernel, tiles, tile, col_tiles),
-        out_shape=[pltpu.VMEM((col_tiles, rows, tile), child.dtype)] * devices,
+        functools.partial(place_kernel, tiles, groups, tile, col_tiles),
+        out_shape=[pltpu.HBM((col_tiles, rows, tile), child.dtype)] * devices,
         in_specs=[pl.BlockSpec(memory_space=pltpu.SMEM), pl.BlockSpec(memory_space=pltpu.HBM)],
-        out_specs=[pl.BlockSpec(memory_space=pltpu.VMEM)] * devices,
-        scratch_shapes=[pltpu.SMEM((tiles,), jnp.int32), pltpu.SemaphoreType.DMA((devices, col_tiles))],
-        compiler_params=pltpu.CompilerParams(vmem_limit_bytes=2 * MIB),
+        out_specs=[pl.BlockSpec(memory_space=pltpu.HBM)] * devices,
+        scratch_shapes=[
+            pltpu.SMEM((tiles,), jnp.int32),
+            pltpu.VMEM(child.shape, child.dtype),
+            pltpu.SemaphoreType.DMA((groups,)),
+            pltpu.SemaphoreType.DMA((devices, col_tiles)),
+        ],
+        compiler_params=pltpu.CompilerParams(vmem_limit_bytes=8 * MIB),
         cost_estimate=pl.CostEstimate(flops=0, bytes_accessed=2 * child.size * 4, transcendentals=0),
         name="place_child",
     )(in_hbm(col_map), in_hbm(child))
@@ -142,6 +157,10 @@
     total = RMAX * row_tiles
 
     whole = pl.BlockSpec(memory_space=pltpu.VMEM)
+
+    def once(array):
+        return pl.BlockSpec(array.shape, lambda i: (0,) * array.ndim, pipeline_mode=pl.Buffered(1))
+
     scalars = pl.BlockSpec(memory_space=pltpu.SMEM)
     block = pl.BlockSpec((tile, width), lambda i: (i, 0))
     pivots = pivots.reshape(1, tile)
@@ -149,7 +168,7 @@
         functools.partial(update_kernel, len(xw), len(vz), per, row_tiles, col_tiles, tile),
         grid=(row_tiles,),
         out_shape=pltpu.VMEM(front.shape, front.dtype),
-        in_specs=[block] + [whole] * 2 + [scalars] * 3 + [whole] * (len(xw) + len(vz)),
+        in_specs=[block] + [whole] * 2 + [scalars] * 3 + [once(array) for array in (*xw, *vz)],
         out_specs=block,
         scratch_shapes=[
             pltpu.VMEM((tile // LANES, total, LANES), jnp.float32),
@@ -160,7 +179,7 @@
         compiler_params=pltpu.CompilerParams(vmem_limit_bytes=8 * MIB),
         cost_estimate=pl.CostEstimate(flops=2 * front.size * 256, bytes_accessed=2 * front.size * 4, transcendentals=0),
         name="front_less_update",
-    )(in_hbm(front), dinv, pivots, rank_rows, rank_cols, admissible, *xw, *vz)
+    )(in_hbm(front), dinv, pivots, rank_rows, rank_cols, admissible, *[in_hbm(array) for array in (*xw, *vz)])
 
 
 def add_kernel(members, tile, row_map, base, *rest):
@@ -254,45 +273,48 @@
     pieces = list(pieces)
     half = devices // 2
     crossing = list(reversed(range(half, devices)))
-    local = [m for pair in zip(reversed(range(NEAR, half)), [3, 2, 1] + [None] * half) for m in pair if m]
-    between = [("xw", m) for m in range(1, NEAR)] + [("vz", m) for m in range(1, lax.axis_size("row"))]
-    ready = len(between)
-    between += [("child", m) for m in local]
+    local = [m for pair in zip(reversed(range(NEAR, half)), [3] + [None] * half) for m in pair if m] + [2, 1]
+    factors = [("xw", m) for m in range(1, NEAR)] + [("vz", m) for m in range(1, lax.axis_size("row"))]
     gaps = len(crossing) - 2
-    turn = [2 + i * gaps // len(between) for i in range(len(between))]
-    update_at = turn[ready - 1] + 2
-    order, spots, xw, vz = [0], {0: None}, [], []
-
-    def got(m):
-        return pieces[0] if m == 0 else sender.arrived[spots[m]]
+    early = gaps * 7 // 6 - len(factors)
+    between = factors + [("child", m) for m in local[:early]]
+    order, spots, xw, vz = [0], {}, [], []
+
+    def send(m):
+        spots[m] = sender.send(pieces[m], GROUP, m)
+        order.append(m)
 
     def add(out, members):
-        return add_child(out, base, [got(m) for m in members], members, row_map, tile)
+        got = [sender.arrived[spots[m]] if m else pieces[0] for m in members]
+        return add_child(out, base, got, members, row_map, tile)
 
     for n, m in enumerate(crossing):
         for i, (kind, other) in enumerate(between):
-            if turn[i] == n and kind == "xw":
-                if not xw:
-                    line = jnp.stack([mine] + [sender.arrived[i] for i in line])
-                xw.append(sender.send(line, GROUP, other))
-            elif turn[i] == n and kind == "vz":
-                if not vz:
-                    both = jnp.concatenate([v_fac, z_fac], axis=0)
-                vz.append(sender.send(both, ("row",), other))
-            elif turn[i] == n:
-                spots[other] = sender.send(pieces[other], GROUP, other)
-                order.append(other)
-        if n == update_at:
-            xw = [line] + [sender.arrived[i] for i in xw]
-            vz = [both] + [sender.arrived[i] for i in vz]
-            base = subtract_update(front, dinv, pivots, rank_rows, rank_cols, admissible, xw, vz)
+            if n == 2 + i * gaps // len(between):
+                if kind == "child":
+                    send(other)
+                elif kind == "xw":
+                    if not xw:
+                        line = jnp.stack([mine] + [sender.arrived[i] for i in line])
+                    xw.append(sender.send(line, GROUP, other))
+                else:
+                    if not vz:
+                        both = jnp.concatenate([v_fac, z_fac], axis=0)
+                    vz.append(sender.send(both, ("row",), other))
+        send(m)
+    xw = [line] + [sender.arrived[i] for i in xw]
+    vz = [both] + [sender.arrived[i] for i in vz]
+    base = subtract_update(front, dinv, pivots, rank_rows, rank_cols, admissible, xw, vz)
+    done = len(order) - WINDOW
+    for n, m in enumerate(local[early:]):
+        if n == 0:
             base, pieces[m] = lax.optimization_barrier((base, pieces[m]))
-        if n == len(crossing) - 1:
-            out = add(None, order[: half - 1])
+        if n == 1:
+            out = add(None, order[:done])
             out, pieces[m] = lax.optimization_barrier((out, pieces[m]))
-        spots[m] = sender.send(pieces[m], GROUP, m)
-        order.append(m)
-    return add(add(out, order[half - 1 : -2]), order[-2:])
+        send(m)
+    out = add(out, order[done : done + WINDOW - 1])
+    return add(out, order[done + WINDOW - 1 :])
 
 
 def solution(mesh):

time: 134 us -> 124 us (0.925); the launches traced: 134 us -> 123 us
  waiting for transfers between devices: 51.7 us -> 38.8 us
  starting transfers between devices: 52 us -> 57.2 us
  local copies, waits for them, and re-layouts: 6.48 us -> 1.4 us
  Pallas kernels: 22.8 us -> 24.2 us
    ppermute x22, waiting for transfers between devices: 51.7 us -> 38.8 us  [send(): lax.ppermute(array, axes, [(d, d ^ m) for d in range(size)])]
    unnamed x46 -> x34, local copies, waits for them, and re-layouts: 6.4 us -> 0.65 us
    ppermute x22, starting transfers between devices: 52 us -> 57.2 us  [send(): lax.ppermute(array, axes, [(d, d ^ m) for d in range(size)])]
  transfers between devices with their start and end apart: 22 -> 22, of which waited for: 7 -> 7; matrix products, arithmetic and copies ran while one was open for 0% -> 1% of each run, Pallas kernels for 16% -> 18%
where the time goes in v2:
time: 124 us; the launch traced here: 123 us
  starting transfers between devices  57.2 us (46%)
  waiting for transfers between devices  38.8 us (31%)
  Pallas kernels  24.2 us (20%)
  local copies, waits for them, and re-layouts  1.4 us (1%)
    ppermute x22, starting transfers between devices, send(): lax.ppermute(array, axes, [(d, d ^ m) for d in range(size)])  57.2 us
    ppermute x22, waiting for transfers between devices, send(): lax.ppermute(array, axes, [(d, d ^ m) for d in range(size)])  38.8 us
    pallas_call x1, Pallas kernels, subtract_update(): pl.pallas_call(functools.partial(update_kernel, len(xw), len(vz), per, ro...  13.5 us
    pallas_call x3, Pallas kernels, add_child(): pl.pallas_call(functools.partial(add_kernel, members, tile), out_shape=pl...  5.49 us
    pallas_call x1, Pallas kernels, place(): pl.pallas_call(functools.partial(place_kernel, tiles, groups, tile, col_t...  5.16 us
  transfers between devices with their start and end apart: 22, of which 7 were waited for; matrix products, arithmetic and copies ran while one was open for 1% of the time, Pallas kernels for 18%

profile of v2, /device:TPU:0, one launch (start us, length us, event | category | flops | bytes accessed | tf_op | source)
XLA Modules:
  0.0 122.7 jit_solution(6278730897955636357)
XLA Ops:
  0.0 0.0 copy-start.2
  0.0 0.8 pad_add_fusion
  0.9 5.1 %collective-permute-start.2 = (f32[16,1024]{1,0:T(8,128)S(1)}, f32[16,1024]{1,0:T(8,128)S(1)}, u32[]{:S(2)}, u32[]{:S(2)}) collective-permute-start(f32[16,1024]{1,0:T(8,128)S(1)} %pad_add_fusion), channel_id=1, source_target_pairs={{0,12},{1,13},{2,14},{3,15},{4,8},{5,9},{6,10},{7,11},{8,4},{9,5},... | collective-permute-start | bytes 196616 | tf_op jit(solution)/shard_map/ppermute | solution.py:240
  5.9 0.0 collective-permute-start.1
  5.9 0.6 collective-permute-start
  6.6 5.2 %place_child.1 = (f32[2,128,256]{2,1,0:T(8,128)}, f32[2,128,256]{2,1,0:T(8,128)}, f32[2,128,256]{2,1,0:T(8,128)}, f32[2,128,256]{2,1,0:T(8,128)}, f32[2,128,256]...) custom-call(s32[32]{0:T(128)} %col_map.1, ...), custom_call_target="tpu_custom_call" | custom-call | bytes 8388608 | tf_op jit(solution)/shard_map/place_child/pallas_call | solution.py:65
  11.7 3.3 %collective-permute-start.5 = (f32[2,128,256]{2,1,0:T(8,128)}, f32[2,128,256]{2,1,0:T(8,128)S(1)}, u32[]{:S(2)}, u32[]{:S(2)}) collective-permute-start(f32[2,128,256]{2,1,0:T(8,128)} %get-tuple-element.108), channel_id=1, source_target_pairs={{0,15},{1,14},{2,13},{3,12},{4,11},{5,10},{6,9},{7,8},{8,7},{9,6},... | collective-permute-start | bytes 786440 | tf_op jit(solution)/shard_map/ppermute | solution.py:240
  15.1 1.5 %collective-permute-start.13 = (f32[2,128,256]{2,1,0:T(8,128)}, f32[2,128,256]{2,1,0:T(8,128)S(1)}, u32[]{:S(2)}, u32[]{:S(2)}) collective-permute-start(f32[2,128,256]{2,1,0:T(8,128)} %get-tuple-element.128), channel_id=1, source_target_pairs={{0,14},{1,15},{2,12},{3,13},{4,10},{5,11},{6,8},{7,9},{8,6},{9,7},... | collective-permute-start | bytes 786440 | tf_op jit(solution)/shard_map/ppermute | solution.py:240
  16.6 0.0 collective-permute-done.2
  16.6 0.0 collective-permute-done.1
  16.6 0.0 collective-permute-done
  16.6 0.0 copy-start.5
  16.6 0.6 collective-permute-start.4
  17.2 0.6 collective-permute-start.3
  17.8 3.2 %collective-permute-start.8 = (f32[2,128,256]{2,1,0:T(8,128)}, f32[2,128,256]{2,1,0:T(8,128)S(1)}, u32[]{:S(2)}, u32[]{:S(2)}) collective-permute-start(f32[2,128,256]{2,1,0:T(8,128)} %get-tuple-element.119), channel_id=1, source_target_pairs={{0,13},{1,12},{2,15},{3,14},{4,9},{5,8},{6,11},{7,10},{8,5},{9,4},... | collective-permute-start | bytes 786440 | tf_op jit(solution)/shard_map/ppermute | solution.py:240
  21.1 2.0 %collective-permute-done.5.rest_1_ = f32[2,128,256]{2,1,0:T(8,128)S(1)} collective-permute-done((f32[2,128,256]{2,1,0:T(8,128)}, f32[2,128,256]{2,1,0:T(8,128)S(1)}, u32[]{:S(2)}, u32[]{:S(2)}) %collective-permute-start.5) | collective-permute-done | bytes 262176 | tf_op jit(solution)/shard_map/ppermute | solution.py:240
  23.1 0.6 collective-permute-start.6
  23.7 5.9 %collective-permute-done.13.rest_2_ = f32[2,128,256]{2,1,0:T(8,128)S(1)} collective-permute-done((f32[2,128,256]{2,1,0:T(8,128)}, f32[2,128,256]{2,1,0:T(8,128)S(1)}, u32[]{:S(2)}, u32[]{:S(2)}) %collective-permute-start.13) | collective-permute-done | bytes 262176 | tf_op jit(solution)/shard_map/ppermute | solution.py:240
  29.6 1.7 %collective-permute-start.14 = (f32[2,128,256]{2,1,0:T(8,128)}, f32[2,128,256]{2,1,0:T(8,128)S(1)}, u32[]{:S(2)}, u32[]{:S(2)}) collective-permute-start(f32[2,128,256]{2,1,0:T(8,128)} %get-tuple-element.132), channel_id=1, source_target_pairs={{0,12},{1,13},{2,14},{3,15},{4,8},{5,9},{6,10},{7,11},{8,4},{9,5},... | collective-permute-start | bytes 786440 | tf_op jit(solution)/shard_map/ppermute | solution.py:240
  31.3 3.5 %collective-permute-done.4.rest_2_ = f32[4,16,1024]{2,1,0:T(8,128)S(1)} collective-permute-done((f32[4,16,1024]{2,1,0:T(8,128)S(1)}, f32[4,16,1024]{2,1,0:T(8,128)S(1)}, u32[]{:S(2)}, u32[]{:S(2)}) %collective-permute-start.4) | collective-permute-done | bytes 262176 | tf_op jit(solution)/shard_map/ppermute | solution.py:240
  34.7 17.8 %collective-permute-start.15 = (f32[2,128,256]{2,1,0:T(8,128)}, f32[2,128,256]{2,1,0:T(8,128)S(1)}, u32[]{:S(2)}, u32[]{:S(2)}) collective-permute-start(f32[2,128,256]{2,1,0:T(8,128)} %get-tuple-element.135), channel_id=1, source_target_pairs={{0,11},{1,10},{2,9},{3,8},{4,15},{5,14},{6,13},{7,12},{8,3},{9,2},... | collective-permute-start | bytes 786440 | tf_op jit(solution)/shard_map/ppermute | solution.py:240
  52.5 0.0 copy-done.11
  52.5 0.0 copy-done.10
  52.5 0.1 pad_maximum_fusion.1.rest_4_
  52.6 0.0 copy-start.6
  52.6 0.0 collective-permute-done.3.rest_1_
  52.6 0.0 copy-start.8
  52.6 1.6 %collective-permute-start.7 = (f32[4,8192]{1,0:T(4,128)S(1)}, f32[4,8192]{1,0:T(4,128)S(1)}, u32[]{:S(2)}, u32[]{:S(2)}) collective-permute-start(f32[4,8192]{1,0:T(4,128)S(1)} %pad_maximum_fusion.1.rest_4_), channel_id=1, source_target_pairs={{0,16},{16,0},{1,17},{17,1},{2,18},{18,2},{3,19},{19,3},{4,20},{20... | collective-permute-start | bytes 393224 | tf_op jit(solution)/shard_map/ppermute | solution.py:240
  54.2 0.0 collective-permute-done.8.rest_3_
  54.2 7.8 %collective-permute-start.9 = (f32[2,128,256]{2,1,0:T(8,128)}, f32[2,128,256]{2,1,0:T(8,128)S(1)}, u32[]{:S(2)}, u32[]{:S(2)}) collective-permute-start(f32[2,128,256]{2,1,0:T(8,128)} %get-tuple-element.120), channel_id=1, source_target_pairs={{0,7},{1,6},{2,5},{3,4},{4,3},{5,2},{6,1},{7,0},{8,15},{9,14},{10,... | collective-permute-start | bytes 786440 | tf_op jit(solution)/shard_map/ppermute | solution.py:240
  62.1 0.0 copy-done.8
  62.1 0.0 collective-permute-done.7.rest_5_
  62.1 0.1 collective-permute-start.18
  62.1 0.6 copy-done.9
  62.7 0.0 collective-permute-done.6.rest_3_
  62.7 6.3 %collective-permute-start.11 = (f32[2,128,256]{2,1,0:T(8,128)}, f32[2,128,256]{2,1,0:T(8,128)S(1)}, u32[]{:S(2)}, u32[]{:S(2)}) collective-permute-start(f32[2,128,256]{2,1,0:T(8,128)} %get-tuple-element.123), channel_id=1, source_target_pairs={{0,10},{1,11},{2,8},{3,9},{4,14},{5,15},{6,12},{7,13},{8,2},{9,3},... | collective-permute-start | bytes 786440 | tf_op jit(solution)/shard_map/ppermute | solution.py:240
  69.0 0.0 collective-permute-done.14.rest_4_
  69.0 0.0 collective-permute-start.16
  69.0 15.1 %collective-permute-done.15.rest_5_ = f32[2,128,256]{2,1,0:T(8,128)S(1)} collective-permute-done((f32[2,128,256]{2,1,0:T(8,128)}, f32[2,128,256]{2,1,0:T(8,128)S(1)}, u32[]{:S(2)}, u32[]{:S(2)}) %collective-permute-start.15) | collective-permute-done | bytes 262176 | tf_op jit(solution)/shard_map/ppermute | solution.py:240
  84.1 0.0 collective-permute-start.20
  84.1 0.8 copy.16.admissible
  84.9 0.0 copy-done.5
  84.9 0.0 copy-done.6
  85.0 13.5 %front_less_update.1.base = f32[2048,512]{1,0:T(8,128)S(1)} custom-call(f32[2048,512]{1,0:T(8,128)} %front.1, f32[256,256]{1,0:T(8,128)S(1)} %copy-done, s32[1,256]{1,0:T(1,128)S(1)} %bitcast.5, s32[8]{0:T(128)S(1)} %copy-done.3, s32[2]{0:T(128)S(1)} %copy-done.4, s32[8,2]{1,0:T(8,128)S(1)} %copy.16.admissible, f32[4,16,1024]{2,1,0:T(8,128)} %copy-done.5, ...), custom_call_target="tpu_custom_call" | custom-call | flops 536870912 | bytes 8388608 | tf_op jit(solution)/shard_map/front_less_update/pallas_call | solution.py:167
  98.5 0.0 collective-permute-done.9.rest_6_
  98.6 3.9 %collective-permute-start.10 = (f32[2,128,256]{2,1,0:T(8,128)S(1)}, f32[2,128,256]{2,1,0:T(8,128)S(1)}, u32[]{:S(2)}, u32[]{:S(2)}) collective-permute-start(f32[2,128,256]{2,1,0:T(8,128)S(1)} %copy-done.16), channel_id=1, source_target_pairs={{0,8},{1,9},{2,10},{3,11},{4,12},{5,13},{6,14},{7,15},{8,0},{9,1},... | collective-permute-start | bytes 786440 | tf_op jit(solution)/shard_map/ppermute | solution.py:240
  102.5 2.0 %add_child.3.rest_4_ = f32[2048,512]{1,0:T(8,128)} custom-call(s32[1,8]{1,0:T(1,128)} %row_map.5, f32[2048,512]{1,0:T(8,128)S(1)} %front_less_update.1.base, f32[2,128,256]{2,1,0:T(8,128)S(1)} %copy-done.1, f32[2,128,256]{2,1,0:T(8,128)S(1)} %collective-permute-done.5.rest_1_, f32[2,128,256]{2,1,0:T(8,128)S(1)} %collective-permute-done.13.rest_2_, ...), custom_call_target="tpu_custom_call" | custom-call | flops 458752 | bytes 1835008 | tf_op jit(solution)/shard_map/add_child/pallas_call | solution.py:215
  104.5 0.0 collective-permute-done.18.rest_2_
  104.5 0.0 copy-done.15
  104.5 0.6 collective-permute-start.19
  105.0 0.0 collective-permute-done.11.rest_0_
  105.1 0.0 collective-permute-start.12
  105.1 0.0 collective-permute-done.16.rest_1_
  105.1 0.0 copy-done.13
  105.1 0.1 collective-permute-start.17
  105.2 0.0 collective-permute-done.20.rest_3_
  105.2 1.7 %collective-permute-start.21 = (f32[2,128,256]{2,1,0:T(8,128)S(1)}, f32[2,128,256]{2,1,0:T(8,128)S(1)}, u32[]{:S(2)}, u32[]{:S(2)}) collective-permute-start(f32[2,128,256]{2,1,0:T(8,128)S(1)} %copy-done.12), channel_id=1, source_target_pairs={{0,1},{1,0},{2,3},{3,2},{4,5},{5,4},{6,7},{7,6},{8,9},{9,8},{10,11... | collective-permute-start | bytes 786440 | tf_op jit(solution)/shard_map/ppermute | solution.py:240
  106.9 1.7 %add_child.4.rest_5_ = f32[2048,512]{1,0:T(8,128)} custom-call(s32[1,8]{1,0:T(1,128)} %row_map.5, f32[2048,512]{1,0:T(8,128)S(1)} %front_less_update.1.base, f32[2,128,256]{2,1,0:T(8,128)S(1)} %collective-permute-done.11.rest_0_, f32[2,128,256]{2,1,0:T(8,128)S(1)} %collective-permute-done.16.rest_1_, ...), custom_call_target="tpu_custom_call", output_to_operand_aliasing={{}: (6, {})} | custom-call | flops 262144 | bytes 1048576 | tf_op jit(solution)/shard_map/add_child/pallas_call | solution.py:215
  108.6 4.9 %collective-permute-done.10.rest_0_ = f32[2,128,256]{2,1,0:T(8,128)S(1)} collective-permute-done((f32[2,128,256]{2,1,0:T(8,128)S(1)}, f32[2,128,256]{2,1,0:T(8,128)S(1)}, u32[]{:S(2)}, u32[]{:S(2)}) %collective-permute-start.10) | collective-permute-done | bytes 262176 | tf_op jit(solution)/shard_map/ppermute | solution.py:240
  113.6 0.0 collective-permute-done.19.rest_3_
  113.6 4.4 %collective-permute-done.12.rest_1_ = f32[2,128,256]{2,1,0:T(8,128)S(1)} collective-permute-done((f32[2,128,256]{2,1,0:T(8,128)S(1)}, f32[2,128,256]{2,1,0:T(8,128)S(1)}, u32[]{:S(2)}, u32[]{:S(2)}) %collective-permute-start.12) | collective-permute-done | bytes 262176 | tf_op jit(solution)/shard_map/ppermute | solution.py:240
  118.0 2.9 %collective-permute-done.17.rest_2_ = f32[2,128,256]{2,1,0:T(8,128)S(1)} collective-permute-done((f32[2,128,256]{2,1,0:T(8,128)S(1)}, f32[2,128,256]{2,1,0:T(8,128)S(1)}, u32[]{:S(2)}, u32[]{:S(2)}) %collective-permute-start.17) | collective-permute-done | bytes 262176 | tf_op jit(solution)/shard_map/ppermute | solution.py:240
  120.9 0.0 collective-permute-done.21.rest_4_
  120.9 1.8 %add_child.5 = f32[2048,512]{1,0:T(8,128)} custom-call(s32[1,8]{1,0:T(1,128)} %row_map.5, f32[2048,512]{1,0:T(8,128)S(1)} %front_less_update.1.base, f32[2,128,256]{2,1,0:T(8,128)S(1)} %collective-permute-done.10.rest_0_, f32[2,128,256]{2,1,0:T(8,128)S(1)} %collective-permute-done.12.rest_1_, ...), custom_call_target="tpu_custom_call", output_to_operand_aliasing={{}: (7, {})} | custom-call | flops 327680 | bytes 1310720 | tf_op jit(solution)/shard_map/add_child/pallas_call | solution.py:215
  (23 shorter events, 0.1 us)
Async XLA Ops:
  0.0 52.5 %copy-start.11 = (f32[2,8192]{1,0:T(2,128)S(1)}, f32[2,8192]{1,0:T(2,128)}, u32[]{:S(2)}) copy-start(f32[2,8192]{1,0:T(2,128)} %param.19) | copy-start | bytes 196612
  0.0 52.5 %copy-start.10 = (f32[2,8192]{1,0:T(2,128)S(1)}, f32[2,8192]{1,0:T(2,128)}, u32[]{:S(2)}) copy-start(f32[2,8192]{1,0:T(2,128)} %param.20) | copy-start | bytes 196612
  0.0 84.9 %copy-start.3 = (s32[8]{0:T(128)S(1)}, s32[8]{0:T(128)}, u32[]{:S(2)}) copy-start(s32[8]{0:T(128)} %rank_rows) | copy-start | bytes 100
  0.0 84.9 %copy-start.4 = (s32[2]{0:T(128)S(1)}, s32[2]{0:T(128)}, u32[]{:S(2)}) copy-start(s32[2]{0:T(128)} %rank_cols) | copy-start | bytes 28
  0.0 84.9 %copy-start = (f32[256,256]{1,0:T(8,128)S(1)}, f32[256,256]{1,0:T(8,128)}, u32[]{:S(2)}) copy-start(f32[256,256]{1,0:T(8,128)} %dinv.1) | copy-start | bytes 786436
  0.0 84.9 %copy-start.2 = (s32[256]{0:T(256)S(1)}, s32[256]{0:T(256)}, u32[]{:S(2)}) copy-start(s32[256]{0:T(256)} %param.22) | copy-start | bytes 3076
  0.9 15.7 %collective-permute-start.2 = (f32[16,1024]{1,0:T(8,128)S(1)}, f32[16,1024]{1,0:T(8,128)S(1)}, u32[]{:S(2)}, u32[]{:S(2)}) collective-permute-start(f32[16,1024]{1,0:T(8,128)S(1)} %pad_add_fusion), channel_id=1, source_target_pairs={{0,12},{1,13},{2,14},{3,15},{4,8},{5,9},{6,10},{7,11},{8,4},{9,5},... | collective-permute-start | bytes 196616 | tf_op jit(solution)/shard_map/ppermute | solution.py:240
  5.9 10.6 %collective-permute-start.1 = (f32[16,1024]{1,0:T(8,128)S(1)}, f32[16,1024]{1,0:T(8,128)S(1)}, u32[]{:S(2)}, u32[]{:S(2)}) collective-permute-start(f32[16,1024]{1,0:T(8,128)S(1)} %pad_add_fusion), channel_id=1, source_target_pairs={{0,8},{1,9},{2,10},{3,11},{4,12},{5,13},{6,14},{7,15},{8,0},{9,1},... | collective-permute-start | bytes 196616 | tf_op jit(solution)/shard_map/ppermute | solution.py:240
  5.9 10.6 %collective-permute-start = (f32[16,1024]{1,0:T(8,128)S(1)}, f32[16,1024]{1,0:T(8,128)S(1)}, u32[]{:S(2)}, u32[]{:S(2)}) collective-permute-start(f32[16,1024]{1,0:T(8,128)S(1)} %pad_add_fusion), channel_id=1, source_target_pairs={{0,4},{1,5},{2,6},{3,7},{4,0},{5,1},{6,2},{7,3},{8,12},{9,13},{10,... | collective-permute-start | bytes 196616 | tf_op jit(solution)/shard_map/ppermute | solution.py:240
  11.7 11.3 %collective-permute-start.5 = (f32[2,128,256]{2,1,0:T(8,128)}, f32[2,128,256]{2,1,0:T(8,128)S(1)}, u32[]{:S(2)}, u32[]{:S(2)}) collective-permute-start(f32[2,128,256]{2,1,0:T(8,128)} %get-tuple-element.108), channel_id=1, source_target_pairs={{0,15},{1,14},{2,13},{3,12},{4,11},{5,10},{6,9},{7,8},{8,7},{9,6},... | collective-permute-start | bytes 786440 | tf_op jit(solution)/shard_map/ppermute | solution.py:240
  15.1 14.5 %collective-permute-start.13 = (f32[2,128,256]{2,1,0:T(8,128)}, f32[2,128,256]{2,1,0:T(8,128)S(1)}, u32[]{:S(2)}, u32[]{:S(2)}) collective-permute-start(f32[2,128,256]{2,1,0:T(8,128)} %get-tuple-element.128), channel_id=1, source_target_pairs={{0,14},{1,15},{2,12},{3,13},{4,10},{5,11},{6,8},{7,9},{8,6},{9,7},... | collective-permute-start | bytes 786440 | tf_op jit(solution)/shard_map/ppermute | solution.py:240
  16.6 68.3 %copy-start.5 = (f32[4,16,1024]{2,1,0:T(8,128)}, f32[4,16,1024]{2,1,0:T(8,128)S(1)}, u32[]{:S(2)}) copy-start(f32[4,16,1024]{2,1,0:T(8,128)S(1)} %pad_maximum_fusion.rest_0_) | copy-start | bytes 786436
  16.6 18.1 %collective-permute-start.4 = (f32[4,16,1024]{2,1,0:T(8,128)S(1)}, f32[4,16,1024]{2,1,0:T(8,128)S(1)}, u32[]{:S(2)}, u32[]{:S(2)}) collective-permute-start(f32[4,16,1024]{2,1,0:T(8,128)S(1)} %pad_maximum_fusion.rest_0_), channel_id=1, source_target_pairs={{0,2},{1,3},{2,0},{3,1},{4,6},{5,7},{6,4},{7,5},{8,10},{9,11},{10,... | collective-permute-start | bytes 786440 | tf_op jit(solution)/shard_map/ppermute | solution.py:240
  17.2 35.4 %collective-permute-start.3 = (f32[4,16,1024]{2,1,0:T(8,128)S(1)}, f32[4,16,1024]{2,1,0:T(8,128)S(1)}, u32[]{:S(2)}, u32[]{:S(2)}) collective-permute-start(f32[4,16,1024]{2,1,0:T(8,128)S(1)} %pad_maximum_fusion.rest_0_), channel_id=1, source_target_pairs={{0,1},{1,0},{2,3},{3,2},{4,5},{5,4},{6,7},{7,6},{8,9},{9,8},{10,11... | collective-permute-start | bytes 786440 | tf_op jit(solution)/shard_map/ppermute | solution.py:240
  17.8 36.4 %collective-permute-start.8 = (f32[2,128,256]{2,1,0:T(8,128)}, f32[2,128,256]{2,1,0:T(8,128)S(1)}, u32[]{:S(2)}, u32[]{:S(2)}) collective-permute-start(f32[2,128,256]{2,1,0:T(8,128)} %get-tuple-element.119), channel_id=1, source_target_pairs={{0,13},{1,12},{2,15},{3,14},{4,9},{5,8},{6,11},{7,10},{8,5},{9,4},... | collective-permute-start | bytes 786440 | tf_op jit(solution)/shard_map/ppermute | solution.py:240
  23.1 39.7 %collective-permute-start.6 = (f32[4,16,1024]{2,1,0:T(8,128)S(1)}, f32[4,16,1024]{2,1,0:T(8,128)}, u32[]{:S(2)}, u32[]{:S(2)}) collective-permute-start(f32[4,16,1024]{2,1,0:T(8,128)S(1)} %pad_maximum_fusion.rest_0_), channel_id=1, source_target_pairs={{0,3},{1,2},{2,1},{3,0},{4,7},{5,6},{6,5},{7,4},{8,11},{9,10},{10,... | collective-permute-start | bytes 786440 | tf_op jit(solution)/shard_map/ppermute | solution.py:240
  29.6 39.5 %collective-permute-start.14 = (f32[2,128,256]{2,1,0:T(8,128)}, f32[2,128,256]{2,1,0:T(8,128)S(1)}, u32[]{:S(2)}, u32[]{:S(2)}) collective-permute-start(f32[2,128,256]{2,1,0:T(8,128)} %get-tuple-element.132), channel_id=1, source_target_pairs={{0,12},{1,13},{2,14},{3,15},{4,8},{5,9},{6,10},{7,11},{8,4},{9,5},... | collective-permute-start | bytes 786440 | tf_op jit(solution)/shard_map/ppermute | solution.py:240
  34.7 50.2 %copy-start.7 = (f32[4,16,1024]{2,1,0:T(8,128)}, f32[4,16,1024]{2,1,0:T(8,128)S(1)}, u32[]{:S(2)}) copy-start(f32[4,16,1024]{2,1,0:T(8,128)S(1)} %collective-permute-done.4.rest_2_) | copy-start | bytes 786436
  34.7 49.4 %collective-permute-start.15 = (f32[2,128,256]{2,1,0:T(8,128)}, f32[2,128,256]{2,1,0:T(8,128)S(1)}, u32[]{:S(2)}, u32[]{:S(2)}) collective-permute-start(f32[2,128,256]{2,1,0:T(8,128)} %get-tuple-element.135), channel_id=1, source_target_pairs={{0,11},{1,10},{2,9},{3,8},{4,15},{5,14},{6,13},{7,12},{8,3},{9,2},... | collective-permute-start | bytes 786440 | tf_op jit(solution)/shard_map/ppermute | solution.py:240
  52.6 32.3 %copy-start.6 = (f32[4,8192]{1,0:T(4,128)}, f32[4,8192]{1,0:T(4,128)S(1)}, u32[]{:S(2)}) copy-start(f32[4,8192]{1,0:T(4,128)S(1)} %pad_maximum_fusion.1.rest_4_) | copy-start | bytes 393220
  52.6 9.4 %copy-start.8 = (f32[4,16,1024]{2,1,0:T(8,128)}, f32[4,16,1024]{2,1,0:T(8,128)S(1)}, u32[]{:S(2)}) copy-start(f32[4,16,1024]{2,1,0:T(8,128)S(1)} %collective-permute-done.3.rest_1_) | copy-start | bytes 786436
  52.6 9.4 %collective-permute-start.7 = (f32[4,8192]{1,0:T(4,128)S(1)}, f32[4,8192]{1,0:T(4,128)S(1)}, u32[]{:S(2)}, u32[]{:S(2)}) collective-permute-start(f32[4,8192]{1,0:T(4,128)S(1)} %pad_maximum_fusion.1.rest_4_), channel_id=1, source_target_pairs={{0,16},{16,0},{1,17},{17,1},{2,18},{18,2},{3,19},{19,3},{4,20},{20... | collective-permute-start | bytes 393224 | tf_op jit(solution)/shard_map/ppermute | solution.py:240
  54.2 44.3 %collective-permute-start.9 = (f32[2,128,256]{2,1,0:T(8,128)}, f32[2,128,256]{2,1,0:T(8,128)S(1)}, u32[]{:S(2)}, u32[]{:S(2)}) collective-permute-start(f32[2,128,256]{2,1,0:T(8,128)} %get-tuple-element.120), channel_id=1, source_target_pairs={{0,7},{1,6},{2,5},{3,4},{4,3},{5,2},{6,1},{7,0},{8,15},{9,14},{10,... | collective-permute-start | bytes 786440 | tf_op jit(solution)/shard_map/ppermute | solution.py:240
  62.1 0.7 copy-start.9
  62.1 42.4 %collective-permute-start.18 = (f32[2,128,256]{2,1,0:T(8,128)}, f32[2,128,256]{2,1,0:T(8,128)S(1)}, u32[]{:S(2)}, u32[]{:S(2)}) collective-permute-start(f32[2,128,256]{2,1,0:T(8,128)} %get-tuple-element.143), channel_id=1, source_target_pairs={{0,9},{1,8},{2,11},{3,10},{4,13},{5,12},{6,15},{7,14},{8,1},{9,0},... | collective-permute-start | bytes 786440 | tf_op jit(solution)/shard_map/ppermute | solution.py:240
  62.7 42.3 %collective-permute-start.11 = (f32[2,128,256]{2,1,0:T(8,128)}, f32[2,128,256]{2,1,0:T(8,128)S(1)}, u32[]{:S(2)}, u32[]{:S(2)}) collective-permute-start(f32[2,128,256]{2,1,0:T(8,128)} %get-tuple-element.123), channel_id=1, source_target_pairs={{0,10},{1,11},{2,8},{3,9},{4,14},{5,15},{6,12},{7,13},{8,2},{9,3},... | collective-permute-start | bytes 786440 | tf_op jit(solution)/shard_map/ppermute | solution.py:240
  69.0 36.0 %collective-permute-start.16 = (f32[2,128,256]{2,1,0:T(8,128)}, f32[2,128,256]{2,1,0:T(8,128)S(1)}, u32[]{:S(2)}, u32[]{:S(2)}) collective-permute-start(f32[2,128,256]{2,1,0:T(8,128)} %get-tuple-element.140), channel_id=1, source_target_pairs={{0,3},{1,2},{2,1},{3,0},{4,7},{5,6},{6,5},{7,4},{8,11},{9,10},{10,... | collective-permute-start | bytes 786440 | tf_op jit(solution)/shard_map/ppermute | solution.py:240
  84.1 21.1 %collective-permute-start.20 = (f32[2,128,256]{2,1,0:T(8,128)}, f32[2,128,256]{2,1,0:T(8,128)S(1)}, u32[]{:S(2)}, u32[]{:S(2)}) collective-permute-start(f32[2,128,256]{2,1,0:T(8,128)} %get-tuple-element.146), channel_id=1, source_target_pairs={{0,6},{1,7},{2,4},{3,5},{4,2},{5,3},{6,0},{7,1},{8,14},{9,15},{10,... | collective-permute-start | bytes 786440 | tf_op jit(solution)/shard_map/ppermute | solution.py:240
  84.9 13.6 %copy-start.16 = (f32[2,128,256]{2,1,0:T(8,128)S(1)}, f32[2,128,256]{2,1,0:T(8,128)}, u32[]{:S(2)}) copy-start(f32[2,128,256]{2,1,0:T(8,128)} %get-tuple-element.121) | copy-start | bytes 786436
  85.0 17.5 %copy-start.1 = (f32[2,128,256]{2,1,0:T(8,128)S(1)}, f32[2,128,256]{2,1,0:T(8,128)}, u32[]{:S(2)}) copy-start(f32[2,128,256]{2,1,0:T(8,128)} %get-tuple-element.125.rest_0_) | copy-start | bytes 786436
  98.5 6.0 %copy-start.15 = (f32[2,128,256]{2,1,0:T(8,128)S(1)}, f32[2,128,256]{2,1,0:T(8,128)}, u32[]{:S(2)}) copy-start(f32[2,128,256]{2,1,0:T(8,128)} %get-tuple-element.144) | copy-start | bytes 786436
  98.5 6.5 %copy-start.14 = (f32[2,128,256]{2,1,0:T(8,128)S(1)}, f32[2,128,256]{2,1,0:T(8,128)}, u32[]{:S(2)}) copy-start(f32[2,128,256]{2,1,0:T(8,128)} %get-tuple-element.124) | copy-start | bytes 786436
  98.5 6.6 %copy-start.13 = (f32[2,128,256]{2,1,0:T(8,128)S(1)}, f32[2,128,256]{2,1,0:T(8,128)}, u32[]{:S(2)}) copy-start(f32[2,128,256]{2,1,0:T(8,128)} %get-tuple-element.141) | copy-start | bytes 786436
  98.5 6.7 %copy-start.12 = (f32[2,128,256]{2,1,0:T(8,128)S(1)}, f32[2,128,256]{2,1,0:T(8,128)}, u32[]{:S(2)}) copy-start(f32[2,128,256]{2,1,0:T(8,128)} %get-tuple-element.147) | copy-start | bytes 786436
  98.6 15.0 %collective-permute-start.10 = (f32[2,128,256]{2,1,0:T(8,128)S(1)}, f32[2,128,256]{2,1,0:T(8,128)S(1)}, u32[]{:S(2)}, u32[]{:S(2)}) collective-permute-start(f32[2,128,256]{2,1,0:T(8,128)S(1)} %copy-done.16), channel_id=1, source_target_pairs={{0,8},{1,9},{2,10},{3,11},{4,12},{5,13},{6,14},{7,15},{8,0},{9,1},... | collective-permute-start | bytes 786440 | tf_op jit(solution)/shard_map/ppermute | solution.py:240
  104.5 9.1 %collective-permute-start.19 = (f32[2,128,256]{2,1,0:T(8,128)S(1)}, f32[2,128,256]{2,1,0:T(8,128)S(1)}, u32[]{:S(2)}, u32[]{:S(2)}) collective-permute-start(f32[2,128,256]{2,1,0:T(8,128)S(1)} %copy-done.15), channel_id=1, source_target_pairs={{0,2},{1,3},{2,0},{3,1},{4,6},{5,7},{6,4},{7,5},{8,10},{9,11},{10,... | collective-permute-start | bytes 786440 | tf_op jit(solution)/shard_map/ppermute | solution.py:240
  105.1 12.9 %collective-permute-start.12 = (f32[2,128,256]{2,1,0:T(8,128)S(1)}, f32[2,128,256]{2,1,0:T(8,128)S(1)}, u32[]{:S(2)}, u32[]{:S(2)}) collective-permute-start(f32[2,128,256]{2,1,0:T(8,128)S(1)} %copy-done.14), channel_id=1, source_target_pairs={{0,5},{1,4},{2,7},{3,6},{4,1},{5,0},{6,3},{7,2},{8,13},{9,12},{10,... | collective-permute-start | bytes 786440 | tf_op jit(solution)/shard_map/ppermute | solution.py:240
  105.1 15.9 %collective-permute-start.17 = (f32[2,128,256]{2,1,0:T(8,128)S(1)}, f32[2,128,256]{2,1,0:T(8,128)S(1)}, u32[]{:S(2)}, u32[]{:S(2)}) collective-permute-start(f32[2,128,256]{2,1,0:T(8,128)S(1)} %copy-done.13), channel_id=1, source_target_pairs={{0,4},{1,5},{2,6},{3,7},{4,0},{5,1},{6,2},{7,3},{8,12},{9,13},{10,... | collective-permute-start | bytes 786440 | tf_op jit(solution)/shard_map/ppermute | solution.py:240
  105.2 15.7 %collective-permute-start.21 = (f32[2,128,256]{2,1,0:T(8,128)S(1)}, f32[2,128,256]{2,1,0:T(8,128)S(1)}, u32[]{:S(2)}, u32[]{:S(2)}) collective-permute-start(f32[2,128,256]{2,1,0:T(8,128)S(1)} %copy-done.12), channel_id=1, source_target_pairs={{0,1},{1,0},{2,3},{3,2},{4,5},{5,4},{6,7},{7,6},{8,9},{9,8},{10,11... | collective-permute-start | bytes 786440 | tf_op jit(solution)/shard_map/ppermute | solution.py:240

commit v3 on v2

v3 whole, which is shorter than its diff:
```python
import functools

import jax
import jax.numpy as jnp
import numpy as np
from jax import lax
from jax.experimental import pallas as pl
from jax.experimental.pallas import tpu as pltpu
from jax.sharding import PartitionSpec as P

RMAX = 64
LANES = 128
NEAR = 4
WINDOW = 5
GROUP = ("col", "leaf")
HIGHEST = lax.Precision.HIGHEST
MIB = 1 << 20


def group_index():
    return lax.axis_index("col") * lax.axis_size("leaf") + lax.axis_index("leaf")


def in_hbm(array):
    return pltpu.with_memory_space_constraint(array, pltpu.HBM)


def place_kernel(tiles, groups, tile, col_tiles, col_map, child, *rest):
    pieces = rest[: tiles // col_tiles]
    inverse, held, in_sem, out_sem = rest[tiles // col_tiles :]
    width = tiles // groups * tile
    me = group_index()

    def fetch(g):
        span = pl.ds(g * width, width)
        return pltpu.make_async_copy(child.at[:, span], held.at[:, span], in_sem.at[g])

    def store(m, j):
        b = inverse[(me ^ m) * col_tiles + j]
        span = pl.ds(pl.multiple_of(b * tile, tile), tile)
        return pltpu.make_async_copy(held.at[:, span], pieces[m].at[j], out_sem.at[m, j])

    for g in range(groups):
        fetch(g).start()
    for b in range(tiles):
        inverse[col_map[b]] = b
    for g in range(groups):
        fetch(g).wait()
    order = [(m, j) for m in reversed(range(len(pieces))) for j in range(col_tiles)]
    for m, j in order:
        store(m, j).start()
    for m, j in order:
        store(m, j).wait()


def in_vmem(array):
    return pltpu.with_memory_space_constraint(array, pltpu.VMEM)


def place(child, col_map, tile, devices):
    rows = child.shape[0]
    tiles = col_map.shape[0]
    col_tiles = tiles // devices
    groups = 8
    return pl.pallas_call(
        functools.partial(place_kernel, tiles, groups, tile, col_tiles),
        out_shape=[pltpu.HBM((col_tiles, rows, tile), child.dtype)] * devices,
        in_specs=[pl.BlockSpec(memory_space=pltpu.SMEM), pl.BlockSpec(memory_space=pltpu.HBM)],
        out_specs=[pl.BlockSpec(memory_space=pltpu.HBM)] * devices,
        scratch_shapes=[
            pltpu.SMEM((tiles,), jnp.int32),
            pltpu.VMEM(child.shape, child.dtype),
            pltpu.SemaphoreType.DMA((groups,)),
            pltpu.SemaphoreType.DMA((devices, col_tiles)),
        ],
        compiler_params=pltpu.CompilerParams(vmem_limit_bytes=8 * MIB),
        cost_estimate=pl.CostEstimate(flops=0, bytes_accessed=2 * child.size * 4, transcendentals=0),
        name="place_child",
    )(in_hbm(col_map), in_hbm(child))


def dot(a, b, contract=((1,), (0,))):
    return lax.dot_general(a, b, (contract, ((), ())), precision=HIGHEST, preferred_element_type=jnp.float32)


def log2(size):
    return size.bit_length() - 1


def factor_kernel(parts, halves, col_tiles, row_tiles, dinv, pivots, rank_rows, rank_cols, admissible, *rest):
    xw = rest[:parts]
    vz = rest[parts : parts + halves]
    left, right, ws, vs, zs = rest[parts + halves :]
    tile = dinv.shape[0]
    per = xw[0].shape[2] // tile
    chunk = vz[0].shape[1] // tile
    slots = xw[0].shape[0]
    rows = slots * row_tiles

    zs[...] = jnp.zeros_like(zs)
    for h in range(halves):
        for j in range(col_tiles):
            for p in range(chunk):
                at = pl.ds(j * RMAX + h * chunk + p, 1)
                span = pl.ds(p * tile, tile)
                vs[at, :] = vz[h][pl.ds(j, 1), span]
                zs[at, pl.ds(j * tile, tile)] = vz[h][pl.ds(col_tiles + j, 1), span]
    for q in range(per):
        for n in range(parts):
            at = pl.ds((q * parts + n) * rows, rows)
            span = pl.ds(q * tile, tile)
            mine = xw[n][:, :row_tiles, span].reshape(rows, tile)
            for g in range(tile // LANES):
                left[g, at, :] = mine[:, g * LANES : (g + 1) * LANES]
            ws[at, :] = xw[n][:, row_tiles:, span].reshape(rows, tile)

    hot = (lax.broadcasted_iota(jnp.int32, (tile, tile), 0) == pivots[...]).astype(jnp.float32)
    dv = dot(dot(hot, dinv[...]), vs[...], ((1,), (1,)))
    core = dot(ws[...], dv)

    row = lax.broadcasted_iota(jnp.int32, (row_tiles, col_tiles * RMAX), 0)
    lane = lax.broadcasted_iota(jnp.int32, (row_tiles, col_tiles * RMAX), 1)
    top_r, top_s = jnp.zeros_like(row), jnp.zeros_like(row)
    for i in range(row_tiles):
        for j in range(col_tiles):
            here = (row == i) & (lane >> log2(RMAX) == j)
            dense = admissible[i, j] == 0
            top_r = jnp.where(here, jnp.where(dense, RMAX, rank_rows[i]), top_r)
            top_s = jnp.where(here, jnp.where(dense, RMAX, rank_cols[j]), top_s)
    half = (lane & (RMAX - 1)) >> log2(chunk)
    s = ((lax.axis_index("row") ^ half) << log2(chunk)) + (lane & (chunk - 1))
    top_r = jnp.where(s < top_s, top_r, 0)
    top_r = jnp.broadcast_to(top_r[None], (RMAX,) + top_r.shape).reshape(core.shape)
    k = lax.broadcasted_iota(jnp.int32, core.shape, 0)
    source = ((k >> log2(row_tiles)) & (slots - 1)) * parts + ((k >> log2(rows)) & (parts - 1))
    r = (group_index() ^ source) * per + (k >> log2(rows * parts))
    product = dot(jnp.where(r < top_r, core, 0.0), zs[...])
    for g in range(right.shape[0]):
        right[g, :, :] = product[:, g * LANES : (g + 1) * LANES]


def factors(dinv, pivots, rank_rows, rank_cols, admissible, xw, vz):
    tile = dinv.shape[0]
    row_tiles, col_tiles = admissible.shape
    total = RMAX * row_tiles
    inner = pl.BlockSpec(memory_space=pltpu.VMEM)
    scalars = pl.BlockSpec(memory_space=pltpu.SMEM)
    return pl.pallas_call(
        functools.partial(factor_kernel, len(xw), len(vz), col_tiles, row_tiles),
        out_shape=[
            pltpu.HBM((tile // LANES, total, LANES), jnp.float32),
            pltpu.HBM((col_tiles * tile // LANES, total, LANES), jnp.float32),
        ],
        in_specs=[inner] * 2 + [scalars] * 3 + [inner] * (len(xw) + len(vz)),
        out_specs=[inner] * 2,
        scratch_shapes=[
            pltpu.VMEM((total, tile), jnp.float32),
            pltpu.VMEM((col_tiles * RMAX, tile), jnp.float32),
            pltpu.VMEM((col_tiles * RMAX, col_tiles * tile), jnp.float32),
        ],
        compiler_params=pltpu.CompilerParams(vmem_limit_bytes=12 * MIB),
        cost_estimate=pl.CostEstimate(flops=2 * total * tile * tile, bytes_accessed=16 * total * tile, transcendentals=0),
        name="update_factors",
    )(dinv, pivots.reshape(1, tile), rank_rows, rank_cols, admissible, *[in_hbm(array) for array in (*xw, *vz)])


def halves_of(array):
    high = array.astype(jnp.bfloat16)
    return high, (array - high.astype(jnp.float32)).astype(jnp.bfloat16)


def finish_kernel(count, tile, row_map, front, left, right, *rest):
    pieces = rest[:count]
    out, held, in_sem, out_sem = rest[count:]
    me = group_index()
    col_tiles, rows, _ = pieces[0].shape
    per_tile = tile // rows
    groups = count // per_tile

    def target(g):
        return row_map[0, lax.div(me ^ (g * per_tile), per_tile)]

    def at(g):
        return pl.ds(pl.multiple_of(target(g) * tile, tile), tile)

    def fetch(g):
        return pltpu.make_async_copy(front.at[at(g), :], held.at[g], in_sem.at[g])

    def store(g):
        return pltpu.make_async_copy(held.at[g], out.at[at(g), :], out_sem.at[g])

    for g in range(groups):
        fetch(g).start()
    for g in range(groups):
        mine = pl.ds(target(g), RMAX, stride=left.shape[1] // RMAX)
        a, b = halves_of(jnp.concatenate([left[n, mine, :] for n in range(left.shape[0])], axis=1))
        c, d = halves_of(jnp.concatenate([right[n, mine, :] for n in range(right.shape[0])], axis=1))
        update = lax.dot_general(
            jnp.concatenate([a, a, b, b], axis=0),
            jnp.concatenate([c, d, c, d], axis=0),
            (((0,), (0,)), ((), ())),
            preferred_element_type=jnp.float32,
        )
        fetch(g).wait()
        held[g] = held[g] - update
        for p in range(per_tile):
            m = g * per_tile + p
            low = pl.ds(pl.multiple_of(lax.rem(me ^ m, per_tile) * rows, rows), rows)
            for j in range(col_tiles):
                span = pl.ds(j * tile, tile)
                held[g, low, span] = held[g, low, span] + pieces[m][j]
        store(g).start()
    for g in range(groups):
        store(g).wait()


def finish(front, left, right, pieces, row_map, tile):
    row_tiles = front.shape[0] // tile
    inner = pl.BlockSpec(memory_space=pltpu.VMEM)
    outer = pl.BlockSpec(memory_space=pltpu.HBM)
    return pl.pallas_call(
        functools.partial(finish_kernel, len(pieces), tile),
        out_shape=pltpu.HBM(front.shape, front.dtype),
        in_specs=[pl.BlockSpec(memory_space=pltpu.SMEM), outer] + [inner] * (2 + len(pieces)),
        out_specs=outer,
        scratch_shapes=[
            pltpu.VMEM((row_tiles, tile, front.shape[1]), front.dtype),
            pltpu.SemaphoreType.DMA((row_tiles,)),
            pltpu.SemaphoreType.DMA((row_tiles,)),
        ],
        compiler_params=pltpu.CompilerParams(vmem_limit_bytes=16 * MIB),
        cost_estimate=pl.CostEstimate(flops=2 * front.size * 256, bytes_accessed=3 * front.size * 4, transcendentals=0),
        name="finish",
    )(in_hbm(row_map), in_hbm(front), left, right, *[in_vmem(piece) for piece in pieces])


class Sender:
    def __init__(self):
        self.arrived = []

    def send(self, array, axes, m):
        spot = len(self.arrived) - WINDOW
        if spot >= 0:
            array, self.arrived[spot] = lax.optimization_barrier((array, self.arrived[spot]))
        size = int(np.prod([lax.axis_size(axis) for axis in axes]))
        self.arrived.append(lax.ppermute(array, axes, [(d, d ^ m) for d in range(size)]))
        return len(self.arrived) - 1


def on_device(
    front,
    child,
    row_map,
    col_map,
    x_fac,
    w_fac,
    v_fac,
    z_fac,
    dinv,
    pivots,
    rank_rows,
    rank_cols,
    admissible,
):
    tile = dinv.shape[0]
    row_tiles = front.shape[0] // tile
    col_tiles = front.shape[1] // tile
    devices = lax.axis_size("col") * lax.axis_size("leaf")

    sender = Sender()
    mine = jnp.pad(x_fac, ((0, row_tiles), (0, 0))) + jnp.pad(w_fac, ((row_tiles, 0), (0, 0)))
    mine, child = lax.optimization_barrier((mine, child))
    line = [sender.send(mine, GROUP, m) for m in range(NEAR, devices, NEAR)]
    pieces = place(child, col_map, tile, devices)
    pieces, v_fac, z_fac, rank_rows, rank_cols, admissible = lax.optimization_barrier(
        (pieces, v_fac, z_fac, rank_rows, rank_cols, admissible)
    )

    pieces = list(pieces)
    half = devices // 2
    crossing = list(reversed(range(half, devices)))
    local = [m for pair in zip(reversed(range(NEAR, half)), [3, 2, 1] + [None] * half) for m in pair if m]
    between = [("xw", m) for m in range(1, NEAR)] + [("vz", m) for m in range(1, lax.axis_size("row"))]
    between += [("child", m) for m in local]
    gaps = len(crossing) - 2
    spots, xw, vz = {}, [], []
    for n, m in enumerate(crossing):
        for i, (kind, other) in enumerate(between):
            if n == 2 + i * gaps // len(between):
                if kind == "child":
                    if other == local[-3]:
                        given = [line] + [sender.arrived[i] for i in xw], [both] + [sender.arrived[i] for i in vz]
                        left, right = factors(dinv, pivots, rank_rows, rank_cols, admissible, *given)
                        left, right, pieces[other] = lax.optimization_barrier((left, right, pieces[other]))
                    spots[other] = sender.send(pieces[other], GROUP, other)
                elif kind == "xw":
                    if not xw:
                        line = jnp.stack([mine] + [sender.arrived[i] for i in line])
                    xw.append(sender.send(line, GROUP, other))
                else:
                    if not vz:
                        both = jnp.concatenate([v_fac, z_fac], axis=0)
                    vz.append(sender.send(both, ("row",), other))
        spots[m] = sender.send(pieces[m], GROUP, m)
    got = [pieces[0]] + [sender.arrived[spots[m]] for m in range(1, devices)]
    return finish(front, left, right, got, row_map, tile)


def solution(mesh):
    return jax.shard_map(
        on_device,
        mesh=mesh,
        in_specs=(
            P("row", GROUP),
            P(("row", "col", "leaf"), None),
            P("row", None),
            P(),
            P("row", GROUP),
            P("row", GROUP),
            P(GROUP, "row"),
            P(GROUP, "row"),
            P(),
            P(),
            P("row"),
            P(GROUP),
            P("row", GROUP),
        ),
        out_specs=P("row", GROUP),
        check_vma=False,
    )
```

time: 124 us -> 114 us (0.919)
  Pallas kernels: 24.2 us -> 14.8 us
  starting transfers between devices: 57.2 us -> 54.4 us
  local copies, waits for them, and re-layouts: 1.4 us -> 4 us
    pallas_call x4 -> x2, Pallas kernels: 19 us -> 9.72 us  [the longest x1 4.89 us: finish(): pl.pallas_call(functools.partial(finish_kernel, len(pieces), tile), out_s...]
    ppermute x22, starting transfers between devices: 57.2 us -> 54.4 us  [send(): lax.ppermute(array, axes, [(d, d ^ m) for d in range(size)])]
    unnamed x34 -> x24, local copies, waits for them, and re-layouts: 0.65 us -> 3.25 us
  transfers between devices with their start and end apart: 22 -> 22, of which waited for: 7 -> 7; matrix products, arithmetic and copies ran while one was open for 1% -> 1% of each run, Pallas kernels for 18% -> 9%
where the time goes in v3:
time: 114 us
  starting transfers between devices  54.4 us (48%)
  waiting for transfers between devices  39.5 us (35%)
  Pallas kernels  14.8 us (13%)
  local copies, waits for them, and re-layouts  4 us (4%)
    ppermute x22, starting transfers between devices, send(): lax.ppermute(array, axes, [(d, d ^ m) for d in range(size)])  54.4 us
    ppermute x22, waiting for transfers between devices, send(): lax.ppermute(array, axes, [(d, d ^ m) for d in range(size)])  39.5 us
    pallas_call x1, Pallas kernels, place(): pl.pallas_call(functools.partial(place_kernel, tiles, groups, tile, col_t...  5.13 us
    pallas_call x1, Pallas kernels, finish(): pl.pallas_call(functools.partial(finish_kernel, len(pieces), tile), out_s...  4.89 us
    pallas_call x1, Pallas kernels, factors(): pl.pallas_call(functools.partial(factor_kernel, len(xw), len(vz), col_til...  4.83 us
    unnamed x24, local copies, waits for them, and re-layouts  3.25 us
  transfers between devices with their start and end apart: 22, of which 7 were waited for; matrix products, arithmetic and copies ran while one was open for 1% of the time, Pallas kernels for 9%

profile of v3, /device:TPU:0, one launch (start us, length us, event | category | flops | bytes accessed | tf_op | source)
XLA Modules:
  0.0 113.8 jit_solution(9130359727187662668)
XLA Ops:
  0.0 0.0 copy-start.3
  0.0 0.8 pad_add_fusion
  0.9 5.1 %collective-permute-start.2 = (f32[16,1024]{1,0:T(8,128)S(1)}, f32[16,1024]{1,0:T(8,128)S(1)}, u32[]{:S(2)}, u32[]{:S(2)}) collective-permute-start(f32[16,1024]{1,0:T(8,128)S(1)} %pad_add_fusion), channel_id=1, source_target_pairs={{0,12},{1,13},{2,14},{3,15},{4,8},{5,9},{6,10},{7,11},{8,4},{9,5},... | collective-permute-start | bytes 196616 | tf_op jit(solution)/shard_map/ppermute | solution.py:246
  5.9 0.0 collective-permute-start.1
  5.9 0.6 collective-permute-start
  6.6 5.1 %place_child.1 = (f32[2,128,256]{2,1,0:T(8,128)}, f32[2,128,256]{2,1,0:T(8,128)}, f32[2,128,256]{2,1,0:T(8,128)}, f32[2,128,256]{2,1,0:T(8,128)}, f32[2,128,256]...) custom-call(s32[32]{0:T(128)} %col_map.1, ...), custom_call_target="tpu_custom_call" | custom-call | bytes 8388608 | tf_op jit(solution)/shard_map/place_child/pallas_call | solution.py:65
  11.7 3.3 %collective-permute-start.5 = (f32[2,128,256]{2,1,0:T(8,128)}, f32[2,128,256]{2,1,0:T(8,128)S(1)}, u32[]{:S(2)}, u32[]{:S(2)}) collective-permute-start(f32[2,128,256]{2,1,0:T(8,128)} %get-tuple-element.108), channel_id=1, source_target_pairs={{0,15},{1,14},{2,13},{3,12},{4,11},{5,10},{6,9},{7,8},{8,7},{9,6},... | collective-permute-start | bytes 786440 | tf_op jit(solution)/shard_map/ppermute | solution.py:246
  15.0 0.0 collective-permute-done.2
  15.0 0.0 collective-permute-done.1
  15.0 0.0 collective-permute-done
  15.1 0.0 copy-start.7
  15.1 1.6 %collective-permute-start.3 = (f32[4,16,1024]{2,1,0:T(8,128)S(1)}, f32[4,16,1024]{2,1,0:T(8,128)S(1)}, u32[]{:S(2)}, u32[]{:S(2)}) collective-permute-start(f32[4,16,1024]{2,1,0:T(8,128)S(1)} %pad_maximum_fusion.rest_0_), channel_id=1, source_target_pairs={{0,1},{1,0},{2,3},{3,2},{4,5},{5,4},{6,7},{7,6},{8,9},{9,8},{10,11... | collective-permute-start | bytes 786440 | tf_op jit(solution)/shard_map/ppermute | solution.py:246
  16.7 0.5 collective-permute-start.4
  17.2 1.1 %collective-permute-start.7 = (f32[2,128,256]{2,1,0:T(8,128)}, f32[2,128,256]{2,1,0:T(8,128)S(1)}, u32[]{:S(2)}, u32[]{:S(2)}) collective-permute-start(f32[2,128,256]{2,1,0:T(8,128)} %get-tuple-element.114), channel_id=1, source_target_pairs={{0,14},{1,15},{2,12},{3,13},{4,10},{5,11},{6,8},{7,9},{8,6},{9,7},... | collective-permute-start | bytes 786440 | tf_op jit(solution)/shard_map/ppermute | solution.py:246
  18.4 2.7 %collective-permute-start.13 = (f32[2,128,256]{2,1,0:T(8,128)}, f32[2,128,256]{2,1,0:T(8,128)S(1)}, u32[]{:S(2)}, u32[]{:S(2)}) collective-permute-start(f32[2,128,256]{2,1,0:T(8,128)} %get-tuple-element.134), channel_id=1, source_target_pairs={{0,13},{1,12},{2,15},{3,14},{4,9},{5,8},{6,11},{7,10},{8,5},{9,4},... | collective-permute-start | bytes 786440 | tf_op jit(solution)/shard_map/ppermute | solution.py:246
  21.1 1.9 %collective-permute-done.5.rest_15_ = f32[2,128,256]{2,1,0:T(8,128)S(1)} collective-permute-done((f32[2,128,256]{2,1,0:T(8,128)}, f32[2,128,256]{2,1,0:T(8,128)S(1)}, u32[]{:S(2)}, u32[]{:S(2)}) %collective-permute-start.5) | collective-permute-done | bytes 262176 | tf_op jit(solution)/shard_map/ppermute | solution.py:246
  23.0 0.6 collective-permute-start.6
  23.6 0.0 collective-permute-done.3.rest_1_
  23.6 11.2 %collective-permute-done.4.rest_2_ = f32[4,16,1024]{2,1,0:T(8,128)} collective-permute-done((f32[4,16,1024]{2,1,0:T(8,128)S(1)}, f32[4,16,1024]{2,1,0:T(8,128)}, u32[]{:S(2)}, u32[]{:S(2)}) %collective-permute-start.4) | collective-permute-done | bytes 262176 | tf_op jit(solution)/shard_map/ppermute | solution.py:246
  34.8 6.2 %collective-permute-start.18 = (f32[2,128,256]{2,1,0:T(8,128)}, f32[2,128,256]{2,1,0:T(8,128)S(1)}, u32[]{:S(2)}, u32[]{:S(2)}) collective-permute-start(f32[2,128,256]{2,1,0:T(8,128)} %get-tuple-element.143), channel_id=1, source_target_pairs={{0,7},{1,6},{2,5},{3,4},{4,3},{5,2},{6,1},{7,0},{8,15},{9,14},{10,... | collective-permute-start | bytes 786440 | tf_op jit(solution)/shard_map/ppermute | solution.py:246
  41.0 2.3 %collective-permute-start.11 = (f32[2,128,256]{2,1,0:T(8,128)}, f32[2,128,256]{2,1,0:T(8,128)S(1)}, u32[]{:S(2)}, u32[]{:S(2)}) collective-permute-start(f32[2,128,256]{2,1,0:T(8,128)} %get-tuple-element.128), channel_id=1, source_target_pairs={{0,12},{1,13},{2,14},{3,15},{4,8},{5,9},{6,10},{7,11},{8,4},{9,5},... | collective-permute-start | bytes 786440 | tf_op jit(solution)/shard_map/ppermute | solution.py:246
  43.3 0.0 copy-done.10
  43.3 0.0 copy-done.11
  43.3 0.1 pad_maximum_fusion.1.rest_4_
  43.3 0.0 copy-start.8
  43.4 0.0 collective-permute-done.7.rest_14_
  43.4 1.6 %collective-permute-start.8 = (f32[4,8192]{1,0:T(4,128)S(1)}, f32[4,8192]{1,0:T(4,128)}, u32[]{:S(2)}, u32[]{:S(2)}) collective-permute-start(f32[4,8192]{1,0:T(4,128)S(1)} %pad_maximum_fusion.1.rest_4_), channel_id=1, source_target_pairs={{0,16},{16,0},{1,17},{17,1},{2,18},{18,2},{3,19},{19,3},{4,20},{20... | collective-permute-start | bytes 393224 | tf_op jit(solution)/shard_map/ppermute | solution.py:246
  45.0 0.0 collective-permute-done.13.rest_13_
  45.0 0.0 collective-permute-start.14
  45.0 3.6 %collective-permute-done.8.rest_5_ = f32[4,8192]{1,0:T(4,128)} collective-permute-done((f32[4,8192]{1,0:T(4,128)S(1)}, f32[4,8192]{1,0:T(4,128)}, u32[]{:S(2)}, u32[]{:S(2)}) %collective-permute-start.8) | collective-permute-done | bytes 131104 | tf_op jit(solution)/shard_map/ppermute | solution.py:246
  48.6 7.9 %collective-permute-start.17 = (f32[2,128,256]{2,1,0:T(8,128)}, f32[2,128,256]{2,1,0:T(8,128)S(1)}, u32[]{:S(2)}, u32[]{:S(2)}) collective-permute-start(f32[2,128,256]{2,1,0:T(8,128)} %get-tuple-element.140), channel_id=1, source_target_pairs={{0,6},{1,7},{2,4},{3,5},{4,2},{5,3},{6,0},{7,1},{8,14},{9,15},{10,... | collective-permute-start | bytes 786440 | tf_op jit(solution)/shard_map/ppermute | solution.py:246
  56.5 0.0 collective-permute-done.6.rest_3_
  56.5 2.3 %collective-permute-start.9 = (f32[2,128,256]{2,1,0:T(8,128)}, f32[2,128,256]{2,1,0:T(8,128)S(1)}, u32[]{:S(2)}, u32[]{:S(2)}) collective-permute-start(f32[2,128,256]{2,1,0:T(8,128)} %get-tuple-element.124), channel_id=1, source_target_pairs={{0,11},{1,10},{2,9},{3,8},{4,15},{5,14},{6,13},{7,12},{8,3},{9,2},... | collective-permute-start | bytes 786440 | tf_op jit(solution)/shard_map/ppermute | solution.py:246
  58.8 0.0 collective-permute-done.18.rest_7_
  58.8 0.0 collective-permute-start.19
  58.8 0.0 collective-permute-done.11.rest_12_
  58.8 1.2 %collective-permute-start.12 = (f32[2,128,256]{2,1,0:T(8,128)}, f32[2,128,256]{2,1,0:T(8,128)S(1)}, u32[]{:S(2)}, u32[]{:S(2)}) collective-permute-start(f32[2,128,256]{2,1,0:T(8,128)} %get-tuple-element.129), channel_id=1, source_target_pairs={{0,2},{1,3},{2,0},{3,1},{4,6},{5,7},{6,4},{7,5},{8,10},{9,11},{10,... | collective-permute-start | bytes 786440 | tf_op jit(solution)/shard_map/ppermute | solution.py:246
  60.0 0.8 copy.14.admissible
  60.8 0.0 copy-done.7
  60.8 0.0 copy-done.9
  60.8 0.0 copy-done.8
  60.8 0.0 copy-done.6
  60.8 0.0 copy-done.5
  60.8 0.0 copy-done.4
  60.8 4.8 %update_factors.1 = (f32[2,512,128]{2,1,0:T(8,128)}, f32[4,512,128]{2,1,0:T(8,128)}) custom-call(f32[256,256]{1,0:T(8,128)S(1)} %copy-done.3, s32[1,256]{1,0:T(1,128)S(1)} %bitcast.5, s32[8]{0:T(128)S(1)} %copy-done.5, s32[2]{0:T(128)S(1)} %copy-done.6, s32[8,2]{1,0:T(8,128)S(1)} %copy.14.admissible, f32[4,16,1024]{2,1,0:T(8,128)} %copy-done.7, ...), custom_call_target="tpu_custom_call" | custom-call | flops 67108864 | bytes 2097152 | tf_op jit(solution)/shard_map/update_factors/pallas_call | solution.py:148
  65.6 0.0 collective-permute-done.14.rest_3_
  65.6 14.1 %collective-permute-start.16 = (f32[2,128,256]{2,1,0:T(8,128)}, f32[2,128,256]{2,1,0:T(8,128)S(1)}, u32[]{:S(2)}, u32[]{:S(2)}) collective-permute-start(f32[2,128,256]{2,1,0:T(8,128)} %get-tuple-element.138), channel_id=1, source_target_pairs={{0,5},{1,4},{2,7},{3,6},{4,1},{5,0},{6,3},{7,2},{8,13},{9,12},{10,... | collective-permute-start | bytes 786440 | tf_op jit(solution)/shard_map/ppermute | solution.py:246
  79.8 0.0 collective-permute-done.17.rest_6_
  79.8 0.0 collective-permute-start.21
  79.8 0.0 collective-permute-done.9.rest_11_
  79.8 0.8 collective-permute-start.10
  80.6 4.0 %collective-permute-done.19.rest_10_ = f32[2,128,256]{2,1,0:T(8,128)S(1)} collective-permute-done((f32[2,128,256]{2,1,0:T(8,128)}, f32[2,128,256]{2,1,0:T(8,128)S(1)}, u32[]{:S(2)}, u32[]{:S(2)}) %collective-permute-start.19) | collective-permute-done | bytes 262176 | tf_op jit(solution)/shard_map/ppermute | solution.py:246
  84.6 0.0 collective-permute-start.20
  84.6 0.0 collective-permute-done.12.rest_2_
  84.6 2.3 %collective-permute-start.15 = (f32[2,128,256]{2,1,0:T(8,128)}, f32[2,128,256]{2,1,0:T(8,128)S(1)}, u32[]{:S(2)}, u32[]{:S(2)}) collective-permute-start(f32[2,128,256]{2,1,0:T(8,128)} %get-tuple-element.137), channel_id=1, source_target_pairs={{0,4},{1,5},{2,6},{3,7},{4,0},{5,1},{6,2},{7,3},{8,12},{9,13},{10,... | collective-permute-start | bytes 786440 | tf_op jit(solution)/shard_map/ppermute | solution.py:246
  86.9 5.8 %collective-permute-done.16.rest_5_ = f32[2,128,256]{2,1,0:T(8,128)S(1)} collective-permute-done((f32[2,128,256]{2,1,0:T(8,128)}, f32[2,128,256]{2,1,0:T(8,128)S(1)}, u32[]{:S(2)}, u32[]{:S(2)}) %collective-permute-start.16) | collective-permute-done | bytes 262176 | tf_op jit(solution)/shard_map/ppermute | solution.py:246
  92.7 8.3 %collective-permute-done.21.rest_9_ = f32[2,128,256]{2,1,0:T(8,128)S(1)} collective-permute-done((f32[2,128,256]{2,1,0:T(8,128)}, f32[2,128,256]{2,1,0:T(8,128)S(1)}, u32[]{:S(2)}, u32[]{:S(2)}) %collective-permute-start.21) | collective-permute-done | bytes 262176 | tf_op jit(solution)/shard_map/ppermute | solution.py:246
  101.0 0.0 collective-permute-done.10.rest_1_
  101.0 4.7 %collective-permute-done.20.rest_8_ = f32[2,128,256]{2,1,0:T(8,128)S(1)} collective-permute-done((f32[2,128,256]{2,1,0:T(8,128)}, f32[2,128,256]{2,1,0:T(8,128)S(1)}, u32[]{:S(2)}, u32[]{:S(2)}) %collective-permute-start.20) | collective-permute-done | bytes 262176 | tf_op jit(solution)/shard_map/ppermute | solution.py:246
  105.7 0.0 collective-permute-done.15.rest_4_
  105.7 1.2 %copy-done = f32[4,512,128]{2,1,0:T(8,128)S(1)} copy-done((f32[4,512,128]{2,1,0:T(8,128)S(1)}, f32[4,512,128]{2,1,0:T(8,128)}, u32[]{:S(2)}) %copy-start) | copy-done | bytes 1048600
  106.9 1.0 copy-done.1
  107.9 0.9 copy-done.2
  108.9 4.9 %finish.1 = f32[2048,512]{1,0:T(8,128)} custom-call(s32[1,8]{1,0:T(1,128)} %row_map.1, f32[2048,512]{1,0:T(8,128)} %front.1, f32[2,512,128]{2,1,0:T(8,128)S(1)} %copy-done.1, f32[4,512,128]{2,1,0:T(8,128)S(1)} %copy-done, f32[2,128,256]{2,1,0:T(8,128)S(1)} %copy-done.2, f32[2,128,256]{2,1,0:T(8,128)S(1)} %collective-permute-done.10.rest_1_, ...), custom_call_target="tpu_custom_call" | custom-call | flops 536870912 | bytes 12582912 | tf_op jit(solution)/shard_map/finish/pallas_call | solution.py:221
  (11 shorter events, 0.0 us)
Async XLA Ops:
  0.0 60.8 %copy-start.6 = (s32[2]{0:T(128)S(1)}, s32[2]{0:T(128)}, u32[]{:S(2)}) copy-start(s32[2]{0:T(128)} %rank_cols) | copy-start | bytes 28
  0.0 60.8 %copy-start.5 = (s32[8]{0:T(128)S(1)}, s32[8]{0:T(128)}, u32[]{:S(2)}) copy-start(s32[8]{0:T(128)} %rank_rows) | copy-start | bytes 100
  0.0 43.3 %copy-start.10 = (f32[2,8192]{1,0:T(2,128)S(1)}, f32[2,8192]{1,0:T(2,128)}, u32[]{:S(2)}) copy-start(f32[2,8192]{1,0:T(2,128)} %param.20) | copy-start | bytes 196612
  0.0 43.3 %copy-start.11 = (f32[2,8192]{1,0:T(2,128)S(1)}, f32[2,8192]{1,0:T(2,128)}, u32[]{:S(2)}) copy-start(f32[2,8192]{1,0:T(2,128)} %param.19) | copy-start | bytes 196612
  0.0 60.8 %copy-start.4 = (s32[256]{0:T(256)S(1)}, s32[256]{0:T(256)}, u32[]{:S(2)}) copy-start(s32[256]{0:T(256)} %param.22) | copy-start | bytes 3076
  0.0 60.8 %copy-start.3 = (f32[256,256]{1,0:T(8,128)S(1)}, f32[256,256]{1,0:T(8,128)}, u32[]{:S(2)}) copy-start(f32[256,256]{1,0:T(8,128)} %dinv.1) | copy-start | bytes 786436
  0.9 14.2 %collective-permute-start.2 = (f32[16,1024]{1,0:T(8,128)S(1)}, f32[16,1024]{1,0:T(8,128)S(1)}, u32[]{:S(2)}, u32[]{:S(2)}) collective-permute-start(f32[16,1024]{1,0:T(8,128)S(1)} %pad_add_fusion), channel_id=1, source_target_pairs={{0,12},{1,13},{2,14},{3,15},{4,8},{5,9},{6,10},{7,11},{8,4},{9,5},... | collective-permute-start | bytes 196616 | tf_op jit(solution)/shard_map/ppermute | solution.py:246
  5.9 9.1 %collective-permute-start.1 = (f32[16,1024]{1,0:T(8,128)S(1)}, f32[16,1024]{1,0:T(8,128)S(1)}, u32[]{:S(2)}, u32[]{:S(2)}) collective-permute-start(f32[16,1024]{1,0:T(8,128)S(1)} %pad_add_fusion), channel_id=1, source_target_pairs={{0,8},{1,9},{2,10},{3,11},{4,12},{5,13},{6,14},{7,15},{8,0},{9,1},... | collective-permute-start | bytes 196616 | tf_op jit(solution)/shard_map/ppermute | solution.py:246
  5.9 9.1 %collective-permute-start = (f32[16,1024]{1,0:T(8,128)S(1)}, f32[16,1024]{1,0:T(8,128)S(1)}, u32[]{:S(2)}, u32[]{:S(2)}) collective-permute-start(f32[16,1024]{1,0:T(8,128)S(1)} %pad_add_fusion), channel_id=1, source_target_pairs={{0,4},{1,5},{2,6},{3,7},{4,0},{5,1},{6,2},{7,3},{8,12},{9,13},{10,... | collective-permute-start | bytes 196616 | tf_op jit(solution)/shard_map/ppermute | solution.py:246
  11.7 11.3 %collective-permute-start.5 = (f32[2,128,256]{2,1,0:T(8,128)}, f32[2,128,256]{2,1,0:T(8,128)S(1)}, u32[]{:S(2)}, u32[]{:S(2)}) collective-permute-start(f32[2,128,256]{2,1,0:T(8,128)} %get-tuple-element.108), channel_id=1, source_target_pairs={{0,15},{1,14},{2,13},{3,12},{4,11},{5,10},{6,9},{7,8},{8,7},{9,6},... | collective-permute-start | bytes 786440 | tf_op jit(solution)/shard_map/ppermute | solution.py:246
  15.1 45.7 %copy-start.7 = (f32[4,16,1024]{2,1,0:T(8,128)}, f32[4,16,1024]{2,1,0:T(8,128)S(1)}, u32[]{:S(2)}) copy-start(f32[4,16,1024]{2,1,0:T(8,128)S(1)} %pad_maximum_fusion.rest_0_) | copy-start | bytes 786436
  15.1 8.5 %collective-permute-start.3 = (f32[4,16,1024]{2,1,0:T(8,128)S(1)}, f32[4,16,1024]{2,1,0:T(8,128)S(1)}, u32[]{:S(2)}, u32[]{:S(2)}) collective-permute-start(f32[4,16,1024]{2,1,0:T(8,128)S(1)} %pad_maximum_fusion.rest_0_), channel_id=1, source_target_pairs={{0,1},{1,0},{2,3},{3,2},{4,5},{5,4},{6,7},{7,6},{8,9},{9,8},{10,11... | collective-permute-start | bytes 786440 | tf_op jit(solution)/shard_map/ppermute | solution.py:246
  16.7 18.1 %collective-permute-start.4 = (f32[4,16,1024]{2,1,0:T(8,128)S(1)}, f32[4,16,1024]{2,1,0:T(8,128)}, u32[]{:S(2)}, u32[]{:S(2)}) collective-permute-start(f32[4,16,1024]{2,1,0:T(8,128)S(1)} %pad_maximum_fusion.rest_0_), channel_id=1, source_target_pairs={{0,2},{1,3},{2,0},{3,1},{4,6},{5,7},{6,4},{7,5},{8,10},{9,11},{10,... | collective-permute-start | bytes 786440 | tf_op jit(solution)/shard_map/ppermute | solution.py:246
  17.2 26.2 %collective-permute-start.7 = (f32[2,128,256]{2,1,0:T(8,128)}, f32[2,128,256]{2,1,0:T(8,128)S(1)}, u32[]{:S(2)}, u32[]{:S(2)}) collective-permute-start(f32[2,128,256]{2,1,0:T(8,128)} %get-tuple-element.114), channel_id=1, source_target_pairs={{0,14},{1,15},{2,12},{3,13},{4,10},{5,11},{6,8},{7,9},{8,6},{9,7},... | collective-permute-start | bytes 786440 | tf_op jit(solution)/shard_map/ppermute | solution.py:246
  18.4 26.6 %collective-permute-start.13 = (f32[2,128,256]{2,1,0:T(8,128)}, f32[2,128,256]{2,1,0:T(8,128)S(1)}, u32[]{:S(2)}, u32[]{:S(2)}) collective-permute-start(f32[2,128,256]{2,1,0:T(8,128)} %get-tuple-element.134), channel_id=1, source_target_pairs={{0,13},{1,12},{2,15},{3,14},{4,9},{5,8},{6,11},{7,10},{8,5},{9,4},... | collective-permute-start | bytes 786440 | tf_op jit(solution)/shard_map/ppermute | solution.py:246
  23.0 33.5 %collective-permute-start.6 = (f32[4,16,1024]{2,1,0:T(8,128)S(1)}, f32[4,16,1024]{2,1,0:T(8,128)}, u32[]{:S(2)}, u32[]{:S(2)}) collective-permute-start(f32[4,16,1024]{2,1,0:T(8,128)S(1)} %pad_maximum_fusion.rest_0_), channel_id=1, source_target_pairs={{0,3},{1,2},{2,1},{3,0},{4,7},{5,6},{6,5},{7,4},{8,11},{9,10},{10,... | collective-permute-start | bytes 786440 | tf_op jit(solution)/shard_map/ppermute | solution.py:246
  23.6 37.2 %copy-start.9 = (f32[4,16,1024]{2,1,0:T(8,128)}, f32[4,16,1024]{2,1,0:T(8,128)S(1)}, u32[]{:S(2)}) copy-start(f32[4,16,1024]{2,1,0:T(8,128)S(1)} %collective-permute-done.3.rest_1_) | copy-start | bytes 786436
  34.8 24.0 %collective-permute-start.18 = (f32[2,128,256]{2,1,0:T(8,128)}, f32[2,128,256]{2,1,0:T(8,128)S(1)}, u32[]{:S(2)}, u32[]{:S(2)}) collective-permute-start(f32[2,128,256]{2,1,0:T(8,128)} %get-tuple-element.143), channel_id=1, source_target_pairs={{0,7},{1,6},{2,5},{3,4},{4,3},{5,2},{6,1},{7,0},{8,15},{9,14},{10,... | collective-permute-start | bytes 786440 | tf_op jit(solution)/shard_map/ppermute | solution.py:246
  41.0 17.8 %collective-permute-start.11 = (f32[2,128,256]{2,1,0:T(8,128)}, f32[2,128,256]{2,1,0:T(8,128)S(1)}, u32[]{:S(2)}, u32[]{:S(2)}) collective-permute-start(f32[2,128,256]{2,1,0:T(8,128)} %get-tuple-element.128), channel_id=1, source_target_pairs={{0,12},{1,13},{2,14},{3,15},{4,8},{5,9},{6,10},{7,11},{8,4},{9,5},... | collective-permute-start | bytes 786440 | tf_op jit(solution)/shard_map/ppermute | solution.py:246
  43.3 17.4 %copy-start.8 = (f32[4,8192]{1,0:T(4,128)}, f32[4,8192]{1,0:T(4,128)S(1)}, u32[]{:S(2)}) copy-start(f32[4,8192]{1,0:T(4,128)S(1)} %pad_maximum_fusion.1.rest_4_) | copy-start | bytes 393220
  43.4 5.2 %collective-permute-start.8 = (f32[4,8192]{1,0:T(4,128)S(1)}, f32[4,8192]{1,0:T(4,128)}, u32[]{:S(2)}, u32[]{:S(2)}) collective-permute-start(f32[4,8192]{1,0:T(4,128)S(1)} %pad_maximum_fusion.1.rest_4_), channel_id=1, source_target_pairs={{0,16},{16,0},{1,17},{17,1},{2,18},{18,2},{3,19},{19,3},{4,20},{20... | collective-permute-start | bytes 393224 | tf_op jit(solution)/shard_map/ppermute | solution.py:246
  45.0 20.7 %collective-permute-start.14 = (f32[2,128,256]{2,1,0:T(8,128)}, f32[2,128,256]{2,1,0:T(8,128)S(1)}, u32[]{:S(2)}, u32[]{:S(2)}) collective-permute-start(f32[2,128,256]{2,1,0:T(8,128)} %get-tuple-element.135), channel_id=1, source_target_pairs={{0,3},{1,2},{2,1},{3,0},{4,7},{5,6},{6,5},{7,4},{8,11},{9,10},{10,... | collective-permute-start | bytes 786440 | tf_op jit(solution)/shard_map/ppermute | solution.py:246
  48.6 31.2 %collective-permute-start.17 = (f32[2,128,256]{2,1,0:T(8,128)}, f32[2,128,256]{2,1,0:T(8,128)S(1)}, u32[]{:S(2)}, u32[]{:S(2)}) collective-permute-start(f32[2,128,256]{2,1,0:T(8,128)} %get-tuple-element.140), channel_id=1, source_target_pairs={{0,6},{1,7},{2,4},{3,5},{4,2},{5,3},{6,0},{7,1},{8,14},{9,15},{10,... | collective-permute-start | bytes 786440 | tf_op jit(solution)/shard_map/ppermute | solution.py:246
  56.5 23.3 %collective-permute-start.9 = (f32[2,128,256]{2,1,0:T(8,128)}, f32[2,128,256]{2,1,0:T(8,128)S(1)}, u32[]{:S(2)}, u32[]{:S(2)}) collective-permute-start(f32[2,128,256]{2,1,0:T(8,128)} %get-tuple-element.124), channel_id=1, source_target_pairs={{0,11},{1,10},{2,9},{3,8},{4,15},{5,14},{6,13},{7,12},{8,3},{9,2},... | collective-permute-start | bytes 786440 | tf_op jit(solution)/shard_map/ppermute | solution.py:246
  58.8 25.8 %collective-permute-start.19 = (f32[2,128,256]{2,1,0:T(8,128)}, f32[2,128,256]{2,1,0:T(8,128)S(1)}, u32[]{:S(2)}, u32[]{:S(2)}) collective-permute-start(f32[2,128,256]{2,1,0:T(8,128)} %get-tuple-element.146), channel_id=1, source_target_pairs={{0,10},{1,11},{2,8},{3,9},{4,14},{5,15},{6,12},{7,13},{8,2},{9,3},... | collective-permute-start | bytes 786440 | tf_op jit(solution)/shard_map/ppermute | solution.py:246
  58.8 25.8 %collective-permute-start.12 = (f32[2,128,256]{2,1,0:T(8,128)}, f32[2,128,256]{2,1,0:T(8,128)S(1)}, u32[]{:S(2)}, u32[]{:S(2)}) collective-permute-start(f32[2,128,256]{2,1,0:T(8,128)} %get-tuple-element.129), channel_id=1, source_target_pairs={{0,2},{1,3},{2,0},{3,1},{4,6},{5,7},{6,4},{7,5},{8,10},{9,11},{10,... | collective-permute-start | bytes 786440 | tf_op jit(solution)/shard_map/ppermute | solution.py:246
  65.6 27.0 %collective-permute-start.16 = (f32[2,128,256]{2,1,0:T(8,128)}, f32[2,128,256]{2,1,0:T(8,128)S(1)}, u32[]{:S(2)}, u32[]{:S(2)}) collective-permute-start(f32[2,128,256]{2,1,0:T(8,128)} %get-tuple-element.138), channel_id=1, source_target_pairs={{0,5},{1,4},{2,7},{3,6},{4,1},{5,0},{6,3},{7,2},{8,13},{9,12},{10,... | collective-permute-start | bytes 786440 | tf_op jit(solution)/shard_map/ppermute | solution.py:246
  79.8 21.2 %collective-permute-start.21 = (f32[2,128,256]{2,1,0:T(8,128)}, f32[2,128,256]{2,1,0:T(8,128)S(1)}, u32[]{:S(2)}, u32[]{:S(2)}) collective-permute-start(f32[2,128,256]{2,1,0:T(8,128)} %get-tuple-element.148), channel_id=1, source_target_pairs={{0,9},{1,8},{2,11},{3,10},{4,13},{5,12},{6,15},{7,14},{8,1},{9,0},... | collective-permute-start | bytes 786440 | tf_op jit(solution)/shard_map/ppermute | solution.py:246
  79.8 21.2 %collective-permute-start.10 = (f32[2,128,256]{2,1,0:T(8,128)}, f32[2,128,256]{2,1,0:T(8,128)S(1)}, u32[]{:S(2)}, u32[]{:S(2)}) collective-permute-start(f32[2,128,256]{2,1,0:T(8,128)} %get-tuple-element.125), channel_id=1, source_target_pairs={{0,1},{1,0},{2,3},{3,2},{4,5},{5,4},{6,7},{7,6},{8,9},{9,8},{10,11... | collective-permute-start | bytes 786440 | tf_op jit(solution)/shard_map/ppermute | solution.py:246
  84.6 21.1 %collective-permute-start.20 = (f32[2,128,256]{2,1,0:T(8,128)}, f32[2,128,256]{2,1,0:T(8,128)S(1)}, u32[]{:S(2)}, u32[]{:S(2)}) collective-permute-start(f32[2,128,256]{2,1,0:T(8,128)} %get-tuple-element.147), channel_id=1, source_target_pairs={{0,8},{1,9},{2,10},{3,11},{4,12},{5,13},{6,14},{7,15},{8,0},{9,1},... | collective-permute-start | bytes 786440 | tf_op jit(solution)/shard_map/ppermute | solution.py:246
  84.6 21.1 %collective-permute-start.15 = (f32[2,128,256]{2,1,0:T(8,128)}, f32[2,128,256]{2,1,0:T(8,128)S(1)}, u32[]{:S(2)}, u32[]{:S(2)}) collective-permute-start(f32[2,128,256]{2,1,0:T(8,128)} %get-tuple-element.137), channel_id=1, source_target_pairs={{0,4},{1,5},{2,6},{3,7},{4,0},{5,1},{6,2},{7,3},{8,12},{9,13},{10,... | collective-permute-start | bytes 786440 | tf_op jit(solution)/shard_map/ppermute | solution.py:246
  105.7 1.2 %copy-start = (f32[4,512,128]{2,1,0:T(8,128)S(1)}, f32[4,512,128]{2,1,0:T(8,128)}, u32[]{:S(2)}) copy-start(f32[4,512,128]{2,1,0:T(8,128)} %get-tuple-element.121.right) | copy-start | bytes 3145732
  106.9 1.0 copy-start.1
  107.9 0.9 copy-start.2

commit v4 on v3

--- a/solution.py
+++ b/solution.py
@@ -25,58 +25,57 @@
     return pltpu.with_memory_space_constraint(array, pltpu.HBM)
 
 
-def place_kernel(tiles, groups, tile, col_tiles, col_map, child, *rest):
-    pieces = rest[: tiles // col_tiles]
-    inverse, held, in_sem, out_sem = rest[tiles // col_tiles :]
-    width = tiles // groups * tile
+def place_kernel(members, tiles, tile, col_tiles, col_map, child, *rest):
+    pieces = rest[: len(members)]
+    inverse, held, in_sem, out_sem = rest[len(members) :]
     me = group_index()
 
-    def fetch(g):
-        span = pl.ds(g * width, width)
-        return pltpu.make_async_copy(child.at[:, span], held.at[:, span], in_sem.at[g])
-
-    def store(m, j):
-        b = inverse[(me ^ m) * col_tiles + j]
+    def fetch(n, j):
+        b = inverse[(me ^ members[n]) * col_tiles + j]
         span = pl.ds(pl.multiple_of(b * tile, tile), tile)
-        return pltpu.make_async_copy(held.at[:, span], pieces[m].at[j], out_sem.at[m, j])
-
-    for g in range(groups):
-        fetch(g).start()
+        return pltpu.make_async_copy(child.at[:, span], held.at[n, j], in_sem.at[n, j])
+
+    def store(n):
+        return pltpu.make_async_copy(held.at[n], pieces[n], out_sem.at[n])
+
     for b in range(tiles):
         inverse[col_map[b]] = b
-    for g in range(groups):
-        fetch(g).wait()
-    order = [(m, j) for m in reversed(range(len(pieces))) for j in range(col_tiles)]
-    for m, j in order:
-        store(m, j).start()
-    for m, j in order:
-        store(m, j).wait()
+    for n in range(len(members)):
+        for j in range(col_tiles):
+            fetch(n, j).start()
+    for n in range(len(members)):
+        for j in range(col_tiles):
+            fetch(n, j).wait()
+        store(n).start()
+    for n in range(len(members)):
+        store(n).wait()
 
 
 def in_vmem(array):
     return pltpu.with_memory_space_constraint(array, pltpu.VMEM)
 
 
-def place(child, col_map, tile, devices):
+def place(child, col_map, tile, devices, members):
     rows = child.shape[0]
     tiles = col_map.shape[0]
     col_tiles = tiles // devices
-    groups = 8
-    return pl.pallas_call(
-        functools.partial(place_kernel, tiles, groups, tile, col_tiles),
-        out_shape=[pltpu.HBM((col_tiles, rows, tile), child.dtype)] * devices,
+    count = len(members)
+    pieces = pl.pallas_call(
+        functools.partial(place_kernel, members, tiles, tile, col_tiles),
+        out_shape=[pltpu.HBM((col_tiles, rows, tile), child.dtype)] * count,
         in_specs=[pl.BlockSpec(memory_space=pltpu.SMEM), pl.BlockSpec(memory_space=pltpu.HBM)],
-        out_specs=[pl.BlockSpec(memory_space=pltpu.HBM)] * devices,
+        out_specs=[pl.BlockSpec(memory_space=pltpu.HBM)] * count,
         scratch_shapes=[
             pltpu.SMEM((tiles,), jnp.int32),
-            pltpu.VMEM(child.shape, child.dtype),
-            pltpu.SemaphoreType.DMA((groups,)),
-            pltpu.SemaphoreType.DMA((devices, col_tiles)),
+            pltpu.VMEM((count, col_tiles, rows, tile), child.dtype),
+            pltpu.SemaphoreType.DMA((count, col_tiles)),
+            pltpu.SemaphoreType.DMA((count,)),
         ],
-        compiler_params=pltpu.CompilerParams(vmem_limit_bytes=8 * MIB),
-        cost_estimate=pl.CostEstimate(flops=0, bytes_accessed=2 * child.size * 4, transcendentals=0),
+        compiler_params=pltpu.CompilerParams(vmem_limit_bytes=6 * MIB),
+        cost_estimate=pl.CostEstimate(flops=0, bytes_accessed=child.size * 4, transcendentals=0),
         name="place_child",
     )(in_hbm(col_map), in_hbm(child))
+    return dict(zip(members, pieces))
 
 
 def dot(a, b, contract=((1,), (0,))):
@@ -148,8 +147,8 @@
     return pl.pallas_call(
         functools.partial(factor_kernel, len(xw), len(vz), col_tiles, row_tiles),
         out_shape=[
-            pltpu.HBM((tile // LANES, total, LANES), jnp.float32),
-            pltpu.HBM((col_tiles * tile // LANES, total, LANES), jnp.float32),
+            pltpu.VMEM((tile // LANES, total, LANES), jnp.float32),
+            pltpu.VMEM((col_tiles * tile // LANES, total, LANES), jnp.float32),
         ],
         in_specs=[inner] * 2 + [scalars] * 3 + [inner] * (len(xw) + len(vz)),
         out_specs=[inner] * 2,
@@ -170,10 +169,10 @@
 
 
 def finish_kernel(count, tile, row_map, front, left, right, *rest):
-    pieces = rest[:count]
-    out, held, in_sem, out_sem = rest[count:]
+    own, out, held, kept, in_sem, out_sem, own_sem = rest[count - 1 :]
+    pieces = (kept, *rest[: count - 1])
     me = group_index()
-    col_tiles, rows, _ = pieces[0].shape
+    col_tiles, rows, _ = kept.shape
     per_tile = tile // rows
     groups = count // per_tile
 
@@ -189,8 +188,11 @@
     def store(g):
         return pltpu.make_async_copy(held.at[g], out.at[at(g), :], out_sem.at[g])
 
+    fetch_own = pltpu.make_async_copy(own, kept, own_sem)
+    fetch_own.start()
     for g in range(groups):
         fetch(g).start()
+    fetch_own.wait()
     for g in range(groups):
         mine = pl.ds(target(g), RMAX, stride=left.shape[1] // RMAX)
         a, b = halves_of(jnp.concatenate([left[n, mine, :] for n in range(left.shape[0])], axis=1))
@@ -221,17 +223,21 @@
     return pl.pallas_call(
         functools.partial(finish_kernel, len(pieces), tile),
         out_shape=pltpu.HBM(front.shape, front.dtype),
-        in_specs=[pl.BlockSpec(memory_space=pltpu.SMEM), outer] + [inner] * (2 + len(pieces)),
+        in_specs=[pl.BlockSpec(memory_space=pltpu.SMEM), outer] + [inner] * (1 + len(pieces)) + [outer],
         out_specs=outer,
         scratch_shapes=[
             pltpu.VMEM((row_tiles, tile, front.shape[1]), front.dtype),
+            pltpu.VMEM(pieces[0].shape, front.dtype),
             pltpu.SemaphoreType.DMA((row_tiles,)),
             pltpu.SemaphoreType.DMA((row_tiles,)),
+            pltpu.SemaphoreType.DMA,
         ],
         compiler_params=pltpu.CompilerParams(vmem_limit_bytes=16 * MIB),
         cost_estimate=pl.CostEstimate(flops=2 * front.size * 256, bytes_accessed=3 * front.size * 4, transcendentals=0),
         name="finish",
-    )(in_hbm(row_map), in_hbm(front), left, right, *[in_vmem(piece) for piece in pieces])
+    )(
+        in_hbm(row_map), in_hbm(front), in_vmem(left), in_vmem(right), *[in_vmem(piece) for piece in pieces[1:]], in_hbm(pieces[0])
+    )
 
 
 class Sender:
@@ -268,41 +274,49 @@
     devices = lax.axis_size("col") * lax.axis_size("leaf")
 
     sender = Sender()
-    mine = jnp.pad(x_fac, ((0, row_tiles), (0, 0))) + jnp.pad(w_fac, ((row_tiles, 0), (0, 0)))
-    mine, child = lax.optimization_barrier((mine, child))
-    line = [sender.send(mine, GROUP, m) for m in range(NEAR, devices, NEAR)]
-    pieces = place(child, col_map, tile, devices)
-    pieces, v_fac, z_fac, rank_rows, rank_cols, admissible = lax.optimization_barrier(
-        (pieces, v_fac, z_fac, rank_rows, rank_cols, admissible)
-    )
-
-    pieces = list(pieces)
+    spots = {}
+
+    def send(m):
+        spots[m] = sender.send(pieces[m], GROUP, m)
+
+    def arrivals(own, chosen):
+        return [own] + [sender.arrived[i] for i in chosen]
+
     half = devices // 2
     crossing = list(reversed(range(half, devices)))
     local = [m for pair in zip(reversed(range(NEAR, half)), [3, 2, 1] + [None] * half) for m in pair if m]
+    mine = jnp.pad(x_fac, ((0, row_tiles), (0, 0))) + jnp.pad(w_fac, ((row_tiles, 0), (0, 0)))
+    mine, child = lax.optimization_barrier((mine, child))
+    first = [sender.send(mine, GROUP, m) for m in range(NEAR, devices, NEAR)]
+    pieces = place(child, col_map, tile, devices, crossing)
+    pieces, child, v_fac, z_fac = lax.optimization_barrier((pieces, child, v_fac, z_fac))
+    for m in crossing[:2]:
+        send(m)
+    pieces.update(place(child, col_map, tile, devices, [*local, 0]))
+
     between = [("xw", m) for m in range(1, NEAR)] + [("vz", m) for m in range(1, lax.axis_size("row"))]
     between += [("child", m) for m in local]
     gaps = len(crossing) - 2
-    spots, xw, vz = {}, [], []
-    for n, m in enumerate(crossing):
+    xw, vz = [], []
+    for n, m in enumerate(crossing[2:]):
         for i, (kind, other) in enumerate(between):
-            if n == 2 + i * gaps // len(between):
+            if n == i * gaps // len(between):
                 if kind == "child":
                     if other == local[-3]:
-                        given = [line] + [sender.arrived[i] for i in xw], [both] + [sender.arrived[i] for i in vz]
+                        given = arrivals(line, xw), arrivals(both, vz)
                         left, right = factors(dinv, pivots, rank_rows, rank_cols, admissible, *given)
                         left, right, pieces[other] = lax.optimization_barrier((left, right, pieces[other]))
-                    spots[other] = sender.send(pieces[other], GROUP, other)
+                    send(other)
                 elif kind == "xw":
                     if not xw:
-                        line = jnp.stack([mine] + [sender.arrived[i] for i in line])
+                        line = jnp.stack(arrivals(mine, first))
                     xw.append(sender.send(line, GROUP, other))
                 else:
                     if not vz:
                         both = jnp.concatenate([v_fac, z_fac], axis=0)
                     vz.append(sender.send(both, ("row",), other))
-        spots[m] = sender.send(pieces[m], GROUP, m)
-    got = [pieces[0]] + [sender.arrived[spots[m]] for m in range(1, devices)]
+        send(m)
+    got = arrivals(pieces[0], [spots[m] for m in range(1, devices)])
     return finish(front, left, right, got, row_map, tile)
 
 

time: 114 us -> 118 us (1.035); the launches traced: 114 us -> 116 us
  starting transfers between devices: 54.4 us -> 61.9 us
  waiting for transfers between devices: 39.5 us -> 34.1 us
  local copies, waits for them, and re-layouts: 4 us -> 2.17 us
  Pallas kernels: 14.8 us -> 16.5 us
    ppermute x22, starting transfers between devices: 54.4 us -> 61.9 us  [send(): lax.ppermute(array, axes, [(d, d ^ m) for d in range(size)])]
    ppermute x22, waiting for transfers between devices: 39.5 us -> 34.1 us  [send(): lax.ppermute(array, axes, [(d, d ^ m) for d in range(size)])]
    pallas_call x1 -> x2, Pallas kernels: 5.13 us -> 6.56 us  [place(): pl.pallas_call(functools.partial(place_kernel, members, tiles, tile, col_...]
    pallas_call x1, Pallas kernels: 4.89 us -> 6.12 us  [finish(): pl.pallas_call(functools.partial(finish_kernel, len(pieces), tile), out_s...]
    unnamed x24 -> x27, local copies, waits for them, and re-layouts: 3.25 us -> 2.17 us
  transfers between devices with their start and end apart: 22 -> 22, of which waited for: 7 -> 8; matrix products, arithmetic and copies ran while one was open for 1% -> 1% of each run, Pallas kernels for 9% -> 9%
where the time goes in v4:
time: 118 us; the launch traced here: 116 us
  starting transfers between devices  61.9 us (52%)
  waiting for transfers between devices  34.1 us (29%)
  Pallas kernels  16.5 us (14%)
  local copies, waits for them, and re-layouts  2.17 us (2%)
    ppermute x22, starting transfers between devices, send(): lax.ppermute(array, axes, [(d, d ^ m) for d in range(size)])  61.9 us
    ppermute x22, waiting for transfers between devices, send(): lax.ppermute(array, axes, [(d, d ^ m) for d in range(size)])  34.1 us
    pallas_call x2, Pallas kernels, place(): pl.pallas_call(functools.partial(place_kernel, members, tiles, tile, col_...  6.56 us
    pallas_call x1, Pallas kernels, finish(): pl.pallas_call(functools.partial(finish_kernel, len(pieces), tile), out_s...  6.12 us
    pallas_call x1, Pallas kernels, factors(): pl.pallas_call(functools.partial(factor_kernel, len(xw), len(vz), col_til...  3.76 us
  transfers between devices with their start and end apart: 22, of which 8 were waited for; matrix products, arithmetic and copies ran while one was open for 1% of the time, Pallas kernels for 9%

profile of v4, /device:TPU:0, one launch (start us, length us, event | category | flops | bytes accessed | tf_op | source)
XLA Modules:
  0.0 115.7 jit_solution(17196511581528540143)
XLA Ops:
  0.0 0.8 pad_add_fusion
  0.8 0.0 copy-start
  0.8 0.0 copy-start.1
  0.8 0.0 copy-start.2
  0.8 0.0 copy-start.3
  0.8 5.1 %collective-permute-start.2 = (f32[16,1024]{1,0:T(8,128)S(1)}, f32[16,1024]{1,0:T(8,128)S(1)}, u32[]{:S(2)}, u32[]{:S(2)}) collective-permute-start(f32[16,1024]{1,0:T(8,128)S(1)} %pad_add_fusion), channel_id=1, source_target_pairs={{0,12},{1,13},{2,14},{3,15},{4,8},{5,9},{6,10},{7,11},{8,4},{9,5},... | collective-permute-start | bytes 196616 | tf_op jit(solution)/shard_map/ppermute | solution.py:252
  6.0 0.0 collective-permute-start.1
  6.0 0.6 collective-permute-start
  6.6 3.3 %place_child.2 = (f32[2,128,256]{2,1,0:T(8,128)}, f32[2,128,256]{2,1,0:T(8,128)}, f32[2,128,256]{2,1,0:T(8,128)}, f32[2,128,256]{2,1,0:T(8,128)}, f32[2,128,256]...) custom-call(s32[32]{0:T(128)} %col_map.3, f32[128,8192]{1,0:T(8,128)} %child.1), custom_call_target="tpu_custom_call" | custom-call | bytes 4194304 | tf_op jit(solution)/shard_map/place_child/pallas_call | solution.py:63
  9.9 0.0 copy-start.12
  9.9 0.0 copy-start.11
  9.9 3.3 %collective-permute-start.5 = (f32[2,128,256]{2,1,0:T(8,128)}, f32[2,128,256]{2,1,0:T(8,128)S(1)}, u32[]{:S(2)}, u32[]{:S(2)}) collective-permute-start(f32[2,128,256]{2,1,0:T(8,128)} %get-tuple-element.88), channel_id=1, source_target_pairs={{0,15},{1,14},{2,13},{3,12},{4,11},{5,10},{6,9},{7,8},{8,7},{9,6},... | collective-permute-start | bytes 786440 | tf_op jit(solution)/shard_map/ppermute | solution.py:252
  13.2 0.0 collective-permute-done.2
  13.3 0.0 collective-permute-done.1
  13.3 0.0 collective-permute-done
  13.3 0.0 copy-start.4
  13.3 1.6 %collective-permute-start.3 = (f32[4,16,1024]{2,1,0:T(8,128)S(1)}, f32[4,16,1024]{2,1,0:T(8,128)S(1)}, u32[]{:S(2)}, u32[]{:S(2)}) collective-permute-start(f32[4,16,1024]{2,1,0:T(8,128)S(1)} %pad_maximum_fusion.rest_0_), channel_id=1, source_target_pairs={{0,1},{1,0},{2,3},{3,2},{4,5},{5,4},{6,7},{7,6},{8,9},{9,8},{10,11... | collective-permute-start | bytes 786440 | tf_op jit(solution)/shard_map/ppermute | solution.py:252
  14.9 0.5 collective-permute-start.4
  15.4 1.1 collective-permute-start.7
  16.6 3.3 %place_child.3 = (f32[2,128,256]{2,1,0:T(8,128)}, f32[2,128,256]{2,1,0:T(8,128)}, f32[2,128,256]{2,1,0:T(8,128)}, f32[2,128,256]{2,1,0:T(8,128)}, f32[2,128,256]...) custom-call(s32[32]{0:T(128)} %col_map.3, f32[128,8192]{1,0:T(8,128)} %child.1), custom_call_target="tpu_custom_call" | custom-call | bytes 4194304 | tf_op jit(solution)/shard_map/place_child/pallas_call | solution.py:63
  19.9 0.0 copy-done.12
  19.9 2.8 %collective-permute-start.13 = (f32[2,128,256]{2,1,0:T(8,128)S(1)}, f32[2,128,256]{2,1,0:T(8,128)S(1)}, u32[]{:S(2)}, u32[]{:S(2)}) collective-permute-start(f32[2,128,256]{2,1,0:T(8,128)S(1)} %copy-done.12), channel_id=1, source_target_pairs={{0,13},{1,12},{2,15},{3,14},{4,9},{5,8},{6,11},{7,10},{8,5},{9,4},... | collective-permute-start | bytes 786440 | tf_op jit(solution)/shard_map/ppermute | solution.py:252
  22.7 0.0 collective-permute-done.5.rest_14_
  22.7 1.1 collective-permute-start.6
  23.8 0.0 collective-permute-done.3.rest_1_
  23.8 0.0 copy-done.11
  23.8 1.6 %collective-permute-start.11 = (f32[2,128,256]{2,1,0:T(8,128)S(1)}, f32[2,128,256]{2,1,0:T(8,128)S(1)}, u32[]{:S(2)}, u32[]{:S(2)}) collective-permute-start(f32[2,128,256]{2,1,0:T(8,128)S(1)} %copy-done.11), channel_id=1, source_target_pairs={{0,12},{1,13},{2,14},{3,15},{4,8},{5,9},{6,10},{7,11},{8,4},{9,5},... | collective-permute-start | bytes 786440 | tf_op jit(solution)/shard_map/ppermute | solution.py:252
  25.4 7.5 %collective-permute-done.4.rest_2_ = f32[4,16,1024]{2,1,0:T(8,128)S(1)} collective-permute-done((f32[4,16,1024]{2,1,0:T(8,128)S(1)}, f32[4,16,1024]{2,1,0:T(8,128)S(1)}, u32[]{:S(2)}, u32[]{:S(2)}) %collective-permute-start.4) | collective-permute-done | bytes 262176 | tf_op jit(solution)/shard_map/ppermute | solution.py:252
  32.9 0.7 copy-done.7
  33.6 13.0 %collective-permute-start.18 = (f32[2,128,256]{2,1,0:T(8,128)}, f32[2,128,256]{2,1,0:T(8,128)S(1)}, u32[]{:S(2)}, u32[]{:S(2)}) collective-permute-start(f32[2,128,256]{2,1,0:T(8,128)} %get-tuple-element.122), channel_id=1, source_target_pairs={{0,7},{1,6},{2,5},{3,4},{4,3},{5,2},{6,1},{7,0},{8,15},{9,14},{10,... | collective-permute-start | bytes 786440 | tf_op jit(solution)/shard_map/ppermute | solution.py:252
  46.6 0.0 copy-done.9
  46.6 0.1 pad_maximum_fusion.1.rest_4_
  46.7 0.0 collective-permute-done.7.rest_13_
  46.7 1.6 %collective-permute-start.8 = (f32[4,8192]{1,0:T(4,128)S(1)}, f32[4,8192]{1,0:T(4,128)S(1)}, u32[]{:S(2)}, u32[]{:S(2)}) collective-permute-start(f32[4,8192]{1,0:T(4,128)S(1)} %pad_maximum_fusion.1.rest_4_), channel_id=1, source_target_pairs={{0,16},{16,0},{1,17},{17,1},{2,18},{18,2},{3,19},{19,3},{4,20},{20... | collective-permute-start | bytes 393224 | tf_op jit(solution)/shard_map/ppermute | solution.py:252
  48.3 0.0 collective-permute-done.13.rest_12_
  48.3 0.3 collective-permute-start.14
  48.6 3.8 %collective-permute-done.8.rest_5_ = f32[4,8192]{1,0:T(4,128)S(1)} collective-permute-done((f32[4,8192]{1,0:T(4,128)S(1)}, f32[4,8192]{1,0:T(4,128)S(1)}, u32[]{:S(2)}, u32[]{:S(2)}) %collective-permute-start.8) | collective-permute-done | bytes 131104 | tf_op jit(solution)/shard_map/ppermute | solution.py:252
  52.4 0.6 copy-done.8
  53.0 2.9 %collective-permute-start.17 = (f32[2,128,256]{2,1,0:T(8,128)}, f32[2,128,256]{2,1,0:T(8,128)S(1)}, u32[]{:S(2)}, u32[]{:S(2)}) collective-permute-start(f32[2,128,256]{2,1,0:T(8,128)} %get-tuple-element.119), channel_id=1, source_target_pairs={{0,6},{1,7},{2,4},{3,5},{4,2},{5,3},{6,0},{7,1},{8,14},{9,15},{10,... | collective-permute-start | bytes 786440 | tf_op jit(solution)/shard_map/ppermute | solution.py:252
  55.9 0.0 collective-permute-done.6.rest_3_
  55.9 11.1 %collective-permute-start.9 = (f32[2,128,256]{2,1,0:T(8,128)}, f32[2,128,256]{2,1,0:T(8,128)S(1)}, u32[]{:S(2)}, u32[]{:S(2)}) collective-permute-start(f32[2,128,256]{2,1,0:T(8,128)} %get-tuple-element.103), channel_id=1, source_target_pairs={{0,11},{1,10},{2,9},{3,8},{4,15},{5,14},{6,13},{7,12},{8,3},{9,2},... | collective-permute-start | bytes 786440 | tf_op jit(solution)/shard_map/ppermute | solution.py:252
  67.1 0.0 collective-permute-done.11.rest_11_
  67.1 0.0 collective-permute-start.12
  67.1 0.0 collective-permute-done.18.rest_6_
  67.1 0.5 collective-permute-start.19
  67.6 0.8 copy.14.admissible
  68.3 0.0 copy-done.5
  68.4 3.8 %update_factors.1 = (f32[2,512,128]{2,1,0:T(8,128)S(1)}, f32[4,512,128]{2,1,0:T(8,128)S(1)}) custom-call(f32[256,256]{1,0:T(8,128)S(1)} %copy-done, s32[1,256]{1,0:T(1,128)S(1)} %bitcast.5, s32[8]{0:T(128)S(1)} %copy-done.2, s32[2]{0:T(128)S(1)} %copy-done.3, s32[8,2]{1,0:T(8,128)S(1)} %copy.14.admissible, f32[4,16,1024]{2,1,0:T(8,128)} %copy-done.4, ...), custom_call_target="tpu_custom_call" | custom-call | flops 67108864 | bytes 2097152 | tf_op jit(solution)/shard_map/update_factors/pallas_call | solution.py:147
  72.1 0.0 collective-permute-done.14.rest_2_
  72.1 10.4 %collective-permute-start.16 = (f32[2,128,256]{2,1,0:T(8,128)}, f32[2,128,256]{2,1,0:T(8,128)S(1)}, u32[]{:S(2)}, u32[]{:S(2)}) collective-permute-start(f32[2,128,256]{2,1,0:T(8,128)} %get-tuple-element.117), channel_id=1, source_target_pairs={{0,5},{1,4},{2,7},{3,6},{4,1},{5,0},{6,3},{7,2},{8,13},{9,12},{10,... | collective-permute-start | bytes 786440 | tf_op jit(solution)/shard_map/ppermute | solution.py:252
  82.6 0.0 collective-permute-done.17.rest_5_
  82.6 0.4 collective-permute-start.21
  83.0 1.8 %collective-permute-done.9.rest_10_ = f32[2,128,256]{2,1,0:T(8,128)S(1)} collective-permute-done((f32[2,128,256]{2,1,0:T(8,128)}, f32[2,128,256]{2,1,0:T(8,128)S(1)}, u32[]{:S(2)}, u32[]{:S(2)}) %collective-permute-start.9) | collective-permute-done | bytes 262176 | tf_op jit(solution)/shard_map/ppermute | solution.py:252
  84.8 1.2 %collective-permute-start.10 = (f32[2,128,256]{2,1,0:T(8,128)}, f32[2,128,256]{2,1,0:T(8,128)S(1)}, u32[]{:S(2)}, u32[]{:S(2)}) collective-permute-start(f32[2,128,256]{2,1,0:T(8,128)} %get-tuple-element.104), channel_id=1, source_target_pairs={{0,1},{1,0},{2,3},{3,2},{4,5},{5,4},{6,7},{7,6},{8,9},{9,8},{10,11... | collective-permute-start | bytes 786440 | tf_op jit(solution)/shard_map/ppermute | solution.py:252
  85.9 0.0 collective-permute-done.12.rest_1_
  86.0 2.5 %collective-permute-start.15 = (f32[2,128,256]{2,1,0:T(8,128)}, f32[2,128,256]{2,1,0:T(8,128)S(1)}, u32[]{:S(2)}, u32[]{:S(2)}) collective-permute-start(f32[2,128,256]{2,1,0:T(8,128)} %get-tuple-element.116), channel_id=1, source_target_pairs={{0,4},{1,5},{2,6},{3,7},{4,0},{5,1},{6,2},{7,3},{8,12},{9,13},{10,... | collective-permute-start | bytes 786440 | tf_op jit(solution)/shard_map/ppermute | solution.py:252
  88.5 3.3 %collective-permute-done.19.rest_9_ = f32[2,128,256]{2,1,0:T(8,128)S(1)} collective-permute-done((f32[2,128,256]{2,1,0:T(8,128)}, f32[2,128,256]{2,1,0:T(8,128)S(1)}, u32[]{:S(2)}, u32[]{:S(2)}) %collective-permute-start.19) | collective-permute-done | bytes 262176 | tf_op jit(solution)/shard_map/ppermute | solution.py:252
  91.7 0.0 collective-permute-start.20
  91.7 5.5 %collective-permute-done.16.rest_4_ = f32[2,128,256]{2,1,0:T(8,128)S(1)} collective-permute-done((f32[2,128,256]{2,1,0:T(8,128)}, f32[2,128,256]{2,1,0:T(8,128)S(1)}, u32[]{:S(2)}, u32[]{:S(2)}) %collective-permute-start.16) | collective-permute-done | bytes 262176 | tf_op jit(solution)/shard_map/ppermute | solution.py:252
  97.2 0.8 collective-permute-done.21.rest_8_
  98.1 0.0 collective-permute-done.10.rest_0_
  98.1 10.3 %collective-permute-done.15.rest_3_ = f32[2,128,256]{2,1,0:T(8,128)S(1)} collective-permute-done((f32[2,128,256]{2,1,0:T(8,128)}, f32[2,128,256]{2,1,0:T(8,128)S(1)}, u32[]{:S(2)}, u32[]{:S(2)}) %collective-permute-start.15) | collective-permute-done | bytes 262176 | tf_op jit(solution)/shard_map/ppermute | solution.py:252
  108.4 1.2 %collective-permute-done.20.rest_7_ = f32[2,128,256]{2,1,0:T(8,128)S(1)} collective-permute-done((f32[2,128,256]{2,1,0:T(8,128)}, f32[2,128,256]{2,1,0:T(8,128)S(1)}, u32[]{:S(2)}, u32[]{:S(2)}) %collective-permute-start.20) | collective-permute-done | bytes 262176 | tf_op jit(solution)/shard_map/ppermute | solution.py:252
  109.6 6.1 %finish.1 = f32[2048,512]{1,0:T(8,128)} custom-call(s32[1,8]{1,0:T(1,128)} %row_map.1, f32[2048,512]{1,0:T(8,128)} %front.1, f32[2,512,128]{2,1,0:T(8,128)S(1)} %get-tuple-element.100.left, f32[4,512,128]{2,1,0:T(8,128)S(1)} %get-tuple-element.101.right, f32[2,128,256]{2,1,0:T(8,128)S(1)} %collective-permute-done.10.rest_0_, ...), custom_call_target="tpu_custom_call" | custom-call | flops 536870912 | bytes 12582912 | tf_op jit(solution)/shard_map/finish/pallas_call | solution.py:223
  (14 shorter events, 0.0 us)
Async XLA Ops:
  0.8 45.9 %copy-start.9 = (f32[2,8192]{1,0:T(2,128)S(1)}, f32[2,8192]{1,0:T(2,128)}, u32[]{:S(2)}) copy-start(f32[2,8192]{1,0:T(2,128)} %param.20) | copy-start | bytes 196612
  0.8 45.9 %copy-start.10 = (f32[2,8192]{1,0:T(2,128)S(1)}, f32[2,8192]{1,0:T(2,128)}, u32[]{:S(2)}) copy-start(f32[2,8192]{1,0:T(2,128)} %param.19) | copy-start | bytes 196612
  0.8 67.5 %copy-start = (f32[256,256]{1,0:T(8,128)S(1)}, f32[256,256]{1,0:T(8,128)}, u32[]{:S(2)}) copy-start(f32[256,256]{1,0:T(8,128)} %dinv.1) | copy-start | bytes 786436
  0.8 67.5 %copy-start.1 = (s32[256]{0:T(256)S(1)}, s32[256]{0:T(256)}, u32[]{:S(2)}) copy-start(s32[256]{0:T(256)} %param.22) | copy-start | bytes 3076
  0.8 67.5 %copy-start.2 = (s32[8]{0:T(128)S(1)}, s32[8]{0:T(128)}, u32[]{:S(2)}) copy-start(s32[8]{0:T(128)} %rank_rows.1) | copy-start | bytes 100
  0.8 67.5 %copy-start.3 = (s32[2]{0:T(128)S(1)}, s32[2]{0:T(128)}, u32[]{:S(2)}) copy-start(s32[2]{0:T(128)} %rank_cols.1) | copy-start | bytes 28
  0.8 12.4 %collective-permute-start.2 = (f32[16,1024]{1,0:T(8,128)S(1)}, f32[16,1024]{1,0:T(8,128)S(1)}, u32[]{:S(2)}, u32[]{:S(2)}) collective-permute-start(f32[16,1024]{1,0:T(8,128)S(1)} %pad_add_fusion), channel_id=1, source_target_pairs={{0,12},{1,13},{2,14},{3,15},{4,8},{5,9},{6,10},{7,11},{8,4},{9,5},... | collective-permute-start | bytes 196616 | tf_op jit(solution)/shard_map/ppermute | solution.py:252
  6.0 7.3 %collective-permute-start.1 = (f32[16,1024]{1,0:T(8,128)S(1)}, f32[16,1024]{1,0:T(8,128)S(1)}, u32[]{:S(2)}, u32[]{:S(2)}) collective-permute-start(f32[16,1024]{1,0:T(8,128)S(1)} %pad_add_fusion), channel_id=1, source_target_pairs={{0,8},{1,9},{2,10},{3,11},{4,12},{5,13},{6,14},{7,15},{8,0},{9,1},... | collective-permute-start | bytes 196616 | tf_op jit(solution)/shard_map/ppermute | solution.py:252
  6.0 7.3 %collective-permute-start = (f32[16,1024]{1,0:T(8,128)S(1)}, f32[16,1024]{1,0:T(8,128)S(1)}, u32[]{:S(2)}, u32[]{:S(2)}) collective-permute-start(f32[16,1024]{1,0:T(8,128)S(1)} %pad_add_fusion), channel_id=1, source_target_pairs={{0,4},{1,5},{2,6},{3,7},{4,0},{5,1},{6,2},{7,3},{8,12},{9,13},{10,... | collective-permute-start | bytes 196616 | tf_op jit(solution)/shard_map/ppermute | solution.py:252
  9.9 10.0 %copy-start.12 = (f32[2,128,256]{2,1,0:T(8,128)S(1)}, f32[2,128,256]{2,1,0:T(8,128)}, u32[]{:S(2)}) copy-start(f32[2,128,256]{2,1,0:T(8,128)} %get-tuple-element.113) | copy-start | bytes 786436
  9.9 13.9 %copy-start.11 = (f32[2,128,256]{2,1,0:T(8,128)S(1)}, f32[2,128,256]{2,1,0:T(8,128)}, u32[]{:S(2)}) copy-start(f32[2,128,256]{2,1,0:T(8,128)} %get-tuple-element.107) | copy-start | bytes 786436
  9.9 12.7 %collective-permute-start.5 = (f32[2,128,256]{2,1,0:T(8,128)}, f32[2,128,256]{2,1,0:T(8,128)S(1)}, u32[]{:S(2)}, u32[]{:S(2)}) collective-permute-start(f32[2,128,256]{2,1,0:T(8,128)} %get-tuple-element.88), channel_id=1, source_target_pairs={{0,15},{1,14},{2,13},{3,12},{4,11},{5,10},{6,9},{7,8},{8,7},{9,6},... | collective-permute-start | bytes 786440 | tf_op jit(solution)/shard_map/ppermute | solution.py:252
  13.3 55.0 %copy-start.4 = (f32[4,16,1024]{2,1,0:T(8,128)}, f32[4,16,1024]{2,1,0:T(8,128)S(1)}, u32[]{:S(2)}) copy-start(f32[4,16,1024]{2,1,0:T(8,128)S(1)} %pad_maximum_fusion.rest_0_) | copy-start | bytes 786436
  13.3 10.5 %collective-permute-start.3 = (f32[4,16,1024]{2,1,0:T(8,128)S(1)}, f32[4,16,1024]{2,1,0:T(8,128)S(1)}, u32[]{:S(2)}, u32[]{:S(2)}) collective-permute-start(f32[4,16,1024]{2,1,0:T(8,128)S(1)} %pad_maximum_fusion.rest_0_), channel_id=1, source_target_pairs={{0,1},{1,0},{2,3},{3,2},{4,5},{5,4},{6,7},{7,6},{8,9},{9,8},{10,11... | collective-permute-start | bytes 786440 | tf_op jit(solution)/shard_map/ppermute | solution.py:252
  14.9 18.0 %collective-permute-start.4 = (f32[4,16,1024]{2,1,0:T(8,128)S(1)}, f32[4,16,1024]{2,1,0:T(8,128)S(1)}, u32[]{:S(2)}, u32[]{:S(2)}) collective-permute-start(f32[4,16,1024]{2,1,0:T(8,128)S(1)} %pad_maximum_fusion.rest_0_), channel_id=1, source_target_pairs={{0,2},{1,3},{2,0},{3,1},{4,6},{5,7},{6,4},{7,5},{8,10},{9,11},{10,... | collective-permute-start | bytes 786440 | tf_op jit(solution)/shard_map/ppermute | solution.py:252
  15.4 31.3 %collective-permute-start.7 = (f32[2,128,256]{2,1,0:T(8,128)}, f32[2,128,256]{2,1,0:T(8,128)S(1)}, u32[]{:S(2)}, u32[]{:S(2)}) collective-permute-start(f32[2,128,256]{2,1,0:T(8,128)} %get-tuple-element.94), channel_id=1, source_target_pairs={{0,14},{1,15},{2,12},{3,13},{4,10},{5,11},{6,8},{7,9},{8,6},{9,7},... | collective-permute-start | bytes 786440 | tf_op jit(solution)/shard_map/ppermute | solution.py:252
  19.9 28.5 %collective-permute-start.13 = (f32[2,128,256]{2,1,0:T(8,128)S(1)}, f32[2,128,256]{2,1,0:T(8,128)S(1)}, u32[]{:S(2)}, u32[]{:S(2)}) collective-permute-start(f32[2,128,256]{2,1,0:T(8,128)S(1)} %copy-done.12), channel_id=1, source_target_pairs={{0,13},{1,12},{2,15},{3,14},{4,9},{5,8},{6,11},{7,10},{8,5},{9,4},... | collective-permute-start | bytes 786440 | tf_op jit(solution)/shard_map/ppermute | solution.py:252
  22.7 33.3 %collective-permute-start.6 = (f32[4,16,1024]{2,1,0:T(8,128)S(1)}, f32[4,16,1024]{2,1,0:T(8,128)}, u32[]{:S(2)}, u32[]{:S(2)}) collective-permute-start(f32[4,16,1024]{2,1,0:T(8,128)S(1)} %pad_maximum_fusion.rest_0_), channel_id=1, source_target_pairs={{0,3},{1,2},{2,1},{3,0},{4,7},{5,6},{6,5},{7,4},{8,11},{9,10},{10,... | collective-permute-start | bytes 786440 | tf_op jit(solution)/shard_map/ppermute | solution.py:252
  23.8 44.5 %copy-start.6 = (f32[4,16,1024]{2,1,0:T(8,128)}, f32[4,16,1024]{2,1,0:T(8,128)S(1)}, u32[]{:S(2)}) copy-start(f32[4,16,1024]{2,1,0:T(8,128)S(1)} %collective-permute-done.3.rest_1_) | copy-start | bytes 786436
  23.8 43.3 %collective-permute-start.11 = (f32[2,128,256]{2,1,0:T(8,128)S(1)}, f32[2,128,256]{2,1,0:T(8,128)S(1)}, u32[]{:S(2)}, u32[]{:S(2)}) collective-permute-start(f32[2,128,256]{2,1,0:T(8,128)S(1)} %copy-done.11), channel_id=1, source_target_pairs={{0,12},{1,13},{2,14},{3,15},{4,8},{5,9},{6,10},{7,11},{8,4},{9,5},... | collective-permute-start | bytes 786440 | tf_op jit(solution)/shard_map/ppermute | solution.py:252
  32.9 0.7 copy-start.7
  33.6 33.4 %collective-permute-start.18 = (f32[2,128,256]{2,1,0:T(8,128)}, f32[2,128,256]{2,1,0:T(8,128)S(1)}, u32[]{:S(2)}, u32[]{:S(2)}) collective-permute-start(f32[2,128,256]{2,1,0:T(8,128)} %get-tuple-element.122), channel_id=1, source_target_pairs={{0,7},{1,6},{2,5},{3,4},{4,3},{5,2},{6,1},{7,0},{8,15},{9,14},{10,... | collective-permute-start | bytes 786440 | tf_op jit(solution)/shard_map/ppermute | solution.py:252
  46.7 21.6 %copy-start.5 = (f32[4,8192]{1,0:T(4,128)}, f32[4,8192]{1,0:T(4,128)S(1)}, u32[]{:S(2)}) copy-start(f32[4,8192]{1,0:T(4,128)S(1)} %pad_maximum_fusion.1.rest_4_) | copy-start | bytes 393220
  46.7 5.6 %collective-permute-start.8 = (f32[4,8192]{1,0:T(4,128)S(1)}, f32[4,8192]{1,0:T(4,128)S(1)}, u32[]{:S(2)}, u32[]{:S(2)}) collective-permute-start(f32[4,8192]{1,0:T(4,128)S(1)} %pad_maximum_fusion.1.rest_4_), channel_id=1, source_target_pairs={{0,16},{16,0},{1,17},{17,1},{2,18},{18,2},{3,19},{19,3},{4,20},{20... | collective-permute-start | bytes 393224 | tf_op jit(solution)/shard_map/ppermute | solution.py:252
  48.3 23.8 %collective-permute-start.14 = (f32[2,128,256]{2,1,0:T(8,128)}, f32[2,128,256]{2,1,0:T(8,128)S(1)}, u32[]{:S(2)}, u32[]{:S(2)}) collective-permute-start(f32[2,128,256]{2,1,0:T(8,128)} %get-tuple-element.114), channel_id=1, source_target_pairs={{0,3},{1,2},{2,1},{3,0},{4,7},{5,6},{6,5},{7,4},{8,11},{9,10},{10,... | collective-permute-start | bytes 786440 | tf_op jit(solution)/shard_map/ppermute | solution.py:252
  52.4 0.6 copy-start.8
  53.0 29.6 %collective-permute-start.17 = (f32[2,128,256]{2,1,0:T(8,128)}, f32[2,128,256]{2,1,0:T(8,128)S(1)}, u32[]{:S(2)}, u32[]{:S(2)}) collective-permute-start(f32[2,128,256]{2,1,0:T(8,128)} %get-tuple-element.119), channel_id=1, source_target_pairs={{0,6},{1,7},{2,4},{3,5},{4,2},{5,3},{6,0},{7,1},{8,14},{9,15},{10,... | collective-permute-start | bytes 786440 | tf_op jit(solution)/shard_map/ppermute | solution.py:252
  55.9 28.8 %collective-permute-start.9 = (f32[2,128,256]{2,1,0:T(8,128)}, f32[2,128,256]{2,1,0:T(8,128)S(1)}, u32[]{:S(2)}, u32[]{:S(2)}) collective-permute-start(f32[2,128,256]{2,1,0:T(8,128)} %get-tuple-element.103), channel_id=1, source_target_pairs={{0,11},{1,10},{2,9},{3,8},{4,15},{5,14},{6,13},{7,12},{8,3},{9,2},... | collective-permute-start | bytes 786440 | tf_op jit(solution)/shard_map/ppermute | solution.py:252
  67.1 18.9 %collective-permute-start.12 = (f32[2,128,256]{2,1,0:T(8,128)}, f32[2,128,256]{2,1,0:T(8,128)S(1)}, u32[]{:S(2)}, u32[]{:S(2)}) collective-permute-start(f32[2,128,256]{2,1,0:T(8,128)} %get-tuple-element.108), channel_id=1, source_target_pairs={{0,2},{1,3},{2,0},{3,1},{4,6},{5,7},{6,4},{7,5},{8,10},{9,11},{10,... | collective-permute-start | bytes 786440 | tf_op jit(solution)/shard_map/ppermute | solution.py:252
  67.1 24.7 %collective-permute-start.19 = (f32[2,128,256]{2,1,0:T(8,128)}, f32[2,128,256]{2,1,0:T(8,128)S(1)}, u32[]{:S(2)}, u32[]{:S(2)}) collective-permute-start(f32[2,128,256]{2,1,0:T(8,128)} %get-tuple-element.125), channel_id=1, source_target_pairs={{0,10},{1,11},{2,8},{3,9},{4,14},{5,15},{6,12},{7,13},{8,2},{9,3},... | collective-permute-start | bytes 786440 | tf_op jit(solution)/shard_map/ppermute | solution.py:252
  72.1 25.1 %collective-permute-start.16 = (f32[2,128,256]{2,1,0:T(8,128)}, f32[2,128,256]{2,1,0:T(8,128)S(1)}, u32[]{:S(2)}, u32[]{:S(2)}) collective-permute-start(f32[2,128,256]{2,1,0:T(8,128)} %get-tuple-element.117), channel_id=1, source_target_pairs={{0,5},{1,4},{2,7},{3,6},{4,1},{5,0},{6,3},{7,2},{8,13},{9,12},{10,... | collective-permute-start | bytes 786440 | tf_op jit(solution)/shard_map/ppermute | solution.py:252
  82.6 15.5 %collective-permute-start.21 = (f32[2,128,256]{2,1,0:T(8,128)}, f32[2,128,256]{2,1,0:T(8,128)S(1)}, u32[]{:S(2)}, u32[]{:S(2)}) collective-permute-start(f32[2,128,256]{2,1,0:T(8,128)} %get-tuple-element.127), channel_id=1, source_target_pairs={{0,9},{1,8},{2,11},{3,10},{4,13},{5,12},{6,15},{7,14},{8,1},{9,0},... | collective-permute-start | bytes 786440 | tf_op jit(solution)/shard_map/ppermute | solution.py:252
  84.8 13.3 %collective-permute-start.10 = (f32[2,128,256]{2,1,0:T(8,128)}, f32[2,128,256]{2,1,0:T(8,128)S(1)}, u32[]{:S(2)}, u32[]{:S(2)}) collective-permute-start(f32[2,128,256]{2,1,0:T(8,128)} %get-tuple-element.104), channel_id=1, source_target_pairs={{0,1},{1,0},{2,3},{3,2},{4,5},{5,4},{6,7},{7,6},{8,9},{9,8},{10,11... | collective-permute-start | bytes 786440 | tf_op jit(solution)/shard_map/ppermute | solution.py:252
  86.0 22.4 %collective-permute-start.15 = (f32[2,128,256]{2,1,0:T(8,128)}, f32[2,128,256]{2,1,0:T(8,128)S(1)}, u32[]{:S(2)}, u32[]{:S(2)}) collective-permute-start(f32[2,128,256]{2,1,0:T(8,128)} %get-tuple-element.116), channel_id=1, source_target_pairs={{0,4},{1,5},{2,6},{3,7},{4,0},{5,1},{6,2},{7,3},{8,12},{9,13},{10,... | collective-permute-start | bytes 786440 | tf_op jit(solution)/shard_map/ppermute | solution.py:252
  91.7 17.8 %collective-permute-start.20 = (f32[2,128,256]{2,1,0:T(8,128)}, f32[2,128,256]{2,1,0:T(8,128)S(1)}, u32[]{:S(2)}, u32[]{:S(2)}) collective-permute-start(f32[2,128,256]{2,1,0:T(8,128)} %get-tuple-element.126), channel_id=1, source_target_pairs={{0,8},{1,9},{2,10},{3,11},{4,12},{5,13},{6,14},{7,15},{8,0},{9,1},... | collective-permute-start | bytes 786440 | tf_op jit(solution)/shard_map/ppermute | solution.py:252

commit v5 on v3

--- a/solution.py
+++ b/solution.py
@@ -148,8 +148,8 @@
     return pl.pallas_call(
         functools.partial(factor_kernel, len(xw), len(vz), col_tiles, row_tiles),
         out_shape=[
-            pltpu.HBM((tile // LANES, total, LANES), jnp.float32),
-            pltpu.HBM((col_tiles * tile // LANES, total, LANES), jnp.float32),
+            pltpu.VMEM((tile // LANES, total, LANES), jnp.float32),
+            pltpu.VMEM((col_tiles * tile // LANES, total, LANES), jnp.float32),
         ],
         in_specs=[inner] * 2 + [scalars] * 3 + [inner] * (len(xw) + len(vz)),
         out_specs=[inner] * 2,
@@ -170,10 +170,10 @@
 
 
 def finish_kernel(count, tile, row_map, front, left, right, *rest):
-    pieces = rest[:count]
-    out, held, in_sem, out_sem = rest[count:]
+    own, out, held, kept, in_sem, out_sem, own_sem = rest[count - 1 :]
+    pieces = (kept, *rest[: count - 1])
     me = group_index()
-    col_tiles, rows, _ = pieces[0].shape
+    col_tiles, rows, _ = kept.shape
     per_tile = tile // rows
     groups = count // per_tile
 
@@ -189,9 +189,11 @@
     def store(g):
         return pltpu.make_async_copy(held.at[g], out.at[at(g), :], out_sem.at[g])
 
-    for g in range(groups):
+    fetch_own = pltpu.make_async_copy(own, kept, own_sem)
+    for g in reversed(range(groups)):
         fetch(g).start()
-    for g in range(groups):
+    fetch_own.start()
+    for g in reversed(range(groups)):
         mine = pl.ds(target(g), RMAX, stride=left.shape[1] // RMAX)
         a, b = halves_of(jnp.concatenate([left[n, mine, :] for n in range(left.shape[0])], axis=1))
         c, d = halves_of(jnp.concatenate([right[n, mine, :] for n in range(right.shape[0])], axis=1))
@@ -205,6 +207,8 @@
         held[g] = held[g] - update
         for p in range(per_tile):
             m = g * per_tile + p
+            if m == 0:
+                fetch_own.wait()
             low = pl.ds(pl.multiple_of(lax.rem(me ^ m, per_tile) * rows, rows), rows)
             for j in range(col_tiles):
                 span = pl.ds(j * tile, tile)
@@ -221,17 +225,21 @@
     return pl.pallas_call(
         functools.partial(finish_kernel, len(pieces), tile),
         out_shape=pltpu.HBM(front.shape, front.dtype),
-        in_specs=[pl.BlockSpec(memory_space=pltpu.SMEM), outer] + [inner] * (2 + len(pieces)),
+        in_specs=[pl.BlockSpec(memory_space=pltpu.SMEM), outer] + [inner] * (1 + len(pieces)) + [outer],
         out_specs=outer,
         scratch_shapes=[
             pltpu.VMEM((row_tiles, tile, front.shape[1]), front.dtype),
+            pltpu.VMEM(pieces[0].shape, front.dtype),
             pltpu.SemaphoreType.DMA((row_tiles,)),
             pltpu.SemaphoreType.DMA((row_tiles,)),
+            pltpu.SemaphoreType.DMA,
         ],
         compiler_params=pltpu.CompilerParams(vmem_limit_bytes=16 * MIB),
         cost_estimate=pl.CostEstimate(flops=2 * front.size * 256, bytes_accessed=3 * front.size * 4, transcendentals=0),
         name="finish",
-    )(in_hbm(row_map), in_hbm(front), left, right, *[in_vmem(piece) for piece in pieces])
+    )(
+        in_hbm(row_map), in_hbm(front), in_vmem(left), in_vmem(right), *[in_vmem(piece) for piece in pieces[1:]], in_hbm(pieces[0])
+    )
 
 
 class Sender:

time: 114 us -> 111 us (0.974)
  local copies, waits for them, and re-layouts: 4 us -> 0.79 us
    unnamed x24 -> x18, local copies, waits for them, and re-layouts: 3.25 us -> 0.04 us
  transfers between devices with their start and end apart: 22 -> 22, of which waited for: 7 -> 7; matrix products, arithmetic and copies ran while one was open for 1% -> 1% of each run, Pallas kernels for 9% -> 8%
where the time goes in v5:
time: 111 us
  starting transfers between devices  55.4 us (50%)
  waiting for transfers between devices  39.5 us (36%)
  Pallas kernels  13.7 us (12%)
    ppermute x22, starting transfers between devices, send(): lax.ppermute(array, axes, [(d, d ^ m) for d in range(size)])  55.4 us
    ppermute x22, waiting for transfers between devices, send(): lax.ppermute(array, axes, [(d, d ^ m) for d in range(size)])  39.5 us
    pallas_call x1, Pallas kernels, place(): pl.pallas_call(functools.partial(place_kernel, tiles, groups, tile, col_t...  5.13 us
    pallas_call x1, Pallas kernels, finish(): pl.pallas_call(functools.partial(finish_kernel, len(pieces), tile), out_s...  4.85 us
    pallas_call x1, Pallas kernels, factors(): pl.pallas_call(functools.partial(factor_kernel, len(xw), len(vz), col_til...  3.76 us
  transfers between devices with their start and end apart: 22, of which 7 were waited for; matrix products, arithmetic and copies ran while one was open for 1% of the time, Pallas kernels for 8%

profile of v5, /device:TPU:0, one launch (start us, length us, event | category | flops | bytes accessed | tf_op | source)
XLA Modules:
  0.0 110.5 jit_solution(9007431525168816874)
XLA Ops:
  0.0 0.0 copy-start.3
  0.0 0.0 copy-start.2
  0.0 0.0 copy-start
  0.0 0.8 pad_add_fusion
  0.9 5.1 %collective-permute-start.2 = (f32[16,1024]{1,0:T(8,128)S(1)}, f32[16,1024]{1,0:T(8,128)S(1)}, u32[]{:S(2)}, u32[]{:S(2)}) collective-permute-start(f32[16,1024]{1,0:T(8,128)S(1)} %pad_add_fusion), channel_id=1, source_target_pairs={{0,12},{1,13},{2,14},{3,15},{4,8},{5,9},{6,10},{7,11},{8,4},{9,5},... | collective-permute-start | bytes 196616 | tf_op jit(solution)/shard_map/ppermute | solution.py:254
  5.9 0.0 collective-permute-start.1
  5.9 0.6 collective-permute-start
  6.6 5.1 %place_child.1 = (f32[2,128,256]{2,1,0:T(8,128)}, f32[2,128,256]{2,1,0:T(8,128)}, f32[2,128,256]{2,1,0:T(8,128)}, f32[2,128,256]{2,1,0:T(8,128)}, f32[2,128,256]...) custom-call(s32[32]{0:T(128)} %col_map.1, ...), custom_call_target="tpu_custom_call" | custom-call | bytes 8388608 | tf_op jit(solution)/shard_map/place_child/pallas_call | solution.py:65
  11.7 3.3 %collective-permute-start.5 = (f32[2,128,256]{2,1,0:T(8,128)}, f32[2,128,256]{2,1,0:T(8,128)S(1)}, u32[]{:S(2)}, u32[]{:S(2)}) collective-permute-start(f32[2,128,256]{2,1,0:T(8,128)} %get-tuple-element.108), channel_id=1, source_target_pairs={{0,15},{1,14},{2,13},{3,12},{4,11},{5,10},{6,9},{7,8},{8,7},{9,6},... | collective-permute-start | bytes 786440 | tf_op jit(solution)/shard_map/ppermute | solution.py:254
  15.0 0.0 collective-permute-done.2
  15.0 0.0 collective-permute-done.1
  15.0 0.0 collective-permute-done
  15.1 0.0 copy-start.4
  15.1 1.6 %collective-permute-start.3 = (f32[4,16,1024]{2,1,0:T(8,128)S(1)}, f32[4,16,1024]{2,1,0:T(8,128)S(1)}, u32[]{:S(2)}, u32[]{:S(2)}) collective-permute-start(f32[4,16,1024]{2,1,0:T(8,128)S(1)} %pad_maximum_fusion.rest_0_), channel_id=1, source_target_pairs={{0,1},{1,0},{2,3},{3,2},{4,5},{5,4},{6,7},{7,6},{8,9},{9,8},{10,11... | collective-permute-start | bytes 786440 | tf_op jit(solution)/shard_map/ppermute | solution.py:254
  16.7 0.5 collective-permute-start.4
  17.2 1.1 %collective-permute-start.7 = (f32[2,128,256]{2,1,0:T(8,128)}, f32[2,128,256]{2,1,0:T(8,128)S(1)}, u32[]{:S(2)}, u32[]{:S(2)}) collective-permute-start(f32[2,128,256]{2,1,0:T(8,128)} %get-tuple-element.114), channel_id=1, source_target_pairs={{0,14},{1,15},{2,12},{3,13},{4,10},{5,11},{6,8},{7,9},{8,6},{9,7},... | collective-permute-start | bytes 786440 | tf_op jit(solution)/shard_map/ppermute | solution.py:254
  18.4 2.7 %collective-permute-start.13 = (f32[2,128,256]{2,1,0:T(8,128)}, f32[2,128,256]{2,1,0:T(8,128)S(1)}, u32[]{:S(2)}, u32[]{:S(2)}) collective-permute-start(f32[2,128,256]{2,1,0:T(8,128)} %get-tuple-element.133), channel_id=1, source_target_pairs={{0,13},{1,12},{2,15},{3,14},{4,9},{5,8},{6,11},{7,10},{8,5},{9,4},... | collective-permute-start | bytes 786440 | tf_op jit(solution)/shard_map/ppermute | solution.py:254
  21.1 1.9 %collective-permute-done.5.rest_14_ = f32[2,128,256]{2,1,0:T(8,128)S(1)} collective-permute-done((f32[2,128,256]{2,1,0:T(8,128)}, f32[2,128,256]{2,1,0:T(8,128)S(1)}, u32[]{:S(2)}, u32[]{:S(2)}) %collective-permute-start.5) | collective-permute-done | bytes 262176 | tf_op jit(solution)/shard_map/ppermute | solution.py:254
  23.0 0.6 collective-permute-start.6
  23.6 0.0 collective-permute-done.3.rest_1_
  23.6 11.2 %collective-permute-done.4.rest_2_ = f32[4,16,1024]{2,1,0:T(8,128)} collective-permute-done((f32[4,16,1024]{2,1,0:T(8,128)S(1)}, f32[4,16,1024]{2,1,0:T(8,128)}, u32[]{:S(2)}, u32[]{:S(2)}) %collective-permute-start.4) | collective-permute-done | bytes 262176 | tf_op jit(solution)/shard_map/ppermute | solution.py:254
  34.8 6.2 %collective-permute-start.18 = (f32[2,128,256]{2,1,0:T(8,128)}, f32[2,128,256]{2,1,0:T(8,128)S(1)}, u32[]{:S(2)}, u32[]{:S(2)}) collective-permute-start(f32[2,128,256]{2,1,0:T(8,128)} %get-tuple-element.142), channel_id=1, source_target_pairs={{0,7},{1,6},{2,5},{3,4},{4,3},{5,2},{6,1},{7,0},{8,15},{9,14},{10,... | collective-permute-start | bytes 786440 | tf_op jit(solution)/shard_map/ppermute | solution.py:254
  41.0 2.3 %collective-permute-start.11 = (f32[2,128,256]{2,1,0:T(8,128)}, f32[2,128,256]{2,1,0:T(8,128)S(1)}, u32[]{:S(2)}, u32[]{:S(2)}) collective-permute-start(f32[2,128,256]{2,1,0:T(8,128)} %get-tuple-element.127), channel_id=1, source_target_pairs={{0,12},{1,13},{2,14},{3,15},{4,8},{5,9},{6,10},{7,11},{8,4},{9,5},... | collective-permute-start | bytes 786440 | tf_op jit(solution)/shard_map/ppermute | solution.py:254
  43.3 0.0 copy-done.7
  43.3 0.0 copy-done.8
  43.3 0.1 pad_maximum_fusion.1.rest_4_
  43.3 0.0 copy-start.5
  43.4 0.0 collective-permute-done.7.rest_13_
  43.4 1.6 %collective-permute-start.8 = (f32[4,8192]{1,0:T(4,128)S(1)}, f32[4,8192]{1,0:T(4,128)}, u32[]{:S(2)}, u32[]{:S(2)}) collective-permute-start(f32[4,8192]{1,0:T(4,128)S(1)} %pad_maximum_fusion.1.rest_4_), channel_id=1, source_target_pairs={{0,16},{16,0},{1,17},{17,1},{2,18},{18,2},{3,19},{19,3},{4,20},{20... | collective-permute-start | bytes 393224 | tf_op jit(solution)/shard_map/ppermute | solution.py:254
  45.0 0.0 collective-permute-done.13.rest_12_
  45.0 0.0 collective-permute-start.14
  45.0 3.6 %collective-permute-done.8.rest_5_ = f32[4,8192]{1,0:T(4,128)} collective-permute-done((f32[4,8192]{1,0:T(4,128)S(1)}, f32[4,8192]{1,0:T(4,128)}, u32[]{:S(2)}, u32[]{:S(2)}) %collective-permute-start.8) | collective-permute-done | bytes 131104 | tf_op jit(solution)/shard_map/ppermute | solution.py:254
  48.6 7.9 %collective-permute-start.17 = (f32[2,128,256]{2,1,0:T(8,128)}, f32[2,128,256]{2,1,0:T(8,128)S(1)}, u32[]{:S(2)}, u32[]{:S(2)}) collective-permute-start(f32[2,128,256]{2,1,0:T(8,128)} %get-tuple-element.139), channel_id=1, source_target_pairs={{0,6},{1,7},{2,4},{3,5},{4,2},{5,3},{6,0},{7,1},{8,14},{9,15},{10,... | collective-permute-start | bytes 786440 | tf_op jit(solution)/shard_map/ppermute | solution.py:254
  56.5 0.0 collective-permute-done.6.rest_3_
  56.5 2.3 %collective-permute-start.9 = (f32[2,128,256]{2,1,0:T(8,128)}, f32[2,128,256]{2,1,0:T(8,128)S(1)}, u32[]{:S(2)}, u32[]{:S(2)}) collective-permute-start(f32[2,128,256]{2,1,0:T(8,128)} %get-tuple-element.123), channel_id=1, source_target_pairs={{0,11},{1,10},{2,9},{3,8},{4,15},{5,14},{6,13},{7,12},{8,3},{9,2},... | collective-permute-start | bytes 786440 | tf_op jit(solution)/shard_map/ppermute | solution.py:254
  58.8 0.0 collective-permute-done.18.rest_6_
  58.8 0.0 collective-permute-start.19
  58.8 0.0 collective-permute-done.11.rest_11_
  58.8 1.2 %collective-permute-start.12 = (f32[2,128,256]{2,1,0:T(8,128)}, f32[2,128,256]{2,1,0:T(8,128)S(1)}, u32[]{:S(2)}, u32[]{:S(2)}) collective-permute-start(f32[2,128,256]{2,1,0:T(8,128)} %get-tuple-element.128), channel_id=1, source_target_pairs={{0,2},{1,3},{2,0},{3,1},{4,6},{5,7},{6,4},{7,5},{8,10},{9,11},{10,... | collective-permute-start | bytes 786440 | tf_op jit(solution)/shard_map/ppermute | solution.py:254
  60.0 0.8 copy.14.admissible
  60.8 0.0 copy-done.4
  60.8 0.0 copy-done.6
  60.8 0.0 copy-done.5
  60.8 0.0 copy-done.3
  60.8 0.0 copy-done.2
  60.8 0.0 copy-done.1
  60.8 0.0 copy-done
  60.8 3.8 %update_factors.1 = (f32[2,512,128]{2,1,0:T(8,128)S(1)}, f32[4,512,128]{2,1,0:T(8,128)S(1)}) custom-call(f32[256,256]{1,0:T(8,128)S(1)} %copy-done, s32[1,256]{1,0:T(1,128)S(1)} %bitcast.5, s32[8]{0:T(128)S(1)} %copy-done.2, s32[2]{0:T(128)S(1)} %copy-done.3, s32[8,2]{1,0:T(8,128)S(1)} %copy.14.admissible, f32[4,16,1024]{2,1,0:T(8,128)} %copy-done.4, ...), custom_call_target="tpu_custom_call" | custom-call | flops 67108864 | bytes 2097152 | tf_op jit(solution)/shard_map/update_factors/pallas_call | solution.py:148
  64.6 0.0 collective-permute-done.14.rest_2_
  64.6 15.2 %collective-permute-start.16 = (f32[2,128,256]{2,1,0:T(8,128)}, f32[2,128,256]{2,1,0:T(8,128)S(1)}, u32[]{:S(2)}, u32[]{:S(2)}) collective-permute-start(f32[2,128,256]{2,1,0:T(8,128)} %get-tuple-element.137), channel_id=1, source_target_pairs={{0,5},{1,4},{2,7},{3,6},{4,1},{5,0},{6,3},{7,2},{8,13},{9,12},{10,... | collective-permute-start | bytes 786440 | tf_op jit(solution)/shard_map/ppermute | solution.py:254
  79.8 0.0 collective-permute-done.17.rest_5_
  79.8 0.0 collective-permute-start.21
  79.8 0.0 collective-permute-done.9.rest_10_
  79.8 0.8 collective-permute-start.10
  80.6 4.0 %collective-permute-done.19.rest_9_ = f32[2,128,256]{2,1,0:T(8,128)S(1)} collective-permute-done((f32[2,128,256]{2,1,0:T(8,128)}, f32[2,128,256]{2,1,0:T(8,128)S(1)}, u32[]{:S(2)}, u32[]{:S(2)}) %collective-permute-start.19) | collective-permute-done | bytes 262176 | tf_op jit(solution)/shard_map/ppermute | solution.py:254
  84.6 0.0 collective-permute-start.20
  84.6 0.0 collective-permute-done.12.rest_1_
  84.6 2.3 %collective-permute-start.15 = (f32[2,128,256]{2,1,0:T(8,128)}, f32[2,128,256]{2,1,0:T(8,128)S(1)}, u32[]{:S(2)}, u32[]{:S(2)}) collective-permute-start(f32[2,128,256]{2,1,0:T(8,128)} %get-tuple-element.136), channel_id=1, source_target_pairs={{0,4},{1,5},{2,6},{3,7},{4,0},{5,1},{6,2},{7,3},{8,12},{9,13},{10,... | collective-permute-start | bytes 786440 | tf_op jit(solution)/shard_map/ppermute | solution.py:254
  86.9 5.8 %collective-permute-done.16.rest_4_ = f32[2,128,256]{2,1,0:T(8,128)S(1)} collective-permute-done((f32[2,128,256]{2,1,0:T(8,128)}, f32[2,128,256]{2,1,0:T(8,128)S(1)}, u32[]{:S(2)}, u32[]{:S(2)}) %collective-permute-start.16) | collective-permute-done | bytes 262176 | tf_op jit(solution)/shard_map/ppermute | solution.py:254
  92.7 8.3 %collective-permute-done.21.rest_8_ = f32[2,128,256]{2,1,0:T(8,128)S(1)} collective-permute-done((f32[2,128,256]{2,1,0:T(8,128)}, f32[2,128,256]{2,1,0:T(8,128)S(1)}, u32[]{:S(2)}, u32[]{:S(2)}) %collective-permute-start.21) | collective-permute-done | bytes 262176 | tf_op jit(solution)/shard_map/ppermute | solution.py:254
  101.0 0.0 collective-permute-done.10.rest_0_
  101.0 4.7 %collective-permute-done.20.rest_7_ = f32[2,128,256]{2,1,0:T(8,128)S(1)} collective-permute-done((f32[2,128,256]{2,1,0:T(8,128)}, f32[2,128,256]{2,1,0:T(8,128)S(1)}, u32[]{:S(2)}, u32[]{:S(2)}) %collective-permute-start.20) | collective-permute-done | bytes 262176 | tf_op jit(solution)/shard_map/ppermute | solution.py:254
  105.7 0.0 collective-permute-done.15.rest_3_
  105.7 4.9 %finish.1 = f32[2048,512]{1,0:T(8,128)} custom-call(s32[1,8]{1,0:T(1,128)} %row_map.1, f32[2048,512]{1,0:T(8,128)} %front.1, f32[2,512,128]{2,1,0:T(8,128)S(1)} %get-tuple-element.120.left, f32[4,512,128]{2,1,0:T(8,128)S(1)} %get-tuple-element.121.right, f32[2,128,256]{2,1,0:T(8,128)S(1)} %collective-permute-done.10.rest_0_, ...), custom_call_target="tpu_custom_call" | custom-call | flops 536870912 | bytes 12582912 | tf_op jit(solution)/shard_map/finish/pallas_call | solution.py:225
  (5 shorter events, 0.0 us)
Async XLA Ops:
  0.0 60.8 %copy-start.3 = (s32[2]{0:T(128)S(1)}, s32[2]{0:T(128)}, u32[]{:S(2)}) copy-start(s32[2]{0:T(128)} %rank_cols) | copy-start | bytes 28
  0.0 60.8 %copy-start.2 = (s32[8]{0:T(128)S(1)}, s32[8]{0:T(128)}, u32[]{:S(2)}) copy-start(s32[8]{0:T(128)} %rank_rows) | copy-start | bytes 100
  0.0 43.3 %copy-start.7 = (f32[2,8192]{1,0:T(2,128)S(1)}, f32[2,8192]{1,0:T(2,128)}, u32[]{:S(2)}) copy-start(f32[2,8192]{1,0:T(2,128)} %param.20) | copy-start | bytes 196612
  0.0 43.3 %copy-start.8 = (f32[2,8192]{1,0:T(2,128)S(1)}, f32[2,8192]{1,0:T(2,128)}, u32[]{:S(2)}) copy-start(f32[2,8192]{1,0:T(2,128)} %param.19) | copy-start | bytes 196612
  0.0 60.8 %copy-start.1 = (s32[256]{0:T(256)S(1)}, s32[256]{0:T(256)}, u32[]{:S(2)}) copy-start(s32[256]{0:T(256)} %param.22) | copy-start | bytes 3076
  0.0 60.8 %copy-start = (f32[256,256]{1,0:T(8,128)S(1)}, f32[256,256]{1,0:T(8,128)}, u32[]{:S(2)}) copy-start(f32[256,256]{1,0:T(8,128)} %dinv.1) | copy-start | bytes 786436
  0.9 14.2 %collective-permute-start.2 = (f32[16,1024]{1,0:T(8,128)S(1)}, f32[16,1024]{1,0:T(8,128)S(1)}, u32[]{:S(2)}, u32[]{:S(2)}) collective-permute-start(f32[16,1024]{1,0:T(8,128)S(1)} %pad_add_fusion), channel_id=1, source_target_pairs={{0,12},{1,13},{2,14},{3,15},{4,8},{5,9},{6,10},{7,11},{8,4},{9,5},... | collective-permute-start | bytes 196616 | tf_op jit(solution)/shard_map/ppermute | solution.py:254
  5.9 9.1 %collective-permute-start.1 = (f32[16,1024]{1,0:T(8,128)S(1)}, f32[16,1024]{1,0:T(8,128)S(1)}, u32[]{:S(2)}, u32[]{:S(2)}) collective-permute-start(f32[16,1024]{1,0:T(8,128)S(1)} %pad_add_fusion), channel_id=1, source_target_pairs={{0,8},{1,9},{2,10},{3,11},{4,12},{5,13},{6,14},{7,15},{8,0},{9,1},... | collective-permute-start | bytes 196616 | tf_op jit(solution)/shard_map/ppermute | solution.py:254
  5.9 9.1 %collective-permute-start = (f32[16,1024]{1,0:T(8,128)S(1)}, f32[16,1024]{1,0:T(8,128)S(1)}, u32[]{:S(2)}, u32[]{:S(2)}) collective-permute-start(f32[16,1024]{1,0:T(8,128)S(1)} %pad_add_fusion), channel_id=1, source_target_pairs={{0,4},{1,5},{2,6},{3,7},{4,0},{5,1},{6,2},{7,3},{8,12},{9,13},{10,... | collective-permute-start | bytes 196616 | tf_op jit(solution)/shard_map/ppermute | solution.py:254
  11.7 11.3 %collective-permute-start.5 = (f32[2,128,256]{2,1,0:T(8,128)}, f32[2,128,256]{2,1,0:T(8,128)S(1)}, u32[]{:S(2)}, u32[]{:S(2)}) collective-permute-start(f32[2,128,256]{2,1,0:T(8,128)} %get-tuple-element.108), channel_id=1, source_target_pairs={{0,15},{1,14},{2,13},{3,12},{4,11},{5,10},{6,9},{7,8},{8,7},{9,6},... | collective-permute-start | bytes 786440 | tf_op jit(solution)/shard_map/ppermute | solution.py:254
  15.1 45.7 %copy-start.4 = (f32[4,16,1024]{2,1,0:T(8,128)}, f32[4,16,1024]{2,1,0:T(8,128)S(1)}, u32[]{:S(2)}) copy-start(f32[4,16,1024]{2,1,0:T(8,128)S(1)} %pad_maximum_fusion.rest_0_) | copy-start | bytes 786436
  15.1 8.5 %collective-permute-start.3 = (f32[4,16,1024]{2,1,0:T(8,128)S(1)}, f32[4,16,1024]{2,1,0:T(8,128)S(1)}, u32[]{:S(2)}, u32[]{:S(2)}) collective-permute-start(f32[4,16,1024]{2,1,0:T(8,128)S(1)} %pad_maximum_fusion.rest_0_), channel_id=1, source_target_pairs={{0,1},{1,0},{2,3},{3,2},{4,5},{5,4},{6,7},{7,6},{8,9},{9,8},{10,11... | collective-permute-start | bytes 786440 | tf_op jit(solution)/shard_map/ppermute | solution.py:254
  16.7 18.1 %collective-permute-start.4 = (f32[4,16,1024]{2,1,0:T(8,128)S(1)}, f32[4,16,1024]{2,1,0:T(8,128)}, u32[]{:S(2)}, u32[]{:S(2)}) collective-permute-start(f32[4,16,1024]{2,1,0:T(8,128)S(1)} %pad_maximum_fusion.rest_0_), channel_id=1, source_target_pairs={{0,2},{1,3},{2,0},{3,1},{4,6},{5,7},{6,4},{7,5},{8,10},{9,11},{10,... | collective-permute-start | bytes 786440 | tf_op jit(solution)/shard_map/ppermute | solution.py:254
  17.2 26.2 %collective-permute-start.7 = (f32[2,128,256]{2,1,0:T(8,128)}, f32[2,128,256]{2,1,0:T(8,128)S(1)}, u32[]{:S(2)}, u32[]{:S(2)}) collective-permute-start(f32[2,128,256]{2,1,0:T(8,128)} %get-tuple-element.114), channel_id=1, source_target_pairs={{0,14},{1,15},{2,12},{3,13},{4,10},{5,11},{6,8},{7,9},{8,6},{9,7},... | collective-permute-start | bytes 786440 | tf_op jit(solution)/shard_map/ppermute | solution.py:254
  18.4 26.6 %collective-permute-start.13 = (f32[2,128,256]{2,1,0:T(8,128)}, f32[2,128,256]{2,1,0:T(8,128)S(1)}, u32[]{:S(2)}, u32[]{:S(2)}) collective-permute-start(f32[2,128,256]{2,1,0:T(8,128)} %get-tuple-element.133), channel_id=1, source_target_pairs={{0,13},{1,12},{2,15},{3,14},{4,9},{5,8},{6,11},{7,10},{8,5},{9,4},... | collective-permute-start | bytes 786440 | tf_op jit(solution)/shard_map/ppermute | solution.py:254
  23.0 33.5 %collective-permute-start.6 = (f32[4,16,1024]{2,1,0:T(8,128)S(1)}, f32[4,16,1024]{2,1,0:T(8,128)}, u32[]{:S(2)}, u32[]{:S(2)}) collective-permute-start(f32[4,16,1024]{2,1,0:T(8,128)S(1)} %pad_maximum_fusion.rest_0_), channel_id=1, source_target_pairs={{0,3},{1,2},{2,1},{3,0},{4,7},{5,6},{6,5},{7,4},{8,11},{9,10},{10,... | collective-permute-start | bytes 786440 | tf_op jit(solution)/shard_map/ppermute | solution.py:254
  23.6 37.2 %copy-start.6 = (f32[4,16,1024]{2,1,0:T(8,128)}, f32[4,16,1024]{2,1,0:T(8,128)S(1)}, u32[]{:S(2)}) copy-start(f32[4,16,1024]{2,1,0:T(8,128)S(1)} %collective-permute-done.3.rest_1_) | copy-start | bytes 786436
  34.8 24.0 %collective-permute-start.18 = (f32[2,128,256]{2,1,0:T(8,128)}, f32[2,128,256]{2,1,0:T(8,128)S(1)}, u32[]{:S(2)}, u32[]{:S(2)}) collective-permute-start(f32[2,128,256]{2,1,0:T(8,128)} %get-tuple-element.142), channel_id=1, source_target_pairs={{0,7},{1,6},{2,5},{3,4},{4,3},{5,2},{6,1},{7,0},{8,15},{9,14},{10,... | collective-permute-start | bytes 786440 | tf_op jit(solution)/shard_map/ppermute | solution.py:254
  41.0 17.8 %collective-permute-start.11 = (f32[2,128,256]{2,1,0:T(8,128)}, f32[2,128,256]{2,1,0:T(8,128)S(1)}, u32[]{:S(2)}, u32[]{:S(2)}) collective-permute-start(f32[2,128,256]{2,1,0:T(8,128)} %get-tuple-element.127), channel_id=1, source_target_pairs={{0,12},{1,13},{2,14},{3,15},{4,8},{5,9},{6,10},{7,11},{8,4},{9,5},... | collective-permute-start | bytes 786440 | tf_op jit(solution)/shard_map/ppermute | solution.py:254
  43.3 17.4 %copy-start.5 = (f32[4,8192]{1,0:T(4,128)}, f32[4,8192]{1,0:T(4,128)S(1)}, u32[]{:S(2)}) copy-start(f32[4,8192]{1,0:T(4,128)S(1)} %pad_maximum_fusion.1.rest_4_) | copy-start | bytes 393220
  43.4 5.2 %collective-permute-start.8 = (f32[4,8192]{1,0:T(4,128)S(1)}, f32[4,8192]{1,0:T(4,128)}, u32[]{:S(2)}, u32[]{:S(2)}) collective-permute-start(f32[4,8192]{1,0:T(4,128)S(1)} %pad_maximum_fusion.1.rest_4_), channel_id=1, source_target_pairs={{0,16},{16,0},{1,17},{17,1},{2,18},{18,2},{3,19},{19,3},{4,20},{20... | collective-permute-start | bytes 393224 | tf_op jit(solution)/shard_map/ppermute | solution.py:254
  45.0 19.6 %collective-permute-start.14 = (f32[2,128,256]{2,1,0:T(8,128)}, f32[2,128,256]{2,1,0:T(8,128)S(1)}, u32[]{:S(2)}, u32[]{:S(2)}) collective-permute-start(f32[2,128,256]{2,1,0:T(8,128)} %get-tuple-element.134), channel_id=1, source_target_pairs={{0,3},{1,2},{2,1},{3,0},{4,7},{5,6},{6,5},{7,4},{8,11},{9,10},{10,... | collective-permute-start | bytes 786440 | tf_op jit(solution)/shard_map/ppermute | solution.py:254
  48.6 31.2 %collective-permute-start.17 = (f32[2,128,256]{2,1,0:T(8,128)}, f32[2,128,256]{2,1,0:T(8,128)S(1)}, u32[]{:S(2)}, u32[]{:S(2)}) collective-permute-start(f32[2,128,256]{2,1,0:T(8,128)} %get-tuple-element.139), channel_id=1, source_target_pairs={{0,6},{1,7},{2,4},{3,5},{4,2},{5,3},{6,0},{7,1},{8,14},{9,15},{10,... | collective-permute-start | bytes 786440 | tf_op jit(solution)/shard_map/ppermute | solution.py:254
  56.5 23.3 %collective-permute-start.9 = (f32[2,128,256]{2,1,0:T(8,128)}, f32[2,128,256]{2,1,0:T(8,128)S(1)}, u32[]{:S(2)}, u32[]{:S(2)}) collective-permute-start(f32[2,128,256]{2,1,0:T(8,128)} %get-tuple-element.123), channel_id=1, source_target_pairs={{0,11},{1,10},{2,9},{3,8},{4,15},{5,14},{6,13},{7,12},{8,3},{9,2},... | collective-permute-start | bytes 786440 | tf_op jit(solution)/shard_map/ppermute | solution.py:254
  58.8 25.8 %collective-permute-start.19 = (f32[2,128,256]{2,1,0:T(8,128)}, f32[2,128,256]{2,1,0:T(8,128)S(1)}, u32[]{:S(2)}, u32[]{:S(2)}) collective-permute-start(f32[2,128,256]{2,1,0:T(8,128)} %get-tuple-element.145), channel_id=1, source_target_pairs={{0,10},{1,11},{2,8},{3,9},{4,14},{5,15},{6,12},{7,13},{8,2},{9,3},... | collective-permute-start | bytes 786440 | tf_op jit(solution)/shard_map/ppermute | solution.py:254
  58.8 25.8 %collective-permute-start.12 = (f32[2,128,256]{2,1,0:T(8,128)}, f32[2,128,256]{2,1,0:T(8,128)S(1)}, u32[]{:S(2)}, u32[]{:S(2)}) collective-permute-start(f32[2,128,256]{2,1,0:T(8,128)} %get-tuple-element.128), channel_id=1, source_target_pairs={{0,2},{1,3},{2,0},{3,1},{4,6},{5,7},{6,4},{7,5},{8,10},{9,11},{10,... | collective-permute-start | bytes 786440 | tf_op jit(solution)/shard_map/ppermute | solution.py:254
  64.6 28.1 %collective-permute-start.16 = (f32[2,128,256]{2,1,0:T(8,128)}, f32[2,128,256]{2,1,0:T(8,128)S(1)}, u32[]{:S(2)}, u32[]{:S(2)}) collective-permute-start(f32[2,128,256]{2,1,0:T(8,128)} %get-tuple-element.137), channel_id=1, source_target_pairs={{0,5},{1,4},{2,7},{3,6},{4,1},{5,0},{6,3},{7,2},{8,13},{9,12},{10,... | collective-permute-start | bytes 786440 | tf_op jit(solution)/shard_map/ppermute | solution.py:254
  79.8 21.2 %collective-permute-start.21 = (f32[2,128,256]{2,1,0:T(8,128)}, f32[2,128,256]{2,1,0:T(8,128)S(1)}, u32[]{:S(2)}, u32[]{:S(2)}) collective-permute-start(f32[2,128,256]{2,1,0:T(8,128)} %get-tuple-element.147), channel_id=1, source_target_pairs={{0,9},{1,8},{2,11},{3,10},{4,13},{5,12},{6,15},{7,14},{8,1},{9,0},... | collective-permute-start | bytes 786440 | tf_op jit(solution)/shard_map/ppermute | solution.py:254
  79.8 21.2 %collective-permute-start.10 = (f32[2,128,256]{2,1,0:T(8,128)}, f32[2,128,256]{2,1,0:T(8,128)S(1)}, u32[]{:S(2)}, u32[]{:S(2)}) collective-permute-start(f32[2,128,256]{2,1,0:T(8,128)} %get-tuple-element.124), channel_id=1, source_target_pairs={{0,1},{1,0},{2,3},{3,2},{4,5},{5,4},{6,7},{7,6},{8,9},{9,8},{10,11... | collective-permute-start | bytes 786440 | tf_op jit(solution)/shard_map/ppermute | solution.py:254
  84.6 21.1 %collective-permute-start.20 = (f32[2,128,256]{2,1,0:T(8,128)}, f32[2,128,256]{2,1,0:T(8,128)S(1)}, u32[]{:S(2)}, u32[]{:S(2)}) collective-permute-start(f32[2,128,256]{2,1,0:T(8,128)} %get-tuple-element.146), channel_id=1, source_target_pairs={{0,8},{1,9},{2,10},{3,11},{4,12},{5,13},{6,14},{7,15},{8,0},{9,1},... | collective-permute-start | bytes 786440 | tf_op jit(solution)/shard_map/ppermute | solution.py:254
  84.6 21.1 %collective-permute-start.15 = (f32[2,128,256]{2,1,0:T(8,128)}, f32[2,128,256]{2,1,0:T(8,128)S(1)}, u32[]{:S(2)}, u32[]{:S(2)}) collective-permute-start(f32[2,128,256]{2,1,0:T(8,128)} %get-tuple-element.136), channel_id=1, source_target_pairs={{0,4},{1,5},{2,6},{3,7},{4,0},{5,1},{6,2},{7,3},{8,12},{9,13},{10,... | collective-permute-start | bytes 786440 | tf_op jit(solution)/shard_map/ppermute | solution.py:254

commit v6 on v5

--- a/solution.py
+++ b/solution.py
@@ -287,29 +287,33 @@
     pieces = list(pieces)
     half = devices // 2
     crossing = list(reversed(range(half, devices)))
-    local = [m for pair in zip(reversed(range(NEAR, half)), [3, 2, 1] + [None] * half) for m in pair if m]
-    between = [("xw", m) for m in range(1, NEAR)] + [("vz", m) for m in range(1, lax.axis_size("row"))]
-    between += [("child", m) for m in local]
-    gaps = len(crossing) - 2
+    middle = list(range(NEAR, half))
+    local = [middle[-1], 3, middle[-2], *middle[:-2], 2, 1]
     spots, xw, vz = {}, [], []
-    for n, m in enumerate(crossing):
-        for i, (kind, other) in enumerate(between):
-            if n == 2 + i * gaps // len(between):
-                if kind == "child":
-                    if other == local[-3]:
-                        given = [line] + [sender.arrived[i] for i in xw], [both] + [sender.arrived[i] for i in vz]
-                        left, right = factors(dinv, pivots, rank_rows, rank_cols, admissible, *given)
-                        left, right, pieces[other] = lax.optimization_barrier((left, right, pieces[other]))
-                    spots[other] = sender.send(pieces[other], GROUP, other)
-                elif kind == "xw":
-                    if not xw:
-                        line = jnp.stack([mine] + [sender.arrived[i] for i in line])
-                    xw.append(sender.send(line, GROUP, other))
-                else:
-                    if not vz:
-                        both = jnp.concatenate([v_fac, z_fac], axis=0)
-                    vz.append(sender.send(both, ("row",), other))
-        spots[m] = sender.send(pieces[m], GROUP, m)
+
+    def send(kind, m):
+        if kind == "child":
+            spots[m] = sender.send(pieces[m], GROUP, m)
+        elif kind == "xw":
+            xw.append(sender.send(line, GROUP, m))
+        else:
+            vz.append(sender.send(both, ("row",), m))
+
+    other = [("xw", 3)] + [("vz", m) for m in range(1, lax.axis_size("row"))] + [("child", m) for m in local]
+    last = len(other) - 4
+    gaps = len(crossing) - 3
+    send("child", crossing[0])
+    line = jnp.stack([mine] + [sender.arrived[i] for i in line])
+    both = jnp.concatenate([v_fac, z_fac], axis=0)
+    order = [("xw", 1), ("xw", 2), ("child", crossing[1]), ("child", crossing[2])]
+    for n, m in enumerate(crossing[3:]):
+        order += other[n * last // gaps : (n + 1) * last // gaps] + [("child", m)]
+    for kind, m in order + other[last:]:
+        if (kind, m) == ("child", local[2]):
+            given = [line] + [sender.arrived[i] for i in xw], [both] + [sender.arrived[i] for i in vz]
+            left, right = factors(dinv, pivots, rank_rows, rank_cols, admissible, *given)
+            left, right, pieces[m] = lax.optimization_barrier((left, right, pieces[m]))
+        send(kind, m)
     got = [pieces[0]] + [sender.arrived[spots[m]] for m in range(1, devices)]
     return finish(front, left, right, got, row_map, tile)
 

time: 111 us -> 122 us (1.099)
  starting transfers between devices: 55.4 us -> 69.7 us
  waiting for transfers between devices: 39.5 us -> 36.8 us
    ppermute x22, starting transfers between devices: 55.4 us -> 69.7 us  [send(): lax.ppermute(array, axes, [(d, d ^ m) for d in range(size)])]
    ppermute x22, waiting for transfers between devices: 39.5 us -> 36.8 us  [send(): lax.ppermute(array, axes, [(d, d ^ m) for d in range(size)])]
  transfers between devices with their start and end apart: 22 -> 22, of which waited for: 7 -> 8; matrix products, arithmetic and copies ran while one was open for 1% -> 0% of each run, Pallas kernels for 8% -> 7%
where the time goes in v6:
time: 122 us
  starting transfers between devices  69.7 us (57%)
  waiting for transfers between devices  36.8 us (30%)
  Pallas kernels  13.8 us (11%)
    ppermute x22, starting transfers between devices, send(): lax.ppermute(array, axes, [(d, d ^ m) for d in range(size)])  69.7 us
    ppermute x22, waiting for transfers between devices, send(): lax.ppermute(array, axes, [(d, d ^ m) for d in range(size)])  36.8 us
    pallas_call x1, Pallas kernels, place(): pl.pallas_call(functools.partial(place_kernel, tiles, groups, tile, col_t...  5.13 us
    pallas_call x1, Pallas kernels, finish(): pl.pallas_call(functools.partial(finish_kernel, len(pieces), tile), out_s...  4.85 us
    pallas_call x1, Pallas kernels, factors(): pl.pallas_call(functools.partial(factor_kernel, len(xw), len(vz), col_til...  3.76 us
  transfers between devices with their start and end apart: 22, of which 8 were waited for; matrix products, arithmetic and copies ran while one was open for 0% of the time, Pallas kernels for 7%

profile of v6, /device:TPU:0, one launch (start us, length us, event | category | flops | bytes accessed | tf_op | source)
XLA Modules:
  0.0 122.2 jit_solution(10577113228599865392)
XLA Ops:
  0.0 0.0 copy-start.1
  0.0 0.0 copy-start
  0.0 0.9 pad_add_fusion
  0.9 5.0 %collective-permute-start.2 = (f32[16,1024]{1,0:T(8,128)S(1)}, f32[16,1024]{1,0:T(8,128)S(1)}, u32[]{:S(2)}, u32[]{:S(2)}) collective-permute-start(f32[16,1024]{1,0:T(8,128)S(1)} %pad_add_fusion), channel_id=1, source_target_pairs={{0,12},{1,13},{2,14},{3,15},{4,8},{5,9},{6,10},{7,11},{8,4},{9,5},... | collective-permute-start | bytes 196616 | tf_op jit(solution)/shard_map/ppermute | solution.py:254
  5.9 0.0 collective-permute-start.1
  5.9 0.6 collective-permute-start
  6.6 5.1 %place_child.1 = (f32[2,128,256]{2,1,0:T(8,128)}, f32[2,128,256]{2,1,0:T(8,128)}, f32[2,128,256]{2,1,0:T(8,128)}, f32[2,128,256]{2,1,0:T(8,128)}, f32[2,128,256]...) custom-call(s32[32]{0:T(128)} %col_map.1, ...), custom_call_target="tpu_custom_call" | custom-call | bytes 8388608 | tf_op jit(solution)/shard_map/place_child/pallas_call | solution.py:65
  11.7 3.3 %collective-permute-start.5 = (f32[2,128,256]{2,1,0:T(8,128)}, f32[2,128,256]{2,1,0:T(8,128)S(1)}, u32[]{:S(2)}, u32[]{:S(2)}) collective-permute-start(f32[2,128,256]{2,1,0:T(8,128)} %get-tuple-element.108), channel_id=1, source_target_pairs={{0,15},{1,14},{2,13},{3,12},{4,11},{5,10},{6,9},{7,8},{8,7},{9,6},... | collective-permute-start | bytes 786440 | tf_op jit(solution)/shard_map/ppermute | solution.py:254
  15.1 0.0 collective-permute-done.2
  15.1 0.0 collective-permute-done.1
  15.1 0.0 collective-permute-done
  15.1 0.0 copy-start.4
  15.1 1.6 %collective-permute-start.3 = (f32[4,16,1024]{2,1,0:T(8,128)S(1)}, f32[4,16,1024]{2,1,0:T(8,128)S(1)}, u32[]{:S(2)}, u32[]{:S(2)}) collective-permute-start(f32[4,16,1024]{2,1,0:T(8,128)S(1)} %pad_maximum_fusion.rest_0_), channel_id=1, source_target_pairs={{0,1},{1,0},{2,3},{3,2},{4,5},{5,4},{6,7},{7,6},{8,9},{9,8},{10,11... | collective-permute-start | bytes 786440 | tf_op jit(solution)/shard_map/ppermute | solution.py:254
  16.7 0.1 collective-permute-start.8
  16.8 1.6 %collective-permute-start.4 = (f32[4,16,1024]{2,1,0:T(8,128)S(1)}, f32[4,16,1024]{2,1,0:T(8,128)S(1)}, u32[]{:S(2)}, u32[]{:S(2)}) collective-permute-start(f32[4,16,1024]{2,1,0:T(8,128)S(1)} %pad_maximum_fusion.rest_0_), channel_id=1, source_target_pairs={{0,2},{1,3},{2,0},{3,1},{4,6},{5,7},{6,4},{7,5},{8,10},{9,11},{10,... | collective-permute-start | bytes 786440 | tf_op jit(solution)/shard_map/ppermute | solution.py:254
  18.4 2.7 %collective-permute-start.19 = (f32[2,128,256]{2,1,0:T(8,128)}, f32[2,128,256]{2,1,0:T(8,128)S(1)}, u32[]{:S(2)}, u32[]{:S(2)}) collective-permute-start(f32[2,128,256]{2,1,0:T(8,128)} %get-tuple-element.143), channel_id=1, source_target_pairs={{0,13},{1,12},{2,15},{3,14},{4,9},{5,8},{6,11},{7,10},{8,5},{9,4},... | collective-permute-start | bytes 786440 | tf_op jit(solution)/shard_map/ppermute | solution.py:254
  21.1 1.9 %collective-permute-done.5.rest_14_ = f32[2,128,256]{2,1,0:T(8,128)S(1)} collective-permute-done((f32[2,128,256]{2,1,0:T(8,128)}, f32[2,128,256]{2,1,0:T(8,128)S(1)}, u32[]{:S(2)}, u32[]{:S(2)}) %collective-permute-start.5) | collective-permute-done | bytes 262176 | tf_op jit(solution)/shard_map/ppermute | solution.py:254
  23.0 0.6 collective-permute-start.6
  23.6 0.0 collective-permute-done.3.rest_1_
  23.6 5.9 %collective-permute-done.8.rest_13_ = f32[2,128,256]{2,1,0:T(8,128)S(1)} collective-permute-done((f32[2,128,256]{2,1,0:T(8,128)}, f32[2,128,256]{2,1,0:T(8,128)S(1)}, u32[]{:S(2)}, u32[]{:S(2)}) %collective-permute-start.8) | collective-permute-done | bytes 262176 | tf_op jit(solution)/shard_map/ppermute | solution.py:254
  29.5 17.1 %collective-permute-start.9 = (f32[2,128,256]{2,1,0:T(8,128)}, f32[2,128,256]{2,1,0:T(8,128)S(1)}, u32[]{:S(2)}, u32[]{:S(2)}) collective-permute-start(f32[2,128,256]{2,1,0:T(8,128)} %get-tuple-element.124), channel_id=1, source_target_pairs={{0,11},{1,10},{2,9},{3,8},{4,15},{5,14},{6,13},{7,12},{8,3},{9,2},... | collective-permute-start | bytes 786440 | tf_op jit(solution)/shard_map/ppermute | solution.py:254
  46.6 1.5 %collective-permute-start.14 = (f32[2,128,256]{2,1,0:T(8,128)}, f32[2,128,256]{2,1,0:T(8,128)S(1)}, u32[]{:S(2)}, u32[]{:S(2)}) collective-permute-start(f32[2,128,256]{2,1,0:T(8,128)} %get-tuple-element.132), channel_id=1, source_target_pairs={{0,12},{1,13},{2,14},{3,15},{4,8},{5,9},{6,10},{7,11},{8,4},{9,5},... | collective-permute-start | bytes 786440 | tf_op jit(solution)/shard_map/ppermute | solution.py:254
  48.1 0.0 copy-done.10
  48.1 0.0 copy-done.11
  48.1 0.1 pad_maximum_fusion.1.rest_4_
  48.1 0.0 copy-start.5
  48.1 0.0 collective-permute-done.4.rest_2_
  48.1 0.0 copy-start.7
  48.2 1.6 %collective-permute-start.7 = (f32[4,8192]{1,0:T(4,128)S(1)}, f32[4,8192]{1,0:T(4,128)S(1)}, u32[]{:S(2)}, u32[]{:S(2)}) collective-permute-start(f32[4,8192]{1,0:T(4,128)S(1)} %pad_maximum_fusion.1.rest_4_), channel_id=1, source_target_pairs={{0,16},{16,0},{1,17},{17,1},{2,18},{18,2},{3,19},{19,3},{4,20},{20... | collective-permute-start | bytes 393224 | tf_op jit(solution)/shard_map/ppermute | solution.py:254
  49.7 0.0 copy-done.12
  49.7 0.1 copy.14.admissible
  49.8 0.0 collective-permute-done.19.rest_12_
  49.8 12.1 %collective-permute-start.20 = (f32[2,128,256]{2,1,0:T(8,128)}, f32[2,128,256]{2,1,0:T(8,128)S(1)}, u32[]{:S(2)}, u32[]{:S(2)}) collective-permute-start(f32[2,128,256]{2,1,0:T(8,128)} %get-tuple-element.144), channel_id=1, source_target_pairs={{0,7},{1,6},{2,5},{3,4},{4,3},{5,2},{6,1},{7,0},{8,15},{9,14},{10,... | collective-permute-start | bytes 786440 | tf_op jit(solution)/shard_map/ppermute | solution.py:254
  61.9 0.0 collective-permute-done.7.rest_5_
  61.9 0.0 collective-permute-start.12
  62.0 0.0 collective-permute-done.6.rest_3_
  62.0 0.0 copy-done.4
  62.0 0.0 copy-done.6
  62.0 0.0 copy-done.5
  62.0 0.6 copy-done.9
  62.6 0.1 copy-done.8
  62.7 0.0 copy-done.1
  62.7 3.8 %update_factors.1 = (f32[2,512,128]{2,1,0:T(8,128)S(1)}, f32[4,512,128]{2,1,0:T(8,128)S(1)}) custom-call(f32[256,256]{1,0:T(8,128)S(1)} %copy-done, s32[1,256]{1,0:T(1,128)S(1)} %bitcast.5, s32[8]{0:T(128)S(1)} %copy-done.2, s32[2]{0:T(128)S(1)} %copy-done.3, s32[8,2]{1,0:T(8,128)S(1)} %copy.14.admissible, f32[4,16,1024]{2,1,0:T(8,128)} %copy-done.4, ...), custom_call_target="tpu_custom_call" | custom-call | flops 67108864 | bytes 2097152 | tf_op jit(solution)/shard_map/update_factors/pallas_call | solution.py:148
  66.5 3.8 %collective-permute-start.16 = (f32[2,128,256]{2,1,0:T(8,128)}, f32[2,128,256]{2,1,0:T(8,128)S(1)}, u32[]{:S(2)}, u32[]{:S(2)}) collective-permute-start(f32[2,128,256]{2,1,0:T(8,128)} %get-tuple-element.136), channel_id=1, source_target_pairs={{0,10},{1,11},{2,8},{3,9},{4,14},{5,15},{6,12},{7,13},{8,2},{9,3},... | collective-permute-start | bytes 786440 | tf_op jit(solution)/shard_map/ppermute | solution.py:254
  70.3 0.0 collective-permute-done.14.rest_11_
  70.3 0.0 collective-permute-start.15
  70.3 0.0 collective-permute-done.9.rest_10_
  70.3 15.3 %collective-permute-start.10 = (f32[2,128,256]{2,1,0:T(8,128)}, f32[2,128,256]{2,1,0:T(8,128)S(1)}, u32[]{:S(2)}, u32[]{:S(2)}) collective-permute-start(f32[2,128,256]{2,1,0:T(8,128)} %get-tuple-element.125), channel_id=1, source_target_pairs={{0,6},{1,7},{2,4},{3,5},{4,2},{5,3},{6,0},{7,1},{8,14},{9,15},{10,... | collective-permute-start | bytes 786440 | tf_op jit(solution)/shard_map/ppermute | solution.py:254
  85.6 0.0 collective-permute-done.20.rest_6_
  85.6 0.0 collective-permute-start.21
  85.6 4.2 %collective-permute-done.12.rest_8_ = f32[2,128,256]{2,1,0:T(8,128)S(1)} collective-permute-done((f32[2,128,256]{2,1,0:T(8,128)}, f32[2,128,256]{2,1,0:T(8,128)S(1)}, u32[]{:S(2)}, u32[]{:S(2)}) %collective-permute-start.12) | collective-permute-done | bytes 262176 | tf_op jit(solution)/shard_map/ppermute | solution.py:254
  89.9 0.6 collective-permute-start.13
  90.4 10.7 %collective-permute-done.16.rest_9_ = f32[2,128,256]{2,1,0:T(8,128)S(1)} collective-permute-done((f32[2,128,256]{2,1,0:T(8,128)}, f32[2,128,256]{2,1,0:T(8,128)S(1)}, u32[]{:S(2)}, u32[]{:S(2)}) %collective-permute-start.16) | collective-permute-done | bytes 262176 | tf_op jit(solution)/shard_map/ppermute | solution.py:254
  101.2 0.0 collective-permute-start.17
  101.2 0.0 collective-permute-done.15.rest_2_
  101.2 1.4 %collective-permute-start.18 = (f32[2,128,256]{2,1,0:T(8,128)}, f32[2,128,256]{2,1,0:T(8,128)S(1)}, u32[]{:S(2)}, u32[]{:S(2)}) collective-permute-start(f32[2,128,256]{2,1,0:T(8,128)} %get-tuple-element.138), channel_id=1, source_target_pairs={{0,5},{1,4},{2,7},{3,6},{4,1},{5,0},{6,3},{7,2},{8,13},{9,12},{10,... | collective-permute-start | bytes 786440 | tf_op jit(solution)/shard_map/ppermute | solution.py:254
  102.5 0.0 collective-permute-done.10.rest_5_
  102.5 0.8 collective-permute-start.11
  103.3 2.5 %collective-permute-done.21.rest_7_ = f32[2,128,256]{2,1,0:T(8,128)S(1)} collective-permute-done((f32[2,128,256]{2,1,0:T(8,128)}, f32[2,128,256]{2,1,0:T(8,128)S(1)}, u32[]{:S(2)}, u32[]{:S(2)}) %collective-permute-start.21) | collective-permute-done | bytes 262176 | tf_op jit(solution)/shard_map/ppermute | solution.py:254
  105.8 0.9 collective-permute-done.13.rest_1_
  106.7 5.2 %collective-permute-done.17.rest_3_ = f32[2,128,256]{2,1,0:T(8,128)S(1)} collective-permute-done((f32[2,128,256]{2,1,0:T(8,128)}, f32[2,128,256]{2,1,0:T(8,128)S(1)}, u32[]{:S(2)}, u32[]{:S(2)}) %collective-permute-start.17) | collective-permute-done | bytes 262176 | tf_op jit(solution)/shard_map/ppermute | solution.py:254
  111.9 5.4 %collective-permute-done.18.rest_4_ = f32[2,128,256]{2,1,0:T(8,128)S(1)} collective-permute-done((f32[2,128,256]{2,1,0:T(8,128)}, f32[2,128,256]{2,1,0:T(8,128)S(1)}, u32[]{:S(2)}, u32[]{:S(2)}) %collective-permute-start.18) | collective-permute-done | bytes 262176 | tf_op jit(solution)/shard_map/ppermute | solution.py:254
  117.3 0.0 collective-permute-done.11.rest_0_
  117.4 4.9 %finish.1 = f32[2048,512]{1,0:T(8,128)} custom-call(s32[1,8]{1,0:T(1,128)} %row_map.1, f32[2048,512]{1,0:T(8,128)} %front.1, f32[2,512,128]{2,1,0:T(8,128)S(1)} %get-tuple-element.117.left, f32[4,512,128]{2,1,0:T(8,128)S(1)} %get-tuple-element.118.right, f32[2,128,256]{2,1,0:T(8,128)S(1)} %collective-permute-done.11.rest_0_, ...), custom_call_target="tpu_custom_call" | custom-call | flops 536870912 | bytes 12582912 | tf_op jit(solution)/shard_map/finish/pallas_call | solution.py:225
  (13 shorter events, 0.0 us)
Async XLA Ops:
  0.0 49.7 %copy-start.12 = (s32[8,2]{0,1:T(2,128)S(1)}, s32[8,2]{0,1:T(2,128)}, u32[]{:S(2)}) copy-start(s32[8,2]{0,1:T(2,128)} %param.25) | copy-start | bytes 196
  0.0 62.7 %copy-start.3 = (s32[2]{0:T(128)S(1)}, s32[2]{0:T(128)}, u32[]{:S(2)}) copy-start(s32[2]{0:T(128)} %rank_cols) | copy-start | bytes 28
  0.0 62.7 %copy-start.2 = (s32[8]{0:T(128)S(1)}, s32[8]{0:T(128)}, u32[]{:S(2)}) copy-start(s32[8]{0:T(128)} %rank_rows) | copy-start | bytes 100
  0.0 48.0 %copy-start.10 = (f32[2,8192]{1,0:T(2,128)S(1)}, f32[2,8192]{1,0:T(2,128)}, u32[]{:S(2)}) copy-start(f32[2,8192]{1,0:T(2,128)} %param.20) | copy-start | bytes 196612
  0.0 48.0 %copy-start.11 = (f32[2,8192]{1,0:T(2,128)S(1)}, f32[2,8192]{1,0:T(2,128)}, u32[]{:S(2)}) copy-start(f32[2,8192]{1,0:T(2,128)} %param.19) | copy-start | bytes 196612
  0.0 62.7 %copy-start.1 = (s32[256]{0:T(256)S(1)}, s32[256]{0:T(256)}, u32[]{:S(2)}) copy-start(s32[256]{0:T(256)} %param.22) | copy-start | bytes 3076
  0.0 62.7 %copy-start = (f32[256,256]{1,0:T(8,128)S(1)}, f32[256,256]{1,0:T(8,128)}, u32[]{:S(2)}) copy-start(f32[256,256]{1,0:T(8,128)} %dinv.1) | copy-start | bytes 786436
  0.9 14.2 %collective-permute-start.2 = (f32[16,1024]{1,0:T(8,128)S(1)}, f32[16,1024]{1,0:T(8,128)S(1)}, u32[]{:S(2)}, u32[]{:S(2)}) collective-permute-start(f32[16,1024]{1,0:T(8,128)S(1)} %pad_add_fusion), channel_id=1, source_target_pairs={{0,12},{1,13},{2,14},{3,15},{4,8},{5,9},{6,10},{7,11},{8,4},{9,5},... | collective-permute-start | bytes 196616 | tf_op jit(solution)/shard_map/ppermute | solution.py:254
  5.9 9.1 %collective-permute-start.1 = (f32[16,1024]{1,0:T(8,128)S(1)}, f32[16,1024]{1,0:T(8,128)S(1)}, u32[]{:S(2)}, u32[]{:S(2)}) collective-permute-start(f32[16,1024]{1,0:T(8,128)S(1)} %pad_add_fusion), channel_id=1, source_target_pairs={{0,8},{1,9},{2,10},{3,11},{4,12},{5,13},{6,14},{7,15},{8,0},{9,1},... | collective-permute-start | bytes 196616 | tf_op jit(solution)/shard_map/ppermute | solution.py:254
  5.9 9.1 %collective-permute-start = (f32[16,1024]{1,0:T(8,128)S(1)}, f32[16,1024]{1,0:T(8,128)S(1)}, u32[]{:S(2)}, u32[]{:S(2)}) collective-permute-start(f32[16,1024]{1,0:T(8,128)S(1)} %pad_add_fusion), channel_id=1, source_target_pairs={{0,4},{1,5},{2,6},{3,7},{4,0},{5,1},{6,2},{7,3},{8,12},{9,13},{10,... | collective-permute-start | bytes 196616 | tf_op jit(solution)/shard_map/ppermute | solution.py:254
  11.7 11.3 %collective-permute-start.5 = (f32[2,128,256]{2,1,0:T(8,128)}, f32[2,128,256]{2,1,0:T(8,128)S(1)}, u32[]{:S(2)}, u32[]{:S(2)}) collective-permute-start(f32[2,128,256]{2,1,0:T(8,128)} %get-tuple-element.108), channel_id=1, source_target_pairs={{0,15},{1,14},{2,13},{3,12},{4,11},{5,10},{6,9},{7,8},{8,7},{9,6},... | collective-permute-start | bytes 786440 | tf_op jit(solution)/shard_map/ppermute | solution.py:254
  15.1 46.9 %copy-start.4 = (f32[4,16,1024]{2,1,0:T(8,128)}, f32[4,16,1024]{2,1,0:T(8,128)S(1)}, u32[]{:S(2)}) copy-start(f32[4,16,1024]{2,1,0:T(8,128)S(1)} %pad_maximum_fusion.rest_0_) | copy-start | bytes 786436
  15.1 8.5 %collective-permute-start.3 = (f32[4,16,1024]{2,1,0:T(8,128)S(1)}, f32[4,16,1024]{2,1,0:T(8,128)S(1)}, u32[]{:S(2)}, u32[]{:S(2)}) collective-permute-start(f32[4,16,1024]{2,1,0:T(8,128)S(1)} %pad_maximum_fusion.rest_0_), channel_id=1, source_target_pairs={{0,1},{1,0},{2,3},{3,2},{4,5},{5,4},{6,7},{7,6},{8,9},{9,8},{10,11... | collective-permute-start | bytes 786440 | tf_op jit(solution)/shard_map/ppermute | solution.py:254
  16.7 12.8 %collective-permute-start.8 = (f32[2,128,256]{2,1,0:T(8,128)}, f32[2,128,256]{2,1,0:T(8,128)S(1)}, u32[]{:S(2)}, u32[]{:S(2)}) collective-permute-start(f32[2,128,256]{2,1,0:T(8,128)} %get-tuple-element.123), channel_id=1, source_target_pairs={{0,14},{1,15},{2,12},{3,13},{4,10},{5,11},{6,8},{7,9},{8,6},{9,7},... | collective-permute-start | bytes 786440 | tf_op jit(solution)/shard_map/ppermute | solution.py:254
  16.8 31.4 %collective-permute-start.4 = (f32[4,16,1024]{2,1,0:T(8,128)S(1)}, f32[4,16,1024]{2,1,0:T(8,128)S(1)}, u32[]{:S(2)}, u32[]{:S(2)}) collective-permute-start(f32[4,16,1024]{2,1,0:T(8,128)S(1)} %pad_maximum_fusion.rest_0_), channel_id=1, source_target_pairs={{0,2},{1,3},{2,0},{3,1},{4,6},{5,7},{6,4},{7,5},{8,10},{9,11},{10,... | collective-permute-start | bytes 786440 | tf_op jit(solution)/shard_map/ppermute | solution.py:254
  18.4 31.4 %collective-permute-start.19 = (f32[2,128,256]{2,1,0:T(8,128)}, f32[2,128,256]{2,1,0:T(8,128)S(1)}, u32[]{:S(2)}, u32[]{:S(2)}) collective-permute-start(f32[2,128,256]{2,1,0:T(8,128)} %get-tuple-element.143), channel_id=1, source_target_pairs={{0,13},{1,12},{2,15},{3,14},{4,9},{5,8},{6,11},{7,10},{8,5},{9,4},... | collective-permute-start | bytes 786440 | tf_op jit(solution)/shard_map/ppermute | solution.py:254
  23.0 38.9 %collective-permute-start.6 = (f32[4,16,1024]{2,1,0:T(8,128)S(1)}, f32[4,16,1024]{2,1,0:T(8,128)S(1)}, u32[]{:S(2)}, u32[]{:S(2)}) collective-permute-start(f32[4,16,1024]{2,1,0:T(8,128)S(1)} %pad_maximum_fusion.rest_0_), channel_id=1, source_target_pairs={{0,3},{1,2},{2,1},{3,0},{4,7},{5,6},{6,5},{7,4},{8,11},{9,10},{10,... | collective-permute-start | bytes 786440 | tf_op jit(solution)/shard_map/ppermute | solution.py:254
  23.6 38.3 %copy-start.6 = (f32[4,16,1024]{2,1,0:T(8,128)}, f32[4,16,1024]{2,1,0:T(8,128)S(1)}, u32[]{:S(2)}) copy-start(f32[4,16,1024]{2,1,0:T(8,128)S(1)} %collective-permute-done.3.rest_1_) | copy-start | bytes 786436
  29.5 40.8 %collective-permute-start.9 = (f32[2,128,256]{2,1,0:T(8,128)}, f32[2,128,256]{2,1,0:T(8,128)S(1)}, u32[]{:S(2)}, u32[]{:S(2)}) collective-permute-start(f32[2,128,256]{2,1,0:T(8,128)} %get-tuple-element.124), channel_id=1, source_target_pairs={{0,11},{1,10},{2,9},{3,8},{4,15},{5,14},{6,13},{7,12},{8,3},{9,2},... | collective-permute-start | bytes 786440 | tf_op jit(solution)/shard_map/ppermute | solution.py:254
  46.6 23.7 %collective-permute-start.14 = (f32[2,128,256]{2,1,0:T(8,128)}, f32[2,128,256]{2,1,0:T(8,128)S(1)}, u32[]{:S(2)}, u32[]{:S(2)}) collective-permute-start(f32[2,128,256]{2,1,0:T(8,128)} %get-tuple-element.132), channel_id=1, source_target_pairs={{0,12},{1,13},{2,14},{3,15},{4,8},{5,9},{6,10},{7,11},{8,4},{9,5},... | collective-permute-start | bytes 786440 | tf_op jit(solution)/shard_map/ppermute | solution.py:254
  48.1 13.9 %copy-start.5 = (f32[4,8192]{1,0:T(4,128)}, f32[4,8192]{1,0:T(4,128)S(1)}, u32[]{:S(2)}) copy-start(f32[4,8192]{1,0:T(4,128)S(1)} %pad_maximum_fusion.1.rest_4_) | copy-start | bytes 393220
  48.1 13.8 %copy-start.7 = (f32[4,16,1024]{2,1,0:T(8,128)}, f32[4,16,1024]{2,1,0:T(8,128)S(1)}, u32[]{:S(2)}) copy-start(f32[4,16,1024]{2,1,0:T(8,128)S(1)} %collective-permute-done.4.rest_2_) | copy-start | bytes 786436
  48.2 13.8 %collective-permute-start.7 = (f32[4,8192]{1,0:T(4,128)S(1)}, f32[4,8192]{1,0:T(4,128)S(1)}, u32[]{:S(2)}, u32[]{:S(2)}) collective-permute-start(f32[4,8192]{1,0:T(4,128)S(1)} %pad_maximum_fusion.1.rest_4_), channel_id=1, source_target_pairs={{0,16},{16,0},{1,17},{17,1},{2,18},{18,2},{3,19},{19,3},{4,20},{20... | collective-permute-start | bytes 393224 | tf_op jit(solution)/shard_map/ppermute | solution.py:254
  49.8 35.8 %collective-permute-start.20 = (f32[2,128,256]{2,1,0:T(8,128)}, f32[2,128,256]{2,1,0:T(8,128)S(1)}, u32[]{:S(2)}, u32[]{:S(2)}) collective-permute-start(f32[2,128,256]{2,1,0:T(8,128)} %get-tuple-element.144), channel_id=1, source_target_pairs={{0,7},{1,6},{2,5},{3,4},{4,3},{5,2},{6,1},{7,0},{8,15},{9,14},{10,... | collective-permute-start | bytes 786440 | tf_op jit(solution)/shard_map/ppermute | solution.py:254
  61.9 0.7 copy-start.9
  61.9 27.9 %collective-permute-start.12 = (f32[2,128,256]{2,1,0:T(8,128)}, f32[2,128,256]{2,1,0:T(8,128)S(1)}, u32[]{:S(2)}, u32[]{:S(2)}) collective-permute-start(f32[2,128,256]{2,1,0:T(8,128)} %get-tuple-element.128), channel_id=1, source_target_pairs={{0,9},{1,8},{2,11},{3,10},{4,13},{5,12},{6,15},{7,14},{8,1},{9,0},... | collective-permute-start | bytes 786440 | tf_op jit(solution)/shard_map/ppermute | solution.py:254
  62.0 0.7 copy-start.8
  66.5 34.7 %collective-permute-start.16 = (f32[2,128,256]{2,1,0:T(8,128)}, f32[2,128,256]{2,1,0:T(8,128)S(1)}, u32[]{:S(2)}, u32[]{:S(2)}) collective-permute-start(f32[2,128,256]{2,1,0:T(8,128)} %get-tuple-element.136), channel_id=1, source_target_pairs={{0,10},{1,11},{2,8},{3,9},{4,14},{5,15},{6,12},{7,13},{8,2},{9,3},... | collective-permute-start | bytes 786440 | tf_op jit(solution)/shard_map/ppermute | solution.py:254
  70.3 30.8 %collective-permute-start.15 = (f32[2,128,256]{2,1,0:T(8,128)}, f32[2,128,256]{2,1,0:T(8,128)S(1)}, u32[]{:S(2)}, u32[]{:S(2)}) collective-permute-start(f32[2,128,256]{2,1,0:T(8,128)} %get-tuple-element.133), channel_id=1, source_target_pairs={{0,3},{1,2},{2,1},{3,0},{4,7},{5,6},{6,5},{7,4},{8,11},{9,10},{10,... | collective-permute-start | bytes 786440 | tf_op jit(solution)/shard_map/ppermute | solution.py:254
  70.3 32.2 %collective-permute-start.10 = (f32[2,128,256]{2,1,0:T(8,128)}, f32[2,128,256]{2,1,0:T(8,128)S(1)}, u32[]{:S(2)}, u32[]{:S(2)}) collective-permute-start(f32[2,128,256]{2,1,0:T(8,128)} %get-tuple-element.125), channel_id=1, source_target_pairs={{0,6},{1,7},{2,4},{3,5},{4,2},{5,3},{6,0},{7,1},{8,14},{9,15},{10,... | collective-permute-start | bytes 786440 | tf_op jit(solution)/shard_map/ppermute | solution.py:254
  85.6 20.2 %collective-permute-start.21 = (f32[2,128,256]{2,1,0:T(8,128)}, f32[2,128,256]{2,1,0:T(8,128)S(1)}, u32[]{:S(2)}, u32[]{:S(2)}) collective-permute-start(f32[2,128,256]{2,1,0:T(8,128)} %get-tuple-element.146), channel_id=1, source_target_pairs={{0,8},{1,9},{2,10},{3,11},{4,12},{5,13},{6,14},{7,15},{8,0},{9,1},... | collective-permute-start | bytes 786440 | tf_op jit(solution)/shard_map/ppermute | solution.py:254
  89.9 16.8 %collective-permute-start.13 = (f32[2,128,256]{2,1,0:T(8,128)}, f32[2,128,256]{2,1,0:T(8,128)S(1)}, u32[]{:S(2)}, u32[]{:S(2)}) collective-permute-start(f32[2,128,256]{2,1,0:T(8,128)} %get-tuple-element.129), channel_id=1, source_target_pairs={{0,2},{1,3},{2,0},{3,1},{4,6},{5,7},{6,4},{7,5},{8,10},{9,11},{10,... | collective-permute-start | bytes 786440 | tf_op jit(solution)/shard_map/ppermute | solution.py:254
  101.2 10.7 %collective-permute-start.17 = (f32[2,128,256]{2,1,0:T(8,128)}, f32[2,128,256]{2,1,0:T(8,128)S(1)}, u32[]{:S(2)}, u32[]{:S(2)}) collective-permute-start(f32[2,128,256]{2,1,0:T(8,128)} %get-tuple-element.137), channel_id=1, source_target_pairs={{0,4},{1,5},{2,6},{3,7},{4,0},{5,1},{6,2},{7,3},{8,12},{9,13},{10,... | collective-permute-start | bytes 786440 | tf_op jit(solution)/shard_map/ppermute | solution.py:254
  101.2 16.2 %collective-permute-start.18 = (f32[2,128,256]{2,1,0:T(8,128)}, f32[2,128,256]{2,1,0:T(8,128)S(1)}, u32[]{:S(2)}, u32[]{:S(2)}) collective-permute-start(f32[2,128,256]{2,1,0:T(8,128)} %get-tuple-element.138), channel_id=1, source_target_pairs={{0,5},{1,4},{2,7},{3,6},{4,1},{5,0},{6,3},{7,2},{8,13},{9,12},{10,... | collective-permute-start | bytes 786440 | tf_op jit(solution)/shard_map/ppermute | solution.py:254
  102.5 14.8 %collective-permute-start.11 = (f32[2,128,256]{2,1,0:T(8,128)}, f32[2,128,256]{2,1,0:T(8,128)S(1)}, u32[]{:S(2)}, u32[]{:S(2)}) collective-permute-start(f32[2,128,256]{2,1,0:T(8,128)} %get-tuple-element.126), channel_id=1, source_target_pairs={{0,1},{1,0},{2,3},{3,2},{4,5},{5,4},{6,7},{7,6},{8,9},{9,8},{10,11... | collective-permute-start | bytes 786440 | tf_op jit(solution)/shard_map/ppermute | solution.py:254

commit v7 on v5

--- a/solution.py
+++ b/solution.py
@@ -25,32 +25,31 @@
     return pltpu.with_memory_space_constraint(array, pltpu.HBM)
 
 
-def place_kernel(tiles, groups, tile, col_tiles, col_map, child, *rest):
-    pieces = rest[: tiles // col_tiles]
-    inverse, held, in_sem, out_sem = rest[tiles // col_tiles :]
-    width = tiles // groups * tile
+def place_kernel(tiles, tile, col_tiles, col_map, child, *rest):
+    count = tiles // col_tiles
+    pieces = rest[:count]
+    inverse, held, in_sem, out_sem = rest[count:]
     me = group_index()
 
-    def fetch(g):
-        span = pl.ds(g * width, width)
-        return pltpu.make_async_copy(child.at[:, span], held.at[:, span], in_sem.at[g])
-
-    def store(m, j):
+    def fetch(m, j):
         b = inverse[(me ^ m) * col_tiles + j]
         span = pl.ds(pl.multiple_of(b * tile, tile), tile)
-        return pltpu.make_async_copy(held.at[:, span], pieces[m].at[j], out_sem.at[m, j])
-
-    for g in range(groups):
-        fetch(g).start()
+        return pltpu.make_async_copy(child.at[:, span], held.at[m, j], in_sem.at[m, j])
+
+    def store(m):
+        return pltpu.make_async_copy(held.at[m], pieces[m], out_sem.at[m])
+
     for b in range(tiles):
         inverse[col_map[b]] = b
-    for g in range(groups):
-        fetch(g).wait()
-    order = [(m, j) for m in reversed(range(len(pieces))) for j in range(col_tiles)]
-    for m, j in order:
-        store(m, j).start()
-    for m, j in order:
-        store(m, j).wait()
+    for m in reversed(range(count)):
+        for j in range(col_tiles):
+            fetch(m, j).start()
+    for m in reversed(range(count)):
+        for j in range(col_tiles):
+            fetch(m, j).wait()
+        store(m).start()
+    for m in reversed(range(count)):
+        store(m).wait()
 
 
 def in_vmem(array):
@@ -61,17 +60,16 @@
     rows = child.shape[0]
     tiles = col_map.shape[0]
     col_tiles = tiles // devices
-    groups = 8
     return pl.pallas_call(
-        functools.partial(place_kernel, tiles, groups, tile, col_tiles),
+        functools.partial(place_kernel, tiles, tile, col_tiles),
         out_shape=[pltpu.HBM((col_tiles, rows, tile), child.dtype)] * devices,
         in_specs=[pl.BlockSpec(memory_space=pltpu.SMEM), pl.BlockSpec(memory_space=pltpu.HBM)],
         out_specs=[pl.BlockSpec(memory_space=pltpu.HBM)] * devices,
         scratch_shapes=[
             pltpu.SMEM((tiles,), jnp.int32),
-            pltpu.VMEM(child.shape, child.dtype),
-            pltpu.SemaphoreType.DMA((groups,)),
+            pltpu.VMEM((devices, col_tiles, rows, tile), child.dtype),
             pltpu.SemaphoreType.DMA((devices, col_tiles)),
+            pltpu.SemaphoreType.DMA((devices,)),
         ],
         compiler_params=pltpu.CompilerParams(vmem_limit_bytes=8 * MIB),
         cost_estimate=pl.CostEstimate(flops=0, bytes_accessed=2 * child.size * 4, transcendentals=0),
@@ -87,10 +85,12 @@
     return size.bit_length() - 1
 
 
-def factor_kernel(parts, halves, col_tiles, row_tiles, dinv, pivots, rank_rows, rank_cols, admissible, *rest):
+def factor_kernel(parts, halves, col_tiles, row_tiles, front, dinv, pivots, rank_rows, rank_cols, admissible, *rest):
     xw = rest[:parts]
     vz = rest[parts : parts + halves]
-    left, right, ws, vs, zs = rest[parts + halves :]
+    left, right, staged, ws, vs, zs, sem = rest[parts + halves :]
+    stage = pltpu.make_async_copy(front, staged, sem)
+    stage.start()
     tile = dinv.shape[0]
     per = xw[0].shape[2] // tile
     chunk = vz[0].shape[1] // tile
@@ -137,9 +137,10 @@
     product = dot(jnp.where(r < top_r, core, 0.0), zs[...])
     for g in range(right.shape[0]):
         right[g, :, :] = product[:, g * LANES : (g + 1) * LANES]
-
-
-def factors(dinv, pivots, rank_rows, rank_cols, admissible, xw, vz):
+    stage.wait()
+
+
+def factors(front, dinv, pivots, rank_rows, rank_cols, admissible, xw, vz):
     tile = dinv.shape[0]
     row_tiles, col_tiles = admissible.shape
     total = RMAX * row_tiles
@@ -150,18 +151,20 @@
         out_shape=[
             pltpu.VMEM((tile // LANES, total, LANES), jnp.float32),
             pltpu.VMEM((col_tiles * tile // LANES, total, LANES), jnp.float32),
+            pltpu.VMEM(front.shape, front.dtype),
         ],
-        in_specs=[inner] * 2 + [scalars] * 3 + [inner] * (len(xw) + len(vz)),
-        out_specs=[inner] * 2,
+        in_specs=[pl.BlockSpec(memory_space=pltpu.HBM)] + [inner] * 2 + [scalars] * 3 + [inner] * (len(xw) + len(vz)),
+        out_specs=[inner] * 3,
         scratch_shapes=[
             pltpu.VMEM((total, tile), jnp.float32),
             pltpu.VMEM((col_tiles * RMAX, tile), jnp.float32),
             pltpu.VMEM((col_tiles * RMAX, col_tiles * tile), jnp.float32),
+            pltpu.SemaphoreType.DMA,
         ],
         compiler_params=pltpu.CompilerParams(vmem_limit_bytes=12 * MIB),
         cost_estimate=pl.CostEstimate(flops=2 * total * tile * tile, bytes_accessed=16 * total * tile, transcendentals=0),
         name="update_factors",
-    )(dinv, pivots.reshape(1, tile), rank_rows, rank_cols, admissible, *[in_hbm(array) for array in (*xw, *vz)])
+    )(in_hbm(front), dinv, pivots.reshape(1, tile), rank_rows, rank_cols, admissible, *[in_hbm(array) for array in (*xw, *vz)])
 
 
 def halves_of(array):
@@ -170,7 +173,7 @@
 
 
 def finish_kernel(count, tile, row_map, front, left, right, *rest):
-    own, out, held, kept, in_sem, out_sem, own_sem = rest[count - 1 :]
+    own, out, held, kept, out_sem, own_sem = rest[count - 1 :]
     pieces = (kept, *rest[: count - 1])
     me = group_index()
     col_tiles, rows, _ = kept.shape
@@ -183,15 +186,10 @@
     def at(g):
         return pl.ds(pl.multiple_of(target(g) * tile, tile), tile)
 
-    def fetch(g):
-        return pltpu.make_async_copy(front.at[at(g), :], held.at[g], in_sem.at[g])
-
     def store(g):
         return pltpu.make_async_copy(held.at[g], out.at[at(g), :], out_sem.at[g])
 
     fetch_own = pltpu.make_async_copy(own, kept, own_sem)
-    for g in reversed(range(groups)):
-        fetch(g).start()
     fetch_own.start()
     for g in reversed(range(groups)):
         mine = pl.ds(target(g), RMAX, stride=left.shape[1] // RMAX)
@@ -203,8 +201,7 @@
             (((0,), (0,)), ((), ())),
             preferred_element_type=jnp.float32,
         )
-        fetch(g).wait()
-        held[g] = held[g] - update
+        held[g] = front[at(g), :] - update
         for p in range(per_tile):
             m = g * per_tile + p
             if m == 0:
@@ -225,20 +222,19 @@
     return pl.pallas_call(
         functools.partial(finish_kernel, len(pieces), tile),
         out_shape=pltpu.HBM(front.shape, front.dtype),
-        in_specs=[pl.BlockSpec(memory_space=pltpu.SMEM), outer] + [inner] * (1 + len(pieces)) + [outer],
+        in_specs=[pl.BlockSpec(memory_space=pltpu.SMEM)] + [inner] * (2 + len(pieces)) + [outer],
         out_specs=outer,
         scratch_shapes=[
             pltpu.VMEM((row_tiles, tile, front.shape[1]), front.dtype),
             pltpu.VMEM(pieces[0].shape, front.dtype),
             pltpu.SemaphoreType.DMA((row_tiles,)),
-            pltpu.SemaphoreType.DMA((row_tiles,)),
             pltpu.SemaphoreType.DMA,
         ],
-        compiler_params=pltpu.CompilerParams(vmem_limit_bytes=16 * MIB),
+        compiler_params=pltpu.CompilerParams(vmem_limit_bytes=8 * MIB),
         cost_estimate=pl.CostEstimate(flops=2 * front.size * 256, bytes_accessed=3 * front.size * 4, transcendentals=0),
         name="finish",
     )(
-        in_hbm(row_map), in_hbm(front), in_vmem(left), in_vmem(right), *[in_vmem(piece) for piece in pieces[1:]], in_hbm(pieces[0])
+        in_hbm(row_map), in_vmem(front), in_vmem(left), in_vmem(right), *[in_vmem(piece) for piece in pieces[1:]], in_hbm(pieces[0])
     )
 
 
@@ -298,8 +294,8 @@
                 if kind == "child":
                     if other == local[-3]:
                         given = [line] + [sender.arrived[i] for i in xw], [both] + [sender.arrived[i] for i in vz]
-                        left, right = factors(dinv, pivots, rank_rows, rank_cols, admissible, *given)
-                        left, right, pieces[other] = lax.optimization_barrier((left, right, pieces[other]))
+                        *ready, staged = factors(front, dinv, pivots, rank_rows, rank_cols, admissible, *given)
+                        ready, staged, pieces[other] = lax.optimization_barrier((ready, staged, pieces[other]))
                     spots[other] = sender.send(pieces[other], GROUP, other)
                 elif kind == "xw":
                     if not xw:
@@ -311,7 +307,7 @@
                     vz.append(sender.send(both, ("row",), other))
         spots[m] = sender.send(pieces[m], GROUP, m)
     got = [pieces[0]] + [sender.arrived[spots[m]] for m in range(1, devices)]
-    return finish(front, left, right, got, row_map, tile)
+    return finish(staged, *ready, got, row_map, tile)
 
 
 def solution(mesh):

time: 111 us -> 110 us (level)
    pallas_call x1, Pallas kernels: 3.76 us -> 5.06 us  [factors(): pl.pallas_call(functools.partial(factor_kernel, len(xw), len(vz), col_til...]
  transfers between devices with their start and end apart: 22 -> 22, of which waited for: 7 -> 7; matrix products, arithmetic and copies ran while one was open for 1% -> 1% of each run, Pallas kernels for 8% -> 9%
where the time goes in v7:
time: 110 us
  starting transfers between devices  54.3 us (49%)
  waiting for transfers between devices  39.2 us (36%)
  Pallas kernels  14.5 us (13%)
    ppermute x22, starting transfers between devices, send(): lax.ppermute(array, axes, [(d, d ^ m) for d in range(size)])  54.3 us
    ppermute x22, waiting for transfers between devices, send(): lax.ppermute(array, axes, [(d, d ^ m) for d in range(size)])  39.2 us
    pallas_call x1, Pallas kernels, place(): pl.pallas_call(functools.partial(place_kernel, tiles, tile, col_tiles), o...  5.08 us
    pallas_call x1, Pallas kernels, factors(): pl.pallas_call(functools.partial(factor_kernel, len(xw), len(vz), col_til...  5.06 us
    pallas_call x1, Pallas kernels, finish(): pl.pallas_call(functools.partial(finish_kernel, len(pieces), tile), out_s...  4.38 us
  transfers between devices with their start and end apart: 22, of which 7 were waited for; matrix products, arithmetic and copies ran while one was open for 1% of the time, Pallas kernels for 9%

profile of v7, /device:TPU:0, one launch (start us, length us, event | category | flops | bytes accessed | tf_op | source)
XLA Modules:
  0.0 110.0 jit_solution(15543762009712834206)
XLA Ops:
  0.0 0.0 copy-start
  0.0 0.8 pad_add_fusion
  0.9 5.1 %collective-permute-start.2 = (f32[16,1024]{1,0:T(8,128)S(1)}, f32[16,1024]{1,0:T(8,128)S(1)}, u32[]{:S(2)}, u32[]{:S(2)}) collective-permute-start(f32[16,1024]{1,0:T(8,128)S(1)} %pad_add_fusion), channel_id=1, source_target_pairs={{0,12},{1,13},{2,14},{3,15},{4,8},{5,9},{6,10},{7,11},{8,4},{9,5},... | collective-permute-start | bytes 196616 | tf_op jit(solution)/shard_map/ppermute | solution.py:250
  5.9 0.0 collective-permute-start.1
  5.9 0.6 collective-permute-start
  6.6 5.1 %place_child.1 = (f32[2,128,256]{2,1,0:T(8,128)}, f32[2,128,256]{2,1,0:T(8,128)}, f32[2,128,256]{2,1,0:T(8,128)}, f32[2,128,256]{2,1,0:T(8,128)}, f32[2,128,256]...) custom-call(s32[32]{0:T(128)} %col_map.1, ...), custom_call_target="tpu_custom_call" | custom-call | bytes 8388608 | tf_op jit(solution)/shard_map/place_child/pallas_call | solution.py:63
  11.6 3.3 %collective-permute-start.5 = (f32[2,128,256]{2,1,0:T(8,128)}, f32[2,128,256]{2,1,0:T(8,128)S(1)}, u32[]{:S(2)}, u32[]{:S(2)}) collective-permute-start(f32[2,128,256]{2,1,0:T(8,128)} %get-tuple-element.110), channel_id=1, source_target_pairs={{0,15},{1,14},{2,13},{3,12},{4,11},{5,10},{6,9},{7,8},{8,7},{9,6},... | collective-permute-start | bytes 786440 | tf_op jit(solution)/shard_map/ppermute | solution.py:250
  15.0 0.0 collective-permute-done.2
  15.0 0.0 collective-permute-done.1
  15.0 0.0 collective-permute-done
  15.0 0.0 copy-start.4
  15.0 1.6 %collective-permute-start.3 = (f32[4,16,1024]{2,1,0:T(8,128)S(1)}, f32[4,16,1024]{2,1,0:T(8,128)S(1)}, u32[]{:S(2)}, u32[]{:S(2)}) collective-permute-start(f32[4,16,1024]{2,1,0:T(8,128)S(1)} %pad_maximum_fusion.rest_0_), channel_id=1, source_target_pairs={{0,1},{1,0},{2,3},{3,2},{4,5},{5,4},{6,7},{7,6},{8,9},{9,8},{10,11... | collective-permute-start | bytes 786440 | tf_op jit(solution)/shard_map/ppermute | solution.py:250
  16.6 0.5 collective-permute-start.4
  17.2 1.1 %collective-permute-start.7 = (f32[2,128,256]{2,1,0:T(8,128)}, f32[2,128,256]{2,1,0:T(8,128)S(1)}, u32[]{:S(2)}, u32[]{:S(2)}) collective-permute-start(f32[2,128,256]{2,1,0:T(8,128)} %get-tuple-element.116), channel_id=1, source_target_pairs={{0,14},{1,15},{2,12},{3,13},{4,10},{5,11},{6,8},{7,9},{8,6},{9,7},... | collective-permute-start | bytes 786440 | tf_op jit(solution)/shard_map/ppermute | solution.py:250
  18.3 2.7 %collective-permute-start.13 = (f32[2,128,256]{2,1,0:T(8,128)}, f32[2,128,256]{2,1,0:T(8,128)S(1)}, u32[]{:S(2)}, u32[]{:S(2)}) collective-permute-start(f32[2,128,256]{2,1,0:T(8,128)} %get-tuple-element.137), channel_id=1, source_target_pairs={{0,13},{1,12},{2,15},{3,14},{4,9},{5,8},{6,11},{7,10},{8,5},{9,4},... | collective-permute-start | bytes 786440 | tf_op jit(solution)/shard_map/ppermute | solution.py:250
  21.0 1.9 %collective-permute-done.5.rest_14_ = f32[2,128,256]{2,1,0:T(8,128)S(1)} collective-permute-done((f32[2,128,256]{2,1,0:T(8,128)}, f32[2,128,256]{2,1,0:T(8,128)S(1)}, u32[]{:S(2)}, u32[]{:S(2)}) %collective-permute-start.5) | collective-permute-done | bytes 262176 | tf_op jit(solution)/shard_map/ppermute | solution.py:250
  23.0 0.6 collective-permute-start.6
  23.6 0.0 collective-permute-done.3.rest_1_
  23.6 11.2 %collective-permute-done.4.rest_2_ = f32[4,16,1024]{2,1,0:T(8,128)} collective-permute-done((f32[4,16,1024]{2,1,0:T(8,128)S(1)}, f32[4,16,1024]{2,1,0:T(8,128)}, u32[]{:S(2)}, u32[]{:S(2)}) %collective-permute-start.4) | collective-permute-done | bytes 262176 | tf_op jit(solution)/shard_map/ppermute | solution.py:250
  34.8 6.2 %collective-permute-start.18 = (f32[2,128,256]{2,1,0:T(8,128)}, f32[2,128,256]{2,1,0:T(8,128)S(1)}, u32[]{:S(2)}, u32[]{:S(2)}) collective-permute-start(f32[2,128,256]{2,1,0:T(8,128)} %get-tuple-element.146), channel_id=1, source_target_pairs={{0,7},{1,6},{2,5},{3,4},{4,3},{5,2},{6,1},{7,0},{8,15},{9,14},{10,... | collective-permute-start | bytes 786440 | tf_op jit(solution)/shard_map/ppermute | solution.py:250
  40.9 2.3 %collective-permute-start.11 = (f32[2,128,256]{2,1,0:T(8,128)}, f32[2,128,256]{2,1,0:T(8,128)S(1)}, u32[]{:S(2)}, u32[]{:S(2)}) collective-permute-start(f32[2,128,256]{2,1,0:T(8,128)} %get-tuple-element.131), channel_id=1, source_target_pairs={{0,12},{1,13},{2,14},{3,15},{4,8},{5,9},{6,10},{7,11},{8,4},{9,5},... | collective-permute-start | bytes 786440 | tf_op jit(solution)/shard_map/ppermute | solution.py:250
  43.2 0.0 copy-done.7
  43.2 0.0 copy-done.8
  43.2 0.1 pad_maximum_fusion.1.rest_4_
  43.3 0.0 copy-start.5
  43.3 0.0 collective-permute-done.7.rest_13_
  43.3 1.6 %collective-permute-start.8 = (f32[4,8192]{1,0:T(4,128)S(1)}, f32[4,8192]{1,0:T(4,128)}, u32[]{:S(2)}, u32[]{:S(2)}) collective-permute-start(f32[4,8192]{1,0:T(4,128)S(1)} %pad_maximum_fusion.1.rest_4_), channel_id=1, source_target_pairs={{0,16},{16,0},{1,17},{17,1},{2,18},{18,2},{3,19},{19,3},{4,20},{20... | collective-permute-start | bytes 393224 | tf_op jit(solution)/shard_map/ppermute | solution.py:250
  44.9 0.0 collective-permute-done.13.rest_12_
  44.9 0.0 collective-permute-start.14
  44.9 3.6 %collective-permute-done.8.rest_5_ = f32[4,8192]{1,0:T(4,128)} collective-permute-done((f32[4,8192]{1,0:T(4,128)S(1)}, f32[4,8192]{1,0:T(4,128)}, u32[]{:S(2)}, u32[]{:S(2)}) %collective-permute-start.8) | collective-permute-done | bytes 131104 | tf_op jit(solution)/shard_map/ppermute | solution.py:250
  48.5 7.9 %collective-permute-start.17 = (f32[2,128,256]{2,1,0:T(8,128)}, f32[2,128,256]{2,1,0:T(8,128)S(1)}, u32[]{:S(2)}, u32[]{:S(2)}) collective-permute-start(f32[2,128,256]{2,1,0:T(8,128)} %get-tuple-element.143), channel_id=1, source_target_pairs={{0,6},{1,7},{2,4},{3,5},{4,2},{5,3},{6,0},{7,1},{8,14},{9,15},{10,... | collective-permute-start | bytes 786440 | tf_op jit(solution)/shard_map/ppermute | solution.py:250
  56.4 0.0 collective-permute-done.6.rest_3_
  56.4 2.3 %collective-permute-start.9 = (f32[2,128,256]{2,1,0:T(8,128)}, f32[2,128,256]{2,1,0:T(8,128)S(1)}, u32[]{:S(2)}, u32[]{:S(2)}) collective-permute-start(f32[2,128,256]{2,1,0:T(8,128)} %get-tuple-element.127), channel_id=1, source_target_pairs={{0,11},{1,10},{2,9},{3,8},{4,15},{5,14},{6,13},{7,12},{8,3},{9,2},... | collective-permute-start | bytes 786440 | tf_op jit(solution)/shard_map/ppermute | solution.py:250
  58.7 0.0 collective-permute-done.18.rest_6_
  58.7 0.0 collective-permute-start.19
  58.7 0.0 collective-permute-done.11.rest_11_
  58.7 1.2 %collective-permute-start.12 = (f32[2,128,256]{2,1,0:T(8,128)}, f32[2,128,256]{2,1,0:T(8,128)S(1)}, u32[]{:S(2)}, u32[]{:S(2)}) collective-permute-start(f32[2,128,256]{2,1,0:T(8,128)} %get-tuple-element.132), channel_id=1, source_target_pairs={{0,2},{1,3},{2,0},{3,1},{4,6},{5,7},{6,4},{7,5},{8,10},{9,11},{10,... | collective-permute-start | bytes 786440 | tf_op jit(solution)/shard_map/ppermute | solution.py:250
  60.0 0.8 copy.14.admissible
  60.7 0.0 copy-start.9
  60.7 0.0 copy-done.4
  60.8 0.0 copy-done.6
  60.8 0.0 copy-done.5
  60.8 0.0 copy-done.3
  60.8 0.0 copy-done.2
  60.8 0.0 copy-done.1
  60.8 5.1 %update_factors.1 = (f32[2,512,128]{2,1,0:T(8,128)S(1)}, f32[4,512,128]{2,1,0:T(8,128)S(1)}, f32[2048,512]{1,0:T(8,128)S(1)}) custom-call(f32[2048,512]{1,0:T(8,128)} %front.1, f32[256,256]{1,0:T(8,128)S(1)} %copy-done, s32[1,256]{1,0:T(1,128)S(1)} %bitcast.5, s32[8]{0:T(128)S(1)} %copy-done.2, s32[2]{0:T(128)S(1)} %copy-done.3, ...), custom_call_target="tpu_custom_call" | custom-call | flops 67108864 | bytes 2097152 | tf_op jit(solution)/shard_map/update_factors/pallas_call | solution.py:149
  65.9 0.0 collective-permute-done.14.rest_2_
  65.9 13.8 %collective-permute-start.16 = (f32[2,128,256]{2,1,0:T(8,128)S(1)}, f32[2,128,256]{2,1,0:T(8,128)S(1)}, u32[]{:S(2)}, u32[]{:S(2)}) collective-permute-start(f32[2,128,256]{2,1,0:T(8,128)S(1)} %copy-done.13), channel_id=1, source_target_pairs={{0,5},{1,4},{2,7},{3,6},{4,1},{5,0},{6,3},{7,2},{8,13},{9,12},{10,... | collective-permute-start | bytes 786440 | tf_op jit(solution)/shard_map/ppermute | solution.py:250
  79.7 0.0 collective-permute-done.17.rest_5_
  79.7 0.0 copy-done.12
  79.7 0.0 collective-permute-start.21
  79.7 0.0 collective-permute-done.9.rest_10_
  79.8 0.9 collective-permute-start.10
  80.6 3.9 %collective-permute-done.19.rest_9_ = f32[2,128,256]{2,1,0:T(8,128)S(1)} collective-permute-done((f32[2,128,256]{2,1,0:T(8,128)}, f32[2,128,256]{2,1,0:T(8,128)S(1)}, u32[]{:S(2)}, u32[]{:S(2)}) %collective-permute-start.19) | collective-permute-done | bytes 262176 | tf_op jit(solution)/shard_map/ppermute | solution.py:250
  84.5 0.0 collective-permute-start.20
  84.5 0.0 collective-permute-done.12.rest_1_
  84.5 0.0 copy-done.9
  84.5 2.5 %collective-permute-start.15 = (f32[2,128,256]{2,1,0:T(8,128)S(1)}, f32[2,128,256]{2,1,0:T(8,128)S(1)}, u32[]{:S(2)}, u32[]{:S(2)}) collective-permute-start(f32[2,128,256]{2,1,0:T(8,128)S(1)} %copy-done.9), channel_id=1, source_target_pairs={{0,4},{1,5},{2,6},{3,7},{4,0},{5,1},{6,2},{7,3},{8,12},{9,13},{10,... | collective-permute-start | bytes 786440 | tf_op jit(solution)/shard_map/ppermute | solution.py:250
  87.1 5.3 %collective-permute-done.16.rest_4_ = f32[2,128,256]{2,1,0:T(8,128)S(1)} collective-permute-done((f32[2,128,256]{2,1,0:T(8,128)S(1)}, f32[2,128,256]{2,1,0:T(8,128)S(1)}, u32[]{:S(2)}, u32[]{:S(2)}) %collective-permute-start.16) | collective-permute-done | bytes 262176 | tf_op jit(solution)/shard_map/ppermute | solution.py:250
  92.4 8.5 %collective-permute-done.21.rest_8_ = f32[2,128,256]{2,1,0:T(8,128)S(1)} collective-permute-done((f32[2,128,256]{2,1,0:T(8,128)S(1)}, f32[2,128,256]{2,1,0:T(8,128)S(1)}, u32[]{:S(2)}, u32[]{:S(2)}) %collective-permute-start.21) | collective-permute-done | bytes 262176 | tf_op jit(solution)/shard_map/ppermute | solution.py:250
  101.0 0.0 collective-permute-done.10.rest_0_
  101.0 4.7 %collective-permute-done.20.rest_7_ = f32[2,128,256]{2,1,0:T(8,128)S(1)} collective-permute-done((f32[2,128,256]{2,1,0:T(8,128)S(1)}, f32[2,128,256]{2,1,0:T(8,128)S(1)}, u32[]{:S(2)}, u32[]{:S(2)}) %collective-permute-start.20) | collective-permute-done | bytes 262176 | tf_op jit(solution)/shard_map/ppermute | solution.py:250
  105.6 0.0 collective-permute-done.15.rest_3_
  105.6 4.4 %finish.1 = f32[2048,512]{1,0:T(8,128)} custom-call(s32[1,8]{1,0:T(1,128)} %row_map.1, f32[2048,512]{1,0:T(8,128)S(1)} %get-tuple-element.123.front, f32[2,512,128]{2,1,0:T(8,128)S(1)} %get-tuple-element.124.left, f32[4,512,128]{2,1,0:T(8,128)S(1)} %get-tuple-element.125.right, f32[2,128,256]{2,1,0:T(8,128)S(1)} %collective-permute-done.10.rest_0_, ...), custom_call_target="tpu_custom_call" | custom-call | flops 536870912 | bytes 12582912 | tf_op jit(solution)/shard_map/finish/pallas_call | solution.py:222
  (15 shorter events, 0.0 us)
Async XLA Ops:
  0.0 60.8 %copy-start.3 = (s32[2]{0:T(128)S(1)}, s32[2]{0:T(128)}, u32[]{:S(2)}) copy-start(s32[2]{0:T(128)} %rank_cols) | copy-start | bytes 28
  0.0 60.8 %copy-start.2 = (s32[8]{0:T(128)S(1)}, s32[8]{0:T(128)}, u32[]{:S(2)}) copy-start(s32[8]{0:T(128)} %rank_rows) | copy-start | bytes 100
  0.0 43.2 %copy-start.7 = (f32[2,8192]{1,0:T(2,128)S(1)}, f32[2,8192]{1,0:T(2,128)}, u32[]{:S(2)}) copy-start(f32[2,8192]{1,0:T(2,128)} %param.20) | copy-start | bytes 196612
  0.0 43.2 %copy-start.8 = (f32[2,8192]{1,0:T(2,128)S(1)}, f32[2,8192]{1,0:T(2,128)}, u32[]{:S(2)}) copy-start(f32[2,8192]{1,0:T(2,128)} %param.19) | copy-start | bytes 196612
  0.0 60.8 %copy-start.1 = (s32[256]{0:T(256)S(1)}, s32[256]{0:T(256)}, u32[]{:S(2)}) copy-start(s32[256]{0:T(256)} %param.22) | copy-start | bytes 3076
  0.0 60.8 %copy-start = (f32[256,256]{1,0:T(8,128)S(1)}, f32[256,256]{1,0:T(8,128)}, u32[]{:S(2)}) copy-start(f32[256,256]{1,0:T(8,128)} %dinv.1) | copy-start | bytes 786436
  0.9 14.1 %collective-permute-start.2 = (f32[16,1024]{1,0:T(8,128)S(1)}, f32[16,1024]{1,0:T(8,128)S(1)}, u32[]{:S(2)}, u32[]{:S(2)}) collective-permute-start(f32[16,1024]{1,0:T(8,128)S(1)} %pad_add_fusion), channel_id=1, source_target_pairs={{0,12},{1,13},{2,14},{3,15},{4,8},{5,9},{6,10},{7,11},{8,4},{9,5},... | collective-permute-start | bytes 196616 | tf_op jit(solution)/shard_map/ppermute | solution.py:250
  5.9 9.1 %collective-permute-start.1 = (f32[16,1024]{1,0:T(8,128)S(1)}, f32[16,1024]{1,0:T(8,128)S(1)}, u32[]{:S(2)}, u32[]{:S(2)}) collective-permute-start(f32[16,1024]{1,0:T(8,128)S(1)} %pad_add_fusion), channel_id=1, source_target_pairs={{0,8},{1,9},{2,10},{3,11},{4,12},{5,13},{6,14},{7,15},{8,0},{9,1},... | collective-permute-start | bytes 196616 | tf_op jit(solution)/shard_map/ppermute | solution.py:250
  5.9 9.1 %collective-permute-start = (f32[16,1024]{1,0:T(8,128)S(1)}, f32[16,1024]{1,0:T(8,128)S(1)}, u32[]{:S(2)}, u32[]{:S(2)}) collective-permute-start(f32[16,1024]{1,0:T(8,128)S(1)} %pad_add_fusion), channel_id=1, source_target_pairs={{0,4},{1,5},{2,6},{3,7},{4,0},{5,1},{6,2},{7,3},{8,12},{9,13},{10,... | collective-permute-start | bytes 196616 | tf_op jit(solution)/shard_map/ppermute | solution.py:250
  11.6 11.3 %collective-permute-start.5 = (f32[2,128,256]{2,1,0:T(8,128)}, f32[2,128,256]{2,1,0:T(8,128)S(1)}, u32[]{:S(2)}, u32[]{:S(2)}) collective-permute-start(f32[2,128,256]{2,1,0:T(8,128)} %get-tuple-element.110), channel_id=1, source_target_pairs={{0,15},{1,14},{2,13},{3,12},{4,11},{5,10},{6,9},{7,8},{8,7},{9,6},... | collective-permute-start | bytes 786440 | tf_op jit(solution)/shard_map/ppermute | solution.py:250
  15.0 45.7 %copy-start.4 = (f32[4,16,1024]{2,1,0:T(8,128)}, f32[4,16,1024]{2,1,0:T(8,128)S(1)}, u32[]{:S(2)}) copy-start(f32[4,16,1024]{2,1,0:T(8,128)S(1)} %pad_maximum_fusion.rest_0_) | copy-start | bytes 786436
  15.0 8.5 %collective-permute-start.3 = (f32[4,16,1024]{2,1,0:T(8,128)S(1)}, f32[4,16,1024]{2,1,0:T(8,128)S(1)}, u32[]{:S(2)}, u32[]{:S(2)}) collective-permute-start(f32[4,16,1024]{2,1,0:T(8,128)S(1)} %pad_maximum_fusion.rest_0_), channel_id=1, source_target_pairs={{0,1},{1,0},{2,3},{3,2},{4,5},{5,4},{6,7},{7,6},{8,9},{9,8},{10,11... | collective-permute-start | bytes 786440 | tf_op jit(solution)/shard_map/ppermute | solution.py:250
  16.6 18.1 %collective-permute-start.4 = (f32[4,16,1024]{2,1,0:T(8,128)S(1)}, f32[4,16,1024]{2,1,0:T(8,128)}, u32[]{:S(2)}, u32[]{:S(2)}) collective-permute-start(f32[4,16,1024]{2,1,0:T(8,128)S(1)} %pad_maximum_fusion.rest_0_), channel_id=1, source_target_pairs={{0,2},{1,3},{2,0},{3,1},{4,6},{5,7},{6,4},{7,5},{8,10},{9,11},{10,... | collective-permute-start | bytes 786440 | tf_op jit(solution)/shard_map/ppermute | solution.py:250
  17.2 26.2 %collective-permute-start.7 = (f32[2,128,256]{2,1,0:T(8,128)}, f32[2,128,256]{2,1,0:T(8,128)S(1)}, u32[]{:S(2)}, u32[]{:S(2)}) collective-permute-start(f32[2,128,256]{2,1,0:T(8,128)} %get-tuple-element.116), channel_id=1, source_target_pairs={{0,14},{1,15},{2,12},{3,13},{4,10},{5,11},{6,8},{7,9},{8,6},{9,7},... | collective-permute-start | bytes 786440 | tf_op jit(solution)/shard_map/ppermute | solution.py:250
  18.3 26.6 %collective-permute-start.13 = (f32[2,128,256]{2,1,0:T(8,128)}, f32[2,128,256]{2,1,0:T(8,128)S(1)}, u32[]{:S(2)}, u32[]{:S(2)}) collective-permute-start(f32[2,128,256]{2,1,0:T(8,128)} %get-tuple-element.137), channel_id=1, source_target_pairs={{0,13},{1,12},{2,15},{3,14},{4,9},{5,8},{6,11},{7,10},{8,5},{9,4},... | collective-permute-start | bytes 786440 | tf_op jit(solution)/shard_map/ppermute | solution.py:250
  23.0 33.5 %collective-permute-start.6 = (f32[4,16,1024]{2,1,0:T(8,128)S(1)}, f32[4,16,1024]{2,1,0:T(8,128)}, u32[]{:S(2)}, u32[]{:S(2)}) collective-permute-start(f32[4,16,1024]{2,1,0:T(8,128)S(1)} %pad_maximum_fusion.rest_0_), channel_id=1, source_target_pairs={{0,3},{1,2},{2,1},{3,0},{4,7},{5,6},{6,5},{7,4},{8,11},{9,10},{10,... | collective-permute-start | bytes 786440 | tf_op jit(solution)/shard_map/ppermute | solution.py:250
  23.6 37.2 %copy-start.6 = (f32[4,16,1024]{2,1,0:T(8,128)}, f32[4,16,1024]{2,1,0:T(8,128)S(1)}, u32[]{:S(2)}) copy-start(f32[4,16,1024]{2,1,0:T(8,128)S(1)} %collective-permute-done.3.rest_1_) | copy-start | bytes 786436
  34.8 24.0 %collective-permute-start.18 = (f32[2,128,256]{2,1,0:T(8,128)}, f32[2,128,256]{2,1,0:T(8,128)S(1)}, u32[]{:S(2)}, u32[]{:S(2)}) collective-permute-start(f32[2,128,256]{2,1,0:T(8,128)} %get-tuple-element.146), channel_id=1, source_target_pairs={{0,7},{1,6},{2,5},{3,4},{4,3},{5,2},{6,1},{7,0},{8,15},{9,14},{10,... | collective-permute-start | bytes 786440 | tf_op jit(solution)/shard_map/ppermute | solution.py:250
  40.9 17.8 %collective-permute-start.11 = (f32[2,128,256]{2,1,0:T(8,128)}, f32[2,128,256]{2,1,0:T(8,128)S(1)}, u32[]{:S(2)}, u32[]{:S(2)}) collective-permute-start(f32[2,128,256]{2,1,0:T(8,128)} %get-tuple-element.131), channel_id=1, source_target_pairs={{0,12},{1,13},{2,14},{3,15},{4,8},{5,9},{6,10},{7,11},{8,4},{9,5},... | collective-permute-start | bytes 786440 | tf_op jit(solution)/shard_map/ppermute | solution.py:250
  43.3 17.5 %copy-start.5 = (f32[4,8192]{1,0:T(4,128)}, f32[4,8192]{1,0:T(4,128)S(1)}, u32[]{:S(2)}) copy-start(f32[4,8192]{1,0:T(4,128)S(1)} %pad_maximum_fusion.1.rest_4_) | copy-start | bytes 393220
  43.3 5.2 %collective-permute-start.8 = (f32[4,8192]{1,0:T(4,128)S(1)}, f32[4,8192]{1,0:T(4,128)}, u32[]{:S(2)}, u32[]{:S(2)}) collective-permute-start(f32[4,8192]{1,0:T(4,128)S(1)} %pad_maximum_fusion.1.rest_4_), channel_id=1, source_target_pairs={{0,16},{16,0},{1,17},{17,1},{2,18},{18,2},{3,19},{19,3},{4,20},{20... | collective-permute-start | bytes 393224 | tf_op jit(solution)/shard_map/ppermute | solution.py:250
  44.9 21.0 %collective-permute-start.14 = (f32[2,128,256]{2,1,0:T(8,128)}, f32[2,128,256]{2,1,0:T(8,128)S(1)}, u32[]{:S(2)}, u32[]{:S(2)}) collective-permute-start(f32[2,128,256]{2,1,0:T(8,128)} %get-tuple-element.138), channel_id=1, source_target_pairs={{0,3},{1,2},{2,1},{3,0},{4,7},{5,6},{6,5},{7,4},{8,11},{9,10},{10,... | collective-permute-start | bytes 786440 | tf_op jit(solution)/shard_map/ppermute | solution.py:250
  48.5 31.2 %collective-permute-start.17 = (f32[2,128,256]{2,1,0:T(8,128)}, f32[2,128,256]{2,1,0:T(8,128)S(1)}, u32[]{:S(2)}, u32[]{:S(2)}) collective-permute-start(f32[2,128,256]{2,1,0:T(8,128)} %get-tuple-element.143), channel_id=1, source_target_pairs={{0,6},{1,7},{2,4},{3,5},{4,2},{5,3},{6,0},{7,1},{8,14},{9,15},{10,... | collective-permute-start | bytes 786440 | tf_op jit(solution)/shard_map/ppermute | solution.py:250
  56.4 23.3 %collective-permute-start.9 = (f32[2,128,256]{2,1,0:T(8,128)}, f32[2,128,256]{2,1,0:T(8,128)S(1)}, u32[]{:S(2)}, u32[]{:S(2)}) collective-permute-start(f32[2,128,256]{2,1,0:T(8,128)} %get-tuple-element.127), channel_id=1, source_target_pairs={{0,11},{1,10},{2,9},{3,8},{4,15},{5,14},{6,13},{7,12},{8,3},{9,2},... | collective-permute-start | bytes 786440 | tf_op jit(solution)/shard_map/ppermute | solution.py:250
  58.7 25.8 %collective-permute-start.19 = (f32[2,128,256]{2,1,0:T(8,128)}, f32[2,128,256]{2,1,0:T(8,128)S(1)}, u32[]{:S(2)}, u32[]{:S(2)}) collective-permute-start(f32[2,128,256]{2,1,0:T(8,128)} %get-tuple-element.149), channel_id=1, source_target_pairs={{0,10},{1,11},{2,8},{3,9},{4,14},{5,15},{6,12},{7,13},{8,2},{9,3},... | collective-permute-start | bytes 786440 | tf_op jit(solution)/shard_map/ppermute | solution.py:250
  58.7 25.8 %collective-permute-start.12 = (f32[2,128,256]{2,1,0:T(8,128)}, f32[2,128,256]{2,1,0:T(8,128)S(1)}, u32[]{:S(2)}, u32[]{:S(2)}) collective-permute-start(f32[2,128,256]{2,1,0:T(8,128)} %get-tuple-element.132), channel_id=1, source_target_pairs={{0,2},{1,3},{2,0},{3,1},{4,6},{5,7},{6,4},{7,5},{8,10},{9,11},{10,... | collective-permute-start | bytes 786440 | tf_op jit(solution)/shard_map/ppermute | solution.py:250
  60.7 5.2 %copy-start.13 = (f32[2,128,256]{2,1,0:T(8,128)S(1)}, f32[2,128,256]{2,1,0:T(8,128)}, u32[]{:S(2)}) copy-start(f32[2,128,256]{2,1,0:T(8,128)} %get-tuple-element.141) | copy-start | bytes 786436
  60.7 19.0 %copy-start.12 = (f32[2,128,256]{2,1,0:T(8,128)S(1)}, f32[2,128,256]{2,1,0:T(8,128)}, u32[]{:S(2)}) copy-start(f32[2,128,256]{2,1,0:T(8,128)} %get-tuple-element.151) | copy-start | bytes 786436
  60.7 19.0 %copy-start.11 = (f32[2,128,256]{2,1,0:T(8,128)S(1)}, f32[2,128,256]{2,1,0:T(8,128)}, u32[]{:S(2)}) copy-start(f32[2,128,256]{2,1,0:T(8,128)} %get-tuple-element.128) | copy-start | bytes 786436
  60.7 23.8 %copy-start.10 = (f32[2,128,256]{2,1,0:T(8,128)S(1)}, f32[2,128,256]{2,1,0:T(8,128)}, u32[]{:S(2)}) copy-start(f32[2,128,256]{2,1,0:T(8,128)} %get-tuple-element.150) | copy-start | bytes 786436
  60.7 23.8 %copy-start.9 = (f32[2,128,256]{2,1,0:T(8,128)S(1)}, f32[2,128,256]{2,1,0:T(8,128)}, u32[]{:S(2)}) copy-start(f32[2,128,256]{2,1,0:T(8,128)} %get-tuple-element.140) | copy-start | bytes 786436
  65.9 26.5 %collective-permute-start.16 = (f32[2,128,256]{2,1,0:T(8,128)S(1)}, f32[2,128,256]{2,1,0:T(8,128)S(1)}, u32[]{:S(2)}, u32[]{:S(2)}) collective-permute-start(f32[2,128,256]{2,1,0:T(8,128)S(1)} %copy-done.13), channel_id=1, source_target_pairs={{0,5},{1,4},{2,7},{3,6},{4,1},{5,0},{6,3},{7,2},{8,13},{9,12},{10,... | collective-permute-start | bytes 786440 | tf_op jit(solution)/shard_map/ppermute | solution.py:250
  79.7 21.2 %collective-permute-start.21 = (f32[2,128,256]{2,1,0:T(8,128)S(1)}, f32[2,128,256]{2,1,0:T(8,128)S(1)}, u32[]{:S(2)}, u32[]{:S(2)}) collective-permute-start(f32[2,128,256]{2,1,0:T(8,128)S(1)} %copy-done.12), channel_id=1, source_target_pairs={{0,9},{1,8},{2,11},{3,10},{4,13},{5,12},{6,15},{7,14},{8,1},{9,0},... | collective-permute-start | bytes 786440 | tf_op jit(solution)/shard_map/ppermute | solution.py:250
  79.8 21.2 %collective-permute-start.10 = (f32[2,128,256]{2,1,0:T(8,128)S(1)}, f32[2,128,256]{2,1,0:T(8,128)S(1)}, u32[]{:S(2)}, u32[]{:S(2)}) collective-permute-start(f32[2,128,256]{2,1,0:T(8,128)S(1)} %copy-done.11), channel_id=1, source_target_pairs={{0,1},{1,0},{2,3},{3,2},{4,5},{5,4},{6,7},{7,6},{8,9},{9,8},{10,11... | collective-permute-start | bytes 786440 | tf_op jit(solution)/shard_map/ppermute | solution.py:250
  84.5 21.1 %collective-permute-start.20 = (f32[2,128,256]{2,1,0:T(8,128)S(1)}, f32[2,128,256]{2,1,0:T(8,128)S(1)}, u32[]{:S(2)}, u32[]{:S(2)}) collective-permute-start(f32[2,128,256]{2,1,0:T(8,128)S(1)} %copy-done.10), channel_id=1, source_target_pairs={{0,8},{1,9},{2,10},{3,11},{4,12},{5,13},{6,14},{7,15},{8,0},{9,1},... | collective-permute-start | bytes 786440 | tf_op jit(solution)/shard_map/ppermute | solution.py:250
  84.5 21.1 %collective-permute-start.15 = (f32[2,128,256]{2,1,0:T(8,128)S(1)}, f32[2,128,256]{2,1,0:T(8,128)S(1)}, u32[]{:S(2)}, u32[]{:S(2)}) collective-permute-start(f32[2,128,256]{2,1,0:T(8,128)S(1)} %copy-done.9), channel_id=1, source_target_pairs={{0,4},{1,5},{2,6},{3,7},{4,0},{5,1},{6,2},{7,3},{8,12},{9,13},{10,... | collective-permute-start | bytes 786440 | tf_op jit(solution)/shard_map/ppermute | solution.py:250

commit v8 on v7

--- a/solution.py
+++ b/solution.py
@@ -287,25 +287,28 @@
     between = [("xw", m) for m in range(1, NEAR)] + [("vz", m) for m in range(1, lax.axis_size("row"))]
     between += [("child", m) for m in local]
     gaps = len(crossing) - 2
+    turn = [2 + i * gaps // len(between) for i in range(len(between))]
+    order = []
+    for n, m in enumerate(crossing[:-2]):
+        order += [item for i, item in enumerate(between[:-4]) if turn[i] == n] + [("child", m)]
+    order += [item for i, item in enumerate(between[:-4]) if turn[i] >= len(crossing) - 2]
+    order += [("child", m) for m in (crossing[-2], local[-3], local[-4], crossing[-1], local[-1], local[-2])]
     spots, xw, vz = {}, [], []
-    for n, m in enumerate(crossing):
-        for i, (kind, other) in enumerate(between):
-            if n == 2 + i * gaps // len(between):
-                if kind == "child":
-                    if other == local[-3]:
-                        given = [line] + [sender.arrived[i] for i in xw], [both] + [sender.arrived[i] for i in vz]
-                        *ready, staged = factors(front, dinv, pivots, rank_rows, rank_cols, admissible, *given)
-                        ready, staged, pieces[other] = lax.optimization_barrier((ready, staged, pieces[other]))
-                    spots[other] = sender.send(pieces[other], GROUP, other)
-                elif kind == "xw":
-                    if not xw:
-                        line = jnp.stack([mine] + [sender.arrived[i] for i in line])
-                    xw.append(sender.send(line, GROUP, other))
-                else:
-                    if not vz:
-                        both = jnp.concatenate([v_fac, z_fac], axis=0)
-                    vz.append(sender.send(both, ("row",), other))
-        spots[m] = sender.send(pieces[m], GROUP, m)
+    for kind, m in order:
+        if kind == "xw":
+            if not xw:
+                line = jnp.stack([mine] + [sender.arrived[i] for i in line])
+            xw.append(sender.send(line, GROUP, m))
+        elif kind == "vz":
+            if not vz:
+                both = jnp.concatenate([v_fac, z_fac], axis=0)
+            vz.append(sender.send(both, ("row",), m))
+        else:
+            if m == local[-3]:
+                given = [line] + [sender.arrived[i] for i in xw], [both] + [sender.arrived[i] for i in vz]
+                *ready, staged = factors(front, dinv, pivots, rank_rows, rank_cols, admissible, *given)
+                ready, staged, pieces[m] = lax.optimization_barrier((ready, staged, pieces[m]))
+            spots[m] = sender.send(pieces[m], GROUP, m)
     got = [pieces[0]] + [sender.arrived[spots[m]] for m in range(1, devices)]
     return finish(staged, *ready, got, row_map, tile)
 

time: 110 us -> 116 us (1.055)
  waiting for transfers between devices: 39.2 us -> 53.6 us
  starting transfers between devices: 54.3 us -> 46 us
    ppermute x22, waiting for transfers between devices: 39.2 us -> 53.6 us  [send(): lax.ppermute(array, axes, [(d, d ^ m) for d in range(size)])]
    ppermute x22, starting transfers between devices: 54.3 us -> 46 us  [send(): lax.ppermute(array, axes, [(d, d ^ m) for d in range(size)])]
  transfers between devices with their start and end apart: 22 -> 22, of which waited for: 7 -> 8; matrix products, arithmetic and copies ran while one was open for 1% -> 1% of each run, Pallas kernels for 9% -> 9%
where the time goes in v8:
time: 116 us
  waiting for transfers between devices  53.6 us (46%)
  starting transfers between devices  46 us (40%)
  Pallas kernels  14.5 us (12%)
    ppermute x22, waiting for transfers between devices, send(): lax.ppermute(array, axes, [(d, d ^ m) for d in range(size)])  53.6 us
    ppermute x22, starting transfers between devices, send(): lax.ppermute(array, axes, [(d, d ^ m) for d in range(size)])  46 us
    pallas_call x1, Pallas kernels, place(): pl.pallas_call(functools.partial(place_kernel, tiles, tile, col_tiles), o...  5.08 us
    pallas_call x1, Pallas kernels, factors(): pl.pallas_call(functools.partial(factor_kernel, len(xw), len(vz), col_til...  5.06 us
    pallas_call x1, Pallas kernels, finish(): pl.pallas_call(functools.partial(finish_kernel, len(pieces), tile), out_s...  4.38 us
  transfers between devices with their start and end apart: 22, of which 8 were waited for; matrix products, arithmetic and copies ran while one was open for 1% of the time, Pallas kernels for 9%

profile of v8, /device:TPU:0, one launch (start us, length us, event | category | flops | bytes accessed | tf_op | source)
XLA Modules:
  0.0 116.0 jit_solution(4062162389367647221)
XLA Ops:
  0.0 0.0 copy-start
  0.0 0.8 pad_add_fusion
  0.9 5.1 %collective-permute-start.2 = (f32[16,1024]{1,0:T(8,128)S(1)}, f32[16,1024]{1,0:T(8,128)S(1)}, u32[]{:S(2)}, u32[]{:S(2)}) collective-permute-start(f32[16,1024]{1,0:T(8,128)S(1)} %pad_add_fusion), channel_id=1, source_target_pairs={{0,12},{1,13},{2,14},{3,15},{4,8},{5,9},{6,10},{7,11},{8,4},{9,5},... | collective-permute-start | bytes 196616 | tf_op jit(solution)/shard_map/ppermute | solution.py:250
  5.9 0.0 collective-permute-start.1
  5.9 0.6 collective-permute-start
  6.6 5.1 %place_child.1 = (f32[2,128,256]{2,1,0:T(8,128)}, f32[2,128,256]{2,1,0:T(8,128)}, f32[2,128,256]{2,1,0:T(8,128)}, f32[2,128,256]{2,1,0:T(8,128)}, f32[2,128,256]...) custom-call(s32[32]{0:T(128)} %col_map.1, ...), custom_call_target="tpu_custom_call" | custom-call | bytes 8388608 | tf_op jit(solution)/shard_map/place_child/pallas_call | solution.py:63
  11.6 3.3 %collective-permute-start.5 = (f32[2,128,256]{2,1,0:T(8,128)}, f32[2,128,256]{2,1,0:T(8,128)S(1)}, u32[]{:S(2)}, u32[]{:S(2)}) collective-permute-start(f32[2,128,256]{2,1,0:T(8,128)} %get-tuple-element.110), channel_id=1, source_target_pairs={{0,15},{1,14},{2,13},{3,12},{4,11},{5,10},{6,9},{7,8},{8,7},{9,6},... | collective-permute-start | bytes 786440 | tf_op jit(solution)/shard_map/ppermute | solution.py:250
  15.0 0.0 collective-permute-done.2
  15.0 0.0 collective-permute-done.1
  15.0 0.0 collective-permute-done
  15.0 0.0 copy-start.4
  15.0 1.6 %collective-permute-start.3 = (f32[4,16,1024]{2,1,0:T(8,128)S(1)}, f32[4,16,1024]{2,1,0:T(8,128)S(1)}, u32[]{:S(2)}, u32[]{:S(2)}) collective-permute-start(f32[4,16,1024]{2,1,0:T(8,128)S(1)} %pad_maximum_fusion.rest_0_), channel_id=1, source_target_pairs={{0,1},{1,0},{2,3},{3,2},{4,5},{5,4},{6,7},{7,6},{8,9},{9,8},{10,11... | collective-permute-start | bytes 786440 | tf_op jit(solution)/shard_map/ppermute | solution.py:250
  16.6 0.5 collective-permute-start.4
  17.2 1.1 collective-permute-start.7
  18.3 2.7 %collective-permute-start.14 = (f32[2,128,256]{2,1,0:T(8,128)}, f32[2,128,256]{2,1,0:T(8,128)S(1)}, u32[]{:S(2)}, u32[]{:S(2)}) collective-permute-start(f32[2,128,256]{2,1,0:T(8,128)} %get-tuple-element.137), channel_id=1, source_target_pairs={{0,13},{1,12},{2,15},{3,14},{4,9},{5,8},{6,11},{7,10},{8,5},{9,4},... | collective-permute-start | bytes 786440 | tf_op jit(solution)/shard_map/ppermute | solution.py:250
  21.0 1.9 %collective-permute-done.5.rest_14_ = f32[2,128,256]{2,1,0:T(8,128)S(1)} collective-permute-done((f32[2,128,256]{2,1,0:T(8,128)}, f32[2,128,256]{2,1,0:T(8,128)S(1)}, u32[]{:S(2)}, u32[]{:S(2)}) %collective-permute-start.5) | collective-permute-done | bytes 262176 | tf_op jit(solution)/shard_map/ppermute | solution.py:250
  23.0 0.6 collective-permute-start.6
  23.6 0.0 collective-permute-done.3.rest_1_
  23.6 11.2 %collective-permute-done.4.rest_2_ = f32[4,16,1024]{2,1,0:T(8,128)} collective-permute-done((f32[4,16,1024]{2,1,0:T(8,128)S(1)}, f32[4,16,1024]{2,1,0:T(8,128)}, u32[]{:S(2)}, u32[]{:S(2)}) %collective-permute-start.4) | collective-permute-done | bytes 262176 | tf_op jit(solution)/shard_map/ppermute | solution.py:250
  34.8 6.2 %collective-permute-start.9 = (f32[2,128,256]{2,1,0:T(8,128)}, f32[2,128,256]{2,1,0:T(8,128)S(1)}, u32[]{:S(2)}, u32[]{:S(2)}) collective-permute-start(f32[2,128,256]{2,1,0:T(8,128)} %get-tuple-element.128), channel_id=1, source_target_pairs={{0,7},{1,6},{2,5},{3,4},{4,3},{5,2},{6,1},{7,0},{8,15},{9,14},{10,... | collective-permute-start | bytes 786440 | tf_op jit(solution)/shard_map/ppermute | solution.py:250
  40.9 2.3 %collective-permute-start.16 = (f32[2,128,256]{2,1,0:T(8,128)}, f32[2,128,256]{2,1,0:T(8,128)S(1)}, u32[]{:S(2)}, u32[]{:S(2)}) collective-permute-start(f32[2,128,256]{2,1,0:T(8,128)} %get-tuple-element.142), channel_id=1, source_target_pairs={{0,12},{1,13},{2,14},{3,15},{4,8},{5,9},{6,10},{7,11},{8,4},{9,5},... | collective-permute-start | bytes 786440 | tf_op jit(solution)/shard_map/ppermute | solution.py:250
  43.2 0.0 copy-done.7
  43.2 0.0 copy-done.8
  43.2 0.1 pad_maximum_fusion.1.rest_4_
  43.3 0.0 copy-start.5
  43.3 0.0 collective-permute-done.7.rest_13_
  43.3 1.6 %collective-permute-start.8 = (f32[4,8192]{1,0:T(4,128)S(1)}, f32[4,8192]{1,0:T(4,128)}, u32[]{:S(2)}, u32[]{:S(2)}) collective-permute-start(f32[4,8192]{1,0:T(4,128)S(1)} %pad_maximum_fusion.1.rest_4_), channel_id=1, source_target_pairs={{0,16},{16,0},{1,17},{17,1},{2,18},{18,2},{3,19},{19,3},{4,20},{20... | collective-permute-start | bytes 393224 | tf_op jit(solution)/shard_map/ppermute | solution.py:250
  44.9 0.0 collective-permute-done.14.rest_12_
  44.9 0.0 collective-permute-start.15
  44.9 3.6 %collective-permute-done.8.rest_5_ = f32[4,8192]{1,0:T(4,128)} collective-permute-done((f32[4,8192]{1,0:T(4,128)S(1)}, f32[4,8192]{1,0:T(4,128)}, u32[]{:S(2)}, u32[]{:S(2)}) %collective-permute-start.8) | collective-permute-done | bytes 131104 | tf_op jit(solution)/shard_map/ppermute | solution.py:250
  48.5 7.9 %collective-permute-start.20 = (f32[2,128,256]{2,1,0:T(8,128)}, f32[2,128,256]{2,1,0:T(8,128)S(1)}, u32[]{:S(2)}, u32[]{:S(2)}) collective-permute-start(f32[2,128,256]{2,1,0:T(8,128)} %get-tuple-element.147), channel_id=1, source_target_pairs={{0,6},{1,7},{2,4},{3,5},{4,2},{5,3},{6,0},{7,1},{8,14},{9,15},{10,... | collective-permute-start | bytes 786440 | tf_op jit(solution)/shard_map/ppermute | solution.py:250
  56.4 0.0 collective-permute-done.6.rest_3_
  56.4 2.3 %collective-permute-start.12 = (f32[2,128,256]{2,1,0:T(8,128)}, f32[2,128,256]{2,1,0:T(8,128)S(1)}, u32[]{:S(2)}, u32[]{:S(2)}) collective-permute-start(f32[2,128,256]{2,1,0:T(8,128)} %get-tuple-element.132), channel_id=1, source_target_pairs={{0,11},{1,10},{2,9},{3,8},{4,15},{5,14},{6,13},{7,12},{8,3},{9,2},... | collective-permute-start | bytes 786440 | tf_op jit(solution)/shard_map/ppermute | solution.py:250
  58.7 0.0 collective-permute-done.9.rest_6_
  58.7 0.0 collective-permute-start.10
  58.7 0.0 collective-permute-done.16.rest_11_
  58.7 4.0 %collective-permute-start.17 = (f32[2,128,256]{2,1,0:T(8,128)}, f32[2,128,256]{2,1,0:T(8,128)S(1)}, u32[]{:S(2)}, u32[]{:S(2)}) collective-permute-start(f32[2,128,256]{2,1,0:T(8,128)} %get-tuple-element.143), channel_id=1, source_target_pairs={{0,10},{1,11},{2,8},{3,9},{4,14},{5,15},{6,12},{7,13},{8,2},{9,3},... | collective-permute-start | bytes 786440 | tf_op jit(solution)/shard_map/ppermute | solution.py:250
  62.8 0.8 copy.14.admissible
  63.5 0.0 copy-start.9
  63.5 0.0 copy-done.4
  63.6 0.0 copy-done.6
  63.6 0.0 copy-done.5
  63.6 0.0 copy-done.3
  63.6 0.0 copy-done.2
  63.6 0.0 copy-done.1
  63.6 5.1 %update_factors.1 = (f32[2,512,128]{2,1,0:T(8,128)S(1)}, f32[4,512,128]{2,1,0:T(8,128)S(1)}, f32[2048,512]{1,0:T(8,128)S(1)}) custom-call(f32[2048,512]{1,0:T(8,128)} %front.1, f32[256,256]{1,0:T(8,128)S(1)} %copy-done, s32[1,256]{1,0:T(1,128)S(1)} %bitcast.5, s32[8]{0:T(128)S(1)} %copy-done.2, s32[2]{0:T(128)S(1)} %copy-done.3, ...), custom_call_target="tpu_custom_call" | custom-call | flops 67108864 | bytes 2097152 | tf_op jit(solution)/shard_map/update_factors/pallas_call | solution.py:149
  68.7 0.0 collective-permute-done.15.rest_2_
  68.7 5.4 %collective-permute-start.19 = (f32[2,128,256]{2,1,0:T(8,128)S(1)}, f32[2,128,256]{2,1,0:T(8,128)S(1)}, u32[]{:S(2)}, u32[]{:S(2)}) collective-permute-start(f32[2,128,256]{2,1,0:T(8,128)S(1)} %copy-done.13), channel_id=1, source_target_pairs={{0,5},{1,4},{2,7},{3,6},{4,1},{5,0},{6,3},{7,2},{8,13},{9,12},{10,... | collective-permute-start | bytes 786440 | tf_op jit(solution)/shard_map/ppermute | solution.py:250
  74.1 0.0 collective-permute-done.20.rest_5_
  74.1 0.0 copy-done.12
  74.1 0.0 collective-permute-start.21
  74.1 11.5 %collective-permute-done.12.rest_10_ = f32[2,128,256]{2,1,0:T(8,128)S(1)} collective-permute-done((f32[2,128,256]{2,1,0:T(8,128)}, f32[2,128,256]{2,1,0:T(8,128)S(1)}, u32[]{:S(2)}, u32[]{:S(2)}) %collective-permute-start.12) | collective-permute-done | bytes 262176 | tf_op jit(solution)/shard_map/ppermute | solution.py:250
  85.6 0.7 collective-permute-start.13
  86.3 9.0 %collective-permute-done.10.rest_8_ = f32[2,128,256]{2,1,0:T(8,128)S(1)} collective-permute-done((f32[2,128,256]{2,1,0:T(8,128)}, f32[2,128,256]{2,1,0:T(8,128)S(1)}, u32[]{:S(2)}, u32[]{:S(2)}) %collective-permute-start.10) | collective-permute-done | bytes 262176 | tf_op jit(solution)/shard_map/ppermute | solution.py:250
  95.3 0.0 copy-done.10
  95.3 0.0 collective-permute-start.11
  95.3 6.0 %collective-permute-done.17.rest_9_ = f32[2,128,256]{2,1,0:T(8,128)S(1)} collective-permute-done((f32[2,128,256]{2,1,0:T(8,128)}, f32[2,128,256]{2,1,0:T(8,128)S(1)}, u32[]{:S(2)}, u32[]{:S(2)}) %collective-permute-start.17) | collective-permute-done | bytes 262176 | tf_op jit(solution)/shard_map/ppermute | solution.py:250
  101.3 0.0 collective-permute-start.18
  101.3 0.0 collective-permute-done.19.rest_4_
  101.3 4.4 %collective-permute-done.21.rest_7_ = f32[2,128,256]{2,1,0:T(8,128)S(1)} collective-permute-done((f32[2,128,256]{2,1,0:T(8,128)S(1)}, f32[2,128,256]{2,1,0:T(8,128)S(1)}, u32[]{:S(2)}, u32[]{:S(2)}) %collective-permute-start.21) | collective-permute-done | bytes 262176 | tf_op jit(solution)/shard_map/ppermute | solution.py:250
  105.7 0.0 collective-permute-done.13.rest_1_
  105.7 0.0 collective-permute-done.11.rest_0_
  105.7 6.0 %collective-permute-done.18.rest_3_ = f32[2,128,256]{2,1,0:T(8,128)S(1)} collective-permute-done((f32[2,128,256]{2,1,0:T(8,128)S(1)}, f32[2,128,256]{2,1,0:T(8,128)S(1)}, u32[]{:S(2)}, u32[]{:S(2)}) %collective-permute-start.18) | collective-permute-done | bytes 262176 | tf_op jit(solution)/shard_map/ppermute | solution.py:250
  111.7 4.4 %finish.1 = f32[2048,512]{1,0:T(8,128)} custom-call(s32[1,8]{1,0:T(1,128)} %row_map.1, f32[2048,512]{1,0:T(8,128)S(1)} %get-tuple-element.123.front, f32[2,512,128]{2,1,0:T(8,128)S(1)} %get-tuple-element.124.left, f32[4,512,128]{2,1,0:T(8,128)S(1)} %get-tuple-element.125.right, f32[2,128,256]{2,1,0:T(8,128)S(1)} %collective-permute-done.11.rest_0_, ...), custom_call_target="tpu_custom_call" | custom-call | flops 536870912 | bytes 12582912 | tf_op jit(solution)/shard_map/finish/pallas_call | solution.py:222
  (15 shorter events, 0.0 us)
Async XLA Ops:
  0.0 63.6 %copy-start.3 = (s32[2]{0:T(128)S(1)}, s32[2]{0:T(128)}, u32[]{:S(2)}) copy-start(s32[2]{0:T(128)} %rank_cols) | copy-start | bytes 28
  0.0 63.6 %copy-start.2 = (s32[8]{0:T(128)S(1)}, s32[8]{0:T(128)}, u32[]{:S(2)}) copy-start(s32[8]{0:T(128)} %rank_rows) | copy-start | bytes 100
  0.0 43.2 %copy-start.7 = (f32[2,8192]{1,0:T(2,128)S(1)}, f32[2,8192]{1,0:T(2,128)}, u32[]{:S(2)}) copy-start(f32[2,8192]{1,0:T(2,128)} %param.20) | copy-start | bytes 196612
  0.0 43.2 %copy-start.8 = (f32[2,8192]{1,0:T(2,128)S(1)}, f32[2,8192]{1,0:T(2,128)}, u32[]{:S(2)}) copy-start(f32[2,8192]{1,0:T(2,128)} %param.19) | copy-start | bytes 196612
  0.0 63.6 %copy-start.1 = (s32[256]{0:T(256)S(1)}, s32[256]{0:T(256)}, u32[]{:S(2)}) copy-start(s32[256]{0:T(256)} %param.22) | copy-start | bytes 3076
  0.0 63.6 %copy-start = (f32[256,256]{1,0:T(8,128)S(1)}, f32[256,256]{1,0:T(8,128)}, u32[]{:S(2)}) copy-start(f32[256,256]{1,0:T(8,128)} %dinv.1) | copy-start | bytes 786436
  0.9 14.1 %collective-permute-start.2 = (f32[16,1024]{1,0:T(8,128)S(1)}, f32[16,1024]{1,0:T(8,128)S(1)}, u32[]{:S(2)}, u32[]{:S(2)}) collective-permute-start(f32[16,1024]{1,0:T(8,128)S(1)} %pad_add_fusion), channel_id=1, source_target_pairs={{0,12},{1,13},{2,14},{3,15},{4,8},{5,9},{6,10},{7,11},{8,4},{9,5},... | collective-permute-start | bytes 196616 | tf_op jit(solution)/shard_map/ppermute | solution.py:250
  5.9 9.1 %collective-permute-start.1 = (f32[16,1024]{1,0:T(8,128)S(1)}, f32[16,1024]{1,0:T(8,128)S(1)}, u32[]{:S(2)}, u32[]{:S(2)}) collective-permute-start(f32[16,1024]{1,0:T(8,128)S(1)} %pad_add_fusion), channel_id=1, source_target_pairs={{0,8},{1,9},{2,10},{3,11},{4,12},{5,13},{6,14},{7,15},{8,0},{9,1},... | collective-permute-start | bytes 196616 | tf_op jit(solution)/shard_map/ppermute | solution.py:250
  5.9 9.1 %collective-permute-start = (f32[16,1024]{1,0:T(8,128)S(1)}, f32[16,1024]{1,0:T(8,128)S(1)}, u32[]{:S(2)}, u32[]{:S(2)}) collective-permute-start(f32[16,1024]{1,0:T(8,128)S(1)} %pad_add_fusion), channel_id=1, source_target_pairs={{0,4},{1,5},{2,6},{3,7},{4,0},{5,1},{6,2},{7,3},{8,12},{9,13},{10,... | collective-permute-start | bytes 196616 | tf_op jit(solution)/shard_map/ppermute | solution.py:250
  11.6 11.3 %collective-permute-start.5 = (f32[2,128,256]{2,1,0:T(8,128)}, f32[2,128,256]{2,1,0:T(8,128)S(1)}, u32[]{:S(2)}, u32[]{:S(2)}) collective-permute-start(f32[2,128,256]{2,1,0:T(8,128)} %get-tuple-element.110), channel_id=1, source_target_pairs={{0,15},{1,14},{2,13},{3,12},{4,11},{5,10},{6,9},{7,8},{8,7},{9,6},... | collective-permute-start | bytes 786440 | tf_op jit(solution)/shard_map/ppermute | solution.py:250
  15.0 48.5 %copy-start.4 = (f32[4,16,1024]{2,1,0:T(8,128)}, f32[4,16,1024]{2,1,0:T(8,128)S(1)}, u32[]{:S(2)}) copy-start(f32[4,16,1024]{2,1,0:T(8,128)S(1)} %pad_maximum_fusion.rest_0_) | copy-start | bytes 786436
  15.0 8.5 %collective-permute-start.3 = (f32[4,16,1024]{2,1,0:T(8,128)S(1)}, f32[4,16,1024]{2,1,0:T(8,128)S(1)}, u32[]{:S(2)}, u32[]{:S(2)}) collective-permute-start(f32[4,16,1024]{2,1,0:T(8,128)S(1)} %pad_maximum_fusion.rest_0_), channel_id=1, source_target_pairs={{0,1},{1,0},{2,3},{3,2},{4,5},{5,4},{6,7},{7,6},{8,9},{9,8},{10,11... | collective-permute-start | bytes 786440 | tf_op jit(solution)/shard_map/ppermute | solution.py:250
  16.6 18.1 %collective-permute-start.4 = (f32[4,16,1024]{2,1,0:T(8,128)S(1)}, f32[4,16,1024]{2,1,0:T(8,128)}, u32[]{:S(2)}, u32[]{:S(2)}) collective-permute-start(f32[4,16,1024]{2,1,0:T(8,128)S(1)} %pad_maximum_fusion.rest_0_), channel_id=1, source_target_pairs={{0,2},{1,3},{2,0},{3,1},{4,6},{5,7},{6,4},{7,5},{8,10},{9,11},{10,... | collective-permute-start | bytes 786440 | tf_op jit(solution)/shard_map/ppermute | solution.py:250
  17.2 26.2 %collective-permute-start.7 = (f32[2,128,256]{2,1,0:T(8,128)}, f32[2,128,256]{2,1,0:T(8,128)S(1)}, u32[]{:S(2)}, u32[]{:S(2)}) collective-permute-start(f32[2,128,256]{2,1,0:T(8,128)} %get-tuple-element.116), channel_id=1, source_target_pairs={{0,14},{1,15},{2,12},{3,13},{4,10},{5,11},{6,8},{7,9},{8,6},{9,7},... | collective-permute-start | bytes 786440 | tf_op jit(solution)/shard_map/ppermute | solution.py:250
  18.3 26.6 %collective-permute-start.14 = (f32[2,128,256]{2,1,0:T(8,128)}, f32[2,128,256]{2,1,0:T(8,128)S(1)}, u32[]{:S(2)}, u32[]{:S(2)}) collective-permute-start(f32[2,128,256]{2,1,0:T(8,128)} %get-tuple-element.137), channel_id=1, source_target_pairs={{0,13},{1,12},{2,15},{3,14},{4,9},{5,8},{6,11},{7,10},{8,5},{9,4},... | collective-permute-start | bytes 786440 | tf_op jit(solution)/shard_map/ppermute | solution.py:250
  23.0 33.5 %collective-permute-start.6 = (f32[4,16,1024]{2,1,0:T(8,128)S(1)}, f32[4,16,1024]{2,1,0:T(8,128)}, u32[]{:S(2)}, u32[]{:S(2)}) collective-permute-start(f32[4,16,1024]{2,1,0:T(8,128)S(1)} %pad_maximum_fusion.rest_0_), channel_id=1, source_target_pairs={{0,3},{1,2},{2,1},{3,0},{4,7},{5,6},{6,5},{7,4},{8,11},{9,10},{10,... | collective-permute-start | bytes 786440 | tf_op jit(solution)/shard_map/ppermute | solution.py:250
  23.6 40.0 %copy-start.6 = (f32[4,16,1024]{2,1,0:T(8,128)}, f32[4,16,1024]{2,1,0:T(8,128)S(1)}, u32[]{:S(2)}) copy-start(f32[4,16,1024]{2,1,0:T(8,128)S(1)} %collective-permute-done.3.rest_1_) | copy-start | bytes 786436
  34.8 24.0 %collective-permute-start.9 = (f32[2,128,256]{2,1,0:T(8,128)}, f32[2,128,256]{2,1,0:T(8,128)S(1)}, u32[]{:S(2)}, u32[]{:S(2)}) collective-permute-start(f32[2,128,256]{2,1,0:T(8,128)} %get-tuple-element.128), channel_id=1, source_target_pairs={{0,7},{1,6},{2,5},{3,4},{4,3},{5,2},{6,1},{7,0},{8,15},{9,14},{10,... | collective-permute-start | bytes 786440 | tf_op jit(solution)/shard_map/ppermute | solution.py:250
  40.9 17.8 %collective-permute-start.16 = (f32[2,128,256]{2,1,0:T(8,128)}, f32[2,128,256]{2,1,0:T(8,128)S(1)}, u32[]{:S(2)}, u32[]{:S(2)}) collective-permute-start(f32[2,128,256]{2,1,0:T(8,128)} %get-tuple-element.142), channel_id=1, source_target_pairs={{0,12},{1,13},{2,14},{3,15},{4,8},{5,9},{6,10},{7,11},{8,4},{9,5},... | collective-permute-start | bytes 786440 | tf_op jit(solution)/shard_map/ppermute | solution.py:250
  43.3 20.3 %copy-start.5 = (f32[4,8192]{1,0:T(4,128)}, f32[4,8192]{1,0:T(4,128)S(1)}, u32[]{:S(2)}) copy-start(f32[4,8192]{1,0:T(4,128)S(1)} %pad_maximum_fusion.1.rest_4_) | copy-start | bytes 393220
  43.3 5.2 %collective-permute-start.8 = (f32[4,8192]{1,0:T(4,128)S(1)}, f32[4,8192]{1,0:T(4,128)}, u32[]{:S(2)}, u32[]{:S(2)}) collective-permute-start(f32[4,8192]{1,0:T(4,128)S(1)} %pad_maximum_fusion.1.rest_4_), channel_id=1, source_target_pairs={{0,16},{16,0},{1,17},{17,1},{2,18},{18,2},{3,19},{19,3},{4,20},{20... | collective-permute-start | bytes 393224 | tf_op jit(solution)/shard_map/ppermute | solution.py:250
  44.9 23.8 %collective-permute-start.15 = (f32[2,128,256]{2,1,0:T(8,128)}, f32[2,128,256]{2,1,0:T(8,128)S(1)}, u32[]{:S(2)}, u32[]{:S(2)}) collective-permute-start(f32[2,128,256]{2,1,0:T(8,128)} %get-tuple-element.138), channel_id=1, source_target_pairs={{0,3},{1,2},{2,1},{3,0},{4,7},{5,6},{6,5},{7,4},{8,11},{9,10},{10,... | collective-permute-start | bytes 786440 | tf_op jit(solution)/shard_map/ppermute | solution.py:250
  48.5 25.6 %collective-permute-start.20 = (f32[2,128,256]{2,1,0:T(8,128)}, f32[2,128,256]{2,1,0:T(8,128)S(1)}, u32[]{:S(2)}, u32[]{:S(2)}) collective-permute-start(f32[2,128,256]{2,1,0:T(8,128)} %get-tuple-element.147), channel_id=1, source_target_pairs={{0,6},{1,7},{2,4},{3,5},{4,2},{5,3},{6,0},{7,1},{8,14},{9,15},{10,... | collective-permute-start | bytes 786440 | tf_op jit(solution)/shard_map/ppermute | solution.py:250
  56.4 29.2 %collective-permute-start.12 = (f32[2,128,256]{2,1,0:T(8,128)}, f32[2,128,256]{2,1,0:T(8,128)S(1)}, u32[]{:S(2)}, u32[]{:S(2)}) collective-permute-start(f32[2,128,256]{2,1,0:T(8,128)} %get-tuple-element.132), channel_id=1, source_target_pairs={{0,11},{1,10},{2,9},{3,8},{4,15},{5,14},{6,13},{7,12},{8,3},{9,2},... | collective-permute-start | bytes 786440 | tf_op jit(solution)/shard_map/ppermute | solution.py:250
  58.7 36.6 %collective-permute-start.10 = (f32[2,128,256]{2,1,0:T(8,128)}, f32[2,128,256]{2,1,0:T(8,128)S(1)}, u32[]{:S(2)}, u32[]{:S(2)}) collective-permute-start(f32[2,128,256]{2,1,0:T(8,128)} %get-tuple-element.129), channel_id=1, source_target_pairs={{0,9},{1,8},{2,11},{3,10},{4,13},{5,12},{6,15},{7,14},{8,1},{9,0},... | collective-permute-start | bytes 786440 | tf_op jit(solution)/shard_map/ppermute | solution.py:250
  58.7 42.5 %collective-permute-start.17 = (f32[2,128,256]{2,1,0:T(8,128)}, f32[2,128,256]{2,1,0:T(8,128)S(1)}, u32[]{:S(2)}, u32[]{:S(2)}) collective-permute-start(f32[2,128,256]{2,1,0:T(8,128)} %get-tuple-element.143), channel_id=1, source_target_pairs={{0,10},{1,11},{2,8},{3,9},{4,14},{5,15},{6,12},{7,13},{8,2},{9,3},... | collective-permute-start | bytes 786440 | tf_op jit(solution)/shard_map/ppermute | solution.py:250
  63.5 5.2 %copy-start.13 = (f32[2,128,256]{2,1,0:T(8,128)S(1)}, f32[2,128,256]{2,1,0:T(8,128)}, u32[]{:S(2)}) copy-start(f32[2,128,256]{2,1,0:T(8,128)} %get-tuple-element.145) | copy-start | bytes 786436
  63.5 10.6 %copy-start.12 = (f32[2,128,256]{2,1,0:T(8,128)S(1)}, f32[2,128,256]{2,1,0:T(8,128)}, u32[]{:S(2)}) copy-start(f32[2,128,256]{2,1,0:T(8,128)} %get-tuple-element.150) | copy-start | bytes 786436
  63.5 22.1 %copy-start.11 = (f32[2,128,256]{2,1,0:T(8,128)S(1)}, f32[2,128,256]{2,1,0:T(8,128)}, u32[]{:S(2)}) copy-start(f32[2,128,256]{2,1,0:T(8,128)} %get-tuple-element.133) | copy-start | bytes 786436
  63.5 31.8 %copy-start.10 = (f32[2,128,256]{2,1,0:T(8,128)S(1)}, f32[2,128,256]{2,1,0:T(8,128)}, u32[]{:S(2)}) copy-start(f32[2,128,256]{2,1,0:T(8,128)} %get-tuple-element.130) | copy-start | bytes 786436
  63.5 37.7 %copy-start.9 = (f32[2,128,256]{2,1,0:T(8,128)S(1)}, f32[2,128,256]{2,1,0:T(8,128)}, u32[]{:S(2)}) copy-start(f32[2,128,256]{2,1,0:T(8,128)} %get-tuple-element.144) | copy-start | bytes 786436
  68.7 32.6 %collective-permute-start.19 = (f32[2,128,256]{2,1,0:T(8,128)S(1)}, f32[2,128,256]{2,1,0:T(8,128)S(1)}, u32[]{:S(2)}, u32[]{:S(2)}) collective-permute-start(f32[2,128,256]{2,1,0:T(8,128)S(1)} %copy-done.13), channel_id=1, source_target_pairs={{0,5},{1,4},{2,7},{3,6},{4,1},{5,0},{6,3},{7,2},{8,13},{9,12},{10,... | collective-permute-start | bytes 786440 | tf_op jit(solution)/shard_map/ppermute | solution.py:250
  74.1 31.6 %collective-permute-start.21 = (f32[2,128,256]{2,1,0:T(8,128)S(1)}, f32[2,128,256]{2,1,0:T(8,128)S(1)}, u32[]{:S(2)}, u32[]{:S(2)}) collective-permute-start(f32[2,128,256]{2,1,0:T(8,128)S(1)} %copy-done.12), channel_id=1, source_target_pairs={{0,8},{1,9},{2,10},{3,11},{4,12},{5,13},{6,14},{7,15},{8,0},{9,1},... | collective-permute-start | bytes 786440 | tf_op jit(solution)/shard_map/ppermute | solution.py:250
  85.6 20.0 %collective-permute-start.13 = (f32[2,128,256]{2,1,0:T(8,128)S(1)}, f32[2,128,256]{2,1,0:T(8,128)S(1)}, u32[]{:S(2)}, u32[]{:S(2)}) collective-permute-start(f32[2,128,256]{2,1,0:T(8,128)S(1)} %copy-done.11), channel_id=1, source_target_pairs={{0,2},{1,3},{2,0},{3,1},{4,6},{5,7},{6,4},{7,5},{8,10},{9,11},{10,... | collective-permute-start | bytes 786440 | tf_op jit(solution)/shard_map/ppermute | solution.py:250
  95.3 10.4 %collective-permute-start.11 = (f32[2,128,256]{2,1,0:T(8,128)S(1)}, f32[2,128,256]{2,1,0:T(8,128)S(1)}, u32[]{:S(2)}, u32[]{:S(2)}) collective-permute-start(f32[2,128,256]{2,1,0:T(8,128)S(1)} %copy-done.10), channel_id=1, source_target_pairs={{0,1},{1,0},{2,3},{3,2},{4,5},{5,4},{6,7},{7,6},{8,9},{9,8},{10,11... | collective-permute-start | bytes 786440 | tf_op jit(solution)/shard_map/ppermute | solution.py:250
  101.3 10.4 %collective-permute-start.18 = (f32[2,128,256]{2,1,0:T(8,128)S(1)}, f32[2,128,256]{2,1,0:T(8,128)S(1)}, u32[]{:S(2)}, u32[]{:S(2)}) collective-permute-start(f32[2,128,256]{2,1,0:T(8,128)S(1)} %copy-done.9), channel_id=1, source_target_pairs={{0,4},{1,5},{2,6},{3,7},{4,0},{5,1},{6,2},{7,3},{8,12},{9,13},{10,... | collective-permute-start | bytes 786440 | tf_op jit(solution)/shard_map/ppermute | solution.py:250

commit v9 on v7

--- a/solution.py
+++ b/solution.py
@@ -25,56 +25,57 @@
     return pltpu.with_memory_space_constraint(array, pltpu.HBM)
 
 
-def place_kernel(tiles, tile, col_tiles, col_map, child, *rest):
-    count = tiles // col_tiles
-    pieces = rest[:count]
-    inverse, held, in_sem, out_sem = rest[count:]
+def place_kernel(members, tiles, tile, col_tiles, col_map, child, *rest):
+    pieces = rest[: len(members)]
+    inverse, held, in_sem, out_sem = rest[len(members) :]
     me = group_index()
 
-    def fetch(m, j):
-        b = inverse[(me ^ m) * col_tiles + j]
+    def fetch(n, j):
+        b = inverse[(me ^ members[n]) * col_tiles + j]
         span = pl.ds(pl.multiple_of(b * tile, tile), tile)
-        return pltpu.make_async_copy(child.at[:, span], held.at[m, j], in_sem.at[m, j])
-
-    def store(m):
-        return pltpu.make_async_copy(held.at[m], pieces[m], out_sem.at[m])
+        return pltpu.make_async_copy(child.at[:, span], held.at[n, j], in_sem.at[n, j])
+
+    def store(n):
+        return pltpu.make_async_copy(held.at[n], pieces[n], out_sem.at[n])
 
     for b in range(tiles):
         inverse[col_map[b]] = b
-    for m in reversed(range(count)):
+    for n in range(len(members)):
         for j in range(col_tiles):
-            fetch(m, j).start()
-    for m in reversed(range(count)):
+            fetch(n, j).start()
+    for n in range(len(members)):
         for j in range(col_tiles):
-            fetch(m, j).wait()
-        store(m).start()
-    for m in reversed(range(count)):
-        store(m).wait()
+            fetch(n, j).wait()
+        store(n).start()
+    for n in range(len(members)):
+        store(n).wait()
 
 
 def in_vmem(array):
     return pltpu.with_memory_space_constraint(array, pltpu.VMEM)
 
 
-def place(child, col_map, tile, devices):
+def place(child, col_map, tile, devices, members):
     rows = child.shape[0]
     tiles = col_map.shape[0]
     col_tiles = tiles // devices
-    return pl.pallas_call(
-        functools.partial(place_kernel, tiles, tile, col_tiles),
-        out_shape=[pltpu.HBM((col_tiles, rows, tile), child.dtype)] * devices,
+    count = len(members)
+    pieces = pl.pallas_call(
+        functools.partial(place_kernel, members, tiles, tile, col_tiles),
+        out_shape=[pltpu.HBM((col_tiles, rows, tile), child.dtype)] * count,
         in_specs=[pl.BlockSpec(memory_space=pltpu.SMEM), pl.BlockSpec(memory_space=pltpu.HBM)],
-        out_specs=[pl.BlockSpec(memory_space=pltpu.HBM)] * devices,
+        out_specs=[pl.BlockSpec(memory_space=pltpu.HBM)] * count,
         scratch_shapes=[
             pltpu.SMEM((tiles,), jnp.int32),
-            pltpu.VMEM((devices, col_tiles, rows, tile), child.dtype),
-            pltpu.SemaphoreType.DMA((devices, col_tiles)),
-            pltpu.SemaphoreType.DMA((devices,)),
+            pltpu.VMEM((count, col_tiles, rows, tile), child.dtype),
+            pltpu.SemaphoreType.DMA((count, col_tiles)),
+            pltpu.SemaphoreType.DMA((count,)),
         ],
         compiler_params=pltpu.CompilerParams(vmem_limit_bytes=8 * MIB),
-        cost_estimate=pl.CostEstimate(flops=0, bytes_accessed=2 * child.size * 4, transcendentals=0),
+        cost_estimate=pl.CostEstimate(flops=0, bytes_accessed=8 * count * col_tiles * rows * tile, transcendentals=0),
         name="place_child",
     )(in_hbm(col_map), in_hbm(child))
+    return dict(zip(members, pieces))
 
 
 def dot(a, b, contract=((1,), (0,))):
@@ -275,12 +276,10 @@
     mine = jnp.pad(x_fac, ((0, row_tiles), (0, 0))) + jnp.pad(w_fac, ((row_tiles, 0), (0, 0)))
     mine, child = lax.optimization_barrier((mine, child))
     line = [sender.send(mine, GROUP, m) for m in range(NEAR, devices, NEAR)]
-    pieces = place(child, col_map, tile, devices)
-    pieces, v_fac, z_fac, rank_rows, rank_cols, admissible = lax.optimization_barrier(
-        (pieces, v_fac, z_fac, rank_rows, rank_cols, admissible)
-    )
-
-    pieces = list(pieces)
+    early = [devices - 1, devices - 2, devices - 3]
+    pieces = place(child, col_map, tile, devices, early)
+    pieces, child, v_fac, z_fac = lax.optimization_barrier((pieces, child, v_fac, z_fac))
+    pieces.update(place(child, col_map, tile, devices, list(reversed(range(devices - 3)))))
     half = devices // 2
     crossing = list(reversed(range(half, devices)))
     local = [m for pair in zip(reversed(range(NEAR, half)), [3, 2, 1] + [None] * half) for m in pair if m]

time: 110 us -> 108 us (0.982)
  waiting for transfers between devices: 39.2 us -> 34.2 us
  local copies, waits for them, and re-layouts: 0.81 us -> 2.88 us
  Pallas kernels: 14.5 us -> 16.4 us
    ppermute x22, waiting for transfers between devices: 39.2 us -> 34.2 us  [send(): lax.ppermute(array, axes, [(d, d ^ m) for d in range(size)])]
    unnamed x28 -> x37, local copies, waits for them, and re-layouts: 0.06 us -> 2.88 us
    pallas_call x1 -> x2, Pallas kernels: 5.08 us -> 6.85 us  [place(): pl.pallas_call(functools.partial(place_kernel, members, tiles, tile, col_...]
  transfers between devices with their start and end apart: 22 -> 22, of which waited for: 7 -> 6; matrix products, arithmetic and copies ran while one was open for 1% -> 1% of each run, Pallas kernels for 9% -> 11%
where the time goes in v9:
time: 108 us
  starting transfers between devices  53.3 us (49%)
  waiting for transfers between devices  34.2 us (32%)
  Pallas kernels  16.4 us (15%)
  local copies, waits for them, and re-layouts  2.88 us (3%)
    ppermute x22, starting transfers between devices, send(): lax.ppermute(array, axes, [(d, d ^ m) for d in range(size)])  53.3 us
    ppermute x22, waiting for transfers between devices, send(): lax.ppermute(array, axes, [(d, d ^ m) for d in range(size)])  34.2 us
    pallas_call x2, Pallas kernels, place(): pl.pallas_call(functools.partial(place_kernel, members, tiles, tile, col_...  6.85 us
    pallas_call x1, Pallas kernels, factors(): pl.pallas_call(functools.partial(factor_kernel, len(xw), len(vz), col_til...  5.06 us
    pallas_call x1, Pallas kernels, finish(): pl.pallas_call(functools.partial(finish_kernel, len(pieces), tile), out_s...  4.44 us
    unnamed x37, local copies, waits for them, and re-layouts  2.88 us
  transfers between devices with their start and end apart: 22, of which 6 were waited for; matrix products, arithmetic and copies ran while one was open for 1% of the time, Pallas kernels for 11%

profile of v9, /device:TPU:0, one launch (start us, length us, event | category | flops | bytes accessed | tf_op | source)
XLA Modules:
  0.0 107.8 jit_solution(11011503703092812866)
XLA Ops:
  0.0 0.8 pad_add_fusion
  0.8 0.0 copy-start
  0.8 0.0 copy-start.1
  0.8 0.0 copy-start.2
  0.8 0.0 copy-start.3
  0.8 5.1 %collective-permute-start.2 = (f32[16,1024]{1,0:T(8,128)S(1)}, f32[16,1024]{1,0:T(8,128)S(1)}, u32[]{:S(2)}, u32[]{:S(2)}) collective-permute-start(f32[16,1024]{1,0:T(8,128)S(1)} %pad_add_fusion), channel_id=1, source_target_pairs={{0,12},{1,13},{2,14},{3,15},{4,8},{5,9},{6,10},{7,11},{8,4},{9,5},... | collective-permute-start | bytes 196616 | tf_op jit(solution)/shard_map/ppermute | solution.py:251
  6.0 0.0 collective-permute-start.1
  6.0 0.6 collective-permute-start
  6.6 2.7 %place_child.2 = (f32[2,128,256]{2,1,0:T(8,128)}, f32[2,128,256]{2,1,0:T(8,128)}, f32[2,128,256]{2,1,0:T(8,128)}) custom-call(s32[32]{0:T(128)} %col_map.3, f32[128,8192]{1,0:T(8,128)} %child.1), custom_call_target="tpu_custom_call" | custom-call | bytes 1572864 | tf_op jit(solution)/shard_map/place_child/pallas_call | solution.py:63
  9.3 0.0 copy-start.17
  9.3 3.3 %collective-permute-start.5 = (f32[2,128,256]{2,1,0:T(8,128)}, f32[2,128,256]{2,1,0:T(8,128)S(1)}, u32[]{:S(2)}, u32[]{:S(2)}) collective-permute-start(f32[2,128,256]{2,1,0:T(8,128)} %get-tuple-element.80), channel_id=1, source_target_pairs={{0,15},{1,14},{2,13},{3,12},{4,11},{5,10},{6,9},{7,8},{8,7},{9,6},... | collective-permute-start | bytes 786440 | tf_op jit(solution)/shard_map/ppermute | solution.py:251
  12.7 0.0 collective-permute-done.2
  12.7 0.0 collective-permute-done.1
  12.7 0.0 collective-permute-done
  12.7 0.0 copy-start.4
  12.7 1.6 %collective-permute-start.3 = (f32[4,16,1024]{2,1,0:T(8,128)S(1)}, f32[4,16,1024]{2,1,0:T(8,128)S(1)}, u32[]{:S(2)}, u32[]{:S(2)}) collective-permute-start(f32[4,16,1024]{2,1,0:T(8,128)S(1)} %pad_maximum_fusion.rest_0_), channel_id=1, source_target_pairs={{0,1},{1,0},{2,3},{3,2},{4,5},{5,4},{6,7},{7,6},{8,9},{9,8},{10,11... | collective-permute-start | bytes 786440 | tf_op jit(solution)/shard_map/ppermute | solution.py:251
  14.3 0.5 collective-permute-start.4
  14.8 1.2 %collective-permute-start.7 = (f32[2,128,256]{2,1,0:T(8,128)}, f32[2,128,256]{2,1,0:T(8,128)S(1)}, u32[]{:S(2)}, u32[]{:S(2)}) collective-permute-start(f32[2,128,256]{2,1,0:T(8,128)} %get-tuple-element.86), channel_id=1, source_target_pairs={{0,14},{1,15},{2,12},{3,13},{4,10},{5,11},{6,8},{7,9},{8,6},{9,7},... | collective-permute-start | bytes 786440 | tf_op jit(solution)/shard_map/ppermute | solution.py:251
  16.0 4.1 %place_child.3 = (f32[2,128,256]{2,1,0:T(8,128)}, f32[2,128,256]{2,1,0:T(8,128)}, f32[2,128,256]{2,1,0:T(8,128)}, f32[2,128,256]{2,1,0:T(8,128)}, f32[2,128,256]...) custom-call(s32[32]{0:T(128)} %col_map.3, ...), custom_call_target="tpu_custom_call" | custom-call | bytes 6815744 | tf_op jit(solution)/shard_map/place_child/pallas_call | solution.py:63
  20.1 0.0 copy-done.17
  20.2 2.8 %collective-permute-start.13 = (f32[2,128,256]{2,1,0:T(8,128)S(1)}, f32[2,128,256]{2,1,0:T(8,128)S(1)}, u32[]{:S(2)}, u32[]{:S(2)}) collective-permute-start(f32[2,128,256]{2,1,0:T(8,128)S(1)} %copy-done.17), channel_id=1, source_target_pairs={{0,13},{1,12},{2,15},{3,14},{4,9},{5,8},{6,11},{7,10},{8,5},{9,4},... | collective-permute-start | bytes 786440 | tf_op jit(solution)/shard_map/ppermute | solution.py:251
  22.9 0.0 collective-permute-done.5.rest_14_
  22.9 1.1 %collective-permute-start.6 = (f32[4,16,1024]{2,1,0:T(8,128)S(1)}, f32[4,16,1024]{2,1,0:T(8,128)S(1)}, u32[]{:S(2)}, u32[]{:S(2)}) collective-permute-start(f32[4,16,1024]{2,1,0:T(8,128)S(1)} %pad_maximum_fusion.rest_0_), channel_id=1, source_target_pairs={{0,3},{1,2},{2,1},{3,0},{4,7},{5,6},{6,5},{7,4},{8,11},{9,10},{10,... | collective-permute-start | bytes 786440 | tf_op jit(solution)/shard_map/ppermute | solution.py:251
  24.1 0.0 collective-permute-done.3.rest_1_
  24.1 8.2 %collective-permute-done.4.rest_2_ = f32[4,16,1024]{2,1,0:T(8,128)S(1)} collective-permute-done((f32[4,16,1024]{2,1,0:T(8,128)S(1)}, f32[4,16,1024]{2,1,0:T(8,128)S(1)}, u32[]{:S(2)}, u32[]{:S(2)}) %collective-permute-start.4) | collective-permute-done | bytes 262176 | tf_op jit(solution)/shard_map/ppermute | solution.py:251
  32.3 0.7 copy-done.7
  33.0 6.2 %collective-permute-start.18 = (f32[2,128,256]{2,1,0:T(8,128)}, f32[2,128,256]{2,1,0:T(8,128)S(1)}, u32[]{:S(2)}, u32[]{:S(2)}) collective-permute-start(f32[2,128,256]{2,1,0:T(8,128)} %get-tuple-element.116), channel_id=1, source_target_pairs={{0,7},{1,6},{2,5},{3,4},{4,3},{5,2},{6,1},{7,0},{8,15},{9,14},{10,... | collective-permute-start | bytes 786440 | tf_op jit(solution)/shard_map/ppermute | solution.py:251
  39.3 2.3 %collective-permute-start.11 = (f32[2,128,256]{2,1,0:T(8,128)}, f32[2,128,256]{2,1,0:T(8,128)S(1)}, u32[]{:S(2)}, u32[]{:S(2)}) collective-permute-start(f32[2,128,256]{2,1,0:T(8,128)} %get-tuple-element.101), channel_id=1, source_target_pairs={{0,12},{1,13},{2,14},{3,15},{4,8},{5,9},{6,10},{7,11},{8,4},{9,5},... | collective-permute-start | bytes 786440 | tf_op jit(solution)/shard_map/ppermute | solution.py:251
  41.6 0.0 copy-done.10
  41.6 0.0 copy-done.11
  41.6 0.1 pad_maximum_fusion.1.rest_4_
  41.6 0.0 copy-start.5
  41.6 0.0 collective-permute-done.7.rest_13_
  41.7 1.6 %collective-permute-start.8 = (f32[4,8192]{1,0:T(4,128)S(1)}, f32[4,8192]{1,0:T(4,128)S(1)}, u32[]{:S(2)}, u32[]{:S(2)}) collective-permute-start(f32[4,8192]{1,0:T(4,128)S(1)} %pad_maximum_fusion.1.rest_4_), channel_id=1, source_target_pairs={{0,16},{16,0},{1,17},{17,1},{2,18},{18,2},{3,19},{19,3},{4,20},{20... | collective-permute-start | bytes 393224 | tf_op jit(solution)/shard_map/ppermute | solution.py:251
  43.2 0.0 collective-permute-done.13.rest_12_
  43.2 0.0 collective-permute-start.14
  43.3 3.5 %collective-permute-done.8.rest_5_ = f32[4,8192]{1,0:T(4,128)S(1)} collective-permute-done((f32[4,8192]{1,0:T(4,128)S(1)}, f32[4,8192]{1,0:T(4,128)S(1)}, u32[]{:S(2)}, u32[]{:S(2)}) %collective-permute-start.8) | collective-permute-done | bytes 131104 | tf_op jit(solution)/shard_map/ppermute | solution.py:251
  46.7 0.7 copy-done.9
  47.4 2.7 %collective-permute-start.17 = (f32[2,128,256]{2,1,0:T(8,128)}, f32[2,128,256]{2,1,0:T(8,128)S(1)}, u32[]{:S(2)}, u32[]{:S(2)}) collective-permute-start(f32[2,128,256]{2,1,0:T(8,128)} %get-tuple-element.113), channel_id=1, source_target_pairs={{0,6},{1,7},{2,4},{3,5},{4,2},{5,3},{6,0},{7,1},{8,14},{9,15},{10,... | collective-permute-start | bytes 786440 | tf_op jit(solution)/shard_map/ppermute | solution.py:251
  50.1 0.0 collective-permute-done.6.rest_3_
  50.1 0.7 copy-done.8
  50.8 6.8 %collective-permute-start.9 = (f32[2,128,256]{2,1,0:T(8,128)}, f32[2,128,256]{2,1,0:T(8,128)S(1)}, u32[]{:S(2)}, u32[]{:S(2)}) collective-permute-start(f32[2,128,256]{2,1,0:T(8,128)} %get-tuple-element.97), channel_id=1, source_target_pairs={{0,11},{1,10},{2,9},{3,8},{4,15},{5,14},{6,13},{7,12},{8,3},{9,2},... | collective-permute-start | bytes 786440 | tf_op jit(solution)/shard_map/ppermute | solution.py:251
  57.6 0.0 collective-permute-done.18.rest_6_
  57.6 0.0 collective-permute-start.19
  57.6 0.0 collective-permute-done.11.rest_11_
  57.6 0.3 collective-permute-start.12
  58.0 0.8 copy.14.admissible
  58.8 5.1 %update_factors.1 = (f32[2,512,128]{2,1,0:T(8,128)S(1)}, f32[4,512,128]{2,1,0:T(8,128)S(1)}, f32[2048,512]{1,0:T(8,128)S(1)}) custom-call(f32[2048,512]{1,0:T(8,128)} %front.1, f32[256,256]{1,0:T(8,128)S(1)} %copy-done, s32[1,256]{1,0:T(1,128)S(1)} %bitcast.5, s32[8]{0:T(128)S(1)} %copy-done.2, s32[2]{0:T(128)S(1)} %copy-done.3, ...), custom_call_target="tpu_custom_call" | custom-call | flops 67108864 | bytes 2097152 | tf_op jit(solution)/shard_map/update_factors/pallas_call | solution.py:150
  63.9 0.0 collective-permute-done.14.rest_2_
  63.9 12.5 %collective-permute-start.16 = (f32[2,128,256]{2,1,0:T(8,128)S(1)}, f32[2,128,256]{2,1,0:T(8,128)S(1)}, u32[]{:S(2)}, u32[]{:S(2)}) collective-permute-start(f32[2,128,256]{2,1,0:T(8,128)S(1)} %copy-done.16), channel_id=1, source_target_pairs={{0,5},{1,4},{2,7},{3,6},{4,1},{5,0},{6,3},{7,2},{8,13},{9,12},{10,... | collective-permute-start | bytes 786440 | tf_op jit(solution)/shard_map/ppermute | solution.py:251
  76.4 0.0 collective-permute-done.17.rest_5_
  76.4 0.0 collective-permute-start.21
  76.4 0.0 collective-permute-done.9.rest_10_
  76.4 2.1 %collective-permute-start.10 = (f32[2,128,256]{2,1,0:T(8,128)S(1)}, f32[2,128,256]{2,1,0:T(8,128)S(1)}, u32[]{:S(2)}, u32[]{:S(2)}) collective-permute-start(f32[2,128,256]{2,1,0:T(8,128)S(1)} %copy-done.14), channel_id=1, source_target_pairs={{0,1},{1,0},{2,3},{3,2},{4,5},{5,4},{6,7},{7,6},{8,9},{9,8},{10,11... | collective-permute-start | bytes 786440 | tf_op jit(solution)/shard_map/ppermute | solution.py:251
  78.5 3.4 %collective-permute-done.19.rest_9_ = f32[2,128,256]{2,1,0:T(8,128)S(1)} collective-permute-done((f32[2,128,256]{2,1,0:T(8,128)}, f32[2,128,256]{2,1,0:T(8,128)S(1)}, u32[]{:S(2)}, u32[]{:S(2)}) %collective-permute-start.19) | collective-permute-done | bytes 262176 | tf_op jit(solution)/shard_map/ppermute | solution.py:251
  81.9 0.0 collective-permute-start.20
  81.9 0.0 collective-permute-done.12.rest_1_
  81.9 2.4 %collective-permute-start.15 = (f32[2,128,256]{2,1,0:T(8,128)S(1)}, f32[2,128,256]{2,1,0:T(8,128)S(1)}, u32[]{:S(2)}, u32[]{:S(2)}) collective-permute-start(f32[2,128,256]{2,1,0:T(8,128)S(1)} %copy-done.12), channel_id=1, source_target_pairs={{0,4},{1,5},{2,6},{3,7},{4,0},{5,1},{6,2},{7,3},{8,12},{9,13},{10,... | collective-permute-start | bytes 786440 | tf_op jit(solution)/shard_map/ppermute | solution.py:251
  84.4 5.3 %collective-permute-done.16.rest_4_ = f32[2,128,256]{2,1,0:T(8,128)S(1)} collective-permute-done((f32[2,128,256]{2,1,0:T(8,128)S(1)}, f32[2,128,256]{2,1,0:T(8,128)S(1)}, u32[]{:S(2)}, u32[]{:S(2)}) %collective-permute-start.16) | collective-permute-done | bytes 262176 | tf_op jit(solution)/shard_map/ppermute | solution.py:251
  89.7 8.8 %collective-permute-done.21.rest_8_ = f32[2,128,256]{2,1,0:T(8,128)S(1)} collective-permute-done((f32[2,128,256]{2,1,0:T(8,128)S(1)}, f32[2,128,256]{2,1,0:T(8,128)S(1)}, u32[]{:S(2)}, u32[]{:S(2)}) %collective-permute-start.21) | collective-permute-done | bytes 262176 | tf_op jit(solution)/shard_map/ppermute | solution.py:251
  98.5 0.0 collective-permute-done.10.rest_0_
  98.5 4.9 %collective-permute-done.20.rest_7_ = f32[2,128,256]{2,1,0:T(8,128)S(1)} collective-permute-done((f32[2,128,256]{2,1,0:T(8,128)S(1)}, f32[2,128,256]{2,1,0:T(8,128)S(1)}, u32[]{:S(2)}, u32[]{:S(2)}) %collective-permute-start.20) | collective-permute-done | bytes 262176 | tf_op jit(solution)/shard_map/ppermute | solution.py:251
  103.4 0.0 collective-permute-done.15.rest_3_
  103.4 4.4 %finish.1 = f32[2048,512]{1,0:T(8,128)} custom-call(s32[1,8]{1,0:T(1,128)} %row_map.1, f32[2048,512]{1,0:T(8,128)S(1)} %get-tuple-element.93.front, f32[2,512,128]{2,1,0:T(8,128)S(1)} %get-tuple-element.94.left, f32[4,512,128]{2,1,0:T(8,128)S(1)} %get-tuple-element.95.right, f32[2,128,256]{2,1,0:T(8,128)S(1)} %collective-permute-done.10.rest_0_, ...), custom_call_target="tpu_custom_call" | custom-call | flops 536870912 | bytes 12582912 | tf_op jit(solution)/shard_map/finish/pallas_call | solution.py:223
  (24 shorter events, 0.1 us)
Async XLA Ops:
  0.8 40.8 %copy-start.10 = (f32[2,8192]{1,0:T(2,128)S(1)}, f32[2,8192]{1,0:T(2,128)}, u32[]{:S(2)}) copy-start(f32[2,8192]{1,0:T(2,128)} %param.20) | copy-start | bytes 196612
  0.8 40.8 %copy-start.11 = (f32[2,8192]{1,0:T(2,128)S(1)}, f32[2,8192]{1,0:T(2,128)}, u32[]{:S(2)}) copy-start(f32[2,8192]{1,0:T(2,128)} %param.19) | copy-start | bytes 196612
  0.8 58.0 %copy-start = (f32[256,256]{1,0:T(8,128)S(1)}, f32[256,256]{1,0:T(8,128)}, u32[]{:S(2)}) copy-start(f32[256,256]{1,0:T(8,128)} %dinv.1) | copy-start | bytes 786436
  0.8 58.0 %copy-start.1 = (s32[256]{0:T(256)S(1)}, s32[256]{0:T(256)}, u32[]{:S(2)}) copy-start(s32[256]{0:T(256)} %param.22) | copy-start | bytes 3076
  0.8 58.0 %copy-start.2 = (s32[8]{0:T(128)S(1)}, s32[8]{0:T(128)}, u32[]{:S(2)}) copy-start(s32[8]{0:T(128)} %rank_rows.1) | copy-start | bytes 100
  0.8 58.0 %copy-start.3 = (s32[2]{0:T(128)S(1)}, s32[2]{0:T(128)}, u32[]{:S(2)}) copy-start(s32[2]{0:T(128)} %rank_cols.1) | copy-start | bytes 28
  0.8 11.8 %collective-permute-start.2 = (f32[16,1024]{1,0:T(8,128)S(1)}, f32[16,1024]{1,0:T(8,128)S(1)}, u32[]{:S(2)}, u32[]{:S(2)}) collective-permute-start(f32[16,1024]{1,0:T(8,128)S(1)} %pad_add_fusion), channel_id=1, source_target_pairs={{0,12},{1,13},{2,14},{3,15},{4,8},{5,9},{6,10},{7,11},{8,4},{9,5},... | collective-permute-start | bytes 196616 | tf_op jit(solution)/shard_map/ppermute | solution.py:251
  6.0 6.7 %collective-permute-start.1 = (f32[16,1024]{1,0:T(8,128)S(1)}, f32[16,1024]{1,0:T(8,128)S(1)}, u32[]{:S(2)}, u32[]{:S(2)}) collective-permute-start(f32[16,1024]{1,0:T(8,128)S(1)} %pad_add_fusion), channel_id=1, source_target_pairs={{0,8},{1,9},{2,10},{3,11},{4,12},{5,13},{6,14},{7,15},{8,0},{9,1},... | collective-permute-start | bytes 196616 | tf_op jit(solution)/shard_map/ppermute | solution.py:251
  6.0 6.7 %collective-permute-start = (f32[16,1024]{1,0:T(8,128)S(1)}, f32[16,1024]{1,0:T(8,128)S(1)}, u32[]{:S(2)}, u32[]{:S(2)}) collective-permute-start(f32[16,1024]{1,0:T(8,128)S(1)} %pad_add_fusion), channel_id=1, source_target_pairs={{0,4},{1,5},{2,6},{3,7},{4,0},{5,1},{6,2},{7,3},{8,12},{9,13},{10,... | collective-permute-start | bytes 196616 | tf_op jit(solution)/shard_map/ppermute | solution.py:251
  9.3 10.8 %copy-start.17 = (f32[2,128,256]{2,1,0:T(8,128)S(1)}, f32[2,128,256]{2,1,0:T(8,128)}, u32[]{:S(2)}) copy-start(f32[2,128,256]{2,1,0:T(8,128)} %get-tuple-element.107) | copy-start | bytes 786436
  9.3 13.6 %collective-permute-start.5 = (f32[2,128,256]{2,1,0:T(8,128)}, f32[2,128,256]{2,1,0:T(8,128)S(1)}, u32[]{:S(2)}, u32[]{:S(2)}) collective-permute-start(f32[2,128,256]{2,1,0:T(8,128)} %get-tuple-element.80), channel_id=1, source_target_pairs={{0,15},{1,14},{2,13},{3,12},{4,11},{5,10},{6,9},{7,8},{8,7},{9,6},... | collective-permute-start | bytes 786440 | tf_op jit(solution)/shard_map/ppermute | solution.py:251
  12.7 46.0 %copy-start.4 = (f32[4,16,1024]{2,1,0:T(8,128)}, f32[4,16,1024]{2,1,0:T(8,128)S(1)}, u32[]{:S(2)}) copy-start(f32[4,16,1024]{2,1,0:T(8,128)S(1)} %pad_maximum_fusion.rest_0_) | copy-start | bytes 786436
  12.7 11.4 %collective-permute-start.3 = (f32[4,16,1024]{2,1,0:T(8,128)S(1)}, f32[4,16,1024]{2,1,0:T(8,128)S(1)}, u32[]{:S(2)}, u32[]{:S(2)}) collective-permute-start(f32[4,16,1024]{2,1,0:T(8,128)S(1)} %pad_maximum_fusion.rest_0_), channel_id=1, source_target_pairs={{0,1},{1,0},{2,3},{3,2},{4,5},{5,4},{6,7},{7,6},{8,9},{9,8},{10,11... | collective-permute-start | bytes 786440 | tf_op jit(solution)/shard_map/ppermute | solution.py:251
  14.3 18.0 %collective-permute-start.4 = (f32[4,16,1024]{2,1,0:T(8,128)S(1)}, f32[4,16,1024]{2,1,0:T(8,128)S(1)}, u32[]{:S(2)}, u32[]{:S(2)}) collective-permute-start(f32[4,16,1024]{2,1,0:T(8,128)S(1)} %pad_maximum_fusion.rest_0_), channel_id=1, source_target_pairs={{0,2},{1,3},{2,0},{3,1},{4,6},{5,7},{6,4},{7,5},{8,10},{9,11},{10,... | collective-permute-start | bytes 786440 | tf_op jit(solution)/shard_map/ppermute | solution.py:251
  14.8 26.8 %collective-permute-start.7 = (f32[2,128,256]{2,1,0:T(8,128)}, f32[2,128,256]{2,1,0:T(8,128)S(1)}, u32[]{:S(2)}, u32[]{:S(2)}) collective-permute-start(f32[2,128,256]{2,1,0:T(8,128)} %get-tuple-element.86), channel_id=1, source_target_pairs={{0,14},{1,15},{2,12},{3,13},{4,10},{5,11},{6,8},{7,9},{8,6},{9,7},... | collective-permute-start | bytes 786440 | tf_op jit(solution)/shard_map/ppermute | solution.py:251
  20.2 23.1 %collective-permute-start.13 = (f32[2,128,256]{2,1,0:T(8,128)S(1)}, f32[2,128,256]{2,1,0:T(8,128)S(1)}, u32[]{:S(2)}, u32[]{:S(2)}) collective-permute-start(f32[2,128,256]{2,1,0:T(8,128)S(1)} %copy-done.17), channel_id=1, source_target_pairs={{0,13},{1,12},{2,15},{3,14},{4,9},{5,8},{6,11},{7,10},{8,5},{9,4},... | collective-permute-start | bytes 786440 | tf_op jit(solution)/shard_map/ppermute | solution.py:251
  22.9 27.2 %collective-permute-start.6 = (f32[4,16,1024]{2,1,0:T(8,128)S(1)}, f32[4,16,1024]{2,1,0:T(8,128)S(1)}, u32[]{:S(2)}, u32[]{:S(2)}) collective-permute-start(f32[4,16,1024]{2,1,0:T(8,128)S(1)} %pad_maximum_fusion.rest_0_), channel_id=1, source_target_pairs={{0,3},{1,2},{2,1},{3,0},{4,7},{5,6},{6,5},{7,4},{8,11},{9,10},{10,... | collective-permute-start | bytes 786440 | tf_op jit(solution)/shard_map/ppermute | solution.py:251
  24.1 34.7 %copy-start.6 = (f32[4,16,1024]{2,1,0:T(8,128)}, f32[4,16,1024]{2,1,0:T(8,128)S(1)}, u32[]{:S(2)}) copy-start(f32[4,16,1024]{2,1,0:T(8,128)S(1)} %collective-permute-done.3.rest_1_) | copy-start | bytes 786436
  32.3 0.7 copy-start.7
  33.0 24.6 %collective-permute-start.18 = (f32[2,128,256]{2,1,0:T(8,128)}, f32[2,128,256]{2,1,0:T(8,128)S(1)}, u32[]{:S(2)}, u32[]{:S(2)}) collective-permute-start(f32[2,128,256]{2,1,0:T(8,128)} %get-tuple-element.116), channel_id=1, source_target_pairs={{0,7},{1,6},{2,5},{3,4},{4,3},{5,2},{6,1},{7,0},{8,15},{9,14},{10,... | collective-permute-start | bytes 786440 | tf_op jit(solution)/shard_map/ppermute | solution.py:251
  39.3 18.4 %collective-permute-start.11 = (f32[2,128,256]{2,1,0:T(8,128)}, f32[2,128,256]{2,1,0:T(8,128)S(1)}, u32[]{:S(2)}, u32[]{:S(2)}) collective-permute-start(f32[2,128,256]{2,1,0:T(8,128)} %get-tuple-element.101), channel_id=1, source_target_pairs={{0,12},{1,13},{2,14},{3,15},{4,8},{5,9},{6,10},{7,11},{8,4},{9,5},... | collective-permute-start | bytes 786440 | tf_op jit(solution)/shard_map/ppermute | solution.py:251
  41.6 17.1 %copy-start.5 = (f32[4,8192]{1,0:T(4,128)}, f32[4,8192]{1,0:T(4,128)S(1)}, u32[]{:S(2)}) copy-start(f32[4,8192]{1,0:T(4,128)S(1)} %pad_maximum_fusion.1.rest_4_) | copy-start | bytes 393220
  41.7 5.1 %collective-permute-start.8 = (f32[4,8192]{1,0:T(4,128)S(1)}, f32[4,8192]{1,0:T(4,128)S(1)}, u32[]{:S(2)}, u32[]{:S(2)}) collective-permute-start(f32[4,8192]{1,0:T(4,128)S(1)} %pad_maximum_fusion.1.rest_4_), channel_id=1, source_target_pairs={{0,16},{16,0},{1,17},{17,1},{2,18},{18,2},{3,19},{19,3},{4,20},{20... | collective-permute-start | bytes 393224 | tf_op jit(solution)/shard_map/ppermute | solution.py:251
  43.2 20.6 %collective-permute-start.14 = (f32[2,128,256]{2,1,0:T(8,128)}, f32[2,128,256]{2,1,0:T(8,128)S(1)}, u32[]{:S(2)}, u32[]{:S(2)}) collective-permute-start(f32[2,128,256]{2,1,0:T(8,128)} %get-tuple-element.108), channel_id=1, source_target_pairs={{0,3},{1,2},{2,1},{3,0},{4,7},{5,6},{6,5},{7,4},{8,11},{9,10},{10,... | collective-permute-start | bytes 786440 | tf_op jit(solution)/shard_map/ppermute | solution.py:251
  46.7 0.7 copy-start.9
  47.4 29.0 %collective-permute-start.17 = (f32[2,128,256]{2,1,0:T(8,128)}, f32[2,128,256]{2,1,0:T(8,128)S(1)}, u32[]{:S(2)}, u32[]{:S(2)}) collective-permute-start(f32[2,128,256]{2,1,0:T(8,128)} %get-tuple-element.113), channel_id=1, source_target_pairs={{0,6},{1,7},{2,4},{3,5},{4,2},{5,3},{6,0},{7,1},{8,14},{9,15},{10,... | collective-permute-start | bytes 786440 | tf_op jit(solution)/shard_map/ppermute | solution.py:251
  50.1 0.7 copy-start.8
  50.8 25.6 %collective-permute-start.9 = (f32[2,128,256]{2,1,0:T(8,128)}, f32[2,128,256]{2,1,0:T(8,128)S(1)}, u32[]{:S(2)}, u32[]{:S(2)}) collective-permute-start(f32[2,128,256]{2,1,0:T(8,128)} %get-tuple-element.97), channel_id=1, source_target_pairs={{0,11},{1,10},{2,9},{3,8},{4,15},{5,14},{6,13},{7,12},{8,3},{9,2},... | collective-permute-start | bytes 786440 | tf_op jit(solution)/shard_map/ppermute | solution.py:251
  57.6 24.3 %collective-permute-start.19 = (f32[2,128,256]{2,1,0:T(8,128)}, f32[2,128,256]{2,1,0:T(8,128)S(1)}, u32[]{:S(2)}, u32[]{:S(2)}) collective-permute-start(f32[2,128,256]{2,1,0:T(8,128)} %get-tuple-element.119), channel_id=1, source_target_pairs={{0,10},{1,11},{2,8},{3,9},{4,14},{5,15},{6,12},{7,13},{8,2},{9,3},... | collective-permute-start | bytes 786440 | tf_op jit(solution)/shard_map/ppermute | solution.py:251
  57.6 24.3 %collective-permute-start.12 = (f32[2,128,256]{2,1,0:T(8,128)}, f32[2,128,256]{2,1,0:T(8,128)S(1)}, u32[]{:S(2)}, u32[]{:S(2)}) collective-permute-start(f32[2,128,256]{2,1,0:T(8,128)} %get-tuple-element.102), channel_id=1, source_target_pairs={{0,2},{1,3},{2,0},{3,1},{4,6},{5,7},{6,4},{7,5},{8,10},{9,11},{10,... | collective-permute-start | bytes 786440 | tf_op jit(solution)/shard_map/ppermute | solution.py:251
  58.7 5.2 %copy-start.16 = (f32[2,128,256]{2,1,0:T(8,128)S(1)}, f32[2,128,256]{2,1,0:T(8,128)}, u32[]{:S(2)}) copy-start(f32[2,128,256]{2,1,0:T(8,128)} %get-tuple-element.111) | copy-start | bytes 786436
  58.7 17.7 %copy-start.15 = (f32[2,128,256]{2,1,0:T(8,128)S(1)}, f32[2,128,256]{2,1,0:T(8,128)}, u32[]{:S(2)}) copy-start(f32[2,128,256]{2,1,0:T(8,128)} %get-tuple-element.121) | copy-start | bytes 786436
  58.7 17.7 %copy-start.14 = (f32[2,128,256]{2,1,0:T(8,128)S(1)}, f32[2,128,256]{2,1,0:T(8,128)}, u32[]{:S(2)}) copy-start(f32[2,128,256]{2,1,0:T(8,128)} %get-tuple-element.98) | copy-start | bytes 786436
  58.7 23.2 %copy-start.13 = (f32[2,128,256]{2,1,0:T(8,128)S(1)}, f32[2,128,256]{2,1,0:T(8,128)}, u32[]{:S(2)}) copy-start(f32[2,128,256]{2,1,0:T(8,128)} %get-tuple-element.120) | copy-start | bytes 786436
  58.7 23.2 %copy-start.12 = (f32[2,128,256]{2,1,0:T(8,128)S(1)}, f32[2,128,256]{2,1,0:T(8,128)}, u32[]{:S(2)}) copy-start(f32[2,128,256]{2,1,0:T(8,128)} %get-tuple-element.110) | copy-start | bytes 786436
  63.9 25.8 %collective-permute-start.16 = (f32[2,128,256]{2,1,0:T(8,128)S(1)}, f32[2,128,256]{2,1,0:T(8,128)S(1)}, u32[]{:S(2)}, u32[]{:S(2)}) collective-permute-start(f32[2,128,256]{2,1,0:T(8,128)S(1)} %copy-done.16), channel_id=1, source_target_pairs={{0,5},{1,4},{2,7},{3,6},{4,1},{5,0},{6,3},{7,2},{8,13},{9,12},{10,... | collective-permute-start | bytes 786440 | tf_op jit(solution)/shard_map/ppermute | solution.py:251
  76.4 22.1 %collective-permute-start.21 = (f32[2,128,256]{2,1,0:T(8,128)S(1)}, f32[2,128,256]{2,1,0:T(8,128)S(1)}, u32[]{:S(2)}, u32[]{:S(2)}) collective-permute-start(f32[2,128,256]{2,1,0:T(8,128)S(1)} %copy-done.15), channel_id=1, source_target_pairs={{0,9},{1,8},{2,11},{3,10},{4,13},{5,12},{6,15},{7,14},{8,1},{9,0},... | collective-permute-start | bytes 786440 | tf_op jit(solution)/shard_map/ppermute | solution.py:251
  76.4 22.1 %collective-permute-start.10 = (f32[2,128,256]{2,1,0:T(8,128)S(1)}, f32[2,128,256]{2,1,0:T(8,128)S(1)}, u32[]{:S(2)}, u32[]{:S(2)}) collective-permute-start(f32[2,128,256]{2,1,0:T(8,128)S(1)} %copy-done.14), channel_id=1, source_target_pairs={{0,1},{1,0},{2,3},{3,2},{4,5},{5,4},{6,7},{7,6},{8,9},{9,8},{10,11... | collective-permute-start | bytes 786440 | tf_op jit(solution)/shard_map/ppermute | solution.py:251
  81.9 21.5 %collective-permute-start.20 = (f32[2,128,256]{2,1,0:T(8,128)S(1)}, f32[2,128,256]{2,1,0:T(8,128)S(1)}, u32[]{:S(2)}, u32[]{:S(2)}) collective-permute-start(f32[2,128,256]{2,1,0:T(8,128)S(1)} %copy-done.13), channel_id=1, source_target_pairs={{0,8},{1,9},{2,10},{3,11},{4,12},{5,13},{6,14},{7,15},{8,0},{9,1},... | collective-permute-start | bytes 786440 | tf_op jit(solution)/shard_map/ppermute | solution.py:251
  81.9 21.5 %collective-permute-start.15 = (f32[2,128,256]{2,1,0:T(8,128)S(1)}, f32[2,128,256]{2,1,0:T(8,128)S(1)}, u32[]{:S(2)}, u32[]{:S(2)}) collective-permute-start(f32[2,128,256]{2,1,0:T(8,128)S(1)} %copy-done.12), channel_id=1, source_target_pairs={{0,4},{1,5},{2,6},{3,7},{4,0},{5,1},{6,2},{7,3},{8,12},{9,13},{10,... | collective-permute-start | bytes 786440 | tf_op jit(solution)/shard_map/ppermute | solution.py:251

commit v10 on v9

--- a/solution.py
+++ b/solution.py
@@ -276,10 +276,10 @@
     mine = jnp.pad(x_fac, ((0, row_tiles), (0, 0))) + jnp.pad(w_fac, ((row_tiles, 0), (0, 0)))
     mine, child = lax.optimization_barrier((mine, child))
     line = [sender.send(mine, GROUP, m) for m in range(NEAR, devices, NEAR)]
-    early = [devices - 1, devices - 2, devices - 3]
+    early = [devices - 1, devices - 2]
     pieces = place(child, col_map, tile, devices, early)
     pieces, child, v_fac, z_fac = lax.optimization_barrier((pieces, child, v_fac, z_fac))
-    pieces.update(place(child, col_map, tile, devices, list(reversed(range(devices - 3)))))
+    pieces.update(place(child, col_map, tile, devices, list(reversed(range(devices - 2)))))
     half = devices // 2
     crossing = list(reversed(range(half, devices)))
     local = [m for pair in zip(reversed(range(NEAR, half)), [3, 2, 1] + [None] * half) for m in pair if m]

time: 108 us -> 108 us (level)
    unnamed x37 -> x35, local copies, waits for them, and re-layouts: 2.88 us -> 2.85 us
where the time goes in v10:
time: 108 us
  starting transfers between devices  53.3 us (49%)
  waiting for transfers between devices  33.8 us (31%)
  Pallas kernels  16.5 us (15%)
  local copies, waits for them, and re-layouts  2.85 us (3%)
    ppermute x22, starting transfers between devices, send(): lax.ppermute(array, axes, [(d, d ^ m) for d in range(size)])  53.3 us
    ppermute x22, waiting for transfers between devices, send(): lax.ppermute(array, axes, [(d, d ^ m) for d in range(size)])  33.8 us
    pallas_call x2, Pallas kernels, place(): pl.pallas_call(functools.partial(place_kernel, members, tiles, tile, col_...  7.02 us
    pallas_call x1, Pallas kernels, factors(): pl.pallas_call(functools.partial(factor_kernel, len(xw), len(vz), col_til...  5.06 us
    pallas_call x1, Pallas kernels, finish(): pl.pallas_call(functools.partial(finish_kernel, len(pieces), tile), out_s...  4.44 us
    unnamed x35, local copies, waits for them, and re-layouts  2.85 us
  transfers between devices with their start and end apart: 22, of which 6 were waited for; matrix products, arithmetic and copies ran while one was open for 1% of the time, Pallas kernels for 11%

profile of v10, /device:TPU:0, one launch (start us, length us, event | category | flops | bytes accessed | tf_op | source)
XLA Modules:
  0.0 107.7 jit_solution(12889415224300701664)
XLA Ops:
  0.0 0.8 pad_add_fusion
  0.8 0.0 copy-start
  0.8 0.0 copy-start.1
  0.8 0.0 copy-start.2
  0.8 0.0 copy-start.3
  0.8 5.1 %collective-permute-start.2 = (f32[16,1024]{1,0:T(8,128)S(1)}, f32[16,1024]{1,0:T(8,128)S(1)}, u32[]{:S(2)}, u32[]{:S(2)}) collective-permute-start(f32[16,1024]{1,0:T(8,128)S(1)} %pad_add_fusion), channel_id=1, source_target_pairs={{0,12},{1,13},{2,14},{3,15},{4,8},{5,9},{6,10},{7,11},{8,4},{9,5},... | collective-permute-start | bytes 196616 | tf_op jit(solution)/shard_map/ppermute | solution.py:251
  6.0 0.0 collective-permute-start.1
  6.0 0.6 collective-permute-start
  6.6 2.5 %place_child.2 = (f32[2,128,256]{2,1,0:T(8,128)}, f32[2,128,256]{2,1,0:T(8,128)}) custom-call(s32[32]{0:T(128)} %col_map.3, f32[128,8192]{1,0:T(8,128)} %child.1), custom_call_target="tpu_custom_call" | custom-call | bytes 1048576 | tf_op jit(solution)/shard_map/place_child/pallas_call | solution.py:63
  9.2 3.3 %collective-permute-start.5 = (f32[2,128,256]{2,1,0:T(8,128)}, f32[2,128,256]{2,1,0:T(8,128)S(1)}, u32[]{:S(2)}, u32[]{:S(2)}) collective-permute-start(f32[2,128,256]{2,1,0:T(8,128)} %get-tuple-element.78), channel_id=1, source_target_pairs={{0,15},{1,14},{2,13},{3,12},{4,11},{5,10},{6,9},{7,8},{8,7},{9,6},... | collective-permute-start | bytes 786440 | tf_op jit(solution)/shard_map/ppermute | solution.py:251
  12.5 0.0 collective-permute-done.2
  12.5 0.0 collective-permute-done.1
  12.5 0.0 collective-permute-done
  12.5 0.0 copy-start.4
  12.5 1.6 %collective-permute-start.3 = (f32[4,16,1024]{2,1,0:T(8,128)S(1)}, f32[4,16,1024]{2,1,0:T(8,128)S(1)}, u32[]{:S(2)}, u32[]{:S(2)}) collective-permute-start(f32[4,16,1024]{2,1,0:T(8,128)S(1)} %pad_maximum_fusion.rest_0_), channel_id=1, source_target_pairs={{0,1},{1,0},{2,3},{3,2},{4,5},{5,4},{6,7},{7,6},{8,9},{9,8},{10,11... | collective-permute-start | bytes 786440 | tf_op jit(solution)/shard_map/ppermute | solution.py:251
  14.1 0.5 collective-permute-start.4
  14.7 1.3 %collective-permute-start.7 = (f32[2,128,256]{2,1,0:T(8,128)}, f32[2,128,256]{2,1,0:T(8,128)S(1)}, u32[]{:S(2)}, u32[]{:S(2)}) collective-permute-start(f32[2,128,256]{2,1,0:T(8,128)} %get-tuple-element.84), channel_id=1, source_target_pairs={{0,14},{1,15},{2,12},{3,13},{4,10},{5,11},{6,8},{7,9},{8,6},{9,7},... | collective-permute-start | bytes 786440 | tf_op jit(solution)/shard_map/ppermute | solution.py:251
  15.9 4.5 %place_child.3 = (f32[2,128,256]{2,1,0:T(8,128)}, f32[2,128,256]{2,1,0:T(8,128)}, f32[2,128,256]{2,1,0:T(8,128)}, f32[2,128,256]{2,1,0:T(8,128)}, f32[2,128,256]...) custom-call(s32[32]{0:T(128)} %col_map.3, ...), custom_call_target="tpu_custom_call" | custom-call | bytes 7340032 | tf_op jit(solution)/shard_map/place_child/pallas_call | solution.py:63
  20.4 2.7 %collective-permute-start.13 = (f32[2,128,256]{2,1,0:T(8,128)}, f32[2,128,256]{2,1,0:T(8,128)S(1)}, u32[]{:S(2)}, u32[]{:S(2)}) collective-permute-start(f32[2,128,256]{2,1,0:T(8,128)} %get-tuple-element.105), channel_id=1, source_target_pairs={{0,13},{1,12},{2,15},{3,14},{4,9},{5,8},{6,11},{7,10},{8,5},{9,4},... | collective-permute-start | bytes 786440 | tf_op jit(solution)/shard_map/ppermute | solution.py:251
  23.1 0.0 collective-permute-done.5.rest_14_
  23.1 1.1 %collective-permute-start.6 = (f32[4,16,1024]{2,1,0:T(8,128)S(1)}, f32[4,16,1024]{2,1,0:T(8,128)S(1)}, u32[]{:S(2)}, u32[]{:S(2)}) collective-permute-start(f32[4,16,1024]{2,1,0:T(8,128)S(1)} %pad_maximum_fusion.rest_0_), channel_id=1, source_target_pairs={{0,3},{1,2},{2,1},{3,0},{4,7},{5,6},{6,5},{7,4},{8,11},{9,10},{10,... | collective-permute-start | bytes 786440 | tf_op jit(solution)/shard_map/ppermute | solution.py:251
  24.2 0.0 collective-permute-done.3.rest_1_
  24.2 7.9 %collective-permute-done.4.rest_2_ = f32[4,16,1024]{2,1,0:T(8,128)S(1)} collective-permute-done((f32[4,16,1024]{2,1,0:T(8,128)S(1)}, f32[4,16,1024]{2,1,0:T(8,128)S(1)}, u32[]{:S(2)}, u32[]{:S(2)}) %collective-permute-start.4) | collective-permute-done | bytes 262176 | tf_op jit(solution)/shard_map/ppermute | solution.py:251
  32.2 0.7 copy-done.7
  32.9 6.2 %collective-permute-start.18 = (f32[2,128,256]{2,1,0:T(8,128)}, f32[2,128,256]{2,1,0:T(8,128)S(1)}, u32[]{:S(2)}, u32[]{:S(2)}) collective-permute-start(f32[2,128,256]{2,1,0:T(8,128)} %get-tuple-element.114), channel_id=1, source_target_pairs={{0,7},{1,6},{2,5},{3,4},{4,3},{5,2},{6,1},{7,0},{8,15},{9,14},{10,... | collective-permute-start | bytes 786440 | tf_op jit(solution)/shard_map/ppermute | solution.py:251
  39.1 2.3 %collective-permute-start.11 = (f32[2,128,256]{2,1,0:T(8,128)}, f32[2,128,256]{2,1,0:T(8,128)S(1)}, u32[]{:S(2)}, u32[]{:S(2)}) collective-permute-start(f32[2,128,256]{2,1,0:T(8,128)} %get-tuple-element.99), channel_id=1, source_target_pairs={{0,12},{1,13},{2,14},{3,15},{4,8},{5,9},{6,10},{7,11},{8,4},{9,5},... | collective-permute-start | bytes 786440 | tf_op jit(solution)/shard_map/ppermute | solution.py:251
  41.4 0.0 copy-done.10
  41.4 0.0 copy-done.11
  41.4 0.1 pad_maximum_fusion.1.rest_4_
  41.5 0.0 collective-permute-done.7.rest_13_
  41.5 1.6 %collective-permute-start.8 = (f32[4,8192]{1,0:T(4,128)S(1)}, f32[4,8192]{1,0:T(4,128)S(1)}, u32[]{:S(2)}, u32[]{:S(2)}) collective-permute-start(f32[4,8192]{1,0:T(4,128)S(1)} %pad_maximum_fusion.1.rest_4_), channel_id=1, source_target_pairs={{0,16},{16,0},{1,17},{17,1},{2,18},{18,2},{3,19},{19,3},{4,20},{20... | collective-permute-start | bytes 393224 | tf_op jit(solution)/shard_map/ppermute | solution.py:251
  43.1 0.0 collective-permute-done.13.rest_12_
  43.1 0.0 collective-permute-start.14
  43.1 3.5 %collective-permute-done.8.rest_5_ = f32[4,8192]{1,0:T(4,128)S(1)} collective-permute-done((f32[4,8192]{1,0:T(4,128)S(1)}, f32[4,8192]{1,0:T(4,128)S(1)}, u32[]{:S(2)}, u32[]{:S(2)}) %collective-permute-start.8) | collective-permute-done | bytes 131104 | tf_op jit(solution)/shard_map/ppermute | solution.py:251
  46.6 0.6 copy-done.9
  47.2 2.7 %collective-permute-start.17 = (f32[2,128,256]{2,1,0:T(8,128)}, f32[2,128,256]{2,1,0:T(8,128)S(1)}, u32[]{:S(2)}, u32[]{:S(2)}) collective-permute-start(f32[2,128,256]{2,1,0:T(8,128)} %get-tuple-element.111), channel_id=1, source_target_pairs={{0,6},{1,7},{2,4},{3,5},{4,2},{5,3},{6,0},{7,1},{8,14},{9,15},{10,... | collective-permute-start | bytes 786440 | tf_op jit(solution)/shard_map/ppermute | solution.py:251
  49.9 0.0 collective-permute-done.6.rest_3_
  49.9 0.7 copy-done.8
  50.6 6.8 %collective-permute-start.9 = (f32[2,128,256]{2,1,0:T(8,128)}, f32[2,128,256]{2,1,0:T(8,128)S(1)}, u32[]{:S(2)}, u32[]{:S(2)}) collective-permute-start(f32[2,128,256]{2,1,0:T(8,128)} %get-tuple-element.95), channel_id=1, source_target_pairs={{0,11},{1,10},{2,9},{3,8},{4,15},{5,14},{6,13},{7,12},{8,3},{9,2},... | collective-permute-start | bytes 786440 | tf_op jit(solution)/shard_map/ppermute | solution.py:251
  57.5 0.0 collective-permute-done.18.rest_6_
  57.5 0.0 collective-permute-start.19
  57.5 0.0 collective-permute-done.11.rest_11_
  57.5 0.3 collective-permute-start.12
  57.8 0.8 copy.14.admissible
  58.6 5.1 %update_factors.1 = (f32[2,512,128]{2,1,0:T(8,128)S(1)}, f32[4,512,128]{2,1,0:T(8,128)S(1)}, f32[2048,512]{1,0:T(8,128)S(1)}) custom-call(f32[2048,512]{1,0:T(8,128)} %front.1, f32[256,256]{1,0:T(8,128)S(1)} %copy-done, s32[1,256]{1,0:T(1,128)S(1)} %bitcast.5, s32[8]{0:T(128)S(1)} %copy-done.2, s32[2]{0:T(128)S(1)} %copy-done.3, ...), custom_call_target="tpu_custom_call" | custom-call | flops 67108864 | bytes 2097152 | tf_op jit(solution)/shard_map/update_factors/pallas_call | solution.py:150
  63.7 0.0 collective-permute-done.14.rest_2_
  63.7 0.0 copy-done.16
  63.7 12.5 %collective-permute-start.16 = (f32[2,128,256]{2,1,0:T(8,128)S(1)}, f32[2,128,256]{2,1,0:T(8,128)S(1)}, u32[]{:S(2)}, u32[]{:S(2)}) collective-permute-start(f32[2,128,256]{2,1,0:T(8,128)S(1)} %copy-done.16), channel_id=1, source_target_pairs={{0,5},{1,4},{2,7},{3,6},{4,1},{5,0},{6,3},{7,2},{8,13},{9,12},{10,... | collective-permute-start | bytes 786440 | tf_op jit(solution)/shard_map/ppermute | solution.py:251
  76.2 0.0 collective-permute-done.17.rest_5_
  76.2 0.0 collective-permute-start.21
  76.2 0.0 collective-permute-done.9.rest_10_
  76.2 0.0 copy-done.14
  76.2 2.1 %collective-permute-start.10 = (f32[2,128,256]{2,1,0:T(8,128)S(1)}, f32[2,128,256]{2,1,0:T(8,128)S(1)}, u32[]{:S(2)}, u32[]{:S(2)}) collective-permute-start(f32[2,128,256]{2,1,0:T(8,128)S(1)} %copy-done.14), channel_id=1, source_target_pairs={{0,1},{1,0},{2,3},{3,2},{4,5},{5,4},{6,7},{7,6},{8,9},{9,8},{10,11... | collective-permute-start | bytes 786440 | tf_op jit(solution)/shard_map/ppermute | solution.py:251
  78.3 3.4 %collective-permute-done.19.rest_9_ = f32[2,128,256]{2,1,0:T(8,128)S(1)} collective-permute-done((f32[2,128,256]{2,1,0:T(8,128)}, f32[2,128,256]{2,1,0:T(8,128)S(1)}, u32[]{:S(2)}, u32[]{:S(2)}) %collective-permute-start.19) | collective-permute-done | bytes 262176 | tf_op jit(solution)/shard_map/ppermute | solution.py:251
  81.7 0.0 collective-permute-start.20
  81.7 0.0 collective-permute-done.12.rest_1_
  81.7 0.0 copy-done.12
  81.8 2.5 %collective-permute-start.15 = (f32[2,128,256]{2,1,0:T(8,128)S(1)}, f32[2,128,256]{2,1,0:T(8,128)S(1)}, u32[]{:S(2)}, u32[]{:S(2)}) collective-permute-start(f32[2,128,256]{2,1,0:T(8,128)S(1)} %copy-done.12), channel_id=1, source_target_pairs={{0,4},{1,5},{2,6},{3,7},{4,0},{5,1},{6,2},{7,3},{8,12},{9,13},{10,... | collective-permute-start | bytes 786440 | tf_op jit(solution)/shard_map/ppermute | solution.py:251
  84.2 5.3 %collective-permute-done.16.rest_4_ = f32[2,128,256]{2,1,0:T(8,128)S(1)} collective-permute-done((f32[2,128,256]{2,1,0:T(8,128)S(1)}, f32[2,128,256]{2,1,0:T(8,128)S(1)}, u32[]{:S(2)}, u32[]{:S(2)}) %collective-permute-start.16) | collective-permute-done | bytes 262176 | tf_op jit(solution)/shard_map/ppermute | solution.py:251
  89.5 8.8 %collective-permute-done.21.rest_8_ = f32[2,128,256]{2,1,0:T(8,128)S(1)} collective-permute-done((f32[2,128,256]{2,1,0:T(8,128)S(1)}, f32[2,128,256]{2,1,0:T(8,128)S(1)}, u32[]{:S(2)}, u32[]{:S(2)}) %collective-permute-start.21) | collective-permute-done | bytes 262176 | tf_op jit(solution)/shard_map/ppermute | solution.py:251
  98.3 0.0 collective-permute-done.10.rest_0_
  98.3 4.9 %collective-permute-done.20.rest_7_ = f32[2,128,256]{2,1,0:T(8,128)S(1)} collective-permute-done((f32[2,128,256]{2,1,0:T(8,128)S(1)}, f32[2,128,256]{2,1,0:T(8,128)S(1)}, u32[]{:S(2)}, u32[]{:S(2)}) %collective-permute-start.20) | collective-permute-done | bytes 262176 | tf_op jit(solution)/shard_map/ppermute | solution.py:251
  103.2 0.0 collective-permute-done.15.rest_3_
  103.2 4.4 %finish.1 = f32[2048,512]{1,0:T(8,128)} custom-call(s32[1,8]{1,0:T(1,128)} %row_map.1, f32[2048,512]{1,0:T(8,128)S(1)} %get-tuple-element.91.front, f32[2,512,128]{2,1,0:T(8,128)S(1)} %get-tuple-element.92.left, f32[4,512,128]{2,1,0:T(8,128)S(1)} %get-tuple-element.93.right, f32[2,128,256]{2,1,0:T(8,128)S(1)} %collective-permute-done.10.rest_0_, ...), custom_call_target="tpu_custom_call" | custom-call | flops 536870912 | bytes 12582912 | tf_op jit(solution)/shard_map/finish/pallas_call | solution.py:223
  (22 shorter events, 0.1 us)
Async XLA Ops:
  0.8 40.6 %copy-start.10 = (f32[2,8192]{1,0:T(2,128)S(1)}, f32[2,8192]{1,0:T(2,128)}, u32[]{:S(2)}) copy-start(f32[2,8192]{1,0:T(2,128)} %param.20) | copy-start | bytes 196612
  0.8 40.6 %copy-start.11 = (f32[2,8192]{1,0:T(2,128)S(1)}, f32[2,8192]{1,0:T(2,128)}, u32[]{:S(2)}) copy-start(f32[2,8192]{1,0:T(2,128)} %param.19) | copy-start | bytes 196612
  0.8 57.8 %copy-start = (f32[256,256]{1,0:T(8,128)S(1)}, f32[256,256]{1,0:T(8,128)}, u32[]{:S(2)}) copy-start(f32[256,256]{1,0:T(8,128)} %dinv.1) | copy-start | bytes 786436
  0.8 57.8 %copy-start.1 = (s32[256]{0:T(256)S(1)}, s32[256]{0:T(256)}, u32[]{:S(2)}) copy-start(s32[256]{0:T(256)} %param.22) | copy-start | bytes 3076
  0.8 57.8 %copy-start.2 = (s32[8]{0:T(128)S(1)}, s32[8]{0:T(128)}, u32[]{:S(2)}) copy-start(s32[8]{0:T(128)} %rank_rows.1) | copy-start | bytes 100
  0.8 57.8 %copy-start.3 = (s32[2]{0:T(128)S(1)}, s32[2]{0:T(128)}, u32[]{:S(2)}) copy-start(s32[2]{0:T(128)} %rank_cols.1) | copy-start | bytes 28
  0.8 11.7 %collective-permute-start.2 = (f32[16,1024]{1,0:T(8,128)S(1)}, f32[16,1024]{1,0:T(8,128)S(1)}, u32[]{:S(2)}, u32[]{:S(2)}) collective-permute-start(f32[16,1024]{1,0:T(8,128)S(1)} %pad_add_fusion), channel_id=1, source_target_pairs={{0,12},{1,13},{2,14},{3,15},{4,8},{5,9},{6,10},{7,11},{8,4},{9,5},... | collective-permute-start | bytes 196616 | tf_op jit(solution)/shard_map/ppermute | solution.py:251
  6.0 6.5 %collective-permute-start.1 = (f32[16,1024]{1,0:T(8,128)S(1)}, f32[16,1024]{1,0:T(8,128)S(1)}, u32[]{:S(2)}, u32[]{:S(2)}) collective-permute-start(f32[16,1024]{1,0:T(8,128)S(1)} %pad_add_fusion), channel_id=1, source_target_pairs={{0,8},{1,9},{2,10},{3,11},{4,12},{5,13},{6,14},{7,15},{8,0},{9,1},... | collective-permute-start | bytes 196616 | tf_op jit(solution)/shard_map/ppermute | solution.py:251
  6.0 6.5 %collective-permute-start = (f32[16,1024]{1,0:T(8,128)S(1)}, f32[16,1024]{1,0:T(8,128)S(1)}, u32[]{:S(2)}, u32[]{:S(2)}) collective-permute-start(f32[16,1024]{1,0:T(8,128)S(1)} %pad_add_fusion), channel_id=1, source_target_pairs={{0,4},{1,5},{2,6},{3,7},{4,0},{5,1},{6,2},{7,3},{8,12},{9,13},{10,... | collective-permute-start | bytes 196616 | tf_op jit(solution)/shard_map/ppermute | solution.py:251
  9.2 13.9 %collective-permute-start.5 = (f32[2,128,256]{2,1,0:T(8,128)}, f32[2,128,256]{2,1,0:T(8,128)S(1)}, u32[]{:S(2)}, u32[]{:S(2)}) collective-permute-start(f32[2,128,256]{2,1,0:T(8,128)} %get-tuple-element.78), channel_id=1, source_target_pairs={{0,15},{1,14},{2,13},{3,12},{4,11},{5,10},{6,9},{7,8},{8,7},{9,6},... | collective-permute-start | bytes 786440 | tf_op jit(solution)/shard_map/ppermute | solution.py:251
  12.5 46.0 %copy-start.4 = (f32[4,16,1024]{2,1,0:T(8,128)}, f32[4,16,1024]{2,1,0:T(8,128)S(1)}, u32[]{:S(2)}) copy-start(f32[4,16,1024]{2,1,0:T(8,128)S(1)} %pad_maximum_fusion.rest_0_) | copy-start | bytes 786436
  12.5 11.7 %collective-permute-start.3 = (f32[4,16,1024]{2,1,0:T(8,128)S(1)}, f32[4,16,1024]{2,1,0:T(8,128)S(1)}, u32[]{:S(2)}, u32[]{:S(2)}) collective-permute-start(f32[4,16,1024]{2,1,0:T(8,128)S(1)} %pad_maximum_fusion.rest_0_), channel_id=1, source_target_pairs={{0,1},{1,0},{2,3},{3,2},{4,5},{5,4},{6,7},{7,6},{8,9},{9,8},{10,11... | collective-permute-start | bytes 786440 | tf_op jit(solution)/shard_map/ppermute | solution.py:251
  14.1 18.0 %collective-permute-start.4 = (f32[4,16,1024]{2,1,0:T(8,128)S(1)}, f32[4,16,1024]{2,1,0:T(8,128)S(1)}, u32[]{:S(2)}, u32[]{:S(2)}) collective-permute-start(f32[4,16,1024]{2,1,0:T(8,128)S(1)} %pad_maximum_fusion.rest_0_), channel_id=1, source_target_pairs={{0,2},{1,3},{2,0},{3,1},{4,6},{5,7},{6,4},{7,5},{8,10},{9,11},{10,... | collective-permute-start | bytes 786440 | tf_op jit(solution)/shard_map/ppermute | solution.py:251
  14.7 26.8 %collective-permute-start.7 = (f32[2,128,256]{2,1,0:T(8,128)}, f32[2,128,256]{2,1,0:T(8,128)S(1)}, u32[]{:S(2)}, u32[]{:S(2)}) collective-permute-start(f32[2,128,256]{2,1,0:T(8,128)} %get-tuple-element.84), channel_id=1, source_target_pairs={{0,14},{1,15},{2,12},{3,13},{4,10},{5,11},{6,8},{7,9},{8,6},{9,7},... | collective-permute-start | bytes 786440 | tf_op jit(solution)/shard_map/ppermute | solution.py:251
  20.4 22.7 %collective-permute-start.13 = (f32[2,128,256]{2,1,0:T(8,128)}, f32[2,128,256]{2,1,0:T(8,128)S(1)}, u32[]{:S(2)}, u32[]{:S(2)}) collective-permute-start(f32[2,128,256]{2,1,0:T(8,128)} %get-tuple-element.105), channel_id=1, source_target_pairs={{0,13},{1,12},{2,15},{3,14},{4,9},{5,8},{6,11},{7,10},{8,5},{9,4},... | collective-permute-start | bytes 786440 | tf_op jit(solution)/shard_map/ppermute | solution.py:251
  23.1 26.9 %collective-permute-start.6 = (f32[4,16,1024]{2,1,0:T(8,128)S(1)}, f32[4,16,1024]{2,1,0:T(8,128)S(1)}, u32[]{:S(2)}, u32[]{:S(2)}) collective-permute-start(f32[4,16,1024]{2,1,0:T(8,128)S(1)} %pad_maximum_fusion.rest_0_), channel_id=1, source_target_pairs={{0,3},{1,2},{2,1},{3,0},{4,7},{5,6},{6,5},{7,4},{8,11},{9,10},{10,... | collective-permute-start | bytes 786440 | tf_op jit(solution)/shard_map/ppermute | solution.py:251
  24.2 34.3 %copy-start.6 = (f32[4,16,1024]{2,1,0:T(8,128)}, f32[4,16,1024]{2,1,0:T(8,128)S(1)}, u32[]{:S(2)}) copy-start(f32[4,16,1024]{2,1,0:T(8,128)S(1)} %collective-permute-done.3.rest_1_) | copy-start | bytes 786436
  32.1 0.7 copy-start.7
  32.9 24.6 %collective-permute-start.18 = (f32[2,128,256]{2,1,0:T(8,128)}, f32[2,128,256]{2,1,0:T(8,128)S(1)}, u32[]{:S(2)}, u32[]{:S(2)}) collective-permute-start(f32[2,128,256]{2,1,0:T(8,128)} %get-tuple-element.114), channel_id=1, source_target_pairs={{0,7},{1,6},{2,5},{3,4},{4,3},{5,2},{6,1},{7,0},{8,15},{9,14},{10,... | collective-permute-start | bytes 786440 | tf_op jit(solution)/shard_map/ppermute | solution.py:251
  39.1 18.4 %collective-permute-start.11 = (f32[2,128,256]{2,1,0:T(8,128)}, f32[2,128,256]{2,1,0:T(8,128)S(1)}, u32[]{:S(2)}, u32[]{:S(2)}) collective-permute-start(f32[2,128,256]{2,1,0:T(8,128)} %get-tuple-element.99), channel_id=1, source_target_pairs={{0,12},{1,13},{2,14},{3,15},{4,8},{5,9},{6,10},{7,11},{8,4},{9,5},... | collective-permute-start | bytes 786440 | tf_op jit(solution)/shard_map/ppermute | solution.py:251
  41.5 17.1 %copy-start.5 = (f32[4,8192]{1,0:T(4,128)}, f32[4,8192]{1,0:T(4,128)S(1)}, u32[]{:S(2)}) copy-start(f32[4,8192]{1,0:T(4,128)S(1)} %pad_maximum_fusion.1.rest_4_) | copy-start | bytes 393220
  41.5 5.1 %collective-permute-start.8 = (f32[4,8192]{1,0:T(4,128)S(1)}, f32[4,8192]{1,0:T(4,128)S(1)}, u32[]{:S(2)}, u32[]{:S(2)}) collective-permute-start(f32[4,8192]{1,0:T(4,128)S(1)} %pad_maximum_fusion.1.rest_4_), channel_id=1, source_target_pairs={{0,16},{16,0},{1,17},{17,1},{2,18},{18,2},{3,19},{19,3},{4,20},{20... | collective-permute-start | bytes 393224 | tf_op jit(solution)/shard_map/ppermute | solution.py:251
  43.1 20.6 %collective-permute-start.14 = (f32[2,128,256]{2,1,0:T(8,128)}, f32[2,128,256]{2,1,0:T(8,128)S(1)}, u32[]{:S(2)}, u32[]{:S(2)}) collective-permute-start(f32[2,128,256]{2,1,0:T(8,128)} %get-tuple-element.106), channel_id=1, source_target_pairs={{0,3},{1,2},{2,1},{3,0},{4,7},{5,6},{6,5},{7,4},{8,11},{9,10},{10,... | collective-permute-start | bytes 786440 | tf_op jit(solution)/shard_map/ppermute | solution.py:251
  46.6 0.6 copy-start.9
  47.2 29.0 %collective-permute-start.17 = (f32[2,128,256]{2,1,0:T(8,128)}, f32[2,128,256]{2,1,0:T(8,128)S(1)}, u32[]{:S(2)}, u32[]{:S(2)}) collective-permute-start(f32[2,128,256]{2,1,0:T(8,128)} %get-tuple-element.111), channel_id=1, source_target_pairs={{0,6},{1,7},{2,4},{3,5},{4,2},{5,3},{6,0},{7,1},{8,14},{9,15},{10,... | collective-permute-start | bytes 786440 | tf_op jit(solution)/shard_map/ppermute | solution.py:251
  49.9 0.7 copy-start.8
  50.6 25.6 %collective-permute-start.9 = (f32[2,128,256]{2,1,0:T(8,128)}, f32[2,128,256]{2,1,0:T(8,128)S(1)}, u32[]{:S(2)}, u32[]{:S(2)}) collective-permute-start(f32[2,128,256]{2,1,0:T(8,128)} %get-tuple-element.95), channel_id=1, source_target_pairs={{0,11},{1,10},{2,9},{3,8},{4,15},{5,14},{6,13},{7,12},{8,3},{9,2},... | collective-permute-start | bytes 786440 | tf_op jit(solution)/shard_map/ppermute | solution.py:251
  57.5 24.3 %collective-permute-start.19 = (f32[2,128,256]{2,1,0:T(8,128)}, f32[2,128,256]{2,1,0:T(8,128)S(1)}, u32[]{:S(2)}, u32[]{:S(2)}) collective-permute-start(f32[2,128,256]{2,1,0:T(8,128)} %get-tuple-element.117), channel_id=1, source_target_pairs={{0,10},{1,11},{2,8},{3,9},{4,14},{5,15},{6,12},{7,13},{8,2},{9,3},... | collective-permute-start | bytes 786440 | tf_op jit(solution)/shard_map/ppermute | solution.py:251
  57.5 24.3 %collective-permute-start.12 = (f32[2,128,256]{2,1,0:T(8,128)}, f32[2,128,256]{2,1,0:T(8,128)S(1)}, u32[]{:S(2)}, u32[]{:S(2)}) collective-permute-start(f32[2,128,256]{2,1,0:T(8,128)} %get-tuple-element.100), channel_id=1, source_target_pairs={{0,2},{1,3},{2,0},{3,1},{4,6},{5,7},{6,4},{7,5},{8,10},{9,11},{10,... | collective-permute-start | bytes 786440 | tf_op jit(solution)/shard_map/ppermute | solution.py:251
  58.5 5.2 %copy-start.16 = (f32[2,128,256]{2,1,0:T(8,128)S(1)}, f32[2,128,256]{2,1,0:T(8,128)}, u32[]{:S(2)}) copy-start(f32[2,128,256]{2,1,0:T(8,128)} %get-tuple-element.109) | copy-start | bytes 786436
  58.5 17.7 %copy-start.15 = (f32[2,128,256]{2,1,0:T(8,128)S(1)}, f32[2,128,256]{2,1,0:T(8,128)}, u32[]{:S(2)}) copy-start(f32[2,128,256]{2,1,0:T(8,128)} %get-tuple-element.119) | copy-start | bytes 786436
  58.5 17.7 %copy-start.14 = (f32[2,128,256]{2,1,0:T(8,128)S(1)}, f32[2,128,256]{2,1,0:T(8,128)}, u32[]{:S(2)}) copy-start(f32[2,128,256]{2,1,0:T(8,128)} %get-tuple-element.96) | copy-start | bytes 786436
  58.5 23.2 %copy-start.13 = (f32[2,128,256]{2,1,0:T(8,128)S(1)}, f32[2,128,256]{2,1,0:T(8,128)}, u32[]{:S(2)}) copy-start(f32[2,128,256]{2,1,0:T(8,128)} %get-tuple-element.118) | copy-start | bytes 786436
  58.5 23.2 %copy-start.12 = (f32[2,128,256]{2,1,0:T(8,128)S(1)}, f32[2,128,256]{2,1,0:T(8,128)}, u32[]{:S(2)}) copy-start(f32[2,128,256]{2,1,0:T(8,128)} %get-tuple-element.108) | copy-start | bytes 786436
  63.7 25.8 %collective-permute-start.16 = (f32[2,128,256]{2,1,0:T(8,128)S(1)}, f32[2,128,256]{2,1,0:T(8,128)S(1)}, u32[]{:S(2)}, u32[]{:S(2)}) collective-permute-start(f32[2,128,256]{2,1,0:T(8,128)S(1)} %copy-done.16), channel_id=1, source_target_pairs={{0,5},{1,4},{2,7},{3,6},{4,1},{5,0},{6,3},{7,2},{8,13},{9,12},{10,... | collective-permute-start | bytes 786440 | tf_op jit(solution)/shard_map/ppermute | solution.py:251
  76.2 22.1 %collective-permute-start.21 = (f32[2,128,256]{2,1,0:T(8,128)S(1)}, f32[2,128,256]{2,1,0:T(8,128)S(1)}, u32[]{:S(2)}, u32[]{:S(2)}) collective-permute-start(f32[2,128,256]{2,1,0:T(8,128)S(1)} %copy-done.15), channel_id=1, source_target_pairs={{0,9},{1,8},{2,11},{3,10},{4,13},{5,12},{6,15},{7,14},{8,1},{9,0},... | collective-permute-start | bytes 786440 | tf_op jit(solution)/shard_map/ppermute | solution.py:251
  76.2 22.1 %collective-permute-start.10 = (f32[2,128,256]{2,1,0:T(8,128)S(1)}, f32[2,128,256]{2,1,0:T(8,128)S(1)}, u32[]{:S(2)}, u32[]{:S(2)}) collective-permute-start(f32[2,128,256]{2,1,0:T(8,128)S(1)} %copy-done.14), channel_id=1, source_target_pairs={{0,1},{1,0},{2,3},{3,2},{4,5},{5,4},{6,7},{7,6},{8,9},{9,8},{10,11... | collective-permute-start | bytes 786440 | tf_op jit(solution)/shard_map/ppermute | solution.py:251
  81.7 21.5 %collective-permute-start.20 = (f32[2,128,256]{2,1,0:T(8,128)S(1)}, f32[2,128,256]{2,1,0:T(8,128)S(1)}, u32[]{:S(2)}, u32[]{:S(2)}) collective-permute-start(f32[2,128,256]{2,1,0:T(8,128)S(1)} %copy-done.13), channel_id=1, source_target_pairs={{0,8},{1,9},{2,10},{3,11},{4,12},{5,13},{6,14},{7,15},{8,0},{9,1},... | collective-permute-start | bytes 786440 | tf_op jit(solution)/shard_map/ppermute | solution.py:251
  81.8 21.5 %collective-permute-start.15 = (f32[2,128,256]{2,1,0:T(8,128)S(1)}, f32[2,128,256]{2,1,0:T(8,128)S(1)}, u32[]{:S(2)}, u32[]{:S(2)}) collective-permute-start(f32[2,128,256]{2,1,0:T(8,128)S(1)} %copy-done.12), channel_id=1, source_target_pairs={{0,4},{1,5},{2,6},{3,7},{4,0},{5,1},{6,2},{7,3},{8,12},{9,13},{10,... | collective-permute-start | bytes 786440 | tf_op jit(solution)/shard_map/ppermute | solution.py:251
